TPU v7x, 32 devices: a whole 2x2x4 slice. The times are simulated.
32 devices in a mesh: path: 2 (over x), dp: 4 (over y, core), mp: 4 (over z).
Axes of the slice: x: 2, y: 2, z: 4, core: 2. Of those that a mesh axis runs over, the one named last changes fastest.
Arguments:
- tokens: bfloat16 [8, 576, 1024], P('dp'), may hold values from -6 to 6
- hires: bfloat16 [8, 32, 32, 1536], P('dp', None, None, 'mp'), may hold values from -6 to 6
- valid_rows: int32 [8], P('dp'), may hold values from 1 to 24, 144 in all
- cotangent: bfloat16 [8, 576, 1024], P('dp'), may hold values from -6 to 6
- attention_norm_gain: float32 [1024], replicated, may hold values from 0.1 to 1.9
- attention_norm_bias: float32 [1024], replicated, may hold values from -1.5 to 1.5
- w_qkv: bfloat16 [1024, 3, 1024], P(None, None, 'mp'), may hold values from -0.1875 to 0.1875
- qv_bias: float32 [2, 1024], P(None, 'mp'), may hold values from -1.5 to 1.5
- w_out: bfloat16 [1024, 1024], P('mp'), may hold values from -0.75 to 0.75
- out_bias: float32 [1024], replicated, may hold values from -1.5 to 1.5
- mlp_norm_gain: float32 [1024], replicated, may hold values from 0.1 to 1.9
- mlp_norm_bias: float32 [1024], replicated, may hold values from -1.5 to 1.5
- w_fc1: bfloat16 [1024, 4096], P(None, 'mp'), may hold values from -0.1875 to 0.1875
- fc1_bias: float32 [4096], P('mp'), may hold values from -1.5 to 1.5
- down_weight: bfloat16 [4096, 1024], P('mp'), may hold values from -0.09375 to 0.09375
- fc2_bias: float32 [1024], replicated, may hold values from -1.5 to 1.5
- w_adapt: bfloat16 [1536, 1024], P('mp'), may hold values from -0.3125 to 0.3125
- gate_param: float32 [1024], replicated, may hold values from -2 to 2
- dw_kernel: float32 [49, 1536], P(None, 'mp'), may hold values from -0.875 to 0.875
- dw_bias: float32 [1536], P('mp'), may hold values from -1.5 to 1.5
- channel_norm_gain: float32 [1536], replicated, may hold values from 0.1 to 1.9
- channel_norm_bias: float32 [1536], replicated, may hold values from -1.5 to 1.5
- w_pw1: bfloat16 [1536, 6144], P(None, 'mp'), may hold values from -0.15625 to 0.15625
- pw1_bias: float32 [6144], P('mp'), may hold values from -1.5 to 1.5
- w_pw2: bfloat16 [6144, 1536], P('mp'), may hold values from -0.078125 to 0.078125
- pw2_bias: float32 [1536], P('mp'), may hold values from -1.5 to 1.5
- layer_scale: float32 [1536], P('mp'), may hold values from 0.3 to 2
Outputs:
- output: bfloat16 [8, 576, 1024], P('dp', 'path', 'mp')
- tokens_grad: bfloat16 [8, 576, 1024], P('dp', 'path', 'mp')
- hires_grad: bfloat16 [8, 32, 32, 1536], P('dp', 'path', None, 'mp')
- grad_norm1_gain: float32 [1024], replicated
- grad_norm1_bias: float32 [1024], replicated
- grad_w_qkv: float32 [1024, 3, 1024], P(('path', 'dp'), None, 'mp')
- grad_qv_bias: float32 [2, 1024], P(None, 'mp')
- grad_w_out: float32 [1024, 1024], P('mp', ('path', 'dp'))
- grad_out_bias: float32 [1024], replicated
- grad_norm2_gain: float32 [1024], replicated
- grad_norm2_bias: float32 [1024], replicated
- grad_w_fc1: float32 [1024, 4096], P(('path', 'dp'), 'mp')
- grad_fc1_bias: float32 [4096], P('mp')
- grad_w_fc2: float32 [4096, 1024], P('mp', ('path', 'dp'))
- grad_fc2_bias: float32 [1024], replicated
- grad_w_adapt: float32 [1536, 1024], P('mp', ('path', 'dp'))
- grad_gate_param: float32 [1024], replicated
- grad_dw_kernel: float32 [49, 1536], P(None, 'mp')
- grad_dw_bias: float32 [1536], P('mp')
- grad_cnorm_gain: float32 [1536], P('mp')
- grad_cnorm_bias: float32 [1536], P('mp')
- grad_w_pw1: float32 [1536, 6144], P(('path', 'dp'), 'mp')
- grad_pw1_bias: float32 [6144], P('mp')
- grad_w_pw2: float32 [6144, 1536], P('mp', ('path', 'dp'))
- grad_pw2_bias: float32 [1536], P('mp')
- grad_layer_scale: float32 [1536], P('mp')
Inputs may be any that keep to these rules, and one draw needn't show every extreme that they name: `valid_rows`: some image has all 24 rows valid in every draw.
All inputs are finite; a program needn't handle non-finite values. No bound on the sum of `valid_rows` on one device may be relied on, other than what follows from the above.
Results may differ from a plain program's by a relative error of at most 0.02.
Values may be sent and summed in bfloat16 or wider, within the bound.
No kernel may reach another device: no remote copies, remote signals or barrier semaphores. Data moves between devices by JAX's collectives and lax.ppermute only.
A program may use at most 448 MiB of HBM per device.

v0:
```python
import jax
import jax.numpy as jnp
from jax import lax
from jax.sharding import PartitionSpec as P

HEAD_DIM = 64
GRID_LO = 24
GRID_HI = 32


norm_epsilon = 1e-05
channel_epsilon = 1e-06


def passed_along(block, axis, distance):
    devices = range(lax.axis_size(axis))
    route = [(i - distance, i) for i in devices if i - distance in devices]
    return lax.ppermute(block, axis, route)


def from_partner(value, axis, apart):
    mask = 2**apart
    pairs = [(source, source ^ mask) for source in range(lax.axis_size(axis))]
    return lax.ppermute(value, axis, pairs)


def gelu(tensor):
    return (
        0.5
        * tensor
        * (1.0 + jnp.tanh(0.7978845608028654 * (tensor + 0.044715 * tensor * tensor * tensor)))
    )


def pool_weights():
    ratio = GRID_HI / GRID_LO
    target = jnp.arange(GRID_LO, dtype=jnp.float32)[:, None]
    source = jnp.arange(GRID_HI, dtype=jnp.float32)[None, :]
    lower = jnp.maximum(source, target * ratio)
    upper = jnp.minimum(source + 1.0, (target + 1.0) * ratio)
    return jnp.maximum(upper - lower, 0.0) / ratio


def depthwise(field, kernel, bias):
    extent = field.shape[1]
    padded = jnp.pad(field, ((0, 0), (3, 3), (3, 3), (0, 0)))
    result = jnp.zeros_like(field) + bias
    for offset_row in range(7):
        for offset_col in range(7):
            result = (
                result
                + padded[:, offset_row : offset_row + extent, offset_col : offset_col + extent, :]
                * kernel[offset_row * 7 + offset_col]
            )
    return result


def normalize_rows(tensor, eps):
    centred = tensor - jnp.mean(tensor, axis=-1, keepdims=True)
    inverse_deviation = lax.rsqrt(jnp.mean(centred * centred, axis=-1, keepdims=True) + eps)
    return (centred * inverse_deviation, inverse_deviation)


def norm_backward(standardized_gradient, standardized, inverse_deviation):
    return inverse_deviation * (
        standardized_gradient
        - jnp.mean(standardized_gradient, axis=-1, keepdims=True)
        - standardized * jnp.mean(standardized_gradient * standardized, axis=-1, keepdims=True)
    )


def matrix_product(left, right):
    return jnp.dot(left, right, preferred_element_type=jnp.float32)


def product_t(left, right):
    return lax.dot_general(
        left, right, (((1,), (1,)), ((), ())), preferred_element_type=jnp.float32
    )


def inner_rows(left, right):
    return lax.dot_general(
        left, right, (((0,), (0,)), ((), ())), preferred_element_type=jnp.float32
    )


def restricted_to(flag, build):
    return lax.cond(flag, build, lambda: jax.tree.map(jnp.zeros_like, build()))


def pick_half(tensor, reduce_axis, index):
    return lax.dynamic_index_in_dim(tensor, index, reduce_axis, keepdims=False)


def body(
    tokens,
    hires,
    valid_rows,
    cotangent,
    attention_norm_gain,
    attention_norm_bias,
    w_qkv,
    qv_bias,
    w_out,
    out_bias,
    mlp_norm_gain,
    mlp_norm_bias,
    w_fc1,
    fc1_bias,
    down_weight,
    fc2_bias,
    w_adapt,
    gate_param,
    dw_kernel,
    dw_bias,
    channel_norm_gain,
    channel_norm_bias,
    w_pw1,
    pw1_bias,
    w_pw2,
    pw2_bias,
    layer_scale,
):
    path_index = lax.axis_index("path")
    mp_index = lax.axis_index("mp")
    is_transformer = path_index == 0
    is_conv = path_index == 1
    images, length, width = tokens.shape
    rows_all = images * length
    local_width = w_qkv.shape[2]
    head_count = local_width // HEAD_DIM
    grid_size = hires.shape[1]
    channel_partial = hires.shape[3]
    channel_totals = w_pw1.shape[0]
    score_scale = HEAD_DIM ** (-0.5)
    lo_mask = (jnp.arange(GRID_LO)[None, :] < valid_rows[:, None]).astype(jnp.float32)
    hi_rows = (valid_rows * GRID_HI + GRID_LO - 1) // GRID_LO
    hi_mask = (jnp.arange(GRID_HI)[None, :] < hi_rows[:, None]).astype(jnp.float32)
    key_valid = jnp.repeat(lo_mask, GRID_LO, axis=1) > 0.5
    area = pool_weights()
    gate_value = jnp.tanh(gate_param)
    masked = hires.astype(jnp.float32) * hi_mask[:, :, None, None]
    input_rows = tokens.reshape(rows_all, width).astype(jnp.float32)
    dy_low = cotangent.reshape(rows_all, width)
    output_gradient_rows = dy_low.astype(jnp.float32)
    qkv_flat = w_qkv.reshape(width, 3 * local_width)

    def split_heads(tensor):
        return tensor.reshape(images, length, head_count, HEAD_DIM)

    def scores_of(query_matrix, key_matrix_rows):
        raw = (
            jnp.einsum(
                "nthd,nshd->nhts",
                split_heads(query_matrix),
                split_heads(key_matrix_rows),
                preferred_element_type=jnp.float32,
            )
            * score_scale
        )
        return jnp.where(key_valid[:, None, None, :], raw, -1e30)

    def attention_forward():
        first_standardized, first_inverse_std = normalize_rows(input_rows, norm_epsilon)
        first_normalized = (first_standardized * attention_norm_gain + attention_norm_bias).astype(
            jnp.bfloat16
        )
        mixed = matrix_product(first_normalized, qkv_flat).reshape(rows_all, 3, local_width)
        query_matrix = (mixed[:, 0] + qv_bias[0]).astype(jnp.bfloat16)
        key_matrix_rows = mixed[:, 1].astype(jnp.bfloat16)
        value_matrix_rows = (mixed[:, 2] + qv_bias[1]).astype(jnp.bfloat16)
        scores = scores_of(query_matrix, key_matrix_rows)
        row_max = jnp.max(scores, axis=-1, keepdims=True)
        exp_scores = jnp.exp(scores - row_max)
        exp_total = jnp.sum(exp_scores, axis=-1, keepdims=True)
        probs = (exp_scores / exp_total).astype(jnp.bfloat16)
        attended_rows = jnp.einsum(
            "nhts,nshd->nthd",
            probs,
            split_heads(value_matrix_rows),
            preferred_element_type=jnp.float32,
        )
        attended_rows = attended_rows.reshape(rows_all, local_width).astype(jnp.bfloat16)
        return (
            first_standardized,
            first_inverse_std,
            first_normalized,
            query_matrix,
            key_matrix_rows,
            value_matrix_rows,
            row_max + jnp.log(exp_total),
            attended_rows,
            matrix_product(attended_rows, w_out),
        )

    def conv_spatial():
        return depthwise(masked, dw_kernel, dw_bias).astype(jnp.bfloat16)

    (
        first_standardized,
        first_inverse_std,
        first_normalized,
        query_matrix,
        key_matrix_rows,
        value_matrix_rows,
        logarithm_total,
        attended_rows,
        attention_portion,
    ) = restricted_to(is_transformer, attention_forward)
    spatial = restricted_to(is_conv, conv_spatial)
    attn_sum = lax.psum(attention_portion.astype(jnp.bfloat16), "mp").astype(jnp.float32)

    def convnext_mlp(finish_branch):
        collected_rows = lax.all_gather(spatial, "mp", axis=3, tiled=True)

        def local_mlp():
            standardized, inverse_deviation = normalize_rows(
                collected_rows.astype(jnp.float32), channel_epsilon
            )
            normalized_rows = (
                (standardized * channel_norm_gain + channel_norm_bias)
                .astype(jnp.bfloat16)
                .reshape(-1, channel_totals)
            )
            hidden_units = matrix_product(normalized_rows, w_pw1) + pw1_bias
            activated_units = gelu(hidden_units).astype(jnp.bfloat16)
            if finish_branch:
                return (
                    standardized,
                    inverse_deviation,
                    normalized_rows,
                    hidden_units,
                    activated_units,
                    matrix_product(activated_units, w_pw2).reshape(
                        images, grid_size, grid_size, channel_totals
                    ),
                )
            return (standardized, inverse_deviation, normalized_rows, hidden_units, activated_units)

        kept = restricted_to(is_conv, local_mlp)
        if finish_branch:
            branch = (
                lax.psum_scatter(
                    kept[5].astype(jnp.bfloat16), "mp", scatter_dimension=3, tiled=True
                ).astype(jnp.float32)
                + pw2_bias
            )
            return kept[:5] + (branch,)
        return kept

    conv_first = convnext_mlp(True)
    branch_first = conv_first[5]

    def conv_pool():
        refined = masked + layer_scale * branch_first
        pooled = jnp.einsum("ia,nabc->nibc", area, refined)
        pooled = jnp.einsum("jb,nibc->nijc", area, pooled) * lo_mask[:, :, None, None]
        return pooled.astype(jnp.bfloat16).reshape(images, length, channel_partial)

    def feedforward_apply():
        first_hidden = input_rows + attn_sum + out_bias
        second_standardized, second_inverse_std = normalize_rows(first_hidden, norm_epsilon)
        second_normalized = (second_standardized * mlp_norm_gain + mlp_norm_bias).astype(
            jnp.bfloat16
        )
        dense_hidden = matrix_product(second_normalized, w_fc1) + fc1_bias
        dense_activated = gelu(dense_hidden).astype(jnp.bfloat16)
        return (
            first_hidden,
            second_standardized,
            second_inverse_std,
            second_normalized,
            dense_hidden,
            dense_activated,
            matrix_product(dense_activated, down_weight),
        )

    pooled = restricted_to(is_conv, conv_pool)
    (
        first_hidden,
        second_standardized,
        second_inverse_std,
        second_normalized,
        dense_hidden,
        dense_activated,
        feedforward_result,
    ) = restricted_to(is_transformer, feedforward_apply)
    arrived = passed_along(pooled, "path", -1)
    arrived_rows = arrived.reshape(rows_all, channel_partial)

    def adapter():
        adapted = matrix_product(arrived_rows, w_adapt)
        return (adapted, feedforward_result + gate_value * adapted)

    adapted, term = restricted_to(is_transformer, adapter)
    branch_sum = lax.psum(term.astype(jnp.bfloat16), "mp").astype(jnp.float32)

    def feed_back():
        d_adapted = (gate_value * output_gradient_rows).astype(jnp.bfloat16)
        gelu_out, gelu_pull = jax.vjp(gelu, dense_hidden)
        d_inner = gelu_pull(product_t(dy_low, down_weight))[0].astype(jnp.bfloat16)
        grads = (
            inner_rows(second_normalized, d_inner),
            jnp.sum(d_inner.astype(jnp.float32), axis=0),
            inner_rows(dense_activated, dy_low),
            inner_rows(arrived_rows, d_adapted),
        )
        d_pooled = (
            product_t(d_adapted, w_adapt)
            .astype(jnp.bfloat16)
            .reshape(images, length, channel_partial)
        )
        return (
            grads,
            product_t(d_inner, w_fc1),
            jnp.sum(output_gradient_rows * adapted, axis=0),
            d_pooled,
        )

    feed_grads, normed2_part, gate_part, d_pooled = restricted_to(is_transformer, feed_back)
    g_fc1, g_fc1_bias, g_fc2, g_adapt = feed_grads
    second_normalized_gradient, gate_sum = (
        lax.psum(normed2_part.astype(jnp.bfloat16), "mp").astype(jnp.float32),
        lax.psum(gate_part.astype(jnp.bfloat16), "mp").astype(jnp.float32),
    )
    returned = passed_along(d_pooled, "path", 1)
    (
        channel_centred_scaled,
        channel_inverse_std,
        channel_normalized,
        channel_hidden,
        channel_activated,
    ) = convnext_mlp(False)

    def attention_back():
        mlp_norm_gradients = (
            jnp.sum(second_normalized_gradient * second_standardized, axis=0),
            jnp.sum(second_normalized_gradient, axis=0),
        )
        hidden_gradient = output_gradient_rows + norm_backward(
            second_normalized_gradient * mlp_norm_gain, second_standardized, second_inverse_std
        )
        d_attn = hidden_gradient.astype(jnp.bfloat16)
        d_att = product_t(d_attn, w_out).astype(jnp.bfloat16)
        probs = jnp.exp(scores_of(query_matrix, key_matrix_rows) - logarithm_total)
        d_probs = jnp.einsum(
            "nthd,nshd->nhts",
            split_heads(d_att),
            split_heads(value_matrix_rows),
            preferred_element_type=jnp.float32,
        )
        delta = jnp.sum(probs * d_probs, axis=-1, keepdims=True)
        d_scores = (probs * (d_probs - delta)).astype(jnp.bfloat16)
        d_query = (
            jnp.einsum(
                "nhts,nshd->nthd",
                d_scores,
                split_heads(key_matrix_rows),
                preferred_element_type=jnp.float32,
            )
            * score_scale
        ).astype(jnp.bfloat16)
        d_keys = (
            jnp.einsum(
                "nhts,nthd->nshd",
                d_scores,
                split_heads(query_matrix),
                preferred_element_type=jnp.float32,
            )
            * score_scale
        ).astype(jnp.bfloat16)
        d_values = jnp.einsum(
            "nhts,nthd->nshd",
            probs.astype(jnp.bfloat16),
            split_heads(d_att),
            preferred_element_type=jnp.float32,
        ).astype(jnp.bfloat16)
        d_query = d_query.reshape(rows_all, local_width)
        d_values = d_values.reshape(rows_all, local_width)
        d_mixed = jnp.stack(
            [d_query, d_keys.reshape(rows_all, local_width), d_values], axis=1
        ).reshape(rows_all, 3 * local_width)
        bias_grad = jnp.stack(
            [
                jnp.sum(d_query.astype(jnp.float32), axis=0),
                jnp.sum(d_values.astype(jnp.float32), axis=0),
            ]
        )
        grads = (
            inner_rows(first_normalized, d_mixed).reshape(width, 3, local_width),
            bias_grad,
            inner_rows(attended_rows, d_attn),
            jnp.sum(d_attn.astype(jnp.float32), axis=0),
        ) + mlp_norm_gradients
        return (grads, hidden_gradient, product_t(d_mixed, qkv_flat))

    attn_grads, hidden_gradient, normed1_part = restricted_to(is_transformer, attention_back)
    g_qkv, g_qv_bias, g_out, g_out_bias, g_norm2_gain, g_norm2_bias = attn_grads
    first_normalized_gradient = lax.psum(normed1_part.astype(jnp.bfloat16), "mp").astype(
        jnp.float32
    )

    def finish():
        token_gradient = hidden_gradient + norm_backward(
            first_normalized_gradient * attention_norm_gain, first_standardized, first_inverse_std
        )
        result_rows = first_hidden + branch_sum + fc2_bias
        return (
            result_rows,
            token_gradient,
            jnp.sum(first_normalized_gradient * first_standardized, axis=0),
            jnp.sum(first_normalized_gradient, axis=0),
            jnp.sum(output_gradient_rows, axis=0),
            gate_sum * (1.0 - gate_value * gate_value),
        )

    result_rows, token_gradient, g_norm1_gain, g_norm1_bias, g_fc2_bias, g_gate = restricted_to(
        is_transformer, finish
    )

    def conv_back_first():
        d_pool = (
            returned.astype(jnp.float32).reshape(images, GRID_LO, GRID_LO, channel_partial)
            * lo_mask[:, :, None, None]
        )
        d_refined = jnp.einsum("jb,nijc->nibc", area, d_pool)
        d_refined = jnp.einsum("ia,nibc->nabc", area, d_refined)
        g_scale = jnp.sum(d_refined * branch_first, axis=(0, 1, 2))
        return (d_refined, g_scale, (layer_scale * d_refined).astype(jnp.bfloat16))

    d_refined, g_scale, d_branch = restricted_to(is_conv, conv_back_first)
    d_branch_all = lax.all_gather(d_branch, "mp", axis=3, tiled=True)

    def conv_back_second():
        d_flat = d_branch_all.reshape(-1, channel_totals)
        gelu_out, gelu_pull = jax.vjp(gelu, channel_hidden)
        d_inner = gelu_pull(product_t(d_flat, w_pw2))[0].astype(jnp.bfloat16)
        d_normed = product_t(d_inner, w_pw1).reshape(images, grid_size, grid_size, channel_totals)
        weighted_values = d_normed * channel_norm_gain
        row_stats = jnp.stack(
            [
                jnp.sum(weighted_values, axis=-1),
                jnp.sum(weighted_values * channel_centred_scaled, axis=-1),
            ],
            axis=-1,
        )
        tiled_stats = jnp.tile(row_stats, (1, 1, 1, lax.axis_size("mp")))
        grads = (
            inner_rows(channel_activated, d_flat),
            jnp.sum(d_branch.astype(jnp.float32), axis=(0, 1, 2)),
            inner_rows(channel_normalized, d_inner),
            jnp.sum(d_inner.astype(jnp.float32), axis=0),
        )
        return (grads, d_normed, tiled_stats)

    conv_grads, d_normed_all, tiled_stats = restricted_to(is_conv, conv_back_second)
    g_pw2, g_pw2_bias, g_pw1, g_pw1_bias = conv_grads
    partial_normalized_gradient, statistic_totals = (
        lax.psum_scatter(
            d_normed_all.astype(jnp.bfloat16), "mp", scatter_dimension=3, tiled=True
        ).astype(jnp.float32),
        lax.psum_scatter(
            tiled_stats.astype(jnp.bfloat16), "mp", scatter_dimension=3, tiled=True
        ).astype(jnp.float32),
    )

    def conv_back_third():
        start_offset = mp_index * channel_partial
        partial_standardized = lax.dynamic_slice_in_dim(
            channel_centred_scaled, start_offset, channel_partial, 3
        )
        partial_gain = lax.dynamic_slice_in_dim(channel_norm_gain, start_offset, channel_partial, 0)
        standardized_gradient = partial_normalized_gradient * partial_gain
        d_spatial = channel_inverse_std * (
            standardized_gradient
            - statistic_totals[..., 0:1] / channel_totals
            - partial_standardized * statistic_totals[..., 1:2] / channel_totals
        )
        conv_out, conv_pull = jax.vjp(depthwise, masked, dw_kernel, dw_bias)
        d_masked, g_kernel, g_dw_bias = conv_pull(d_spatial)
        d_hires = ((d_masked + d_refined) * hi_mask[:, :, None, None]).astype(jnp.bfloat16)
        return (
            jnp.sum(partial_normalized_gradient * partial_standardized, axis=(0, 1, 2)),
            jnp.sum(partial_normalized_gradient, axis=(0, 1, 2)),
            g_kernel,
            g_dw_bias,
            d_hires,
        )

    g_cnorm_gain, g_cnorm_bias, g_kernel, g_dw_bias, d_hires = restricted_to(
        is_conv, conv_back_third
    )

    def feature_halves(rows_value):
        sliced = lax.dynamic_slice_in_dim(rows_value, mp_index * local_width, local_width, 1)
        return sliced.astype(jnp.bfloat16).reshape(images, 2, length // 2, local_width)

    out_split = feature_halves(result_rows)
    dx_split = feature_halves(token_gradient)
    hr_split = d_hires.reshape(images, 2, grid_size // 2, grid_size, channel_partial)
    other_index = 1 - path_index
    groups = lax.axis_size("path") * lax.axis_size("dp")

    def tiled(tensor):
        return jnp.broadcast_to(tensor[None], (groups,) + tensor.shape)

    summed = (
        lax.psum_scatter(
            g_qkv.astype(jnp.bfloat16), ("path", "dp"), scatter_dimension=0, tiled=True
        ).astype(jnp.float32),
        lax.psum_scatter(
            g_out.astype(jnp.bfloat16), ("path", "dp"), scatter_dimension=1, tiled=True
        ).astype(jnp.float32),
        lax.psum_scatter(
            g_fc1.astype(jnp.bfloat16), ("path", "dp"), scatter_dimension=0, tiled=True
        ).astype(jnp.float32),
        lax.psum_scatter(
            g_fc2.astype(jnp.bfloat16), ("path", "dp"), scatter_dimension=1, tiled=True
        ).astype(jnp.float32),
        lax.psum_scatter(
            g_adapt.astype(jnp.bfloat16), ("path", "dp"), scatter_dimension=1, tiled=True
        ).astype(jnp.float32),
        lax.psum_scatter(
            g_pw1.astype(jnp.bfloat16), ("path", "dp"), scatter_dimension=0, tiled=True
        ).astype(jnp.float32),
        lax.psum_scatter(
            g_pw2.astype(jnp.bfloat16), ("path", "dp"), scatter_dimension=1, tiled=True
        ).astype(jnp.float32),
        lax.psum_scatter(
            tiled(g_norm1_gain).astype(jnp.bfloat16),
            ("path", "dp"),
            scatter_dimension=0,
            tiled=True,
        ).astype(jnp.float32),
        lax.psum_scatter(
            tiled(g_norm1_bias).astype(jnp.bfloat16),
            ("path", "dp"),
            scatter_dimension=0,
            tiled=True,
        ).astype(jnp.float32),
        lax.psum_scatter(
            tiled(g_qv_bias).astype(jnp.bfloat16), ("path", "dp"), scatter_dimension=0, tiled=True
        ).astype(jnp.float32),
        lax.psum_scatter(
            tiled(g_out_bias).astype(jnp.bfloat16), ("path", "dp"), scatter_dimension=0, tiled=True
        ).astype(jnp.float32),
        lax.psum_scatter(
            tiled(g_norm2_gain).astype(jnp.bfloat16),
            ("path", "dp"),
            scatter_dimension=0,
            tiled=True,
        ).astype(jnp.float32),
        lax.psum_scatter(
            tiled(g_norm2_bias).astype(jnp.bfloat16),
            ("path", "dp"),
            scatter_dimension=0,
            tiled=True,
        ).astype(jnp.float32),
        lax.psum_scatter(
            tiled(g_fc1_bias).astype(jnp.bfloat16), ("path", "dp"), scatter_dimension=0, tiled=True
        ).astype(jnp.float32),
        lax.psum_scatter(
            tiled(g_fc2_bias).astype(jnp.bfloat16), ("path", "dp"), scatter_dimension=0, tiled=True
        ).astype(jnp.float32),
        lax.psum_scatter(
            tiled(g_gate).astype(jnp.bfloat16), ("path", "dp"), scatter_dimension=0, tiled=True
        ).astype(jnp.float32),
        lax.psum_scatter(
            tiled(g_kernel).astype(jnp.bfloat16), ("path", "dp"), scatter_dimension=0, tiled=True
        ).astype(jnp.float32),
        lax.psum_scatter(
            tiled(g_dw_bias).astype(jnp.bfloat16), ("path", "dp"), scatter_dimension=0, tiled=True
        ).astype(jnp.float32),
        lax.psum_scatter(
            tiled(g_cnorm_gain).astype(jnp.bfloat16),
            ("path", "dp"),
            scatter_dimension=0,
            tiled=True,
        ).astype(jnp.float32),
        lax.psum_scatter(
            tiled(g_cnorm_bias).astype(jnp.bfloat16),
            ("path", "dp"),
            scatter_dimension=0,
            tiled=True,
        ).astype(jnp.float32),
        lax.psum_scatter(
            tiled(g_pw1_bias).astype(jnp.bfloat16), ("path", "dp"), scatter_dimension=0, tiled=True
        ).astype(jnp.float32),
        lax.psum_scatter(
            tiled(g_pw2_bias).astype(jnp.bfloat16), ("path", "dp"), scatter_dimension=0, tiled=True
        ).astype(jnp.float32),
        lax.psum_scatter(
            tiled(g_scale).astype(jnp.bfloat16), ("path", "dp"), scatter_dimension=0, tiled=True
        ).astype(jnp.float32),
    )
    big_grads = summed[:7]
    small_grads = tuple((member[0] for member in summed[7:]))
    recv_out, recv_dx, recv_hr = from_partner(
        (
            pick_half(out_split, 1, other_index),
            pick_half(dx_split, 1, other_index),
            pick_half(hr_split, 1, other_index),
        ),
        "path",
        0,
    )
    out_final = (
        pick_half(out_split, 1, path_index).astype(jnp.float32) + recv_out.astype(jnp.float32)
    ).astype(jnp.bfloat16)
    dx_final = (
        pick_half(dx_split, 1, path_index).astype(jnp.float32) + recv_dx.astype(jnp.float32)
    ).astype(jnp.bfloat16)
    hr_final = (
        pick_half(hr_split, 1, path_index).astype(jnp.float32) + recv_hr.astype(jnp.float32)
    ).astype(jnp.bfloat16)
    return (
        out_final,
        dx_final,
        hr_final,
        small_grads[0],
        small_grads[1],
        big_grads[0],
        small_grads[2],
        big_grads[1],
        small_grads[3],
        small_grads[4],
        small_grads[5],
        big_grads[2],
        small_grads[6],
        big_grads[3],
        small_grads[7],
        big_grads[4],
        small_grads[8],
        small_grads[9],
        small_grads[10],
        small_grads[11],
        small_grads[12],
        big_grads[5],
        small_grads[13],
        big_grads[6],
        small_grads[14],
        small_grads[15],
    )


def solution(mesh):
    in_specs = (
        P("dp", None, None),
        P("dp", None, None, "mp"),
        P("dp"),
        P("dp", None, None),
        P(),
        P(),
        P(None, None, "mp"),
        P(None, "mp"),
        P("mp", None),
        P(),
        P(),
        P(),
        P(None, "mp"),
        P("mp"),
        P("mp", None),
        P(),
        P("mp", None),
        P(),
        P(None, "mp"),
        P("mp"),
        P(),
        P(),
        P(None, "mp"),
        P("mp"),
        P("mp", None),
        P("mp"),
        P("mp"),
    )
    out_specs = (
        P("dp", "path", "mp"),
        P("dp", "path", "mp"),
        P("dp", "path", None, "mp"),
        P(),
        P(),
        P(("path", "dp"), None, "mp"),
        P(None, "mp"),
        P("mp", ("path", "dp")),
        P(),
        P(),
        P(),
        P(("path", "dp"), "mp"),
        P("mp"),
        P("mp", ("path", "dp")),
        P(),
        P("mp", ("path", "dp")),
        P(),
        P(None, "mp"),
        P("mp"),
        P("mp"),
        P("mp"),
        P(("path", "dp"), "mp"),
        P("mp"),
        P("mp", ("path", "dp")),
        P("mp"),
        P("mp"),
    )
    return jax.shard_map(body, mesh=mesh, in_specs=in_specs, out_specs=out_specs, check_vma=False)
```

profile of v0, /device:TPU:0, one launch (start us, length us, event | category | flops | bytes accessed | tf_op | source)
XLA Modules:
  0.0 1674.4 jit_solution(4075658553577933006)
XLA Ops:
  11.3 143.8 %all-gather.3.cloned.1.call-done = bf16[2,32,32,1536]{3,2,1,0:T(8,128)(2,1)} async-done(((bf16[2,32,32,384]{3,2,1,0:T(8,128)(2,1)}), bf16[2,32,32,1536]{3,2,1,0:T(8,128)(2,1)}) %all-gather.3.cloned.1.call-update) | async-done | bytes 6291472 | tf_op jit(solution)/shard_map/all_gather | solution.py:215
  155.1 19.5 %conditional.16 = (bf16[2,32,32,1536]{3,2,1,0:T(8,128)(2,1)}) conditional(s32[]{:T(128)} %convert_element_type.401, () %tuple.115, (bf16[2,32,32,1536]{3,2,1,0:T(8,128)(2,1)}, f32[1536]{0:T(1024)S(1)}, f32[1536]{0:T(1024)S(1)}, bf16[1536,1536]{1,0:T(8,128)(2,1)}, f32[1536]{0:T(1024)S(1)}, /*index=5*/bf16[1536,1536]{1,0:T(8,128)(2,1)}) %tuple.480), branch_computations={%region_13.14_spmd, %region_14.17_spmd} | conditional | flops 19396560896 | bytes 72443944 | solution.py:89
  174.6 9.0 copy.238
  183.6 33.7 %copy.186 = bf16[2,32,32,1536]{1,2,0,3:T(8,128)(2,1)} copy(bf16[2,32,32,1536]{3,1,2,0:T(8,128)(2,1)} %copy.238) | data formatting | bytes 12582912
  217.3 33.1 %reshape.714 = bf16[1536,2048]{1,0:T(8,128)(2,1)} reshape(bf16[1536,2,32,32]{3,2,1,0:T(8,128)(2,1)} %bitcast.208) | data formatting | bytes 12582912
  258.2 50.3 %conditional.13 = (f32[1152,1024]{1,0:T(8,128)}, f32[1152,1]{0,1:T(1,128)S(1)}, bf16[1152,1024]{1,0:T(8,128)(2,1)}, bf16[1152,256]{0,1:T(8,128)(2,1)}, bf16[1152...) conditional(s32[]{:T(128)} %convert_element_type.396, ...), branch_computations={%region_0.1_spmd, %region_1.6_spmd} | conditional | flops 3140514304 | bytes 147221600 | solution.py:89
  312.9 80.0 %reduce-scatter.34.cloned.1.call-done = bf16[384,2048]{1,0:T(8,128)(2,1)} async-done(((bf16[1536,2048]{1,0:T(8,128)(2,1)}), bf16[384,2048]{1,0:T(8,128)(2,1)}) %reduce-scatter.34.cloned.1.call-update) | async-done | bytes 1572880
  392.9 8.4 reshape.715
  401.3 8.8 copy.187
  420.3 71.1 %all-reduce.123.cloned.1.call-done = bf16[1152,1024]{1,0:T(8,128)(2,1)} async-done(((bf16[1152,1024]{1,0:T(8,128)(2,1)}), bf16[1152,1024]{1,0:T(8,128)(2,1)}) %all-reduce.123.cloned.1.call-update) | async-done | bytes 2359312 | tf_op jit(solution)/shard_map/psum | solution.py:212
  491.5 15.6 conditional.14
  512.2 6.2 conditional.18
  520.8 32.4 %conditional.19 = (bf16[1024,1024]{0,1:T(8,128)(2,1)}, bf16[1024]{0:T(1024)(128)(2,1)S(1)}, bf16[1024,1024]{1,0:T(8,128)(2,1)}, bf16[384,1024]{0,1:T(8,128)(2,1)...) conditional(s32[]{:T(128)} %convert_element_type.396, ...), branch_computations={%region_22.23_spmd, %region_23.26_spmd} | conditional | flops 11513804800 | bytes 136524064 | solution.py:89
  521.0 10.8 convert_reduce_fusion.1
  531.8 6.0 fusion.347
  554.6 19.4 %collective-permute-done.3 = bf16[2,576,384]{2,1,0:T(8,128)(2,1)S(1)} collective-permute-done((bf16[2,576,384]{2,1,0:T(8,128)(2,1)}, bf16[2,576,384]{2,1,0:T(8,128)(2,1)S(1)}, u32[]{:S(2)}, u32[]{:S(2)}) %collective-permute-start.3) | collective-permute-done | bytes 884768 | tf_op jit(solution)/shard_map/ppermute | solution.py:18
  583.8 63.3 %all-reduce.125.cloned.1.call-done = bf16[1152,1024]{1,0:T(8,128)(2,1)} async-done(((bf16[1152,1024]{1,0:T(8,128)(2,1)}), bf16[1152,1024]{1,0:T(8,128)(2,1)}) %all-reduce.125.cloned.1.call-update) | async-done | bytes 2359312 | tf_op jit(solution)/shard_map/psum | solution.py:324
  647.1 70.2 %conditional.20 = (bf16[1024,3,256]{0,2,1:T(8,128)(2,1)}, bf16[2,256]{1,0:T(2,128)(2,1)S(1)}, bf16[256,1024]{0,1:T(8,128)(2,1)}, bf16[1024]{0:T(1024)(128)(2,1)S...) conditional(s32[]{:T(128)} %convert_element_type.396, ...), branch_computations={%region_27.28_spmd, %region_28.37_spmd} | conditional | flops 6598649856 | bytes 299075968 | solution.py:89
  685.3 8.8 multiply_reduce_fusion.5
  737.3 18.5 %conditional.22 = (f32[2,32,32,1536]{3,2,1,0:T(8,128)}, f32[2,32,32,1]{2,1,0,3:T(8,128)S(1)}, bf16[2048,1536]{1,0:T(8,128)(2,1)}, f32[2048,1536]{1,0:T(8,128)}, bf16[2048,1536]{1,0:T(8,128)(2,1)}) conditional(s32[]{:T(128)} %convert_element_type.401, () %tuple.127, (bf16[2,32,32,1536]{3,2,1,0:T(8,128)(2,1)}, f32[1536]{0:T(1024)S(1)}, ...), branch_computations={%region_47.48_spmd, %region_48.51_spmd} | conditional | flops 9732884480 | bytes 107055216 | solution.py:89
  743.3 6.2 broadcast.454
  749.5 6.2 broadcast.451
  755.9 7.1 all-gather.5.cloned.1.call-done
  762.9 17.3 %conditional.24 = (bf16[1536,1536]{1,0:T(8,128)(2,1)}, bf16[384]{0:T(512)(128)(2,1)S(1)}, bf16[1536]{0:T(1024)(128)(2,1)S(1)}, f32[2,32,32,1536]{3,2,1,0:T(8,128...) conditional(s32[]{:T(128)} %convert_element_type.401, () %tuple.129, ...), branch_computations={%region_54.55_spmd, %region_55.60_spmd} | conditional | flops 38753796096 | bytes 182558640 | solution.py:89
  767.9 6.1 broadcast.467
  781.7 6.7 copy.174
  788.5 8.2 convert_element_type.424
  796.7 33.7 %copy.188 = bf16[2,32,32,1536]{2,1,0,3:T(8,128)(2,1)} copy(bf16[2,32,32,1536]{3,2,1,0:T(8,128)(2,1)} %convert_element_type.424) | data formatting | bytes 12582912
  830.4 33.4 %reshape.716 = bf16[1536,2048]{1,0:T(8,128)(2,1)} reshape(bf16[1536,2,32,32]{3,2,1,0:T(8,128)(2,1)} %bitcast.209) | data formatting | bytes 12582912
  864.4 10.2 psum.39
  874.6 61.4 %all-reduce.129.cloned.1.call-done = (bf16[1152,1024]{1,0:T(8,128)(2,1)}, bf16[1152,1024]{1,0:T(8,128)(2,1)}) async-done(((bf16[1152,1024]{1,0:T(8,128)(2,1)}, bf16[1152,1024]{1,0:T(8,128)(2,1)}), (bf16[1152,1024]{1,0:T(8,128)(2,1)}, bf16[1152,1024]{1,0:T(8,128)(2,1)})) %all-reduce.129.cloned.1.call-update) | async-done | bytes 4718608 | tf_op jit(solution)/shard_map/psum | solution.py:297
  936.1 18.7 %conditional.21 = (bf16[1152,1024]{1,0:T(8,128)(2,1)}, bf16[1152,1024]{1,0:T(8,128)(2,1)}, bf16[1024]{0:T(1024)(128)(2,1)S(1)}, bf16[1024]{0:T(1024)(128)(2,1)S(...) conditional(s32[]{:T(128)} %convert_element_type.396, () %tuple.108, (f32[1152,1024]{1,0:T(8,128)}, ...), branch_computations={%region_40.41_spmd, %region_41.47_spmd} | conditional | flops 24774656 | bytes 44904020 | solution.py:89
  936.1 5.4 fusion.206
  948.6 5.6 fusion.203
  959.8 15.8 reduce-scatter.42.cloned.1.call-done
  977.4 36.1 %reduce-scatter.38.cloned.1.call-done = bf16[128,256]{1,0:T(8,128)(2,1)} async-done(((bf16[1024,256]{1,0:T(8,128)(2,1)}), bf16[128,256]{1,0:T(8,128)(2,1)}) %reduce-scatter.38.cloned.1.call-update) | async-done | bytes 65552
  1015.1 43.3 %reduce-scatter.40.cloned.1.call-done = bf16[128,1024]{1,0:T(8,128)(2,1)} async-done(((bf16[1024,1024]{1,0:T(8,128)(2,1)}), bf16[128,1024]{1,0:T(8,128)(2,1)}) %reduce-scatter.40.cloned.1.call-update) | async-done | bytes 262160
  1060.3 42.4 %reduce-scatter.28.cloned.1.call-done = bf16[128,1024]{1,0:T(8,128)(2,1)} async-done(((bf16[1024,1024]{1,0:T(8,128)(2,1)}), bf16[128,1024]{1,0:T(8,128)(2,1)}) %reduce-scatter.28.cloned.1.call-update) | async-done | bytes 262160 | tf_op jit(solution)/shard_map/reduce_scatter | solution.py:515
  1104.5 40.4 %reduce-scatter.26.cloned.1.call-done = bf16[128,3,256]{2,0,1:T(8,128)(2,1)} async-done(((bf16[1024,3,256]{2,0,1:T(8,128)(2,1)}), bf16[128,3,256]{2,0,1:T(8,128)(2,1)}) %reduce-scatter.26.cloned.1.call-update) | async-done | bytes 196624 | tf_op jit(solution)/shard_map/reduce_scatter | solution.py:509
  1148.2 18.7 %reduce-scatter.24.cloned.1.call-done = bf16[2,32,32,2]{2,1,0,3:T(8,128)(2,1)} async-done(((bf16[2,32,32,8]{2,1,0,3:T(8,128)(2,1)}), bf16[2,32,32,2]{2,1,0,3:T(8,128)(2,1)}) %reduce-scatter.24.cloned.1.call-update) | async-done | bytes 8208 | tf_op jit(solution)/shard_map/reduce_scatter | solution.py:463
  1167.6 54.8 %reduce-scatter.30.cloned.1.call-done = bf16[192,1536]{1,0:T(8,128)(2,1)} async-done(((bf16[1536,1536]{1,0:T(8,128)(2,1)}), bf16[192,1536]{1,0:T(8,128)(2,1)}) %reduce-scatter.30.cloned.1.call-update) | async-done | bytes 589840 | tf_op jit(solution)/shard_map/reduce_scatter | solution.py:524
  1224.6 55.4 %reduce-scatter.32.cloned.1.call-done = bf16[1536,192]{0,1:T(8,128)(2,1)} async-done(((bf16[1536,1536]{0,1:T(8,128)(2,1)}), bf16[1536,192]{0,1:T(8,128)(2,1)}) %reduce-scatter.32.cloned.1.call-update) | async-done | bytes 589840 | tf_op jit(solution)/shard_map/reduce_scatter | solution.py:527
  1282.2 110.7 %reduce-scatter.36.cloned.1.call-done = bf16[384,2048]{1,0:T(8,128)(2,1)} async-done(((bf16[1536,2048]{1,0:T(8,128)(2,1)}), bf16[384,2048]{1,0:T(8,128)(2,1)}) %reduce-scatter.36.cloned.1.call-update) | async-done | bytes 1572880
  1393.0 8.4 reshape.717
  1401.3 7.9 copy.189
  1428.6 143.5 %collective-permute-start.4 = (bf16[2,16,32,384]{3,2,1,0:T(8,128)(2,1)S(1)}, bf16[2,16,32,384]{3,2,1,0:T(8,128)(2,1)S(1)}, u32[]{:S(2)}, u32[]{:S(2)}) collective-permute-start(bf16[2,16,32,384]{3,2,1,0:T(8,128)(2,1)S(1)} %dynamic-slice_bitcast_fusion), channel_id=1, source_target_pairs={{0,16},{16,0},{1,17},{17,1},{2,18},{18,2},{3,19},{19,3},{4,20},{20... | collective-permute-start | bytes 2359304 | tf_op jit(solution)/shard_map/ppermute | solution.py:24
  1572.8 55.5 %all-reduce.127.cloned.1.call-done = (bf16[8,1024]{1,0:T(8,128)(2,1)}, bf16[8,1024]{1,0:T(8,128)(2,1)}, bf16[8,2,256]{2,1,0:T(2,128)(2,1)}, bf16[8,1024]{1,0:T(8...) async-done(((bf16[8,1024]{1,0:T(8,128)(2,1)}, ...) | async-done | bytes 194576
  1657.2 6.8 reduce-scatter.44.cloned.1.call-done
  (394 shorter events, 316.5 us)
Async XLA Ops:
  7.2 147.9 %all-gather.3.cloned.1.call-start = ((), (), s32[]{:S(2)}) async-start(), calls=%async_computation.12 | async-start | bytes 7864320 | tf_op jit(solution)/shard_map/all_gather | solution.py:215
  9.7 403.8 %copy-start.2 = (f32[2,32,32,384]{3,2,1,0:T(8,128)}, f32[2,32,32,384]{3,2,1,0:T(8,128)S(1)}, u32[]{:S(2)}) copy-start(f32[2,32,32,384]{3,2,1,0:T(8,128)S(1)} %convert_multiply_fusion.9) | copy-start | bytes 9437188
  9.7 145.4 %copy-start.43 = (f32[1536]{0:T(1024)S(1)}, f32[1536]{0:T(1024)}, u32[]{:S(2)}) copy-start(f32[1536]{0:T(1024)} %param.73) | copy-start | bytes 18436
  9.7 145.4 %copy-start.50 = (f32[1536]{0:T(1024)S(1)}, f32[1536]{0:T(1024)}, u32[]{:S(2)}) copy-start(f32[1536]{0:T(1024)} %param.74) | copy-start | bytes 18436
  9.8 145.4 %copy-start.110 = (f32[1536]{0:T(1024)S(1)}, f32[1536]{0:T(1024)}, u32[]{:S(2)}) copy-start(f32[1536]{0:T(1024)} %param.76) | copy-start | bytes 18436
  11.3 381.6 %reduce-scatter.34.cloned.1.call-start = ((), (), s32[]{:S(2)}) async-start(), calls=%async_computation.20 | async-start | bytes 7864320
  250.4 241.1 %all-reduce.123.cloned.1.call-start = ((), (), s32[]{:S(2)}) async-start(), calls=%async_computation.11 | async-start | bytes 4718592 | tf_op jit(solution)/shard_map/psum | solution.py:212
  312.8 334.3 %all-reduce.125.cloned.1.call-start = ((), (), s32[]{:S(2)}) async-start(), calls=%async_computation.13 | async-start | bytes 4718592 | tf_op jit(solution)/shard_map/psum | solution.py:324
  414.5 92.7 %collective-permute-start = (bf16[2,576,384]{2,1,0:T(8,128)(2,1)}, bf16[2,576,384]{2,1,0:T(8,128)(2,1)}, u32[]{:S(2)}, u32[]{:S(2)}) collective-permute-start(bf16[2,576,384]{2,1,0:T(8,128)(2,1)} %get-tuple-element.1078), channel_id=1, source_target_pairs={{16,0},{17,1},{18,2},{19,3},{20,4},{21,5},{22,6},{23,7},{24,8},{25... | collective-permute-start | bytes 2654216 | tf_op jit(solution)/shard_map/ppermute | solution.py:18
  415.8 102.6 %copy-start.45 = (f32[1024]{0:T(1024)}, f32[1024]{0:T(1024)S(1)}, u32[]{:S(2)}) copy-start(f32[1024]{0:T(1024)S(1)} %tanh.18) | copy-start | bytes 12292
  415.8 75.7 %copy-start.49 = (f32[1024]{0:T(1024)S(1)}, f32[1024]{0:T(1024)}, u32[]{:S(2)}) copy-start(f32[1024]{0:T(1024)} %param.63) | copy-start | bytes 12292
  415.8 75.6 %copy-start.91 = (f32[1024]{0:T(1024)S(1)}, f32[1024]{0:T(1024)}, u32[]{:S(2)}) copy-start(f32[1024]{0:T(1024)} %param.64) | copy-start | bytes 12292
  415.8 75.6 %copy-start.92 = (f32[1024]{0:T(1024)S(1)}, f32[1024]{0:T(1024)}, u32[]{:S(2)}) copy-start(f32[1024]{0:T(1024)} %param.62) | copy-start | bytes 12292
  415.9 75.6 %copy-start.107 = (bf16[1024,1024]{1,0:T(8,128)(2,1)S(1)}, bf16[1024,1024]{1,0:T(8,128)(2,1)}, u32[]{:S(2)}) copy-start(bf16[1024,1024]{1,0:T(8,128)(2,1)} %param.65) | copy-start | bytes 6291460
  415.9 75.6 %copy-start.112 = (f32[1024]{0:T(1024)S(1)}, f32[1024]{0:T(1024)}, u32[]{:S(2)}) copy-start(f32[1024]{0:T(1024)} %param.66) | copy-start | bytes 12292
  491.5 15.7 copy-start.28
  518.4 55.6 %copy-start.10 = (f32[2,32,32,384]{3,1,2,0:T(8,128)S(1)}, f32[2,32,32,384]{3,1,2,0:T(8,128)}, u32[]{:S(2)}) copy-start(f32[2,32,32,384]{3,1,2,0:T(8,128)} %convert_add_fusion.1) | copy-start | bytes 9437188
  521.0 10.9 copy-start.13
  521.0 10.9 copy-start.33
  553.1 20.8 %copy-start.63 = (bf16[1024]{0:T(1024)(128)(2,1)}, bf16[1024]{0:T(1024)(128)(2,1)S(1)}, u32[]{:S(2)}) copy-start(bf16[1024]{0:T(1024)(128)(2,1)S(1)} %get-tuple-element.438) | copy-start | bytes 6148
  553.1 20.8 %copy-start.66 = (bf16[1024]{0:T(1024)(128)(2,1)}, bf16[1024]{0:T(1024)(128)(2,1)S(1)}, u32[]{:S(2)}) copy-start(bf16[1024]{0:T(1024)(128)(2,1)S(1)} %get-tuple-element.415) | copy-start | bytes 6148
  553.2 209.8 %all-gather.5.cloned.1.call-start = ((), (), s32[]{:S(2)}) async-start(), calls=%async_computation.14 | async-start | bytes 7864320 | tf_op jit(solution)/shard_map/all_gather | solution.py:433
  553.2 20.8 %collective-permute-start.3 = (bf16[2,576,384]{2,1,0:T(8,128)(2,1)}, bf16[2,576,384]{2,1,0:T(8,128)(2,1)S(1)}, u32[]{:S(2)}, u32[]{:S(2)}) collective-permute-start(bf16[2,576,384]{2,1,0:T(8,128)(2,1)} %get-tuple-element.419), channel_id=1, source_target_pairs={{0,16},{1,17},{2,18},{3,19},{4,20},{5,21},{6,22},{7,23},{8,24},{9,... | collective-permute-start | bytes 2654216 | tf_op jit(solution)/shard_map/ppermute | solution.py:18
  579.5 356.6 %all-reduce.129.cloned.1.call-start = ((), (), s32[]{:S(2)}) async-start(), calls=%async_computation.27 | async-start | bytes 9437184 | tf_op jit(solution)/shard_map/psum | solution.py:297
  579.5 67.6 %copy-start.37 = (bf16[256,1024]{1,0:T(8,128)(2,1)S(1)}, bf16[256,1024]{1,0:T(8,128)(2,1)}, u32[]{:S(2)}) copy-start(bf16[256,1024]{1,0:T(8,128)(2,1)} %param.61) | copy-start | bytes 1572868
  682.3 11.8 slice-start.2
  721.5 254.1 %reduce-scatter.42.cloned.1.call-start = ((), (), s32[]{:S(2)}) async-start(), calls=%async_computation.24 | async-start | bytes 884736
  724.2 289.3 %reduce-scatter.38.cloned.1.call-start = ((), (), s32[]{:S(2)}) async-start(), calls=%async_computation.22 | async-start | bytes 589824
  726.5 331.9 %reduce-scatter.40.cloned.1.call-start = ((), (), s32[]{:S(2)}) async-start(), calls=%async_computation.23 | async-start | bytes 2359296
  730.5 372.2 %reduce-scatter.28.cloned.1.call-start = ((), (), s32[]{:S(2)}) async-start(), calls=%async_computation.17 | async-start | bytes 2359296 | tf_op jit(solution)/shard_map/reduce_scatter | solution.py:515
  734.6 410.3 %reduce-scatter.26.cloned.1.call-start = ((), (), s32[]{:S(2)}) async-start(), calls=%async_computation.16 | async-start | bytes 1769472 | tf_op jit(solution)/shard_map/reduce_scatter | solution.py:509
  737.2 429.6 %reduce-scatter.24.cloned.1.call-start = ((), (), s32[]{:S(2)}) async-start(), calls=%async_computation.15 | async-start | bytes 163840 | tf_op jit(solution)/shard_map/reduce_scatter | solution.py:463
  737.3 25.6 %copy-start.18 = (bf16[2,32,32,384]{3,1,2,0:T(8,128)(2,1)S(1)}, bf16[2,32,32,384]{3,1,2,0:T(8,128)(2,1)}, u32[]{:S(2)}) copy-start(bf16[2,32,32,384]{3,1,2,0:T(8,128)(2,1)} %copy-done.17) | copy-start | bytes 4718596
  780.9 441.5 %reduce-scatter.30.cloned.1.call-start = ((), (), s32[]{:S(2)}) async-start(), calls=%async_computation.18 | async-start | bytes 5308416 | tf_op jit(solution)/shard_map/reduce_scatter | solution.py:524
  781.7 498.3 %reduce-scatter.32.cloned.1.call-start = ((), (), s32[]{:S(2)}) async-start(), calls=%async_computation.19 | async-start | bytes 5308416 | tf_op jit(solution)/shard_map/reduce_scatter | solution.py:527
  788.4 604.5 %reduce-scatter.36.cloned.1.call-start = ((), (), s32[]{:S(2)}) async-start(), calls=%async_computation.21 | async-start | bytes 7864320
  863.7 72.3 %copy-start.46 = (f32[1024]{0:T(1024)S(1)}, f32[1024]{0:T(1024)}, u32[]{:S(2)}) copy-start(f32[1024]{0:T(1024)} %copy-done.45) | copy-start | bytes 12292
  863.8 72.3 %copy-start.48 = (f32[1024]{0:T(1024)S(1)}, f32[1024]{0:T(1024)}, u32[]{:S(2)}) copy-start(f32[1024]{0:T(1024)} %param.57) | copy-start | bytes 12292
  863.8 72.3 %copy-start.54 = (f32[1152,1]{0,1:T(1,128)S(1)}, f32[1152,1]{0,1:T(1,128)}, u32[]{:S(2)}) copy-start(f32[1152,1]{0,1:T(1,128)} %copy-done.53) | copy-start | bytes 13828
  863.8 72.3 %copy-start.93 = (f32[1024]{0:T(1024)S(1)}, f32[1024]{0:T(1024)}, u32[]{:S(2)}) copy-start(f32[1024]{0:T(1024)} %param.68) | copy-start | bytes 12292
  863.8 764.6 %all-reduce.127.cloned.1.call-start = ((), (), s32[]{:S(2)}) async-start(), calls=%async_computation.26 | async-start | bytes 389120
  954.7 149.8 %copy-start.65 = (bf16[1024]{0:T(1024)(128)(2,1)}, bf16[1024]{0:T(1024)(128)(2,1)S(1)}, u32[]{:S(2)}) copy-start(bf16[1024]{0:T(1024)(128)(2,1)S(1)} %get-tuple-element.429) | copy-start | bytes 6148
  955.9 190.7 %collective-permute-start.2 = (bf16[2,288,256]{2,1,0:T(8,128)(2,1)S(1)}, bf16[2,288,256]{2,1,0:T(8,128)(2,1)S(1)}, u32[]{:S(2)}, u32[]{:S(2)}) collective-permute-start(bf16[2,288,256]{2,1,0:T(8,128)(2,1)S(1)} %dynamic-slice_bitcast_fusion.1), channel_id=1, source_target_pairs={{0,16},{16,0},{1,17},{17,1},{2,18},{18,2},{3,19},{19,3},{4,20},{20... | collective-permute-start | bytes 884744 | tf_op jit(solution)/shard_map/ppermute | solution.py:24
  957.1 190.3 %collective-permute-start.1 = (bf16[2,288,256]{2,1,0:T(8,128)(2,1)S(1)}, bf16[2,288,256]{2,1,0:T(8,128)(2,1)S(1)}, u32[]{:S(2)}, u32[]{:S(2)}) collective-permute-start(bf16[2,288,256]{2,1,0:T(8,128)(2,1)S(1)} %dynamic-slice_bitcast_fusion.2), channel_id=1, source_target_pairs={{0,16},{16,0},{1,17},{17,1},{2,18},{18,2},{3,19},{19,3},{4,20},{20... | collective-permute-start | bytes 884744 | tf_op jit(solution)/shard_map/ppermute | solution.py:24
  1411.3 10.6 copy-start.64
  1411.3 13.6 copy-start.56
  1427.3 236.7 %reduce-scatter.44.cloned.1.call-start = ((), (), s32[]{:S(2)}) async-start(), calls=%async_computation.25 | async-start | bytes 387072
  1428.6 236.8 %collective-permute-start.4 = (bf16[2,16,32,384]{3,2,1,0:T(8,128)(2,1)S(1)}, bf16[2,16,32,384]{3,2,1,0:T(8,128)(2,1)S(1)}, u32[]{:S(2)}, u32[]{:S(2)}) collective-permute-start(bf16[2,16,32,384]{3,2,1,0:T(8,128)(2,1)S(1)} %dynamic-slice_bitcast_fusion), channel_id=1, source_target_pairs={{0,16},{16,0},{1,17},{17,1},{2,18},{18,2},{3,19},{19,3},{4,20},{20... | collective-permute-start | bytes 2359304 | tf_op jit(solution)/shard_map/ppermute | solution.py:24
  (62 other events, 280.8 us)
Sparse Core Ops, SparseCore 0:
  11.4 143.6 all-gather.2
  250.5 142.3 reduce-scatter.33
  395.3 96.1 all-reduce.122
  553.3 93.7 all-reduce.124
  648.5 114.3 all-gather.4
  765.2 170.7 all-reduce.128
  939.8 35.8 reduce-scatter.41
  979.3 34.1 reduce-scatter.37
  1017.1 41.2 reduce-scatter.39
  1061.5 41.1 reduce-scatter.27
  1106.4 38.4 reduce-scatter.25
  1147.7 19.1 reduce-scatter.23
  1170.3 52.0 reduce-scatter.29
  1226.1 53.8 reduce-scatter.31
  1282.2 110.7 reduce-scatter.35
  1427.5 200.8 all-reduce.126
  1631.9 32.1 reduce-scatter.43
where the time goes:
time: 1680 us; the launch traced here: 1670 us
  waiting for transfers between devices  927 us (55%)
  local copies, waits for them, and re-layouts  312 us (19%)
  starting transfers between devices  149 us (9%)
  other arithmetic  137 us (8%)
  matrix products  97.5 us (6%)
  loops' own time  26.7 us (2%)
    unnamed x24, waiting for transfers between devices  349 us
    unnamed x126, local copies, waits for them, and re-layouts  190 us
    ppermute x3, starting transfers between devices, from_partner(): return lax.ppermute(value, axis, pairs)  146 us
    all_gather x1, waiting for transfers between devices, convnext_mlp(): collected_rows = lax.all_gather(spatial, 'mp', axis=3, tiled=True)  144 us
    psum x1, waiting for transfers between devices, body(): lax.psum(attention_portion.astype(jnp.bfloat16), 'mp').astype(jnp.float32)  71.1 us
    psum x1, waiting for transfers between devices, body(): lax.psum(normed2_part.astype(jnp.bfloat16), 'mp').astype(jnp.float32)  63.3 us
    psum x1, waiting for transfers between devices, body(): branch_sum = lax.psum(term.astype(jnp.bfloat16), 'mp').astype(jnp.float32)  61.4 us
    reduce_scatter x1, waiting for transfers between devices, body(): lax.psum_scatter(g_pw2.astype(jnp.bfloat16), ('path', 'dp'), scatter_dime...  55.4 us
  transfers between devices with their start and end apart: 22, of which 18 were waited for; matrix products, arithmetic and copies ran while one was open for 23% of the time, Pallas kernels for 0%

commit v1 on v0

v1 whole, which is shorter than its diff:
```python
import jax
import jax.numpy as jnp
import numpy as np
from jax import lax
from jax.sharding import PartitionSpec as P

HEAD_DIM = 64
GRID_LO = 24
GRID_HI = 32
TOKENS = GRID_LO * GRID_LO
CELLS = GRID_HI * GRID_HI

norm_epsilon = 1e-05
channel_epsilon = 1e-06
F32 = jnp.float32
BF16 = jnp.bfloat16


def gelu(v):
    return 0.5 * v * (1.0 + jnp.tanh(0.7978845608028654 * (v + 0.044715 * v * v * v)))


def gelu_pair(v):
    c = 0.7978845608028654
    square = v * v
    t = jnp.tanh(c * v * (1.0 + 0.044715 * square))
    half = 0.5 * (1.0 + t)
    return v * half, half + 0.5 * v * (1.0 - t * t) * c * (1.0 + 3 * 0.044715 * square)


def pool_rows():
    ratio = GRID_HI / GRID_LO
    target = np.arange(GRID_LO, dtype=np.float64)[:, None]
    source = np.arange(GRID_HI, dtype=np.float64)[None, :]
    lower = np.maximum(source, target * ratio)
    upper = np.minimum(source + 1.0, (target + 1.0) * ratio)
    return np.round(np.maximum(upper - lower, 0.0) / ratio * 4) / 4


def pool_matrix():
    side = pool_rows()
    return jnp.asarray(np.kron(side, side), BF16)


def dot(a, b):
    return jnp.dot(a, b, preferred_element_type=F32)


def dot_nt(a, b):
    return lax.dot_general(a, b, (((1,), (1,)), ((), ())), preferred_element_type=F32)


def dot_tn(a, b):
    return lax.dot_general(a, b, (((0,), (0,)), ((), ())), preferred_element_type=F32)


def standardize(v, eps):
    centred = v - jnp.mean(v, axis=-1, keepdims=True)
    inv = lax.rsqrt(jnp.mean(centred * centred, axis=-1, keepdims=True) + eps)
    return centred * inv, inv


def depthwise(field, kernel, bias):
    extent = field.shape[0]
    padded = jnp.pad(field, ((3, 3), (3, 3), (0, 0)))
    result = jnp.zeros_like(field) + bias
    for r in range(7):
        for s in range(7):
            result = result + padded[r : r + extent, s : s + extent, :] * kernel[r * 7 + s]
    return result


def swap(value, axis, apart):
    n = lax.axis_size(axis)
    return lax.ppermute(value, axis, [(i, i ^ apart) for i in range(n)])


def pick(value, axis, index):
    return lax.dynamic_index_in_dim(value, index, axis, keepdims=False)


def halve(value, dim, axis, apart, bit):
    received = swap(pick(value, dim, 1 - bit), axis, apart)
    return pick(value, dim, bit).astype(F32) + received.astype(F32)


def sum_blocks(value, last_dtype=F32):
    n_path, n_dp = lax.axis_size("path"), lax.axis_size("dp")
    me_path, me_dp = lax.axis_index("path"), lax.axis_index("dp")
    rest = value.shape[1:]
    value = value.astype(BF16)
    size = n_dp
    bit = 0
    while size > 1:
        size //= 2
        value = halve(
            value.reshape((n_path, size, 2) + rest), 2, "dp", 1 << bit, (me_dp >> bit) & 1
        )
        if size > 1 or n_path > 1:
            value = value.astype(BF16)
        bit += 1
    if n_path > 1:
        value = value.reshape((n_path,) + rest)
        value = halve(value, 0, "path", 1, me_path)
    return value.reshape(rest)


def body(
    tokens,
    hires,
    valid_rows,
    cotangent,
    attention_norm_gain,
    attention_norm_bias,
    w_qkv,
    qv_bias,
    w_out,
    out_bias,
    mlp_norm_gain,
    mlp_norm_bias,
    w_fc1,
    fc1_bias,
    down_weight,
    fc2_bias,
    w_adapt,
    gate_param,
    dw_kernel,
    dw_bias,
    channel_norm_gain,
    channel_norm_bias,
    w_pw1,
    pw1_bias,
    w_pw2,
    pw2_bias,
    layer_scale,
):
    path = lax.axis_index("path")
    n_path = lax.axis_size("path")
    mp = lax.axis_index("mp")
    n_mp = lax.axis_size("mp")
    groups = n_path * lax.axis_size("dp")
    assert tokens.shape[0] == n_path == 2
    width = tokens.shape[2]
    heads_width = w_qkv.shape[2]
    head_count = heads_width // HEAD_DIM
    channels = hires.shape[3]
    all_channels = w_pw1.shape[0]
    part_rows = TOKENS // n_mp
    score_scale = HEAD_DIM ** (-0.5)
    pool = pool_matrix()

    valid = pick(valid_rows, 0, path)
    hi_valid = (valid * GRID_HI + GRID_LO - 1) // GRID_LO
    lo_mask = (jnp.arange(TOKENS) < valid * GRID_LO).astype(F32)[:, None]
    hi_mask = (jnp.arange(GRID_HI) < hi_valid).astype(F32)[:, None, None]
    key_valid = jnp.arange(TOKENS) < valid * GRID_LO

    x_rows = pick(tokens, 0, path)
    dy = pick(cotangent, 0, path)
    field = pick(hires, 0, path)
    gate = jnp.tanh(gate_param)

    d_adapted = (gate * dy.astype(F32)).astype(BF16)
    d_pooled = dot_nt(d_adapted, w_adapt).astype(BF16).astype(F32) * lo_mask
    scaled_back = (d_pooled * layer_scale).astype(BF16)
    d_pooled = d_pooled.astype(BF16)

    masked = field.astype(F32) * hi_mask
    spatial = depthwise(masked, dw_kernel, dw_bias).astype(BF16).reshape(CELLS, channels)
    spatial_all = lax.all_gather(spatial, "mp", axis=0, tiled=False)
    scaled_back_all = lax.all_gather(scaled_back, "mp", axis=0, tiled=False)

    xhat1, inv1 = standardize(x_rows.astype(F32), norm_epsilon)
    normed1 = (xhat1 * attention_norm_gain + attention_norm_bias).astype(BF16)
    qkv_flat = w_qkv.reshape(width, 3 * heads_width)
    mixed = dot(normed1, qkv_flat)
    query = (mixed[:, :heads_width] + qv_bias[0]).astype(BF16)
    keys = mixed[:, heads_width : 2 * heads_width].astype(BF16)
    values = (mixed[:, 2 * heads_width :] + qv_bias[1]).astype(BF16)

    def split_heads(v):
        return v.reshape(TOKENS, head_count, HEAD_DIM)

    def scores_of():
        raw = jnp.einsum(
            "thd,shd->hts", split_heads(query), split_heads(keys), preferred_element_type=F32
        )
        return jnp.where(key_valid[None, None, :], raw * score_scale, -1e30)

    scores = scores_of()
    row_max = jnp.max(scores, axis=-1, keepdims=True)
    exp_scores = jnp.exp(scores - row_max)
    exp_total = jnp.sum(exp_scores, axis=-1, keepdims=True)
    probs = (exp_scores / exp_total).astype(BF16)
    log_total = row_max + jnp.log(exp_total)
    attended = (
        jnp.einsum("hts,shd->thd", probs, split_heads(values), preferred_element_type=F32)
        .reshape(TOKENS, heads_width)
        .astype(BF16)
    )
    attention_part = dot(attended, w_out)
    attn_sum = lax.psum(attention_part.astype(BF16), "mp").astype(F32)

    spatial_full = spatial_all.transpose(1, 0, 2).reshape(CELLS, all_channels).astype(F32)
    chat, cinv = standardize(spatial_full, channel_epsilon)
    conv_normed = (chat * channel_norm_gain + channel_norm_bias).astype(BF16)
    conv_active, conv_slope = gelu_pair(dot(conv_normed, w_pw1) + pw1_bias)
    conv_active = conv_active.astype(BF16)
    back_full = scaled_back_all.transpose(1, 0, 2).reshape(TOKENS, all_channels)
    pooled_active = dot(pool, conv_active).astype(BF16)
    w_pw2_blocks = w_pw2.reshape(-1, n_mp, channels)
    branch_part = jnp.einsum("rh,hgc->grc", pooled_active, w_pw2_blocks, preferred_element_type=F32)
    branch_pooled = lax.psum_scatter(
        branch_part.astype(BF16), "mp", scatter_dimension=0, tiled=False
    ).astype(F32)
    branch_pooled = branch_pooled + pw2_bias

    d_active_low = dot_nt(back_full, w_pw2).astype(BF16)
    d_active = dot_tn(pool, d_active_low)
    d_conv_inner = (conv_slope * d_active).astype(BF16)
    w_pw1_blocks = w_pw1.reshape(n_mp, channels, -1)
    d_normed_c = jnp.einsum("rh,gch->grc", d_conv_inner, w_pw1_blocks, preferred_element_type=F32)
    gain_blocks = channel_norm_gain.reshape(n_mp, 1, channels)
    weighted = d_normed_c * gain_blocks
    chat_blocks = (spatial_all.astype(F32) - jnp.mean(spatial_full, axis=-1)[None, :, None]) * cinv
    conv_stats = jnp.stack(
        [jnp.sum(weighted, axis=(0, 2)), jnp.sum(weighted * chat_blocks, axis=(0, 2))]
    )
    d_normed_mine = lax.psum_scatter(
        d_normed_c.astype(BF16), "mp", scatter_dimension=0, tiled=False
    ).astype(F32)
    conv_stats = lax.psum(conv_stats, "mp")

    g_pw1 = dot_tn(conv_normed, d_conv_inner)
    g_pw1_bias = jnp.sum(d_conv_inner.astype(F32), axis=0)
    g_pw2_t = dot_tn(back_full, pooled_active)
    g_pw2_bias = jnp.sum(scaled_back.astype(F32), axis=0)
    g_pw1_mine = sum_blocks(g_pw1.reshape(groups, -1, g_pw1.shape[1]))
    g_pw2_mine = sum_blocks(g_pw2_t.reshape(groups, -1, g_pw2_t.shape[1])).T

    hidden1 = x_rows.astype(F32) + attn_sum + out_bias
    xhat2, inv2 = standardize(hidden1, norm_epsilon)
    normed2 = (xhat2 * mlp_norm_gain + mlp_norm_bias).astype(BF16)
    fc_active, fc_slope = gelu_pair(dot(normed2, w_fc1) + fc1_bias)
    fc_active = fc_active.astype(BF16)
    d_fc_inner = (fc_slope * dot_nt(dy, down_weight)).astype(BF16)
    d_normed2_part = dot_nt(d_fc_inner, w_fc1).reshape(n_mp, part_rows, width)
    d_normed2 = lax.psum_scatter(
        d_normed2_part.astype(BF16), "mp", scatter_dimension=0, tiled=False
    ).astype(F32)
    xhat2_part = lax.dynamic_slice_in_dim(xhat2, mp * part_rows, part_rows, 0)
    inv2_part = lax.dynamic_slice_in_dim(inv2, mp * part_rows, part_rows, 0)
    dy_part = lax.dynamic_slice_in_dim(dy, mp * part_rows, part_rows, 0).astype(F32)
    dxhat2 = d_normed2 * mlp_norm_gain
    d_hidden_part = dy_part + inv2_part * (
        dxhat2
        - jnp.mean(dxhat2, axis=-1, keepdims=True)
        - xhat2_part * jnp.mean(dxhat2 * xhat2_part, axis=-1, keepdims=True)
    )
    d_attn_part = d_hidden_part.astype(BF16)
    d_attn = lax.all_gather(d_attn_part, "mp", axis=0, tiled=True)
    g_norm2_gain = jnp.sum(d_normed2 * xhat2_part, axis=0)
    g_norm2_bias = jnp.sum(d_normed2, axis=0)
    g_out_bias = jnp.sum(d_attn_part.astype(F32), axis=0)

    g_fc1_mine = sum_blocks(dot_tn(normed2, d_fc_inner).reshape(groups, -1, d_fc_inner.shape[1]))
    g_fc2_mine = sum_blocks(dot_tn(dy, fc_active).reshape(groups, -1, fc_active.shape[1])).T
    g_fc1_bias = jnp.sum(d_fc_inner.astype(F32), axis=0)

    field_low = (field.astype(F32) * hi_mask).astype(BF16).reshape(CELLS, channels)
    pooled = (lo_mask * (dot(pool, field_low) + layer_scale * branch_pooled)).astype(BF16)
    g_scale = jnp.sum(d_pooled.astype(F32) * branch_pooled, axis=0)
    adapted = dot(pooled, w_adapt)
    g_gate = (1.0 - gate * gate) * jnp.sum(dy.astype(F32) * adapted, axis=0)
    term = (dot(fc_active, down_weight) + gate * adapted).astype(BF16)
    term = term.reshape(TOKENS, n_mp, heads_width).transpose(1, 0, 2)
    branch_sum = lax.psum_scatter(term, "mp", scatter_dimension=0, tiled=False).astype(F32)
    g_adapt_mine = sum_blocks(dot_tn(d_adapted, pooled).reshape(groups, -1, channels)).T

    def my_features(v):
        return lax.dynamic_slice_in_dim(v, mp * heads_width, heads_width, v.ndim - 1)

    output_rows = (my_features(hidden1 + fc2_bias) + branch_sum).astype(BF16)
    g_fc2_bias = jnp.sum(my_features(dy).astype(F32), axis=0)

    d_att = dot_nt(d_attn, w_out).astype(BF16)
    probs32 = jnp.exp(scores_of() - log_total)
    d_probs = jnp.einsum(
        "thd,shd->hts", split_heads(d_att), split_heads(values), preferred_element_type=F32
    )
    delta = jnp.sum(probs32 * d_probs, axis=-1, keepdims=True)
    d_scores = (probs32 * (d_probs - delta)).astype(BF16)
    d_query = jnp.einsum("hts,shd->thd", d_scores, split_heads(keys), preferred_element_type=F32)
    d_keys = jnp.einsum("hts,thd->shd", d_scores, split_heads(query), preferred_element_type=F32)
    d_values = jnp.einsum(
        "hts,thd->shd", probs32.astype(BF16), split_heads(d_att), preferred_element_type=F32
    )
    d_mixed = jnp.concatenate(
        [
            (d_query * score_scale).astype(BF16).reshape(TOKENS, heads_width),
            (d_keys * score_scale).astype(BF16).reshape(TOKENS, heads_width),
            d_values.astype(BF16).reshape(TOKENS, heads_width),
        ],
        axis=1,
    )
    d_normed1_part = dot_nt(d_mixed, qkv_flat)
    weighted1 = d_normed1_part * attention_norm_gain
    stats1 = jnp.stack([jnp.sum(weighted1, axis=-1), jnp.sum(weighted1 * xhat1, axis=-1)])
    d_normed1 = lax.psum_scatter(
        d_normed1_part.astype(BF16).reshape(TOKENS, n_mp, heads_width).transpose(1, 0, 2),
        "mp",
        scatter_dimension=0,
        tiled=False,
    ).astype(F32)
    stats1 = lax.psum(stats1, "mp") / width
    xhat1_mine = my_features(xhat1)
    tokens_grad_rows = (
        my_features(d_attn).astype(F32)
        + inv1
        * (
            d_normed1 * my_features(attention_norm_gain)
            - stats1[0][:, None]
            - xhat1_mine * stats1[1][:, None]
        )
    ).astype(BF16)
    g_norm1_gain = jnp.sum(d_normed1 * xhat1_mine, axis=0)
    g_norm1_bias = jnp.sum(d_normed1, axis=0)
    d_mixed32 = d_mixed.astype(F32)
    g_qv_bias = jnp.stack(
        [
            jnp.sum(d_mixed32[:, :heads_width], axis=0),
            jnp.sum(d_mixed32[:, 2 * heads_width :], axis=0),
        ]
    )
    g_qkv_mine = sum_blocks(dot_tn(normed1, d_mixed).reshape(groups, -1, 3 * heads_width))
    g_qkv_mine = g_qkv_mine.reshape(-1, 3, heads_width)
    g_out_mine = sum_blocks(dot_tn(d_attn, attended).reshape(groups, -1, heads_width)).T

    chat_mine = pick(chat_blocks, 0, mp)
    my_gain = pick(channel_norm_gain.reshape(n_mp, channels), 0, mp)
    d_spatial = cinv * (
        d_normed_mine * my_gain
        - conv_stats[0][:, None] / all_channels
        - chat_mine * conv_stats[1][:, None] / all_channels
    )
    g_cnorm_gain = jnp.sum(d_normed_mine * chat_mine, axis=0)
    g_cnorm_bias = jnp.sum(d_normed_mine, axis=0)
    d_spatial = d_spatial.reshape(GRID_HI, GRID_HI, channels)
    _, conv_pull = jax.vjp(depthwise, masked, dw_kernel, dw_bias)
    d_masked, g_kernel, g_dw_bias = conv_pull(d_spatial)
    d_refined = dot_tn(pool, d_pooled).reshape(GRID_HI, GRID_HI, channels)
    d_field = ((d_masked + d_refined) * hi_mask).astype(BF16)

    def keep_half(rows):
        halves = rows.reshape((2, rows.shape[0] // 2) + rows.shape[1:])
        other = swap(pick(halves, 0, 1 - path), "path", 1)
        mine = pick(halves, 0, path)
        first = path == 0
        return jnp.stack([jnp.where(first, mine, other), jnp.where(first, other, mine)])

    output = keep_half(output_rows)
    tokens_grad = keep_half(tokens_grad_rows)
    hires_grad = keep_half(d_field)

    def placed(v):
        whole = jnp.zeros((n_mp, v.shape[0]), F32)
        return lax.dynamic_update_slice(whole, v[None], (mp, 0)).reshape(-1)

    wide = jnp.stack(
        [
            placed(g_norm1_gain),
            placed(g_norm1_bias),
            g_out_bias,
            g_norm2_gain,
            g_norm2_bias,
            placed(g_fc2_bias),
            g_gate,
        ]
    )
    wide = lax.psum(wide, ("path", "dp", "mp"))
    local_list = [
        g_qv_bias,
        g_fc1_bias,
        g_kernel,
        g_dw_bias,
        g_cnorm_gain,
        g_cnorm_bias,
        g_pw1_bias,
        g_pw2_bias,
        g_scale,
    ]
    local = lax.psum(tuple(local_list), ("path", "dp"))
    (
        g_qv_bias,
        g_fc1_bias,
        g_kernel,
        g_dw_bias,
        g_cnorm_gain,
        g_cnorm_bias,
        g_pw1_bias,
        g_pw2_bias,
        g_scale,
    ) = local
    return (
        output,
        tokens_grad,
        hires_grad,
        wide[0],
        wide[1],
        g_qkv_mine,
        g_qv_bias,
        g_out_mine,
        wide[2],
        wide[3],
        wide[4],
        g_fc1_mine,
        g_fc1_bias,
        g_fc2_mine,
        wide[5],
        g_adapt_mine,
        wide[6],
        g_kernel,
        g_dw_bias,
        g_cnorm_gain,
        g_cnorm_bias,
        g_pw1_mine,
        g_pw1_bias,
        g_pw2_mine,
        g_pw2_bias,
        g_scale,
    )


def solution(mesh):
    in_specs = (
        P("dp", None, None),
        P("dp", None, None, "mp"),
        P("dp"),
        P("dp", None, None),
        P(),
        P(),
        P(None, None, "mp"),
        P(None, "mp"),
        P("mp", None),
        P(),
        P(),
        P(),
        P(None, "mp"),
        P("mp"),
        P("mp", None),
        P(),
        P("mp", None),
        P(),
        P(None, "mp"),
        P("mp"),
        P(),
        P(),
        P(None, "mp"),
        P("mp"),
        P("mp", None),
        P("mp"),
        P("mp"),
    )
    out_specs = (
        P("dp", "path", "mp"),
        P("dp", "path", "mp"),
        P("dp", "path", None, "mp"),
        P(),
        P(),
        P(("path", "dp"), None, "mp"),
        P(None, "mp"),
        P("mp", ("path", "dp")),
        P(),
        P(),
        P(),
        P(("path", "dp"), "mp"),
        P("mp"),
        P("mp", ("path", "dp")),
        P(),
        P("mp", ("path", "dp")),
        P(),
        P(None, "mp"),
        P("mp"),
        P("mp"),
        P("mp"),
        P(("path", "dp"), "mp"),
        P("mp"),
        P("mp", ("path", "dp")),
        P("mp"),
        P("mp"),
    )
    return jax.shard_map(body, mesh=mesh, in_specs=in_specs, out_specs=out_specs, check_vma=False)
```

time: 1680 us -> 698 us (0.42)
  waiting for transfers between devices: 927 us -> 236 us
  local copies, waits for them, and re-layouts: 312 us -> 72.4 us
  starting transfers between devices: 149 us -> 25.9 us
  blocking collectives: 10.2 us -> 81.9 us
  loops' own time: 26.7 us -> 0 us
  other arithmetic: 137 us -> 154 us
    unnamed x24 -> x10, waiting for transfers between devices: 349 us -> 0.16 us
    reduce_scatter x5, waiting for transfers between devices: 212 us -> 0.77 us  [the longest x1 0.75 us: body(): lax.psum_scatter(term, 'mp', scatter_dimension=0, tiled=False).astype(F32)]
    unnamed x126 -> x351, local copies, waits for them, and re-layouts: 190 us -> 28.6 us
    ppermute x5 -> x24, starting transfers between devices: 148 us -> 24.2 us  [swap(): return lax.ppermute(value, axis, [(i, i ^ apart) for i in range(n)])]
    psum x3 -> x2, waiting for transfers between devices: 196 us -> 85.2 us  [the longest x1 58.5 us: body(): attn_sum = lax.psum(attention_part.astype(BF16), 'mp').astype(F32)]
    all_gather x2 -> x3, waiting for transfers between devices: 151 us -> 64.3 us  [the longest x1 37.9 us: body(): scaled_back_all = lax.all_gather(scaled_back, 'mp', axis=0, tiled=False)]
    psum x1 -> x3, blocking collectives: 10.2 us -> 81.9 us  [the longest x1 41.3 us: body(): wide = lax.psum(wide, ('path', 'dp', 'mp'))]
    ppermute x5 -> x24, waiting for transfers between devices: 19.4 us -> 86.1 us  [swap(): return lax.ppermute(value, axis, [(i, i ^ apart) for i in range(n)])]
  transfers between devices with their start and end apart: 22 -> 34, of which waited for: 18 -> 15; matrix products, arithmetic and copies ran while one was open for 23% -> 30% of each run, Pallas kernels for 0% -> 0%
where the time goes in v1:
time: 698 us; the launch traced here: 691 us
  waiting for transfers between devices  236 us (34%)
  other arithmetic  154 us (22%)
  matrix products  102 us (15%)
  blocking collectives  81.9 us (12%)
  local copies, waits for them, and re-layouts  72.4 us (10%)
  starting transfers between devices  25.9 us (4%)
  between operations  18.7 us (3%)
    ppermute x24, waiting for transfers between devices, swap(): return lax.ppermute(value, axis, [(i, i ^ apart) for i in range(n)])  86.1 us
    psum x1, waiting for transfers between devices, body(): attn_sum = lax.psum(attention_part.astype(BF16), 'mp').astype(F32)  58.5 us
    psum x1, blocking collectives, body(): wide = lax.psum(wide, ('path', 'dp', 'mp'))  41.3 us
    dot_general x9, matrix products, dot_tn(): lax.dot_general(a, b, (((0,), (0,)), ((), ())), preferred_element_type=F32)  40.1 us
    all_gather x1, waiting for transfers between devices, body(): scaled_back_all = lax.all_gather(scaled_back, 'mp', axis=0, tiled=False)  37.9 us
    unnamed x351, local copies, waits for them, and re-layouts  28.6 us
    psum x1, waiting for transfers between devices, body(): local = lax.psum(tuple(local_list), ('path', 'dp'))  26.6 us
    all_gather x1, waiting for transfers between devices, body(): spatial_all = lax.all_gather(spatial, 'mp', axis=0, tiled=False)  26.4 us
  transfers between devices with their start and end apart: 34, of which 15 were waited for; matrix products, arithmetic and copies ran while one was open for 30% of the time, Pallas kernels for 0%

profile of v1, /device:TPU:0, one launch (start us, length us, event | category | flops | bytes accessed | tf_op | source)
XLA Modules:
  0.0 691.0 jit_solution(17416311588753247152)
XLA Ops:
  13.4 2.6 copy.123
  16.0 3.0 fusion.55
  26.8 58.5 %all-reduce.104.cloned.1.call-done = bf16[576,1024]{1,0:T(8,128)(2,1)} async-done(((bf16[576,1024]{1,0:T(8,128)(2,1)}), bf16[576,1024]{1,0:T(8,128)(2,1)}) %all-reduce.104.cloned.1.call-update) | async-done | bytes 1179664 | tf_op jit(solution)/shard_map/psum | solution.py:202
  91.9 3.2 convert_reduce_fusion.3
  102.6 14.1 %add_convert_fusion.5 = bf16[32,32,384]{2,1,0:T(8,128)(2,1)} fusion(f32[32,32,384]{2,1,0:T(8,128)S(1)} %bitcast_multiply_fusion.1, f32[384]{0:T(512)S(1)} %get-tuple-element.184, f32[384]{0:T(512)S(1)} %get-tuple-element.185, f32[384]{0:T(512)S(1)} %get-tuple-element.138, f32[384]{0:T(512)S(1)} %get-tuple-element.139, f32[384]{0:T(512)} %get-tuple-element.140, ...), kind=kLoop, calls=%fused_computation.200 | loop fusion | flops 38928384 | bytes 2436096 | tf_op jit(solution)/shard_map/convert_element_type | solution.py:169
  117.3 4.0 convolution_convert_fusion.4
  136.7 2.6 fusion.42
  149.0 8.9 %collective-permute-done.10 = bf16[2,1,128,1024]{3,2,1,0:T(8,128)(2,1)} collective-permute-done((bf16[2,1,128,1024]{3,2,1,0:T(8,128)(2,1)}, bf16[2,1,128,1024]{3,2,1,0:T(8,128)(2,1)}, u32[]{:S(2)}, u32[]{:S(2)}) %collective-permute-start.10) | collective-permute-done | bytes 524320 | tf_op jit(solution)/shard_map/ppermute | solution.py:75
  164.0 26.4 %all-gather.5.cloned.1.call-done = bf16[4,1024,384]{2,1,0:T(8,128)(2,1)} async-done(((bf16[1,1024,384]{2,1,0:T(8,128)(2,1)}), bf16[4,1024,384]{2,1,0:T(8,128)(2,1)}) %all-gather.5.cloned.1.call-update) | async-done | bytes 3145744 | tf_op jit(solution)/shard_map/all_gather | solution.py:170
  190.4 4.7 copy.128
  195.0 2.6 convert_reduce_fusion.1
  201.9 7.4 %fusion.137 = f32[1024,1536]{1,0:T(8,128)S(1)} fusion(bf16[1024,1536]{0,1:T(8,128)(2,1)S(1)} %fusion.3, bf16[1536,1536]{1,0:T(8,128)(2,1)} %param.50), kind=kOutput, calls=%fused_computation.489 | convolution fusion | flops 4831838208 | bytes 14155776 | tf_op jit(solution)/shard_map/dot_general | solution.py:46
  209.4 3.2 fusion.25
  213.8 4.0 convert_bitcast_fusion.2
  224.3 4.5 collective-permute-done.11
  231.7 3.7 fusion.49
  236.3 4.1 multiply_reduce_fusion.2
  240.4 4.1 multiply_convert_fusion.2
  246.4 3.0 fusion.48
  249.6 5.0 multiply_reduce_fusion.5
  282.1 4.2 collective-permute-done.7
  290.8 2.8 collective-permute-done.8
  294.3 4.2 collective-permute-done.4
  314.6 5.7 collective-permute-done.16
  326.6 37.9 %all-gather.9.cloned.1.call-done = bf16[2304,384]{1,0:T(8,128)(2,1)} async-done(((bf16[576,384]{1,0:T(8,128)(2,1)}), bf16[2304,384]{1,0:T(8,128)(2,1)}) %all-gather.9.cloned.1.call-update) | async-done | bytes 1769488 | tf_op jit(solution)/shard_map/all_gather | solution.py:171
  364.6 2.8 copy.139
  368.1 15.0 %convert_reduce_fusion = (f32[1536]{0:T(1024)}, bf16[1024,1536]{1,0:T(8,128)(2,1)}) fusion(bf16[576,1024]{1,0:T(8,128)(2,1)S(1)} %copy-done.33, bf16[576,1536]{1,0:T(8,128)(2,1)S(1)} %bitcast.423, bf16[1536,1536]{1,0:T(8,128)(2,1)} %param.52, f32[1024,1536]{1,0:T(8,128)} %copy-done.160, f32[1536]{0:T(1024)S(1)} %copy-done.148), kind=kOutput, calls=%fused_computation.55 | convolution fusion | flops 4563761664 | bytes 17117184 | tf_op jit(solution)/shard_map/dot_general | solution.py:54
  385.4 6.1 convolution_convert_fusion
  395.6 5.3 convolution_convert_fusion.1
  405.1 7.5 %subtract_multiply_fusion = (f32[4,1024,384]{1,2,0:T(8,128)}, f32[1024]{0:T(1024)S(1)}, f32[1024,4,384]{0,2,1:T(8,128)S(1)}) fusion(bf16[4,1024,384]{1,2,0:T(8,128)(2,1)S(1)} %copy-done.4, f32[1024]{0:T(1024)S(1)} %add_rsqrt_fusion, f32[1024]{0:T(1024)S(1)} %broadcast_multiply_fusion.50, f32[4,384]{1,0:T(4,128)S(1)} %reshape.761, ...), kind=kOutput, calls=%fused_computation.62 | convolution fusion | flops 4841274368 | bytes 23611392 | tf_op jit(solution)/shard_map/rh,gch->grc/dot_general | solution.py:222
  412.6 2.6 convert_bitcast_fusion.1
  418.7 17.4 %all-reduce.100 = (f32[2,576]{1,0:T(2,128)S(1)}, f32[2,1024]{1,0:T(2,128)S(1)}) all-reduce(f32[2,576]{1,0:T(2,128)S(1)} %pad_maximum_fusion.5, f32[2,1024]{1,0:T(2,128)S(1)} %pad_maximum_fusion.4), channel_id=1, replica_groups=mesh['path'=2,'dp'=4,'mp'=4] {'mp'}, use_global_device_ids=true, to_apply=%region_18.19 | all-reduce | flops 3200 | bytes 25600 | tf_op jit(solution)/shard_map/psum | solution.py:315
  439.3 41.3 %psum.94 = f32[7,1024]{1,0:T(8,128)S(1)} all-reduce(f32[7,1024]{1,0:T(8,128)S(1)} %stack.88), channel_id=1, replica_groups=mesh['path'=2,'dp'=4,'mp'=4] {'path','dp','mp'}, use_global_device_ids=true, to_apply=%region_30.31 | all-reduce | flops 7168 | bytes 57344 | tf_op jit(solution)/shard_map/psum | solution.py:380
  480.6 3.2 fusion.10
  489.6 23.5 %collective-permute-done.19 = bf16[2,1,192,1536]{3,2,1,0:T(8,128)(2,1)S(1)} collective-permute-done((bf16[2,1,192,1536]{3,2,1,0:T(8,128)(2,1)S(1)}, bf16[2,1,192,1536]{3,2,1,0:T(8,128)(2,1)S(1)}, u32[]{:S(2)}, u32[]{:S(2)}) %collective-permute-start.19) | collective-permute-done | bytes 1179680 | tf_op jit(solution)/shard_map/ppermute | solution.py:75
  515.5 20.7 %collective-permute-done.22 = bf16[2,1,192,1536]{3,2,1,0:T(8,128)(2,1)S(1)} collective-permute-done((bf16[2,1,192,1536]{3,2,1,0:T(8,128)(2,1)S(1)}, bf16[2,1,192,1536]{3,2,1,0:T(8,128)(2,1)S(1)}, u32[]{:S(2)}, u32[]{:S(2)}) %collective-permute-start.22) | collective-permute-done | bytes 1179680 | tf_op jit(solution)/shard_map/ppermute | solution.py:75
  539.8 9.9 %collective-permute-done.23 = bf16[192,1536]{1,0:T(8,128)(2,1)S(1)} collective-permute-done((bf16[192,1536]{1,0:T(8,128)(2,1)S(1)}, bf16[192,1536]{1,0:T(8,128)(2,1)S(1)}, u32[]{:S(2)}, u32[]{:S(2)}) %collective-permute-start.23) | collective-permute-done | bytes 589856 | tf_op jit(solution)/shard_map/ppermute | solution.py:75
  550.9 2.6 multiply_reduce_fusion.6
  556.6 13.2 %multiply_reduce_fusion.54 = (f32[384]{0:T(512)S(1)}, f32[384]{0:T(512)S(1)}, f32[384]{0:T(512)S(1)}, f32[384]{0:T(512)S(1)}, f32[384]{0:T(512)S(1)}, /*index=5*...) fusion(f32[32,32,384]{2,1,0:T(8,128)} %copy-done.5, ...), kind=kLoop, calls=%fused_computation.196 | loop fusion | flops 13364352 | bytes 7111812 | tf_op jit(solution)/shard_map/transpose(jvp())/reduce_sum | solution.py:69
  569.8 5.0 multiply_reduce_fusion.55
  575.0 7.8 %broadcast_multiply_fusion.2 = (f32[32,32,384]{2,1,0:T(8,128)}, f32[32,32,384]{2,1,0:T(8,128)}, f32[32,32,384]{2,1,0:T(8,128)}, f32[32,32,384]{2,1,0:T(8,128)}, ...) fusion(f32[32,32,384]{2,1,0:T(8,128)S(1)} %get-tuple-element.20, ...), kind=kLoop, calls=%fused_computation.259 | loop fusion | flops 5111808 | bytes 22040064 | tf_op jit(solution)/shard_map/transpose(jvp())/mul | solution.py:69
  583.1 7.9 %broadcast_multiply_fusion.1 = (f32[32,32,384]{2,1,0:T(8,128)S(1)}, f32[32,32,384]{2,1,0:T(8,128)S(1)}, f32[32,32,384]{2,1,0:T(8,128)S(1)}, f32[32,32,384]{2,1,0...) fusion(f32[32,32,384]{2,1,0:T(8,128)S(1)} %get-tuple-element.20, ...), kind=kLoop, calls=%fused_computation.258 | loop fusion | flops 7077888 | bytes 29912064 | tf_op jit(solution)/shard_map/transpose(jvp())/mul | solution.py:69
  591.2 7.0 %broadcast_multiply_fusion = (f32[32,32,384]{2,1,0:T(8,128)}, f32[32,32,384]{2,1,0:T(8,128)S(1)}, f32[32,32,384]{2,1,0:T(8,128)S(1)}, f32[32,32,384]{2,1,0:T(8,1...) fusion(f32[32,32,384]{2,1,0:T(8,128)S(1)} %get-tuple-element.20, ...), kind=kLoop, calls=%fused_computation.257 | loop fusion | flops 7077888 | bytes 29912064 | tf_op jit(solution)/shard_map/transpose(jvp())/mul | solution.py:69
  598.2 21.9 %pad_add_fusion = f32[38,38,384]{2,1,0:T(8,128)S(1)} fusion(f32[32,32,384]{2,1,0:T(8,128)} %get-tuple-element.232, f32[32,32,384]{2,1,0:T(8,128)} %get-tuple-element.233, f32[32,32,384]{2,1,0:T(8,128)} %get-tuple-element.234, f32[32,32,384]{2,1,0:T(8,128)} %get-tuple-element.235, f32[32,32,384]{2,1,0:T(8,128)} %get-tuple-element.236, ...), kind=kLoop, calls=%fused_computation.123 | loop fusion | flops 23288832 | bytes 69851136 | tf_op jit(solution)/shard_map/transpose(jvp())/add_any | solution.py:69
  620.1 3.2 fusion.40
  624.8 5.2 multiply_reduce_fusion.56
  631.5 23.2 %all-reduce.99 = (f32[2,256]{1,0:T(2,128)}, f32[1024]{0:T(1024)}, f32[384]{0:T(512)}, f32[384]{0:T(512)}, f32[384]{0:T(512)}, /*index=5*/f32[1536]{0:T(1024)}, f32[384]{0:T(512)}, f32[384]{0:T(512)}) all-reduce(f32[2,256]{1,0:T(2,128)S(1)} %pad_maximum_fusion.6, ...), channel_id=1, replica_groups=mesh['path'=2,'dp'=4,'mp'=4] {'path','dp'}, use_global_device_ids=true, to_apply=%region_33.34 | all-reduce | flops 4992 | bytes 39936 | tf_op jit(solution)/shard_map/psum | solution.py:392
  655.7 26.6 %all-reduce.106.cloned.1.call-done = f32[49,384]{1,0:T(8,128)} async-done(((f32[49,384]{1,0:T(8,128)}), f32[49,384]{1,0:T(8,128)}) %all-reduce.106.cloned.1.call-update) | async-done | bytes 75280 | tf_op jit(solution)/shard_map/psum | solution.py:392
  (616 shorter events, 169.1 us)
Async XLA Ops:
  7.2 84.5 %copy-start = (bf16[1024,1024]{1,0:T(8,128)(2,1)S(1)}, bf16[1024,1024]{1,0:T(8,128)(2,1)}, u32[]{:S(2)}) copy-start(bf16[1024,1024]{1,0:T(8,128)(2,1)} %param.42) | copy-start | bytes 6291460
  7.2 78.1 %all-reduce.104.cloned.1.call-start = ((), (), s32[]{:S(2)}) async-start(), calls=%async_computation.5 | async-start | bytes 2359296 | tf_op jit(solution)/shard_map/psum | solution.py:202
  25.0 60.3 %copy-start.134 = (f32[1024]{0:T(1024)S(1)}, f32[1024]{0:T(1024)}, u32[]{:S(2)}) copy-start(f32[1024]{0:T(1024)} %param.37) | copy-start | bytes 12292
  26.6 133.3 %reduce-scatter.10.cloned.1.call-start = ((), (), s32[]{:S(2)}) async-start(), calls=%async_computation.9 | async-start | bytes 1474560 | tf_op jit(solution)/shard_map/reduce_scatter | solution.py:248
  97.7 92.7 %all-gather.5.cloned.1.call-start = ((), (), s32[]{:S(2)}) async-start(), calls=%async_computation.6 | async-start | bytes 3932160 | tf_op jit(solution)/shard_map/all_gather | solution.py:170
  99.0 17.7 %copy-start.49 = (f32[384]{0:T(512)}, f32[384]{0:T(512)S(1)}, u32[]{:S(2)}) copy-start(f32[384]{0:T(512)S(1)} %get-tuple-element.176) | copy-start | bytes 4612
  99.0 17.7 %copy-start.51 = (f32[384]{0:T(512)}, f32[384]{0:T(512)S(1)}, u32[]{:S(2)}) copy-start(f32[384]{0:T(512)S(1)} %get-tuple-element.177) | copy-start | bytes 4612
  99.0 17.7 %copy-start.53 = (f32[384]{0:T(512)}, f32[384]{0:T(512)S(1)}, u32[]{:S(2)}) copy-start(f32[384]{0:T(512)S(1)} %get-tuple-element.178) | copy-start | bytes 4612
  99.0 17.7 %copy-start.55 = (f32[384]{0:T(512)}, f32[384]{0:T(512)S(1)}, u32[]{:S(2)}) copy-start(f32[384]{0:T(512)S(1)} %get-tuple-element.179) | copy-start | bytes 4612
  99.0 17.7 %copy-start.57 = (f32[384]{0:T(512)}, f32[384]{0:T(512)S(1)}, u32[]{:S(2)}) copy-start(f32[384]{0:T(512)S(1)} %get-tuple-element.180) | copy-start | bytes 4612
  117.1 112.5 %all-gather.7.cloned.1.call-start = ((), (), s32[]{:S(2)}) async-start(), calls=%async_computation.10 | async-start | bytes 1474560 | tf_op jit(solution)/shard_map/all_gather | solution.py:261
  123.1 16.3 %collective-permute-start.9 = (bf16[2,2,128,1024]{3,2,1,0:T(8,128)(2,1)}, bf16[2,2,128,1024]{3,2,1,0:T(8,128)(2,1)}, u32[]{:S(2)}, u32[]{:S(2)}) collective-permute-start(bf16[2,2,128,1024]{3,2,1,0:T(8,128)(2,1)} %dynamic-slice_bitcast_fusion.2), channel_id=1, source_target_pairs={{0,4},{4,0},{8,12},{12,8},{1,5},{5,1},{9,13},{13,9},{2,6},{6,2},{1... | collective-permute-start | bytes 3145736 | tf_op jit(solution)/shard_map/ppermute | solution.py:75
  128.5 17.1 %collective-permute-start.12 = (bf16[2,2,128,1024]{2,3,1,0:T(8,128)(2,1)}, bf16[2,2,128,1024]{2,3,1,0:T(8,128)(2,1)}, u32[]{:S(2)}, u32[]{:S(2)}) collective-permute-start(bf16[2,2,128,1024]{2,3,1,0:T(8,128)(2,1)} %bitcast.469), channel_id=1, source_target_pairs={{0,4},{4,0},{8,12},{12,8},{1,5},{5,1},{9,13},{13,9},{2,6},{6,2},{1... | collective-permute-start | bytes 3145736 | tf_op jit(solution)/shard_map/ppermute | solution.py:75
  142.8 15.1 %collective-permute-start.10 = (bf16[2,1,128,1024]{3,2,1,0:T(8,128)(2,1)}, bf16[2,1,128,1024]{3,2,1,0:T(8,128)(2,1)}, u32[]{:S(2)}, u32[]{:S(2)}) collective-permute-start(bf16[2,1,128,1024]{3,2,1,0:T(8,128)(2,1)} %constant_dynamic-slice_fusion.8), channel_id=1, source_target_pairs={{0,8},{4,12},{8,0},{12,4},{1,9},{5,13},{9,1},{13,5},{2,10},{6,14},... | collective-permute-start | bytes 1572872 | tf_op jit(solution)/shard_map/ppermute | solution.py:75
  144.2 121.7 %copy-start.136 = (f32[576]{0:T(1024)}, f32[576]{0:T(1024)S(1)}, u32[]{:S(2)}) copy-start(f32[576]{0:T(1024)S(1)} %fusion.123) | copy-start | bytes 6916
  148.4 72.5 %collective-permute-start.13 = (bf16[2,1,128,1024]{2,3,1,0:T(8,128)(2,1)}, bf16[2,1,128,1024]{2,3,1,0:T(8,128)(2,1)}, u32[]{:S(2)}, u32[]{:S(2)}) collective-permute-start(bf16[2,1,128,1024]{2,3,1,0:T(8,128)(2,1)} %constant_dynamic-slice_fusion.5), channel_id=1, source_target_pairs={{0,8},{4,12},{8,0},{12,4},{1,9},{5,13},{9,1},{13,5},{2,10},{6,14},... | collective-permute-start | bytes 1572872 | tf_op jit(solution)/shard_map/ppermute | solution.py:75
  163.7 102.2 %reduce-scatter.6.cloned.1.call-start = ((), (), s32[]{:S(2)}) async-start(), calls=%async_computation.7 | async-start | bytes 2211840 | tf_op jit(solution)/shard_map/reduce_scatter | solution.py:213
  217.9 91.4 %reduce-scatter.12.cloned.1.call-start = ((), (), s32[]{:S(2)}) async-start(), calls=%async_computation.11 | async-start | bytes 1474560 | tf_op jit(solution)/shard_map/reduce_scatter | solution.py:309
  219.4 9.3 %collective-permute-start.11 = (bf16[128,1024]{1,0:T(8,128)(2,1)S(1)}, bf16[128,1024]{1,0:T(8,128)(2,1)S(1)}, u32[]{:S(2)}, u32[]{:S(2)}) collective-permute-start(bf16[128,1024]{1,0:T(8,128)(2,1)S(1)} %dynamic-slice_bitcast_fusion.8), channel_id=1, source_target_pairs={{0,16},{16,0},{1,17},{17,1},{2,18},{18,2},{3,19},{19,3},{4,20},{20... | collective-permute-start | bytes 786440 | tf_op jit(solution)/shard_map/ppermute | solution.py:75
  223.7 32.3 %collective-permute-start.14 = (bf16[128,1024]{0,1:T(8,128)(2,1)}, bf16[128,1024]{0,1:T(8,128)(2,1)}, u32[]{:S(2)}, u32[]{:S(2)}) collective-permute-start(bf16[128,1024]{0,1:T(8,128)(2,1)} %dynamic-slice_bitcast_fusion.7), channel_id=1, source_target_pairs={{0,16},{16,0},{1,17},{17,1},{2,18},{18,2},{3,19},{19,3},{4,20},{20... | collective-permute-start | bytes 786440 | tf_op jit(solution)/shard_map/ppermute | solution.py:75
  255.7 67.6 %reduce-scatter.8.cloned.1.call-start = ((), (), s32[]{:S(2)}) async-start(), calls=%async_computation.8 | async-start | bytes 1474560 | tf_op jit(solution)/shard_map/reduce_scatter | solution.py:277
  261.6 17.7 %collective-permute-start.6 = (bf16[2,2,128,256]{2,3,1,0:T(8,128)(2,1)}, bf16[2,2,128,256]{2,3,1,0:T(8,128)(2,1)}, u32[]{:S(2)}, u32[]{:S(2)}) collective-permute-start(bf16[2,2,128,256]{2,3,1,0:T(8,128)(2,1)} %bitcast.474), channel_id=1, source_target_pairs={{0,4},{4,0},{8,12},{12,8},{1,5},{5,1},{9,13},{13,9},{2,6},{6,2},{1... | collective-permute-start | bytes 786440 | tf_op jit(solution)/shard_map/ppermute | solution.py:75
  273.1 91.4 %all-gather.9.cloned.1.call-start = ((), (), s32[]{:S(2)}) async-start(), calls=%async_computation.14 | async-start | bytes 2211840 | tf_op jit(solution)/shard_map/all_gather | solution.py:171
  276.7 9.5 %collective-permute-start.3 = (bf16[2,2,128,768]{2,3,1,0:T(8,128)(2,1)}, bf16[2,2,128,768]{2,3,1,0:T(8,128)(2,1)}, u32[]{:S(2)}, u32[]{:S(2)}) collective-permute-start(bf16[2,2,128,768]{2,3,1,0:T(8,128)(2,1)} %bitcast.75), channel_id=1, source_target_pairs={{0,4},{4,0},{8,12},{12,8},{1,5},{5,1},{9,13},{13,9},{2,6},{6,2},{1... | collective-permute-start | bytes 2359304 | tf_op jit(solution)/shard_map/ppermute | solution.py:75
  280.4 5.8 collective-permute-start.7
  287.8 10.7 %collective-permute-start.4 = (bf16[2,1,128,768]{2,3,1,0:T(8,128)(2,1)S(1)}, bf16[2,1,128,768]{2,3,1,0:T(8,128)(2,1)S(1)}, u32[]{:S(2)}, u32[]{:S(2)}) collective-permute-start(bf16[2,1,128,768]{2,3,1,0:T(8,128)(2,1)S(1)} %constant_dynamic-slice_fusion.12), channel_id=1, source_target_pairs={{0,8},{4,12},{8,0},{12,4},{1,9},{5,13},{9,1},{13,5},{2,10},{6,14},... | collective-permute-start | bytes 1179656 | tf_op jit(solution)/shard_map/ppermute | solution.py:75
  289.4 4.3 collective-permute-start.8
  298.6 5.7 collective-permute-start.5
  302.7 248.3 %reduce-scatter.14.cloned.1.call-start = ((), (), s32[]{:S(2)}) async-start(), calls=%async_computation.12 | async-start | bytes 3932160 | tf_op jit(solution)/shard_map/reduce_scatter | solution.py:229
  309.2 3.7 collective-permute-start.15
  313.0 7.3 %collective-permute-start.16 = (bf16[2,1,128,384]{2,3,1,0:T(8,128)(2,1)S(1)}, bf16[2,1,128,384]{2,3,1,0:T(8,128)(2,1)S(1)}, u32[]{:S(2)}, u32[]{:S(2)}) collective-permute-start(bf16[2,1,128,384]{2,3,1,0:T(8,128)(2,1)S(1)} %constant_dynamic-slice_fusion.2), channel_id=1, source_target_pairs={{0,8},{4,12},{8,0},{12,4},{1,9},{5,13},{9,1},{13,5},{2,10},{6,14},... | collective-permute-start | bytes 589832 | tf_op jit(solution)/shard_map/ppermute | solution.py:75
  321.0 94.3 %collective-permute-start.17 = (bf16[128,384]{0,1:T(8,128)(2,1)}, bf16[128,384]{0,1:T(8,128)(2,1)}, u32[]{:S(2)}, u32[]{:S(2)}) collective-permute-start(bf16[128,384]{0,1:T(8,128)(2,1)} %dynamic-slice_bitcast_fusion.12), channel_id=1, source_target_pairs={{0,16},{16,0},{1,17},{17,1},{2,18},{18,2},{3,19},{19,3},{4,20},{20... | collective-permute-start | bytes 294920 | tf_op jit(solution)/shard_map/ppermute | solution.py:75
  325.2 91.8 %collective-permute-start = (bf16[288,256]{1,0:T(8,128)(2,1)}, bf16[288,256]{1,0:T(8,128)(2,1)}, u32[]{:S(2)}, u32[]{:S(2)}) collective-permute-start(bf16[288,256]{1,0:T(8,128)(2,1)} %dynamic-slice_bitcast_fusion.11), channel_id=1, source_target_pairs={{0,16},{16,0},{1,17},{17,1},{2,18},{18,2},{3,19},{19,3},{4,20},{20... | collective-permute-start | bytes 442376 | tf_op jit(solution)/shard_map/ppermute | solution.py:75
  385.4 19.5 %slice-start.4 = ((s8[4718592]{0:T(1024)(128)(4,1)}), s8[4194304]{0:T(1024)(128)(4,1)S(1)}, s32[]{:S(2)}) async-start(s8[4718592]{0:T(1024)(128)(4,1)} %bitcast.506), calls=%async_computation.19 | async-start | bytes 8388608
  404.4 76.3 %collective-permute-start.18 = (bf16[2,2,192,1536]{3,2,1,0:T(8,128)(2,1)}, bf16[2,2,192,1536]{3,2,1,0:T(8,128)(2,1)}, u32[]{:S(2)}, u32[]{:S(2)}) collective-permute-start(bf16[2,2,192,1536]{3,2,1,0:T(8,128)(2,1)} %dynamic-slice_bitcast_fusion.1), channel_id=1, source_target_pairs={{0,4},{4,0},{8,12},{12,8},{1,5},{5,1},{9,13},{13,9},{2,6},{6,2},{1... | collective-permute-start | bytes 7077896 | tf_op jit(solution)/shard_map/ppermute | solution.py:75
  404.4 81.9 %collective-permute-start.21 = (bf16[2,2,192,1536]{3,2,1,0:T(8,128)(2,1)}, bf16[2,2,192,1536]{3,2,1,0:T(8,128)(2,1)}, u32[]{:S(2)}, u32[]{:S(2)}) collective-permute-start(bf16[2,2,192,1536]{3,2,1,0:T(8,128)(2,1)} %dynamic-slice_bitcast_fusion), channel_id=1, source_target_pairs={{0,4},{4,0},{8,12},{12,8},{1,5},{5,1},{9,13},{13,9},{2,6},{6,2},{1... | collective-permute-start | bytes 7077896 | tf_op jit(solution)/shard_map/ppermute | solution.py:75
  415.3 20.8 %copy-start.34 = (bf16[1,576,256]{2,1,0:T(8,128)(2,1)S(1)}, bf16[1,576,256]{2,1,0:T(8,128)(2,1)}, u32[]{:S(2)}) copy-start(bf16[1,576,256]{2,1,0:T(8,128)(2,1)} %reduce-scatter.12.cloned.1.call-done) | copy-start | bytes 884740
  415.3 20.8 %copy-start.139 = (f32[256]{0:T(256)S(1)}, f32[256]{0:T(256)}, u32[]{:S(2)}) copy-start(f32[256]{0:T(256)} %dynamic_slice.188) | copy-start | bytes 3076
  415.3 267.0 %all-reduce.106.cloned.1.call-start = ((), (), s32[]{:S(2)}) async-start(), calls=%async_computation.13 | async-start | bytes 172032 | tf_op jit(solution)/shard_map/psum | solution.py:392
  417.0 22.2 %copy-start.131 = (f32[1,1,4,256]{3,1,2,0:T(1,128)S(1)}, f32[1,1,4,256]{3,1,2,0:T(1,128)}, u32[]{:S(2)}) copy-start(f32[1,1,4,256]{3,1,2,0:T(1,128)} %copy.183) | copy-start | bytes 12292
  437.9 51.7 %collective-permute-start.1 = (bf16[288,256]{1,0:T(8,128)(2,1)S(1)}, bf16[288,256]{1,0:T(8,128)(2,1)S(1)}, u32[]{:S(2)}, u32[]{:S(2)}) collective-permute-start(bf16[288,256]{1,0:T(8,128)(2,1)S(1)} %dynamic-slice_bitcast_fusion.10), channel_id=1, source_target_pairs={{0,16},{16,0},{1,17},{17,1},{2,18},{18,2},{3,19},{19,3},{4,20},{20... | collective-permute-start | bytes 442376 | tf_op jit(solution)/shard_map/ppermute | solution.py:75
  439.3 47.0 %slice-start = ((s8[4718592]{0:T(1024)(128)(4,1)}), s8[524288]{0:T(1024)(128)(4,1)S(1)}, s32[]{:S(2)}) async-start(s8[4718592]{0:T(1024)(128)(4,1)} %bitcast.430), calls=%async_computation.15 | async-start | bytes 1048576
  483.9 29.2 %collective-permute-start.19 = (bf16[2,1,192,1536]{3,2,1,0:T(8,128)(2,1)S(1)}, bf16[2,1,192,1536]{3,2,1,0:T(8,128)(2,1)S(1)}, u32[]{:S(2)}, u32[]{:S(2)}) collective-permute-start(bf16[2,1,192,1536]{3,2,1,0:T(8,128)(2,1)S(1)} %constant_dynamic-slice_fusion.1), channel_id=1, source_target_pairs={{0,8},{4,12},{8,0},{12,4},{1,9},{5,13},{9,1},{13,5},{2,10},{6,14},... | collective-permute-start | bytes 3538952 | tf_op jit(solution)/shard_map/ppermute | solution.py:75
  488.7 47.5 %collective-permute-start.22 = (bf16[2,1,192,1536]{3,2,1,0:T(8,128)(2,1)S(1)}, bf16[2,1,192,1536]{3,2,1,0:T(8,128)(2,1)S(1)}, u32[]{:S(2)}, u32[]{:S(2)}) collective-permute-start(bf16[2,1,192,1536]{3,2,1,0:T(8,128)(2,1)S(1)} %constant_dynamic-slice_fusion), channel_id=1, source_target_pairs={{0,8},{4,12},{8,0},{12,4},{1,9},{5,13},{9,1},{13,5},{2,10},{6,14},... | collective-permute-start | bytes 3538952 | tf_op jit(solution)/shard_map/ppermute | solution.py:75
  513.5 25.2 %collective-permute-start.20 = (bf16[192,1536]{1,0:T(8,128)(2,1)S(1)}, bf16[192,1536]{1,0:T(8,128)(2,1)S(1)}, u32[]{:S(2)}, u32[]{:S(2)}) collective-permute-start(bf16[192,1536]{1,0:T(8,128)(2,1)S(1)} %dynamic-slice_bitcast_fusion.5), channel_id=1, source_target_pairs={{0,16},{16,0},{1,17},{17,1},{2,18},{18,2},{3,19},{19,3},{4,20},{20... | collective-permute-start | bytes 1769480 | tf_op jit(solution)/shard_map/ppermute | solution.py:75
  536.6 13.2 %collective-permute-start.23 = (bf16[192,1536]{1,0:T(8,128)(2,1)S(1)}, bf16[192,1536]{1,0:T(8,128)(2,1)S(1)}, u32[]{:S(2)}, u32[]{:S(2)}) collective-permute-start(bf16[192,1536]{1,0:T(8,128)(2,1)S(1)} %dynamic-slice_bitcast_fusion.4), channel_id=1, source_target_pairs={{0,16},{16,0},{1,17},{17,1},{2,18},{18,2},{3,19},{19,3},{4,20},{20... | collective-permute-start | bytes 1769480 | tf_op jit(solution)/shard_map/ppermute | solution.py:75
  624.1 30.6 %collective-permute-start.2 = (bf16[16,32,384]{2,1,0:T(8,128)(2,1)}, bf16[16,32,384]{2,1,0:T(8,128)(2,1)S(1)}, u32[]{:S(2)}, u32[]{:S(2)}) collective-permute-start(bf16[16,32,384]{2,1,0:T(8,128)(2,1)} %dynamic-slice_bitcast_fusion.6), channel_id=1, source_target_pairs={{0,16},{16,0},{1,17},{17,1},{2,18},{18,2},{3,19},{19,3},{4,20},{20... | collective-permute-start | bytes 1179656 | tf_op jit(solution)/shard_map/ppermute | solution.py:75
  631.5 52.4 %copy-start.1 = (bf16[1024,1024]{1,0:T(8,128)(2,1)S(1)}, bf16[1024,1024]{1,0:T(8,128)(2,1)}, u32[]{:S(2)}) copy-start(bf16[1024,1024]{1,0:T(8,128)(2,1)} %param.42) | copy-start | bytes 6291460
  (156 other events, 1234.3 us)
Sparse Core Ops, SparseCore 0:
  26.7 58.5 all-reduce.103
  97.8 28.7 reduce-scatter.9
  128.1 62.1 all-gather.4
  192.4 29.0 all-gather.6
  223.7 37.5 reduce-scatter.5
  264.1 28.2 reduce-scatter.11
  295.4 27.8 reduce-scatter.7
  325.5 39.0 all-gather.8
  415.4 60.4 reduce-scatter.13
  631.6 50.7 all-reduce.105

commit v2 on v1

v2 whole, which is shorter than its diff:
```python
import functools

import jax
import jax.numpy as jnp
import numpy as np
from jax import lax
from jax.experimental import pallas as pl
from jax.experimental.pallas import tpu as pltpu
from jax.sharding import PartitionSpec as P

HEAD_DIM = 64
GRID_LO = 24
GRID_HI = 32
TOKENS = GRID_LO * GRID_LO
CELLS = GRID_HI * GRID_HI
LANES = 128
STAT_ROWS = 16
CELL_BLOCK = 256
POOL_BLOCK = CELL_BLOCK * 9 // 16

norm_epsilon = 1e-05
channel_epsilon = 1e-06
F32 = jnp.float32
BF16 = jnp.bfloat16
VMEM_BYTES = 60 * 1024 * 1024
CHUNKS = 2


def gelu_pair(v):
    c = 0.7978845608028654
    square = v * v
    t = jnp.tanh(c * v * (1.0 + 0.044715 * square))
    half = 0.5 + 0.5 * t
    return v * half, half + (0.5 * c) * v * (1.0 - t * t) * (1.0 + 3 * 0.044715 * square)


def pool_rows(lo, hi):
    ratio = hi / lo
    target = np.arange(lo, dtype=np.float64)[:, None]
    source = np.arange(hi, dtype=np.float64)[None, :]
    lower = np.maximum(source, target * ratio)
    upper = np.minimum(source + 1.0, (target + 1.0) * ratio)
    return np.round(np.maximum(upper - lower, 0.0) / ratio * 4) / 4


def pool_block():
    rows = CELL_BLOCK // GRID_HI
    return jnp.asarray(np.kron(pool_rows(rows * 3 // 4, rows), pool_rows(GRID_LO, GRID_HI)), BF16)


def dot(a, b):
    return jnp.dot(a, b, preferred_element_type=F32)


def dot_nt(a, b):
    return lax.dot_general(a, b, (((1,), (1,)), ((), ())), preferred_element_type=F32)


def dot_tn(a, b):
    return lax.dot_general(a, b, (((0,), (0,)), ((), ())), preferred_element_type=F32)


def standardize(v, eps):
    centred = v - jnp.mean(v, axis=-1, keepdims=True)
    inv = lax.rsqrt(jnp.mean(centred * centred, axis=-1, keepdims=True) + eps)
    return centred * inv, inv


KERNEL_US = {
    "front": 8,
    "attention_forward": 10,
    "conv_mlp": 21,
    "vit_mlp": 15,
    "norm2_backward": 4,
    "attention_backward": 42,
    "norm1_backward": 3,
    "output_halves": 3,
    "pack": 3,
    "unpack": 3,
    "adapter": 7,
    "conv_backward": 21,
    "grad_fc": 8,
    "grad_pw": 8,
    "grad_qkv": 6,
    "grad_adapt": 5,
    "fold_fc": 2,
    "fold_pw": 2,
    "fold_qkv": 1,
    "fold_adapt": 3,
    "fold_fc_last": 1,
    "fold_pw_last": 5,
    "fold_qkv_last": 3,
    "fold_adapt_last": 3,
}
FLOPS_PER_US = 1.15e9


def call(
    kernel, name, grid, ins, outs, operands, scratch=(), after=(), prefetch=None
):
    lead = 0 if prefetch is None else 1
    count = lead + len(ins)

    def run(*refs):
        kernel(*refs[:count], *refs[count + len(after) :])

    in_specs = list(ins) + [pl.BlockSpec(memory_space=pl.ANY)] * len(after)
    return pl.pallas_call(
        run,
        grid_spec=pltpu.PrefetchScalarGridSpec(
            num_scalar_prefetch=lead,
            grid=grid,
            in_specs=in_specs,
            out_specs=[spec for spec, _ in outs],
            scratch_shapes=list(scratch),
        ),
        out_shape=[shape for _, shape in outs],
        compiler_params=pltpu.CompilerParams(
            dimension_semantics=("arbitrary",) * len(grid), vmem_limit_bytes=VMEM_BYTES
        ),
        name=name,
        cost_estimate=pl.CostEstimate(
            flops=int(KERNEL_US[name] * FLOPS_PER_US), bytes_accessed=1, transcendentals=0
        ),
    )(*(() if prefetch is None else (prefetch,)), *operands, *after)


SCALARS = pl.BlockSpec(memory_space=pltpu.SMEM)


def array(shape, dtype=BF16):
    return jax.ShapeDtypeStruct(shape, dtype)


def held(shape):
    return pl.BlockSpec(shape, lambda *_: (0,) * len(shape), pipeline_mode=pl.Buffered(1))


def whole(shape):
    return pl.BlockSpec(shape, lambda *_: (0,) * len(shape))


def rows_to_lanes(columns):
    rows = columns[0].shape[0]
    lane = lax.broadcasted_iota(jnp.int32, (rows, LANES), 1)
    packed = jnp.zeros((rows, LANES), F32)
    for i, column in enumerate(columns):
        packed = jnp.where(lane == i, column, packed)
    return packed.T


def stat_rows(columns, width):
    lanes = rows_to_lanes(columns)
    pieces = [
        lanes[i : i + 1, t * LANES : (t + 1) * LANES]
        for i in range(2)
        for t in range(lanes.shape[1] // LANES)
    ]
    pieces.append(jnp.zeros((STAT_ROWS - len(pieces), LANES), F32))
    stats = jnp.concatenate(pieces, axis=0).astype(BF16)
    if width % LANES:
        return jnp.concatenate([stats, jnp.zeros((STAT_ROWS, width - LANES), BF16)], axis=1)
    return jnp.concatenate([stats] * (width // LANES), axis=1)


def channel_block(channels):
    return LANES if channels % LANES == 0 else channels


def store_shifted(shifted, a, row):
    column = lax.broadcasted_iota(jnp.int32, row.shape, 0)
    for s in range(7):
        move = s - 3
        if move == 0:
            shifted[s, a] = row
        else:
            rolled = pltpu.roll(row, (-move) % GRID_HI, 0)
            inside = (column + move >= 0) & (column + move < GRID_HI)
            shifted[s, a] = jnp.where(inside, rolled, 0.0)


def correlate(shifted, a0, count, taps, start):
    sums = [start] * count
    for r_in in range(count + 6):
        for s in range(7):
            value = shifted[s, a0 + r_in]
            for o in range(count):
                r = r_in - o
                if 0 <= r < 7:
                    sums[o] = sums[o] + value * taps(r, s)
    return sums


def front_kernel(
    base, count, s_ref, field_ref, k_ref, bias_ref, pool_ref, dy_ref, gate_ref, wa_ref, scale_ref,
    send_ref, field_pooled_ref, d_pooled_ref, d_adapted_ref, sums_ref, shifted,
):
    hi_valid = s_ref[5]
    cb = field_ref.shape[2]

    @pl.when(pl.program_id(0) == 0)
    def _():
        d_adapted_ref[...] = (gate_ref[...] * dy_ref[...].astype(F32)).astype(BF16)

    @pl.loop(0, count + 6)
    def _(a):
        source = base + a - 3
        keep = (source >= 0) & (source < hi_valid)
        row = field_ref[jnp.clip(source, 0, GRID_HI - 1)].astype(F32)
        store_shifted(shifted, a, jnp.where(keep, row, 0.0))

    start = jnp.broadcast_to(bias_ref[...], (GRID_HI, cb))

    @pl.loop(0, count, step=4)
    def _(a0):
        sums = correlate(
            shifted, a0, 4, lambda r, s: k_ref[r * 7 + s : r * 7 + s + 1, :], start
        )
        for o in range(4):
            at = pl.multiple_of((a0 + o) * GRID_HI, GRID_HI)
            send_ref[pl.ds(at, GRID_HI), :] = sums[o].astype(BF16)

    block_rows = CELL_BLOCK // GRID_HI
    for i in range(count // block_rows):
        first = base + i * block_rows
        rows = field_ref[first : first + block_rows]
        row = lax.broadcasted_iota(jnp.int32, rows.shape, 0) + first
        rows = jnp.where(row < hi_valid, rows.astype(F32), 0.0).astype(BF16)
        field_pooled_ref[i * POOL_BLOCK : (i + 1) * POOL_BLOCK] = dot(
            pool_ref[...], rows.reshape(CELL_BLOCK, cb)
        )
    d_pooled = dot_nt(d_adapted_ref[...], wa_ref[...]).astype(BF16).astype(F32)
    row = lax.broadcasted_iota(jnp.int32, d_pooled.shape, 0) + base * GRID_HI * 9 // 16
    d_pooled = jnp.where(row < s_ref[0] * GRID_LO, d_pooled, 0.0)
    d_pooled_ref[...] = d_pooled.astype(BF16)
    scaled = (d_pooled * scale_ref[...]).astype(BF16)
    send_ref[count * GRID_HI :, :] = scaled
    sums_ref[...] = jnp.sum(scaled.astype(F32), axis=0, keepdims=True)


def front(hires, kernel, bias, cotangent, gate, w_adapt, layer_scale, scalars, base, count, after=()):
    channels = hires.shape[3]
    width = cotangent.shape[2]
    cb = channel_block(channels)
    cells = count * GRID_HI
    pooled_rows = cells * 9 // 16
    chunk = base // count

    def column(rows):
        return pl.BlockSpec((rows, cb), lambda j, s: (0, j))

    return call(
        functools.partial(front_kernel, base, count),
        "front",
        (channels // cb,),
        [
            pl.BlockSpec((None, GRID_HI, GRID_HI, cb), lambda j, s: (s[3], 0, 0, j)),
            column(49),
            column(1),
            held((POOL_BLOCK, CELL_BLOCK)),
            pl.BlockSpec((None, pooled_rows, width), lambda j, s: (s[3], chunk, 0)),
            held((1, width)),
            pl.BlockSpec((cb, width), lambda j, s: (j, 0)),
            column(1),
        ],
        [
            (column(cells + pooled_rows), array((cells + pooled_rows, channels))),
            (column(pooled_rows), array((pooled_rows, channels), F32)),
            (column(pooled_rows), array((pooled_rows, channels))),
            (whole((pooled_rows, width)), array((pooled_rows, width))),
            (column(1), array((1, channels), F32)),
        ],
        (hires, kernel, bias.reshape(1, -1), pool_block(), cotangent, gate.reshape(1, -1), w_adapt)
        + (layer_scale.reshape(1, -1),),
        [pltpu.VMEM((7, count + 6, GRID_HI, cb), F32)],
        after,
        prefetch=scalars,
    )


def softmax_rows(q, k, key_valid):
    scores = jnp.where(key_valid, dot_nt(q, k) * HEAD_DIM ** (-0.5), -1e30)
    e = jnp.exp(scores - jnp.max(scores, axis=-1, keepdims=True))
    return e * (1.0 / jnp.sum(e, axis=-1, keepdims=True))


def attention_kernel(
    s_ref, x_ref, gain_ref, shift_ref, wq_ref, wk_ref, wv_ref, bias_ref,
    normed_ref, q_ref, k_ref, v_ref, att_ref,
):
    @pl.when(pl.program_id(0) == 0)
    def _():
        xhat, _ = standardize(x_ref[...].astype(F32), norm_epsilon)
        normed_ref[...] = (xhat * gain_ref[...] + shift_ref[...]).astype(BF16)

    normed = normed_ref[...]
    q_ref[...] = (dot(normed, wq_ref[...]) + bias_ref[0:1]).astype(BF16)
    k_ref[...] = dot(normed, wk_ref[...]).astype(BF16)
    v_ref[...] = (dot(normed, wv_ref[...]) + bias_ref[1:2]).astype(BF16)
    key = lax.broadcasted_iota(jnp.int32, (1, TOKENS), 1)
    key_valid = key < s_ref[0] * GRID_LO
    for h in range(q_ref.shape[1] // HEAD_DIM):
        cut = slice(h * HEAD_DIM, (h + 1) * HEAD_DIM)
        probs = softmax_rows(q_ref[:, cut], k_ref[:, cut], key_valid)
        att_ref[:, cut] = dot(probs.astype(BF16), v_ref[:, cut]).astype(BF16)


def image(width):
    return pl.BlockSpec((None, TOKENS, width), lambda j, s: (s[3], 0, 0))


def attention_forward(tokens, gain, shift, w_flat, qv_bias, scalars, after=()):
    width = tokens.shape[2]
    heads_width = w_flat.shape[1] // 3
    blocks = heads_width // LANES
    column = (pl.BlockSpec((TOKENS, LANES), lambda j, s: (0, j)), array((TOKENS, heads_width)))

    def weight(t):
        return pl.BlockSpec((width, LANES), lambda j, s: (0, t * blocks + j))

    return call(
        attention_kernel,
        "attention_forward",
        (blocks,),
        [image(width), held((1, width)), held((1, width)), weight(0), weight(1), weight(2)]
        + [pl.BlockSpec((2, LANES), lambda j, s: (0, j))],
        [(whole((TOKENS, width)), array((TOKENS, width)))] + [column] * 4,
        (tokens, gain.reshape(1, -1), shift.reshape(1, -1)) + (w_flat,) * 3 + (qv_bias,),
        after=after,
        prefetch=scalars,
    )


def attention_back_kernel(n_mp, scalars_ref, *refs):
    pieces, refs = refs[:n_mp], refs[n_mp:]
    x_ref, gain_ref, w_out_ref, q_ref, k_ref, v_ref, wq_ref, wk_ref, wv_ref = refs[:9]
    d_attn_ref, dq_ref, dk_ref, dv_ref = refs[9:13]
    sends, total = refs[13 : 13 + n_mp], refs[13 + n_mp]
    step = pl.program_id(0)
    mp = scalars_ref[1]
    part = pieces[0].shape[0]

    @pl.when(step == 0)
    def _():
        for k in range(n_mp):
            at = pl.multiple_of((mp ^ k) * part, part)
            total[pl.ds(at, part), :] = pieces[k][...].astype(F32)
        d_attn_ref[...] = total[...].astype(BF16)

    d_att_all = dot_nt(d_attn_ref[...], w_out_ref[...]).astype(BF16)
    key = lax.broadcasted_iota(jnp.int32, (1, TOKENS), 1)
    key_valid = key < scalars_ref[0] * GRID_LO
    scale = HEAD_DIM ** (-0.5)
    for h in range(q_ref.shape[1] // HEAD_DIM):
        cut = slice(h * HEAD_DIM, (h + 1) * HEAD_DIM)
        q, k, v, d_att = q_ref[:, cut], k_ref[:, cut], v_ref[:, cut], d_att_all[:, cut]
        probs = softmax_rows(q, k, key_valid)
        d_probs = dot_nt(d_att, v)
        delta = jnp.sum(probs * d_probs, axis=-1, keepdims=True)
        d_scores = (probs * (d_probs - delta)).astype(BF16)
        dq_ref[:, cut] = (dot(d_scores, k) * scale).astype(BF16)
        dk_ref[:, cut] = (dot_tn(d_scores, q) * scale).astype(BF16)
        dv_ref[:, cut] = dot_tn(probs.astype(BF16), d_att).astype(BF16)
    share = dot_nt(dq_ref[...], wq_ref[...]) + dot_nt(dk_ref[...], wk_ref[...])
    share = share + dot_nt(dv_ref[...], wv_ref[...])

    @pl.when(step == 0)
    def _():
        total[...] = share

    @pl.when(step > 0)
    def _():
        total[...] += share

    @pl.when(step == pl.num_programs(0) - 1)
    def _():
        features = sends[0].shape[1]
        xhat, _ = standardize(x_ref[...].astype(F32), norm_epsilon)
        weighted = total[...] * gain_ref[...]
        ones = jnp.sum(weighted, axis=-1, keepdims=True)
        twos = jnp.sum(weighted * xhat, axis=-1, keepdims=True)
        pad = jnp.zeros((-TOKENS % LANES, 1), F32)
        stats = stat_rows([jnp.concatenate([ones, pad]), jnp.concatenate([twos, pad])], features)
        for k in range(n_mp):
            at = pl.multiple_of((mp ^ k) * features, features)
            sends[k][:TOKENS, :] = total[:, pl.ds(at, features)].astype(BF16)
            sends[k][TOKENS:, :] = stats


def attention_backward(
    n_mp, tokens, gain, d_attn_pieces, w_out, q, k, v, w_flat, scalars, after=()
):
    width = tokens.shape[2]
    heads_width = q.shape[1]
    blocks = heads_width // LANES
    column = pl.BlockSpec((TOKENS, LANES), lambda j, s: (0, j))

    def weight(t):
        return pl.BlockSpec((width, LANES), lambda j, s: (0, t * blocks + j))

    send_shape = (TOKENS + STAT_ROWS, width // n_mp)
    return call(
        functools.partial(attention_back_kernel, n_mp),
        "attention_backward",
        (blocks,),
        [held(d_attn_pieces[0].shape)] * n_mp
        + [image(width), held((1, width)), pl.BlockSpec((LANES, width), lambda j, s: (j, 0))]
        + [column, column, column, weight(0), weight(1), weight(2)],
        [(whole((TOKENS, width)), array((TOKENS, width)))]
        + [(column, array((TOKENS, heads_width)))] * 3
        + [(whole(send_shape), array(send_shape))] * n_mp,
        (*d_attn_pieces, tokens, gain.reshape(1, -1), w_out, q, k, v, w_flat, w_flat, w_flat),
        [pltpu.VMEM((TOKENS, width), F32)],
        after,
        prefetch=scalars,
    )


def conv_mlp_kernel(
    n_mp, cells, rows_ref, gain_ref, shift_ref, w1_hbm, b_ref, w2_hbm, pool_ref,
    normed_ref, inner_ref, pooled_ref, back_ref, send_ref, mean_ref, inv_ref, bias_ref,
    full, w1_ref, w2_ref, sems,
):
    channels = rows_ref.shape[2]
    cut = 256
    steps = w1_ref.shape[1] // cut
    cuts = [slice(j * cut, (j + 1) * cut) for j in range(steps)]
    loads = []
    for j, at in enumerate(cuts):
        loads.append(pltpu.make_async_copy(w1_hbm.at[:, at], w1_ref.at[:, at], sems.at[j]))
        loads.append(pltpu.make_async_copy(w2_hbm.at[at, :], w2_ref.at[at, :], sems.at[steps + j]))
    for load in loads:
        load.start()
    for g in range(n_mp):
        mine = slice(g * channels, (g + 1) * channels)
        full[:, mine] = rows_ref[g, :cells].astype(F32)
        back_ref[:, mine] = rows_ref[g, cells:]
    spatial = full[...]
    mean = jnp.mean(spatial, axis=-1, keepdims=True)
    centred = spatial - mean
    inv = lax.rsqrt(jnp.mean(centred * centred, axis=-1, keepdims=True) + channel_epsilon)
    xhat = centred * inv
    full[...] = xhat
    mean_ref[...] = jnp.broadcast_to(mean, mean_ref.shape)
    inv_ref[...] = jnp.broadcast_to(inv, inv_ref.shape)
    normed_ref[...] = (xhat * gain_ref[...] + shift_ref[...]).astype(BF16)
    for j, at in enumerate(cuts):
        loads[2 * j].wait()
        active, slope = gelu_pair(dot(normed_ref[...], w1_ref[:, at]) + b_ref[:, at])
        active = active.astype(BF16)
        loads[2 * j + 1].wait()
        d_active = dot_nt(back_ref[...], w2_ref[at, :]).astype(BF16)
        backs = []
        for i in range(cells // CELL_BLOCK):
            lo = slice(i * POOL_BLOCK, (i + 1) * POOL_BLOCK)
            hi = slice(i * CELL_BLOCK, (i + 1) * CELL_BLOCK)
            pooled_ref[lo, at] = dot(pool_ref[...], active[hi]).astype(BF16)
            backs.append(dot_tn(pool_ref[...], d_active[lo]))
        d_inner = (slope * jnp.concatenate(backs, axis=0)).astype(BF16)
        inner_ref[:, at] = d_inner
        bias_ref[:, at] = jnp.sum(d_inner.astype(F32), axis=0, keepdims=True)

    branch = dot(pooled_ref[...], w2_ref[...]).astype(BF16)
    d_normed = dot_nt(inner_ref[...], w1_ref[...])
    weighted = d_normed * gain_ref[...]
    ones = jnp.sum(weighted, axis=-1, keepdims=True)
    twos = jnp.sum(weighted * full[...], axis=-1, keepdims=True)
    stats = stat_rows([ones, twos], channels)
    for g in range(n_mp):
        mine = slice(g * channels, (g + 1) * channels)
        send_ref[g, :cells, :] = d_normed[:, mine].astype(BF16)
        send_ref[g, cells : cells + STAT_ROWS, :] = stats
        send_ref[g, cells + STAT_ROWS :, :] = branch[:, mine]


def conv_mlp(rows, gain, shift, w1, b, w2, after=()):
    n_mp, both, channels = rows.shape
    total, hidden = w1.shape
    cells = both * 16 // 25
    pooled = both - cells
    send_shape = (n_mp, both + STAT_ROWS, channels)
    anywhere = pl.BlockSpec(memory_space=pl.ANY)

    def out(shape, dtype=BF16):
        return (held(shape), array(shape, dtype))

    return call(
        functools.partial(conv_mlp_kernel, n_mp, cells),
        "conv_mlp",
        (1,),
        [held((n_mp, both, channels)), held((1, total)), held((1, total)), anywhere]
        + [held((1, hidden)), anywhere, held((POOL_BLOCK, CELL_BLOCK))],
        [
            out((cells, total)),
            out((cells, hidden)),
            out((pooled, hidden)),
            out((pooled, total)),
            out(send_shape),
            out((cells, LANES), F32),
            out((cells, LANES), F32),
            out((1, hidden), F32),
        ],
        (rows, gain.reshape(1, -1), shift.reshape(1, -1), w1, b.reshape(1, -1), w2, pool_block()),
        [
            pltpu.VMEM((cells, total), F32),
            pltpu.VMEM((total, hidden), BF16),
            pltpu.VMEM((hidden, total), BF16),
            pltpu.SemaphoreType.DMA((2 * (hidden // 256),)),
        ],
        after,
    )


def conv_back_kernel(chunks, total_channels, s_ref, *refs):
    (received, spatial, means, invs, d_pooled) = (
        refs[i * chunks : (i + 1) * chunks] for i in range(5)
    )
    refs = refs[5 * chunks :]
    field_ref, k_ref, gain_ref, pool_ref, out_ref, g_kernel_ref, sums_ref, shifted, moved = refs
    hi_valid = s_ref[5]
    cb = field_ref.shape[2]
    gain = gain_ref[...]
    zeros = jnp.zeros((GRID_HI, cb), F32)
    for a in (0, 1, 2, GRID_HI + 3, GRID_HI + 4, GRID_HI + 5):
        for s in range(7):
            shifted[s, a] = zeros
            moved[s, a] = zeros
    g_gain = jnp.zeros((1, cb), F32)
    g_shift = jnp.zeros((1, cb), F32)
    g_bias = jnp.zeros((1, cb), F32)
    block_rows = CELL_BLOCK // GRID_HI
    first = 0
    for c in range(chunks):
        cells = means[c].shape[0]
        per = cells // LANES
        stats = received[c][cells : cells + STAT_ROWS, :LANES].astype(F32)
        rows = [
            jnp.concatenate([stats[k * per + t : k * per + t + 1] for t in range(per)], axis=1)
            for k in range(2)
        ]
        rows.append(jnp.zeros((LANES - 2, cells), F32))
        columns = jnp.concatenate(rows, axis=0).T * (1.0 / total_channels)
        for i in range(cells // CELL_BLOCK):
            at = slice(i * CELL_BLOCK, (i + 1) * CELL_BLOCK)
            d_normed = received[c][at, :].astype(F32)
            column = columns[at]
            if cb > LANES:
                mean, inv = means[c][at, :1], invs[c][at, :1]
            else:
                mean, inv = means[c][at], invs[c][at]
            xhat = (spatial[c][at].astype(F32) - mean) * inv
            d_spatial = inv * (d_normed * gain - column[:, 0:1] - xhat * column[:, 1:2])
            g_gain = g_gain + jnp.sum(d_normed * xhat, axis=0, keepdims=True)
            g_shift = g_shift + jnp.sum(d_normed, axis=0, keepdims=True)
            g_bias = g_bias + jnp.sum(d_spatial, axis=0, keepdims=True)
            for a in range(block_rows):
                store_shifted(moved, first + a + 3, d_spatial[a * GRID_HI : (a + 1) * GRID_HI])
            first += block_rows

    @pl.loop(0, GRID_HI)
    def _(a):
        row = jnp.where(a < hi_valid, field_ref[a].astype(F32), 0.0)
        store_shifted(shifted, a + 3, row)

    g_kernel_ref[...] = jnp.zeros(g_kernel_ref.shape, F32)
    for s in range(7):
        def rows_of(i, sums):
            a0 = i * 2
            grads = [moved[3, a0 + o + 3] for o in range(2)]
            sums = list(sums)
            for r_in in range(8):
                value = shifted[s, a0 + r_in]
                for o in range(2):
                    r = r_in - o
                    if 0 <= r < 7:
                        product = value * grads[o]
                        sums[r] = sums[r] + jnp.sum(product.reshape(GRID_HI // 8, 8, cb), axis=0)
            return tuple(sums)

        sums = lax.fori_loop(0, GRID_HI // 2, rows_of, tuple(jnp.zeros((8, cb), F32) for _ in range(7)))
        for r in range(7):
            t = r * 7 + s
            g_kernel_ref[t : t + 1, :] = jnp.sum(sums[r], axis=0, keepdims=True)
    sums_ref[...] = jnp.concatenate([g_bias, g_gain, g_shift, jnp.zeros((5, cb), F32)], axis=0)

    for i in range(CELLS // CELL_BLOCK):
        each = CELLS // CELL_BLOCK // chunks
        lo = slice((i % each) * POOL_BLOCK, (i % each + 1) * POOL_BLOCK)
        refined = dot_tn(pool_ref[...], d_pooled[i // each][lo, :])
        shifted[0, i * block_rows : (i + 1) * block_rows] = refined.reshape(block_rows, GRID_HI, cb)

    @pl.loop(0, GRID_HI, step=4)
    def _(a0):
        sums = correlate(
            moved, a0, 4, lambda r, s: k_ref[48 - (r * 7 + s) : 49 - (r * 7 + s), :], jnp.zeros((GRID_HI, cb), F32)
        )
        for o in range(4):
            value = sums[o] + shifted[0, a0 + o]
            out_ref[a0 + o] = jnp.where(a0 + o < hi_valid, value, 0.0).astype(BF16)


def conv_backward(
    received, spatial, means, invs, d_pooled, hires, kernel, my_gain, total_channels, scalars, after=()
):
    chunks = len(received)
    channels = hires.shape[3]
    cb = channel_block(channels)
    cells = means[0].shape[0]

    def column(rows):
        return pl.BlockSpec((rows, cb), lambda j, s: (0, j))

    map_block = pl.BlockSpec((GRID_HI, GRID_HI, cb), lambda j, s: (0, 0, j))
    return call(
        functools.partial(conv_back_kernel, chunks, total_channels),
        "conv_backward",
        (channels // cb,),
        [column(cells + STAT_ROWS)] * chunks
        + [column(cells)] * chunks
        + [held((cells, LANES))] * (2 * chunks)
        + [column(d_pooled[0].shape[0])] * chunks
        + [
            pl.BlockSpec((None, GRID_HI, GRID_HI, cb), lambda j, s: (s[3], 0, 0, j)),
            column(49),
            column(1),
            held((POOL_BLOCK, CELL_BLOCK)),
        ],
        [
            (map_block, array((GRID_HI, GRID_HI, channels))),
            (column(49), array((49, channels), F32)),
            (column(8), array((8, channels), F32)),
        ],
        (*received, *spatial, *means, *invs, *d_pooled)
        + (hires, kernel, my_gain.reshape(1, -1), pool_block()),
        [pltpu.VMEM((7, GRID_HI + 6, GRID_HI, cb), F32)] * 2,
        after,
        prefetch=scalars,
    )


def vit_mlp_kernel(n_mp, scalars_ref, *refs):
    pieces, refs = refs[:n_mp], refs[n_mp:]
    x_ref, wo_hbm, ob_ref, gain_ref, shift_ref, w1_hbm, b1_ref, w2_hbm, dy_ref = refs[:9]
    hidden_ref, normed_ref, active_ref, inner_ref, bias_ref = refs[9:14]
    sends, refs = refs[14 : 14 + n_mp], refs[14 + n_mp :]
    d_normed, wo_ref, w1_ref, w2_ref, sems = refs
    step = pl.program_id(0)
    rows = x_ref.shape[0]
    cut = 256
    cuts = [slice(j * cut, (j + 1) * cut) for j in range(w1_ref.shape[1] // cut)]
    loads = [pltpu.make_async_copy(wo_hbm, wo_ref, sems.at[0])]
    for j, at in enumerate(cuts):
        loads.append(pltpu.make_async_copy(w1_hbm.at[:, at], w1_ref.at[:, at], sems.at[2 * j + 1]))
        loads.append(pltpu.make_async_copy(w2_hbm.at[at, :], w2_ref.at[at, :], sems.at[2 * j + 2]))

    @pl.when(step == 0)
    def _():
        for load in loads:
            load.start()
        loads[0].wait()

    hidden = x_ref[...].astype(F32) + ob_ref[...]
    for k in range(n_mp):
        hidden = hidden + dot(pieces[k][...], wo_ref[k])
    hidden_ref[...] = hidden
    xhat, _ = standardize(hidden, norm_epsilon)
    normed_ref[...] = (xhat * gain_ref[...] + shift_ref[...]).astype(BF16)

    @pl.when(step == 0)
    def _():
        for load in loads[1:]:
            load.wait()

    for j, at in enumerate(cuts):
        active, slope = gelu_pair(dot(normed_ref[...], w1_ref[:, at]) + b1_ref[:, at])
        active_ref[:, at] = active.astype(BF16)
        d_inner = (slope * dot_nt(dy_ref[...], w2_ref[at, :])).astype(BF16)
        inner_ref[:, at] = d_inner
        sums = jnp.sum(d_inner.astype(F32), axis=0, keepdims=True)

        @pl.when(step == 0)
        def _():
            bias_ref[:, at] = sums

        @pl.when(step > 0)
        def _():
            bias_ref[:, at] += sums

    d_normed[pl.ds(pl.multiple_of(step * rows, rows), rows), :] = dot_nt(inner_ref[...], w1_ref[...])

    @pl.when(step == pl.num_programs(0) - 1)
    def _():
        part = sends[0].shape[0]
        for k in range(n_mp):
            at = pl.multiple_of((scalars_ref[1] ^ k) * part, part)
            sends[k][...] = d_normed[pl.ds(at, part), :].astype(BF16)


def vit_mlp(
    tokens, attended_pieces, w_out_pieces, out_bias, gain, shift, w1, b1, w2, cotangent, scalars, after=()
):
    n_mp = len(attended_pieces)
    heads_width = attended_pieces[0].shape[1]
    width, hidden = w1.shape
    rows = TOKENS // 2
    image_rows = pl.BlockSpec((None, rows, width), lambda j, s: (s[3], j, 0))
    row = pl.BlockSpec((rows, width), lambda j, s: (j, 0))
    row_hidden = pl.BlockSpec((rows, hidden), lambda j, s: (j, 0))
    one = held((1, width))
    anywhere = pl.BlockSpec(memory_space=pl.ANY)
    send_shape = (TOKENS // n_mp, width)
    return call(
        functools.partial(vit_mlp_kernel, n_mp),
        "vit_mlp",
        (TOKENS // rows,),
        [pl.BlockSpec((rows, heads_width), lambda j, s: (j, 0))] * n_mp
        + [image_rows, anywhere, one, one, one, anywhere, held((1, hidden)), anywhere, image_rows],
        [
            (row, array((TOKENS, width), F32)),
            (row, array((TOKENS, width))),
            (row_hidden, array((TOKENS, hidden))),
            (row_hidden, array((TOKENS, hidden))),
            (whole((1, hidden)), array((1, hidden), F32)),
        ]
        + [(whole(send_shape), array(send_shape))] * n_mp,
        (*attended_pieces, tokens, w_out_pieces, out_bias.reshape(1, -1), gain.reshape(1, -1))
        + (shift.reshape(1, -1), w1, b1.reshape(1, -1), w2, cotangent),
        [
            pltpu.VMEM((TOKENS, width), F32),
            pltpu.VMEM((n_mp, heads_width, width), BF16),
            pltpu.VMEM((width, hidden), BF16),
            pltpu.VMEM((hidden, width), BF16),
            pltpu.SemaphoreType.DMA((1 + 2 * (hidden // 256),)),
        ],
        after,
        prefetch=scalars,
    )


def adapter_kernel(chunks, scalars_ref, *refs):
    received, d_pooled, fields = (refs[i * chunks : (i + 1) * chunks] for i in range(3))
    refs = refs[3 * chunks :]
    pb_ref, scale_ref, wa_ref, active_ref, w2_ref, gate_ref, dy_ref = refs[:7]
    pooled_ref, scale_sum_ref, gate_sum_ref = refs[7:10]
    sends, total = refs[10:-1], refs[-1]
    sums = jnp.zeros(scale_sum_ref.shape, F32)
    first = 0
    for c in range(chunks):
        count = fields[c].shape[0]
        branch = received[c][received[c].shape[0] - count :, :].astype(F32) + pb_ref[...]
        sums = sums + jnp.sum(d_pooled[c][...].astype(F32) * branch, axis=0, keepdims=True)
        value = fields[c][...] + scale_ref[...] * branch
        row = lax.broadcasted_iota(jnp.int32, value.shape, 0) + first
        value = jnp.where(row < scalars_ref[0] * GRID_LO, value, 0.0)
        pooled_ref[first : first + count, :] = value.astype(BF16)
        first += count
    scale_sum_ref[...] = sums
    gate = gate_ref[...]
    adapted = dot(pooled_ref[...], wa_ref[...])
    sums = jnp.sum(dy_ref[...].astype(F32) * adapted, axis=0, keepdims=True)
    gate_sum_ref[...] = (1.0 - gate * gate) * sums
    total[...] = dot(active_ref[...], w2_ref[...]) + gate * adapted
    features = sends[0].shape[1]
    for k, send in enumerate(sends):
        at = pl.multiple_of((scalars_ref[1] ^ k) * features, features)
        send[...] = total[:, pl.ds(at, features)].astype(BF16)


def adapter(
    n_mp, received, d_pooled, fields, pw2_bias, layer_scale, w_adapt, active, w2, gate, cotangent, scalars, after=()
):
    channels, width = w_adapt.shape
    hidden = w2.shape[0]
    send_shape = (TOKENS, width // n_mp)
    return call(
        functools.partial(adapter_kernel, len(fields)),
        "adapter",
        (1,),
        [held(v.shape) for v in (*received, *d_pooled, *fields)]
        + [held((1, channels)), held((1, channels)), held((channels, width))]
        + [held((TOKENS, hidden)), held((hidden, width)), held((1, width)), image(width)],
        [
            (held((TOKENS, channels)), array((TOKENS, channels))),
            (held((1, channels)), array((1, channels), F32)),
            (held((1, width)), array((1, width), F32)),
        ]
        + [(held(send_shape), array(send_shape))] * n_mp,
        (*received, *d_pooled, *fields, pw2_bias.reshape(1, -1), layer_scale.reshape(1, -1), w_adapt)
        + (active, w2, gate.reshape(1, -1), cotangent),
        [pltpu.VMEM((TOKENS, width), F32)],
        after,
        prefetch=scalars,
    )


def weight_grad_kernel(counts, block, scalars_ref, *refs):
    pairs = sum(counts)
    lefts, rights = refs[:pairs], refs[pairs : 2 * pairs]
    keep_ref, send_ref = refs[2 * pairs :]
    core = scalars_ref[2]
    at = 0
    used = sum(refs[pairs + sum(counts[:i])].shape[1] for i in range(len(counts)))
    if used < keep_ref.shape[2]:
        rest = jnp.zeros(keep_ref.shape[:2] + (keep_ref.shape[2] - used,), BF16)
        keep_ref[:, :, used:] = rest
        send_ref[:, :, used:] = rest
    first = 0
    for count in counts:
        total = dot_tn(lefts[first][...], rights[first][...])
        for i in range(first + 1, first + count):
            total = total + dot_tn(lefts[i][...], rights[i][...])
        first += count
        lanes = slice(at, at + total.shape[1])
        at += total.shape[1]
        total = total.astype(BF16)
        for q in range(keep_ref.shape[0]):
            halves = [total[(2 * q + h) * block : (2 * q + h + 1) * block] for h in range(2)]

            @pl.when(core == 0)
            def _():
                keep_ref[q, :, lanes] = halves[0]
                send_ref[q, :, lanes] = halves[1]

            @pl.when(core != 0)
            def _():
                keep_ref[q, :, lanes] = halves[1]
                send_ref[q, :, lanes] = halves[0]


def weight_grads(name, groups, grads, scalars, after=(), lanes=None):
    block = grads[0][0][0].shape[1] // groups
    pairs = [pair for grad in grads for pair in grad]
    quads = 1
    while (2 * block * quads) % LANES:
        quads += 1
    total = lanes or sum(grad[0][1].shape[1] for grad in grads)
    out = (
        pl.BlockSpec((quads, block, total), lambda j: (j, 0, 0)),
        array((groups // 2, block, total)),
    )
    return call(
        functools.partial(weight_grad_kernel, [len(grad) for grad in grads], block),
        name,
        (groups // 2 // quads,),
        [SCALARS]
        + [pl.BlockSpec((left.shape[0], 2 * block * quads), lambda j: (0, j)) for left, _ in pairs]
        + [held(right.shape) for _, right in pairs],
        [out, out],
        (scalars, *(left for left, _ in pairs), *(right for _, right in pairs)),
        after=after,
    )


def fold_kernel(_, *refs):
    count = len(refs) // 4
    for p in range(count):
        keep, got = refs[2 * p : 2 * p + 2]
        send, hold = refs[2 * (count + p) : 2 * (count + p) + 2]

        def total():
            return (keep[...].astype(F32) + got[...].astype(F32)).astype(BF16)

        @pl.when(pl.program_id(0) == 0)
        def _():
            send[...] = total().reshape(send.shape)

        @pl.when(pl.program_id(0) == 1)
        def _():
            hold[...] = total().reshape(hold.shape)


def fold(name, parts, scalars, after=()):
    ins, operands, outs = [], [], []
    for keep, got, dim, slot, lanes, block in parts:
        shape = list(keep.shape)
        shape[dim] //= 2
        shape[-1] = lanes
        assert keep.shape[dim] == 2

        def at(j, s, dim=dim, slot=slot, rank=len(shape), block=block):
            index = [0] * rank
            index[dim] = s[slot] ^ (1 - j)
            index[-1] = block
            return tuple(index)

        ins += [pl.BlockSpec(tuple(shape), at)] * 2
        operands += [keep, got]
        out = tuple(shape[:dim] + shape[dim + 1 :])
        outs += [(whole(out), array(out))] * 2
    return call(
        fold_kernel, name, (2,), ins, outs, operands, after=after, prefetch=scalars
    )


def norm2_back_kernel(n_mp, scalars_ref, *refs):
    got, refs = refs[:n_mp], refs[n_mp:]
    hidden_ref, dy_ref, gain_ref, d_attn_ref, sums_ref = refs
    d_normed = got[0][...].astype(F32)
    for value in got[1:]:
        d_normed = d_normed + value[...].astype(F32)
    xhat, inv = standardize(hidden_ref[...], norm_epsilon)
    dxhat = d_normed * gain_ref[...]
    d_hidden = dy_ref[...].astype(F32) + inv * (
        dxhat
        - jnp.mean(dxhat, axis=-1, keepdims=True)
        - xhat * jnp.mean(dxhat * xhat, axis=-1, keepdims=True)
    )
    d_attn = d_hidden.astype(BF16)
    d_attn_ref[...] = d_attn
    sums_ref[0:1, :] = jnp.sum(d_attn.astype(F32), axis=0, keepdims=True)
    sums_ref[1:2, :] = jnp.sum(d_normed * xhat, axis=0, keepdims=True)
    sums_ref[2:3, :] = jnp.sum(d_normed, axis=0, keepdims=True)
    sums_ref[3:, :] = jnp.zeros((5, sums_ref.shape[1]), F32)


def norm2_backward(got, hidden, cotangent, gain, scalars, after=()):
    n_mp = len(got)
    rows, width = got[0].shape
    mine = pl.BlockSpec((None, rows, width), lambda j, s: (s[1], 0, 0))
    image_rows = pl.BlockSpec((None, None, rows, width), lambda j, s: (s[3], s[1], 0, 0))
    return call(
        functools.partial(norm2_back_kernel, n_mp),
        "norm2_backward",
        (1,),
        [held((rows, width))] * n_mp + [mine, image_rows, held((1, width))],
        [
            (held((rows, width)), array((rows, width))),
            (held((8, width)), array((8, width), F32)),
        ],
        (*got, hidden.reshape(n_mp, rows, width), cotangent.reshape(-1, n_mp, rows, width))
        + (gain.reshape(1, -1),),
        after=after,
        prefetch=scalars,
    )


def norm1_back_kernel(n_mp, scalars_ref, *refs):
    got, refs = refs[:n_mp], refs[n_mp:]
    x_ref, mine_ref, d_attn_ref, gain_ref, dy_ref, keep_ref, send_ref, sums_ref, total = refs
    width = x_ref.shape[1]
    value = got[0][...].astype(F32)
    for piece in got[1:]:
        value = value + piece[...].astype(F32)
    d_normed, stats = value[:TOKENS], value[TOKENS:, :LANES]
    count = -(-TOKENS // LANES)
    rows = [
        jnp.concatenate([stats[k * count + t : k * count + t + 1] for t in range(count)], axis=1)
        for k in range(2)
    ]
    rows.append(jnp.zeros((LANES - 2, count * LANES), F32))
    columns = jnp.concatenate(rows, axis=0).T[:TOKENS] * (1.0 / width)
    x = x_ref[...].astype(F32)
    mean = jnp.mean(x, axis=-1, keepdims=True)
    inv = lax.rsqrt(jnp.mean((x - mean) * (x - mean), axis=-1, keepdims=True) + norm_epsilon)
    xhat = (mine_ref[...].astype(F32) - mean) * inv
    total[...] = d_attn_ref[...].astype(F32) + inv * (
        d_normed * gain_ref[...] - columns[:, 0:1] - xhat * columns[:, 1:2]
    )
    half = TOKENS // 2
    path = scalars_ref[3]
    keep_ref[...] = total[pl.ds(pl.multiple_of(path * half, half), half), :].astype(BF16)
    send_ref[...] = total[pl.ds(pl.multiple_of((1 - path) * half, half), half), :].astype(BF16)
    sums_ref[0:1, :] = jnp.sum(d_normed * xhat, axis=0, keepdims=True)
    sums_ref[1:2, :] = jnp.sum(d_normed, axis=0, keepdims=True)
    sums_ref[2:3, :] = jnp.sum(dy_ref[...].astype(F32), axis=0, keepdims=True)
    sums_ref[3:, :] = jnp.zeros((5, sums_ref.shape[1]), F32)


def norm1_backward(got, tokens, d_attn, gain, cotangent, scalars, after=()):
    n_mp = len(got)
    rows, features = got[0].shape
    width = tokens.shape[2]
    mine = pl.BlockSpec((TOKENS, features), lambda j, s: (0, s[1]))
    mine_of = pl.BlockSpec((None, TOKENS, features), lambda j, s: (s[3], 0, s[1]))
    half = (held((TOKENS // 2, features)), array((TOKENS // 2, features)))
    return call(
        functools.partial(norm1_back_kernel, n_mp),
        "norm1_backward",
        (1,),
        [held((rows, features))] * n_mp
        + [image(width), mine_of, mine]
        + [pl.BlockSpec((1, features), lambda j, s: (0, s[1])), mine_of],
        [half, half, (held((8, features)), array((8, features), F32))],
        (*got, tokens, tokens, d_attn, gain.reshape(1, -1), cotangent),
        [pltpu.VMEM((TOKENS, features), F32)],
        after=after,
        prefetch=scalars,
    )


def output_kernel(n_mp, scalars_ref, *refs):
    got, refs = refs[:n_mp], refs[n_mp:]
    hidden_ref, bias_ref, keep_ref, send_ref, total = refs
    value = hidden_ref[...] + bias_ref[...]
    for piece in got:
        value = value + piece[...].astype(F32)
    total[...] = value
    half = TOKENS // 2
    path = scalars_ref[3]
    keep_ref[...] = total[pl.ds(pl.multiple_of(path * half, half), half), :].astype(BF16)
    send_ref[...] = total[pl.ds(pl.multiple_of((1 - path) * half, half), half), :].astype(BF16)


def output_halves(got, hidden, fc2_bias, scalars, after=()):
    n_mp = len(got)
    features = got[0].shape[1]
    half = (held((TOKENS // 2, features)), array((TOKENS // 2, features)))
    return call(
        functools.partial(output_kernel, n_mp),
        "output_halves",
        (1,),
        [held((TOKENS, features))] * n_mp
        + [pl.BlockSpec((TOKENS, features), lambda j, s: (0, s[1]))]
        + [pl.BlockSpec((1, features), lambda j, s: (0, s[1]))],
        [half, half],
        (*got, hidden, fc2_bias.reshape(1, -1)),
        [pltpu.VMEM((TOKENS, features), F32)],
        after=after,
        prefetch=scalars,
    )


def slots_of(shapes, width):
    row, lane, slots = 0, 0, []
    for rows, n in shapes:
        mine = []
        for _ in range(rows):
            pieces = []
            for at in range(0, n, width):
                size = min(width, n - at)
                if lane + size > width:
                    row, lane = row + 1, 0
                pieces.append((row, lane, at, size))
                lane += size
            mine.append(pieces)
        slots.append(mine)
    return slots, -(-(row + 1) // 8) * 8


def pack_kernel(n_mp, slots, *refs):
    wide, arrays, packed_ref = refs[:n_mp], refs[n_mp:-1], refs[-1]
    packed_ref[...] = jnp.zeros(packed_ref.shape, F32)
    total = wide[0][...]
    for piece in wide[1:]:
        total = total + piece[...]
    for r, pieces in enumerate(slots[0]):
        for row, lane, at, n in pieces:
            packed_ref[row : row + 1, lane : lane + n] = total[r : r + 1, at : at + n]
    for array_ref, mine in zip(arrays, slots[1:]):
        for r, pieces in enumerate(mine):
            for row, lane, at, n in pieces:
                packed_ref[row : row + 1, lane : lane + n] = array_ref[r : r + 1, at : at + n]


def pack(wide_pieces, arrays, rows, after=()):
    width = wide_pieces[0].shape[1]
    shapes = [wide_pieces[0].shape] + [(count, v.shape[1]) for v, count in zip(arrays, rows)]
    slots, total = slots_of(shapes, width)
    packed = call(
        functools.partial(pack_kernel, len(wide_pieces), slots),
        "pack",
        (1,),
        [held(v.shape) for v in (*wide_pieces, *arrays)],
        [(held((total, width)), array((total, width), F32))],
        (*wide_pieces, *arrays),
        after=after,
    )[0]
    return packed, slots


def unpack_kernel(slots, a_ref, b_ref, *outs):
    for out, mine in zip(outs, slots):
        for r, pieces in enumerate(mine):
            for row, lane, at, n in pieces:
                out[r : r + 1, at : at + n] = (
                    a_ref[row : row + 1, lane : lane + n] + b_ref[row : row + 1, lane : lane + n]
                )


def unpack(a, b, slots, after=()):
    shapes = [(len(mine), sum(n for *_, n in mine[0])) for mine in slots]
    return call(
        functools.partial(unpack_kernel, slots),
        "unpack",
        (1,),
        [held(a.shape)] * 2,
        [(held(shape), array(shape, F32)) for shape in shapes],
        (a, b),
        after=after,
    )


def swap(value, axis, apart):
    n = lax.axis_size(axis)
    return lax.ppermute(value, axis, [(i, i ^ apart) for i in range(n)])


def pick(value, axis, index):
    return lax.dynamic_index_in_dim(value, index, axis, keepdims=False)


def gathered(value, axis):
    return [value] + [swap(value, axis, k) for k in range(1, lax.axis_size(axis))]


def exchanged(blocks, axis):
    return blocks[:1] + [swap(block, axis, k) for k, block in enumerate(blocks) if k]


def spread(value, axis):
    value = value[:, None]
    apart = 1
    while apart < lax.axis_size(axis):
        other = swap(value, axis, apart)
        turned = (lax.axis_index(axis) & apart) > 0
        value = jnp.concatenate(
            [jnp.where(turned, other, value), jnp.where(turned, value, other)], axis=1
        )
        apart *= 2
    return value.reshape((value.shape[0], -1) + value.shape[3:])


def halve(value, dim, axis, apart, bit):
    received = swap(pick(value, dim, 1 - bit), axis, apart)
    return pick(value, dim, bit).astype(F32) + received.astype(F32)


def across(halves):
    keep, send = halves
    return keep, swap(send, "dp", 1)


def first_fold(name, keep, got, scalars, after, cut=False):
    n_path, n_dp = lax.axis_size("path"), lax.axis_size("dp")
    block, lanes = keep.shape[1:]
    shape = (n_path, n_dp // 4, 2, block, lanes)
    got = got.reshape(shape)
    keep = keep.reshape(shape)
    if cut:
        half = lanes // 2
        parts = [(keep, got, 0, 3, half, 0), (keep, got, 2, 4, half, 1)]
    else:
        parts = [(keep, got, 0, 3, lanes, 0)]
    out = fold(name, parts, scalars, after)
    result = [(out[1], swap(out[0], "path", 1), False)]
    if cut:
        result.append((out[3], swap(out[2], "dp", 2), True))
    return result


def second_fold(name, parts, scalars, after):
    ins = []
    for hold, got, path_next in parts:
        dim, slot = (0, 3) if path_next else (1, 4)
        ins.append((hold, got, dim, slot, hold.shape[-1], 0))
    out = fold(name, ins, scalars, after)
    result = []
    for i, (_, _, path_next) in enumerate(parts):
        send, hold = out[2 * i : 2 * i + 2]
        result.append((hold, swap(send, *(("path", 1) if path_next else ("dp", 2)))))
    return result


def arrived(parts):
    return tuple(part[1] for part in parts)


def last_sum(hold, got):
    n_dp, me_dp = lax.axis_size("dp"), lax.axis_index("dp")
    value = hold.astype(F32) + got.astype(F32)
    size = value.shape[0]
    b = 2
    while size > 1:
        size //= 2
        shape = (size, 2) + value.shape[1:]
        value = halve(value.astype(BF16).reshape(shape), 1, "dp", 1 << b, (me_dp >> b) & 1)
        b += 1
    return value[0]


def summed_at_once(value, axis):
    return sum(gathered(value, axis))


def summed(value, axes):
    for axis in axes:
        apart = 1
        while apart < lax.axis_size(axis):
            value = value + swap(value, axis, apart)
            apart *= 2
    return value


def body(
    tokens,
    hires,
    valid_rows,
    cotangent,
    attention_norm_gain,
    attention_norm_bias,
    w_qkv,
    qv_bias,
    w_out,
    out_bias,
    mlp_norm_gain,
    mlp_norm_bias,
    w_fc1,
    fc1_bias,
    down_weight,
    fc2_bias,
    w_adapt,
    gate_param,
    dw_kernel,
    dw_bias,
    channel_norm_gain,
    channel_norm_bias,
    w_pw1,
    pw1_bias,
    w_pw2,
    pw2_bias,
    layer_scale,
):
    path = lax.axis_index("path")
    n_path = lax.axis_size("path")
    dp = lax.axis_index("dp")
    mp = lax.axis_index("mp")
    n_mp = lax.axis_size("mp")
    groups = n_path * lax.axis_size("dp")
    assert tokens.shape[0] == n_path == 2
    width = tokens.shape[2]
    heads_width = w_qkv.shape[2]
    features = width // n_mp
    channels = hires.shape[3]
    all_channels = w_pw1.shape[0]
    part_rows = TOKENS // n_mp
    chunk_rows = GRID_HI // CHUNKS

    valid = pick(valid_rows, 0, path)
    hi_valid = (valid * GRID_HI + GRID_LO - 1) // GRID_LO
    scalars = jnp.stack([valid, mp, dp & 1, path, (dp >> 1) & 1, hi_valid])
    gate = jnp.tanh(gate_param)

    def my_features(v):
        return lax.dynamic_slice_in_dim(v, mp * features, features, v.ndim - 1)

    share_rows = heads_width // groups
    share = lax.dynamic_slice_in_dim(
        w_out, (path * lax.axis_size("dp") + dp) * share_rows, share_rows, 0
    )
    w_out_pieces = jnp.stack(gathered(share, "mp"))
    w_out_pieces = spread(spread(w_out_pieces, "dp"), "path")

    rows, rows_all, pooled_field, d_pooled, d_adapted = [], [], [], [], []
    g_pw2_bias = 0.0
    last = ()
    for c in range(CHUNKS):
        send, *chunk, sums = front(
            hires,
            dw_kernel,
            dw_bias,
            cotangent,
            gate,
            w_adapt,
            layer_scale,
            scalars,
            c * chunk_rows,
            chunk_rows,
            last,
        )
        last = (sums,)
        g_pw2_bias = g_pw2_bias + sums
        rows.append(send)
        rows_all.append(lax.all_gather(send, "mp", axis=0, tiled=False))
        for kept, value in zip((pooled_field, d_pooled, d_adapted), chunk):
            kept.append(value)

    w_flat = w_qkv.reshape(width, 3 * heads_width)
    normed1, query, keys, values, attended = attention_forward(
        tokens, attention_norm_gain, attention_norm_bias, w_flat, qv_bias, scalars, last
    )
    attended_pieces = gathered(attended, "mp")
    last = (attended,)

    def conv(c, after):
        out = conv_mlp(
            rows_all[c],
            channel_norm_gain,
            channel_norm_bias,
            w_pw1,
            pw1_bias,
            w_pw2,
            after,
        )
        return out, lax.psum_scatter(out[4], "mp", scatter_dimension=0, tiled=False), (out[7],)

    conv_out, received = [], []
    out, got, last = conv(0, last)
    conv_out.append(out)
    received.append(got)
    hidden1, normed2, fc_active, d_fc_inner, g_fc1_bias, *sends = vit_mlp(
        tokens,
        attended_pieces,
        w_out_pieces,
        out_bias,
        mlp_norm_gain,
        mlp_norm_bias,
        w_fc1,
        fc1_bias,
        down_weight,
        cotangent,
        scalars,
        last,
    )
    last = (g_fc1_bias,)
    d_normed2_pieces = exchanged(sends, "mp")
    dy = pick(cotangent, 0, path)
    fc_halves = weight_grads(
        "grad_fc", groups, [[(normed2, d_fc_inner)], [(dy, fc_active)]], scalars, last
    )
    fc_halves = across(fc_halves)
    last = (fc_halves[0],)
    d_attn_part, norm2_sums = norm2_backward(
        d_normed2_pieces, hidden1, cotangent, mlp_norm_gain, scalars, last
    )
    d_attn_pieces = gathered(d_attn_part, "mp")
    last = (norm2_sums,)
    for c in range(1, CHUNKS):
        out, got, last = conv(c, last)
        conv_out.append(out)
        received.append(got)
    conv_normed, conv_inner, pooled_active, backs, _, means, invs, bias_sums = zip(*conv_out)
    g_pw1_bias = sum(bias_sums)
    pw_halves = weight_grads(
        "grad_pw",
        groups,
        [list(zip(conv_normed, conv_inner)), list(zip(backs, pooled_active))],
        scalars,
        last,
    )
    pw_halves = across(pw_halves)
    last = (pw_halves[0],)

    d_attn, d_query, d_keys, d_values, *sends = attention_backward(
        n_mp,
        tokens,
        attention_norm_gain,
        d_attn_pieces,
        w_out,
        query,
        keys,
        values,
        w_flat,
        scalars,
        last,
    )
    d_normed1_pieces = exchanged(sends, "mp")
    last = (d_query,)
    fc_parts = first_fold("fold_fc", *fc_halves, scalars, last)
    last = (fc_parts[0][0],)
    pw_parts = first_fold("fold_pw", *pw_halves, scalars, last, True)
    last = (pw_parts[0][0],)
    qkv_halves = weight_grads(
        "grad_qkv",
        groups,
        [
            [(normed1, d_query)],
            [(normed1, d_keys)],
            [(normed1, d_values)],
            [(d_attn, attended)],
        ],
        scalars,
        last,
    )
    qkv_halves = across(qkv_halves)
    last = (qkv_halves[0],)
    g_qv_bias = jnp.stack(
        [jnp.sum(d_query.astype(F32), axis=0), jnp.sum(d_values.astype(F32), axis=0)]
    )
    tokens_keep, tokens_send, norm1_sums = norm1_backward(
        d_normed1_pieces,
        tokens,
        d_attn,
        attention_norm_gain,
        cotangent,
        scalars,
        last + arrived(fc_parts)
    )
    last = (norm1_sums,)
    fc_parts = second_fold("fold_fc_last", fc_parts, scalars, last)
    last = (fc_parts[0][0],)
    qkv_parts = first_fold("fold_qkv", *qkv_halves, scalars, last)
    last = (qkv_parts[0][0],)

    pooled, g_scale, g_gate, *sends = adapter(
        n_mp,
        received,
        d_pooled,
        pooled_field,
        pw2_bias,
        layer_scale,
        w_adapt,
        fc_active,
        down_weight,
        gate,
        cotangent,
        scalars,
        last,
    )
    branch_pieces = exchanged(sends, "mp")
    pooled_rows = d_adapted[0].shape[0]
    adapt_halves = weight_grads(
        "grad_adapt",
        groups,
        [
            [
                (d_adapted[c], pooled[c * pooled_rows : (c + 1) * pooled_rows])
                for c in range(CHUNKS)
            ]
        ],
        scalars,
        (g_scale,),
    )
    adapt_halves = across(adapt_halves)
    last = (adapt_halves[0],)
    def placed(v):
        return lax.dynamic_update_slice(jnp.zeros((width,), F32), v, (mp * features,))

    wide = jnp.concatenate(
        [norm2_sums[:3]] + [placed(norm1_sums[i])[None] for i in range(3)] + [g_gate]
    )
    wide_pieces = gathered(wide, "mp")

    d_field, g_kernel, conv_sums = conv_backward(
        received,
        rows,
        means,
        invs,
        d_pooled,
        hires,
        dw_kernel,
        lax.dynamic_slice_in_dim(channel_norm_gain, mp * channels, channels, 0),
        all_channels,
        scalars,
        last + arrived(pw_parts) + arrived(qkv_parts),
    )
    last = (conv_sums,)
    small = [g_qv_bias, g_fc1_bias, g_pw1_bias, g_kernel, conv_sums, g_pw2_bias, g_scale]
    packed, slots = pack(wide_pieces, small, (2, 1, 1, 49, 3, 1, 1), last)
    last = (packed,)
    packed = summed(packed, ("dp",))
    pw_parts = second_fold("fold_pw_last", pw_parts, scalars, last)
    last = (pw_parts[0][0],)
    output_keep, output_send = output_halves(branch_pieces, hidden1, fc2_bias, scalars, last)
    last = (output_keep,)
    qkv_parts = second_fold("fold_qkv_last", qkv_parts, scalars, last)
    last = (qkv_parts[0][0],)
    adapt_parts = first_fold("fold_adapt", *adapt_halves, scalars, last)
    last = (adapt_parts[0][0],)

    def both_images(mine, send):
        other = swap(send, "path", 1)
        first = path == 0
        return jnp.stack([jnp.where(first, mine, other), jnp.where(first, other, mine)])

    def keep_half(rows):
        halves = rows.reshape((2, rows.shape[0] // 2) + rows.shape[1:])
        return both_images(pick(halves, 0, path), pick(halves, 0, 1 - path))

    output = both_images(output_keep, output_send)
    tokens_grad = both_images(tokens_keep, tokens_send)
    hires_grad = keep_half(d_field)
    adapt_parts = second_fold("fold_adapt_last", adapt_parts, scalars, last)

    (both,) = (last_sum(*part) for part in fc_parts)
    g_fc1_mine, g_fc2_mine = both[:, : w_fc1.shape[1]], both[:, w_fc1.shape[1] :]
    g_pw1_mine, g_pw2_mine = (last_sum(*part) for part in pw_parts)
    (g_rest,) = (last_sum(*part) for part in qkv_parts)
    g_qkv_mine = g_rest[:, : 3 * heads_width].reshape(-1, 3, heads_width)
    g_out_mine = g_rest[:, 3 * heads_width :]
    (g_adapt_mine,) = (last_sum(*part) for part in adapt_parts)


    small = unpack(packed, swap(packed, "path", 1), slots)
    wide, g_qv_bias, g_fc1_bias, g_pw1_bias, g_kernel, conv_sums, g_pw2_bias, g_scale = small
    g_out_bias, g_norm2_gain, g_norm2_bias, g_norm1_gain, g_norm1_bias, g_fc2_bias, g_gate = wide
    g_dw_bias, g_cnorm_gain, g_cnorm_bias = conv_sums
    return (
        output,
        tokens_grad,
        hires_grad,
        g_norm1_gain,
        g_norm1_bias,
        g_qkv_mine,
        g_qv_bias,
        g_out_mine.T,
        g_out_bias,
        g_norm2_gain,
        g_norm2_bias,
        g_fc1_mine,
        g_fc1_bias[0],
        g_fc2_mine.T,
        g_fc2_bias,
        g_adapt_mine.T,
        g_gate,
        g_kernel,
        g_dw_bias,
        g_cnorm_gain,
        g_cnorm_bias,
        g_pw1_mine,
        g_pw1_bias[0],
        g_pw2_mine.T,
        g_pw2_bias[0],
        g_scale[0],
    )


def solution(mesh):
    in_specs = (
        P("dp", None, None),
        P("dp", None, None, "mp"),
        P("dp"),
        P("dp", None, None),
        P(),
        P(),
        P(None, None, "mp"),
        P(None, "mp"),
        P("mp", None),
        P(),
        P(),
        P(),
        P(None, "mp"),
        P("mp"),
        P("mp", None),
        P(),
        P("mp", None),
        P(),
        P(None, "mp"),
        P("mp"),
        P(),
        P(),
        P(None, "mp"),
        P("mp"),
        P("mp", None),
        P("mp"),
        P("mp"),
    )
    out_specs = (
        P("dp", "path", "mp"),
        P("dp", "path", "mp"),
        P("dp", "path", None, "mp"),
        P(),
        P(),
        P(("path", "dp"), None, "mp"),
        P(None, "mp"),
        P("mp", ("path", "dp")),
        P(),
        P(),
        P(),
        P(("path", "dp"), "mp"),
        P("mp"),
        P("mp", ("path", "dp")),
        P(),
        P("mp", ("path", "dp")),
        P(),
        P(None, "mp"),
        P("mp"),
        P("mp"),
        P("mp"),
        P(("path", "dp"), "mp"),
        P("mp"),
        P("mp", ("path", "dp")),
        P("mp"),
        P("mp"),
    )
    return jax.shard_map(body, mesh=mesh, in_specs=in_specs, out_specs=out_specs, check_vma=False)
```

time: 698 us -> 467 us (0.67)
  Pallas kernels: 0 us -> 212 us
  other arithmetic: 154 us -> 13.5 us
  waiting for transfers between devices: 236 us -> 99.9 us
  matrix products: 102 us -> 0 us
  blocking collectives: 81.9 us -> 0 us
  starting transfers between devices: 25.9 us -> 80.2 us
  local copies, waits for them, and re-layouts: 72.4 us -> 39.3 us
    pallas_call x0 -> x26, Pallas kernels: none -> 212 us  [call(): pl.pallas_call(run, grid_spec=pltpu.PrefetchScalarGridSpec(num_scalar_pre...]
    dot_general x30 -> x0, matrix products: 102 us -> none  [the longest x9 40.1 us: dot_tn(): lax.dot_general(a, b, (((0,), (0,)), ((), ())), preferred_element_type=F32)]
    psum x2 -> x0, waiting for transfers between devices: 85.2 us -> none  [the longest x1 58.5 us: body(): attn_sum = lax.psum(attention_part.astype(BF16), 'mp').astype(F32)]
    psum x3 -> x0, blocking collectives: 81.9 us -> none  [the longest x1 41.3 us: body(): wide = lax.psum(wide, ('path', 'dp', 'mp'))]
    ppermute x24 -> x44, starting transfers between devices: 24.2 us -> 80.1 us  [swap(): return lax.ppermute(value, axis, [(i, i ^ apart) for i in range(n)])]
    convert_element_type x26 -> x0, other arithmetic: 49.4 us -> none  [the longest x14 15.6 us: sum_blocks(): value = value.astype(BF16)]
    all_gather x3 -> x2, waiting for transfers between devices: 64.3 us -> 18.8 us  [body(): rows_all.append(lax.all_gather(send, 'mp', axis=0, tiled=False))]
    reduce_sum x18 -> x1, other arithmetic: 43.6 us -> 0.11 us  [body(): jnp.sum(d_values.astype(F32), axis=0)]
  transfers between devices with their start and end apart: 34 -> 48, of which waited for: 15 -> 17; matrix products, arithmetic and copies ran while one was open for 30% -> 8% of each run, Pallas kernels for 0% -> 44%
where the time goes in v2:
time: 467 us; the launch traced here: 460 us
  Pallas kernels  212 us (45%)
  waiting for transfers between devices  99.9 us (21%)
  starting transfers between devices  80.2 us (17%)
  local copies, waits for them, and re-layouts  39.3 us (8%)
  between operations  15.3 us (3%)
  other arithmetic  13.5 us (3%)
    pallas_call x26, Pallas kernels, call(): pl.pallas_call(run, grid_spec=pltpu.PrefetchScalarGridSpec(num_scalar_pre...  212 us
    ppermute x44, waiting for transfers between devices, swap(): return lax.ppermute(value, axis, [(i, i ^ apart) for i in range(n)])  81.1 us
    ppermute x44, starting transfers between devices, swap(): return lax.ppermute(value, axis, [(i, i ^ apart) for i in range(n)])  80.1 us
    all_gather x2, waiting for transfers between devices, body(): rows_all.append(lax.all_gather(send, 'mp', axis=0, tiled=False))  18.8 us
    unnamed x105, local copies, waits for them, and re-layouts  13.1 us
  transfers between devices with their start and end apart: 48, of which 17 were waited for; matrix products, arithmetic and copies ran while one was open for 8% of the time, Pallas kernels for 44%

profile of v2, /device:TPU:0, one launch (start us, length us, event | category | flops | bytes accessed | tf_op | source)
XLA Modules:
  0.0 460.1 jit_solution(10063442217232654605)
XLA Ops:
  14.2 7.7 %front.2 = (bf16[800,384]{1,0:T(8,128)(2,1)}, f32[288,384]{1,0:T(8,128)}, bf16[288,384]{1,0:T(8,128)(2,1)}, bf16[288,1024]{1,0:T(8,128)(2,1)}, f32[1,384]{1,0:T(1,128)}) custom-call(s32[6]{0:T(128)} %stack.75.refs_0_, bf16[2,32,32,384]{3,2,1,0:T(8,128)(2,1)} %refs_11_.3, f32[49,384]{1,0:T(8,128)} %refs_12_.3, f32[1,384]{1,0:T(1,128)} %reshape.172.refs_3_, ...), custom_call_target="tpu_custom_call" | custom-call | flops 9200000000 | bytes 1 | tf_op jit(solution)/shard_map/front/pallas_call | solution.py:108
  22.8 4.0 collective-permute-start.4
  31.1 3.4 collective-permute-done.5
  37.8 7.8 %front.3 = (bf16[800,384]{1,0:T(8,128)(2,1)}, f32[288,384]{1,0:T(8,128)}, bf16[288,384]{1,0:T(8,128)(2,1)}, bf16[288,1024]{1,0:T(8,128)(2,1)}, f32[1,384]{1,0:T(1,128)}) custom-call(s32[6]{0:T(128)} %stack.75.refs_0_, bf16[2,32,32,384]{3,2,1,0:T(8,128)(2,1)} %refs_11_.3, f32[49,384]{1,0:T(8,128)} %refs_12_.3, f32[1,384]{1,0:T(1,128)} %reshape.172.refs_3_, ...), custom_call_target="tpu_custom_call" | custom-call | flops 9200000000 | bytes 1 | tf_op jit(solution)/shard_map/front/pallas_call | solution.py:108
  52.0 10.3 %attention_forward.1 = (bf16[576,1024]{1,0:T(8,128)(2,1)}, bf16[576,256]{1,0:T(8,128)(2,1)}, bf16[576,256]{1,0:T(8,128)(2,1)}, bf16[576,256]{1,0:T(8,128)(2,1)}, bf16[576,256]{1,0:T(8,128)(2,1)}) custom-call(s32[6]{0:T(128)} %stack.75.refs_0_, bf16[2,576,1024]{2,1,0:T(8,128)(2,1)} %refs_6_.3, f32[1,1024]{1,0:T(1,128)} %bitcast.139, f32[1,1024]{1,0:T(1,128)} %bitcast.133, ...), custom_call_target="tpu_custom_call" | custom-call | flops 11500000256 | bytes 1 | tf_op jit(solution)/shard_map/attention_forward/pallas_call | solution.py:108
  63.8 3.0 collective-permute-start
  70.4 2.4 dynamic-slice_bitcast_fusion.refs_2_
  72.8 2.2 collective-permute-done.8
  76.9 18.8 %all-gather.5.cloned.1.call-done = bf16[3200,384]{1,0:T(8,128)(2,1)} async-done(((bf16[800,384]{1,0:T(8,128)(2,1)}), bf16[3200,384]{1,0:T(8,128)(2,1)}) %all-gather.5.cloned.1.call-update) | async-done | bytes 2457616 | tf_op jit(solution)/shard_map/all_gather | solution.py:1273
  95.7 21.0 %conv_mlp.2 = (bf16[512,1536]{1,0:T(8,128)(2,1)}, bf16[512,1536]{1,0:T(8,128)(2,1)}, bf16[288,1536]{1,0:T(8,128)(2,1)}, bf16[288,1536]{1,0:T(8,128)(2,1)}, bf16[...) custom-call(bf16[4,800,384]{2,1,0:T(8,128)(2,1)} %bitcast.126, ...), custom_call_target="tpu_custom_call" | custom-call | flops 24149999616 | bytes 1 | tf_op jit(solution)/shard_map/conv_mlp/pallas_call | solution.py:108
  117.6 15.1 %vit_mlp.1 = (f32[576,1024]{1,0:T(8,128)}, bf16[576,1024]{1,0:T(8,128)(2,1)}, bf16[576,1024]{1,0:T(8,128)(2,1)}, bf16[576,1024]{1,0:T(8,128)(2,1)}, f32[1,1024]{...) custom-call(s32[6]{0:T(128)} %stack.75.refs_0_, ...), custom_call_target="tpu_custom_call" | custom-call | flops 17250000896 | bytes 1 | tf_op jit(solution)/shard_map/vit_mlp/pallas_call | solution.py:108
  133.4 3.8 collective-permute-start.11
  137.2 8.2 %grad_fc.1 = (bf16[4,128,2048]{2,1,0:T(8,128)(2,1)}, bf16[4,128,2048]{2,1,0:T(8,128)(2,1)}) custom-call(s32[6]{0:T(128)} %stack.75.refs_0_, bf16[576,1024]{1,0:T(8,128)(2,1)} %get-tuple-element.139.refs_1_, bf16[576,1024]{1,0:T(8,128)(2,1)} %dynamic-slice_bitcast_fusion.refs_2_, bf16[576,1024]{1,0:T(8,128)(2,1)} %get-tuple-element.140.refs_3_, ...), custom_call_target="tpu_custom_call" | custom-call | flops 9200000000 | bytes 1 | tf_op jit(solution)/shard_map/grad_fc/pallas_call | solution.py:108
  145.5 11.9 %collective-permute-done.9.refs_2_ = bf16[144,1024]{1,0:T(8,128)(2,1)S(1)} collective-permute-done((bf16[144,1024]{1,0:T(8,128)(2,1)}, bf16[144,1024]{1,0:T(8,128)(2,1)S(1)}, u32[]{:S(2)}, u32[]{:S(2)}) %collective-permute-start.9) | collective-permute-done | bytes 294944 | tf_op jit(solution)/shard_map/ppermute | solution.py:1095
  157.4 3.7 collective-permute-done.10.refs_3_
  161.0 6.0 %collective-permute-done.11.refs_4_ = bf16[144,1024]{1,0:T(8,128)(2,1)S(1)} collective-permute-done((bf16[144,1024]{1,0:T(8,128)(2,1)}, bf16[144,1024]{1,0:T(8,128)(2,1)S(1)}, u32[]{:S(2)}, u32[]{:S(2)}) %collective-permute-start.11) | collective-permute-done | bytes 294944 | tf_op jit(solution)/shard_map/ppermute | solution.py:1095
  167.7 3.6 norm2_backward.1
  172.2 14.3 %collective-permute-start.13 = (bf16[144,1024]{1,0:T(8,128)(2,1)}, bf16[144,1024]{1,0:T(8,128)(2,1)S(1)}, u32[]{:S(2)}, u32[]{:S(2)}) collective-permute-start(bf16[144,1024]{1,0:T(8,128)(2,1)} %get-tuple-element.151.refs_1_), channel_id=1, source_target_pairs={{0,2},{1,3},{2,0},{3,1},{4,6},{5,7},{6,4},{7,5},{8,10},{9,11},{10,... | collective-permute-start | bytes 884744 | tf_op jit(solution)/shard_map/ppermute | solution.py:1095
  186.5 21.2 %conv_mlp.3 = (bf16[512,1536]{1,0:T(8,128)(2,1)}, bf16[512,1536]{1,0:T(8,128)(2,1)}, bf16[288,1536]{1,0:T(8,128)(2,1)}, bf16[288,1536]{1,0:T(8,128)(2,1)}, bf16[...) custom-call(bf16[4,800,384]{2,1,0:T(8,128)(2,1)} %bitcast.125, ...), custom_call_target="tpu_custom_call" | custom-call | flops 24149999616 | bytes 1 | tf_op jit(solution)/shard_map/conv_mlp/pallas_call | solution.py:108
  207.7 16.9 %grad_pw.1 = (bf16[4,192,3072]{2,1,0:T(8,128)(2,1)}, bf16[4,192,3072]{2,1,0:T(8,128)(2,1)}) custom-call(s32[6]{0:T(128)} %stack.75.refs_0_, bf16[512,1536]{1,0:T(8,128)(2,1)} %get-tuple-element.155.refs_1_, bf16[512,1536]{1,0:T(8,128)(2,1)} %get-tuple-element.156.refs_2_, bf16[288,1536]{1,0:T(8,128)(2,1)} %get-tuple-element.157.refs_3_, ...), custom_call_target="tpu_custom_call" | custom-call | flops 9200000000 | bytes 1 | tf_op jit(solution)/shard_map/grad_pw/pallas_call | solution.py:108
  225.3 9.4 %collective-permute-done.13.refs_3_ = bf16[144,1024]{1,0:T(8,128)(2,1)S(1)} collective-permute-done((bf16[144,1024]{1,0:T(8,128)(2,1)}, bf16[144,1024]{1,0:T(8,128)(2,1)S(1)}, u32[]{:S(2)}, u32[]{:S(2)}) %collective-permute-start.13) | collective-permute-done | bytes 294944 | tf_op jit(solution)/shard_map/ppermute | solution.py:1095
  235.5 16.4 %attention_backward.1 = (bf16[576,1024]{1,0:T(8,128)(2,1)}, bf16[576,256]{1,0:T(8,128)(2,1)}, bf16[576,256]{1,0:T(8,128)(2,1)}, bf16[576,256]{1,0:T(8,128)(2,1)}...) custom-call(s32[6]{0:T(128)} %stack.75.refs_0_, ...), custom_call_target="tpu_custom_call" | custom-call | flops 48299999232 | bytes 1 | tf_op jit(solution)/shard_map/attention_backward/pallas_call | solution.py:108
  253.6 2.7 collective-permute-start.21
  257.7 4.5 fold_fc.1
  264.4 7.2 %fold_pw.1 = (bf16[1,2,192,1536]{3,2,1,0:T(8,128)(2,1)}, bf16[1,2,192,1536]{3,2,1,0:T(8,128)(2,1)}, bf16[2,1,192,1536]{3,2,1,0:T(8,128)(2,1)}, bf16[2,1,192,1536]{3,2,1,0:T(8,128)(2,1)}) custom-call(s32[6]{0:T(128)} %stack.75.refs_0_, bf16[2,1,2,192,3072]{4,3,2,1,0:T(8,128)(2,1)} %bitcast.98, bf16[2,1,2,192,3072]{4,3,2,1,0:T(8,128)(2,1)} %bitcast.30.refs_2_.refs_4_, ...), custom_call_target="tpu_custom_call" | custom-call | flops 2300000000 | bytes 1 | tf_op jit(solution)/shard_map/fold_pw/pallas_call | solution.py:108
  271.5 9.1 %grad_qkv.1 = (bf16[4,128,1024]{2,1,0:T(8,128)(2,1)}, bf16[4,128,1024]{2,1,0:T(8,128)(2,1)}) custom-call(s32[6]{0:T(128)} %stack.75.refs_0_, bf16[576,1024]{1,0:T(8,128)(2,1)} %get-tuple-element.150.refs_1_.refs_2_.refs_3_, bf16[576,1024]{1,0:T(8,128)(2,1)} %get-tuple-element.150.refs_1_.refs_2_.refs_3_, ...), custom_call_target="tpu_custom_call" | custom-call | flops 6899999744 | bytes 1 | tf_op jit(solution)/shard_map/grad_qkv/pallas_call | solution.py:108
  280.6 5.3 %collective-permute-done.20.refs_3_ = bf16[592,256]{1,0:T(8,128)(2,1)S(1)} collective-permute-done((bf16[592,256]{1,0:T(8,128)(2,1)}, bf16[592,256]{1,0:T(8,128)(2,1)S(1)}, u32[]{:S(2)}, u32[]{:S(2)}) %collective-permute-start.20) | collective-permute-done | bytes 303136 | tf_op jit(solution)/shard_map/ppermute | solution.py:1095
  285.9 7.4 %collective-permute-done.21.refs_4_ = bf16[592,256]{1,0:T(8,128)(2,1)S(1)} collective-permute-done((bf16[592,256]{1,0:T(8,128)(2,1)}, bf16[592,256]{1,0:T(8,128)(2,1)S(1)}, u32[]{:S(2)}, u32[]{:S(2)}) %collective-permute-start.21) | collective-permute-done | bytes 303136 | tf_op jit(solution)/shard_map/ppermute | solution.py:1095
  294.3 4.4 norm1_backward.1
  300.4 3.4 fold_fc_last.1
  309.1 9.8 %collective-permute-done.38 = bf16[1,128,2048]{2,1,0:T(8,128)(2,1)S(1)} collective-permute-done((bf16[1,128,2048]{2,1,0:T(8,128)(2,1)}, bf16[1,128,2048]{2,1,0:T(8,128)(2,1)S(1)}, u32[]{:S(2)}, u32[]{:S(2)}) %collective-permute-start.38) | collective-permute-done | bytes 524320 | tf_op jit(solution)/shard_map/ppermute | solution.py:1095
  320.9 3.3 fold_qkv.1
  324.2 7.2 %adapter.1 = (bf16[576,384]{1,0:T(8,128)(2,1)}, f32[1,384]{1,0:T(1,128)}, f32[1,1024]{1,0:T(1,128)}, bf16[576,256]{1,0:T(8,128)(2,1)}, bf16[576,256]{1,0:T(8,128...) custom-call(s32[6]{0:T(128)} %stack.75.refs_0_, bf16[816,384]{1,0:T(8,128)(2,1)} %bitcast.128, ...), custom_call_target="tpu_custom_call" | custom-call | flops 8049999872 | bytes 1 | tf_op jit(solution)/shard_map/adapter/pallas_call | solution.py:108
  332.2 2.6 collective-permute-start.29
  334.7 18.1 %collective-permute-start.28 = (f32[7,1024]{1,0:T(8,128)S(1)}, f32[7,1024]{1,0:T(8,128)S(1)}, u32[]{:S(2)}, u32[]{:S(2)}) collective-permute-start(f32[7,1024]{1,0:T(8,128)S(1)} %concatenate.15.refs_0_), channel_id=1, source_target_pairs={{0,2},{1,3},{2,0},{3,1},{4,6},{5,7},{6,4},{7,5},{8,10},{9,11},{10,... | collective-permute-start | bytes 86024 | tf_op jit(solution)/shard_map/ppermute | solution.py:1095
  353.5 1.8 fusion.2
  355.3 4.5 grad_adapt.1
  360.0 2.0 collective-permute-start.22
  362.0 2.4 collective-permute-start.23
  364.4 21.0 %conv_backward.1 = (bf16[32,32,384]{2,1,0:T(8,128)(2,1)}, f32[49,384]{1,0:T(8,128)}, f32[8,384]{1,0:T(8,128)}) custom-call(s32[6]{0:T(128)} %stack.75.refs_0_, bf16[816,384]{1,0:T(8,128)(2,1)} %bitcast.129, bf16[816,384]{1,0:T(8,128)(2,1)} %bitcast.131, bf16[800,384]{1,0:T(8,128)(2,1)} %get-tuple-element.127.refs_3_, ...), custom_call_target="tpu_custom_call" | custom-call | flops 24149999616 | bytes 1 | tf_op jit(solution)/shard_map/conv_backward/pallas_call | solution.py:108
  385.4 2.2 collective-permute-start.24
  390.5 4.7 %fold_pw_last.1 = (bf16[1,192,1536]{2,1,0:T(8,128)(2,1)}, bf16[1,192,1536]{2,1,0:T(8,128)(2,1)}, bf16[1,192,1536]{2,1,0:T(8,128)(2,1)}, bf16[1,192,1536]{2,1,0:T(8,128)(2,1)}) custom-call(s32[6]{0:T(128)} %stack.75.refs_0_, bf16[1,2,192,1536]{3,2,1,0:T(8,128)(2,1)} %get-tuple-element.172.refs_9_.refs_1_, bf16[1,2,192,1536]{3,2,1,0:T(8,128)(2,1)} %copy-done.23, ...), custom_call_target="tpu_custom_call" | custom-call | flops 5750000128 | bytes 1 | tf_op jit(solution)/shard_map/fold_pw_last/pallas_call | solution.py:108
  395.9 3.1 output_halves.1
  399.7 2.7 fold_qkv_last.1
  403.2 2.8 fold_adapt.1
  414.7 2.6 fold_adapt_last.1
  420.6 12.8 %collective-permute-done.41 = bf16[1,128,384]{2,1,0:T(8,128)(2,1)} collective-permute-done((bf16[1,128,384]{2,1,0:T(8,128)(2,1)}, bf16[1,128,384]{2,1,0:T(8,128)(2,1)}, u32[]{:S(2)}, u32[]{:S(2)}) %collective-permute-start.41) | collective-permute-done | bytes 98336 | tf_op jit(solution)/shard_map/ppermute | solution.py:1095
  437.9 3.6 collective-permute-done.36.refs_1_
  (242 shorter events, 82.8 us)
Async XLA Ops:
  7.2 88.5 %all-gather.5.cloned.1.call-start = ((), (), s32[]{:S(2)}) async-start(), calls=%async_computation.4 | async-start | bytes 3072000 | tf_op jit(solution)/shard_map/all_gather | solution.py:1273
  21.9 164.6 %all-gather.7.cloned.1.call-start = ((), (), s32[]{:S(2)}) async-start(), calls=%async_computation.5 | async-start | bytes 3072000 | tf_op jit(solution)/shard_map/all_gather | solution.py:1273
  22.8 7.1 %collective-permute-start.4 = (bf16[32,1024]{1,0:T(8,128)(2,1)S(1)}, bf16[32,1024]{1,0:T(8,128)(2,1)S(1)}, u32[]{:S(2)}, u32[]{:S(2)}) collective-permute-start(bf16[32,1024]{1,0:T(8,128)(2,1)S(1)} %constant_dynamic-slice_fusion), channel_id=1, source_target_pairs={{0,2},{1,3},{2,0},{3,1},{4,6},{5,7},{6,4},{7,5},{8,10},{9,11},{10,... | collective-permute-start | bytes 196616 | tf_op jit(solution)/shard_map/ppermute | solution.py:1095
  26.9 4.3 collective-permute-start.3
  28.4 6.1 %collective-permute-start.5 = (bf16[32,1024]{1,0:T(8,128)(2,1)S(1)}, bf16[32,1024]{1,0:T(8,128)(2,1)S(1)}, u32[]{:S(2)}, u32[]{:S(2)}) collective-permute-start(bf16[32,1024]{1,0:T(8,128)(2,1)S(1)} %constant_dynamic-slice_fusion), channel_id=1, source_target_pairs={{0,3},{1,2},{2,1},{3,0},{4,7},{5,6},{6,5},{7,4},{8,11},{9,10},{10,... | collective-permute-start | bytes 196616 | tf_op jit(solution)/shard_map/ppermute | solution.py:1095
  34.5 1.6 collective-permute-start.6
  36.3 14.0 %collective-permute-start.7 = (bf16[4,2,32,1024]{3,2,1,0:T(8,128)(2,1)S(1)}, bf16[4,2,32,1024]{3,2,1,0:T(8,128)(2,1)S(1)}, u32[]{:S(2)}, u32[]{:S(2)}) collective-permute-start(bf16[4,2,32,1024]{3,2,1,0:T(8,128)(2,1)S(1)} %pad_maximum_fusion.3), channel_id=1, source_target_pairs={{0,8},{4,12},{8,0},{12,4},{1,9},{5,13},{9,1},{13,5},{2,10},{6,14},... | collective-permute-start | bytes 1572872 | tf_op jit(solution)/shard_map/ppermute | solution.py:1095
  45.6 278.5 %reduce-scatter.3.cloned.1.call-start = ((), (), s32[]{:S(2)}) async-start(), calls=%async_computation.2 | async-start | bytes 3133440 | tf_op jit(solution)/shard_map/reduce_scatter | solution.py:1294
  50.5 24.5 %collective-permute-start.8 = (bf16[4,1,128,1024]{3,2,0,1:T(8,128)(2,1)S(1)}, bf16[4,1,128,1024]{3,2,0,1:T(8,128)(2,1)S(1)}, u32[]{:S(2)}, u32[]{:S(2)}) collective-permute-start(bf16[4,1,128,1024]{3,2,0,1:T(8,128)(2,1)S(1)} %bitcast.101), channel_id=1, source_target_pairs={{0,16},{16,0},{1,17},{17,1},{2,18},{18,2},{3,19},{19,3},{4,20},{20... | collective-permute-start | bytes 3145736 | tf_op jit(solution)/shard_map/ppermute | solution.py:1095
  62.4 54.3 %collective-permute-start.2 = (bf16[576,256]{1,0:T(8,128)(2,1)}, bf16[576,256]{1,0:T(8,128)(2,1)S(1)}, u32[]{:S(2)}, u32[]{:S(2)}) collective-permute-start(bf16[576,256]{1,0:T(8,128)(2,1)} %get-tuple-element.130.refs_7_.refs_1_.refs_8_), channel_id=1, source_target_pairs={{0,3},{1,2},{2,1},{3,0},{4,7},{5,6},{6,5},{7,4},{8,11},{9,10},{10,... | collective-permute-start | bytes 884744 | tf_op jit(solution)/shard_map/ppermute | solution.py:1095
  63.7 53.0 %collective-permute-start.1 = (bf16[576,256]{1,0:T(8,128)(2,1)}, bf16[576,256]{1,0:T(8,128)(2,1)S(1)}, u32[]{:S(2)}, u32[]{:S(2)}) collective-permute-start(bf16[576,256]{1,0:T(8,128)(2,1)} %get-tuple-element.130.refs_7_.refs_1_.refs_8_), channel_id=1, source_target_pairs={{0,2},{1,3},{2,0},{3,1},{4,6},{5,7},{6,4},{7,5},{8,10},{9,11},{10,... | collective-permute-start | bytes 884744 | tf_op jit(solution)/shard_map/ppermute | solution.py:1095
  63.8 52.9 %collective-permute-start = (bf16[576,256]{1,0:T(8,128)(2,1)}, bf16[576,256]{1,0:T(8,128)(2,1)S(1)}, u32[]{:S(2)}, u32[]{:S(2)}) collective-permute-start(bf16[576,256]{1,0:T(8,128)(2,1)} %get-tuple-element.130.refs_7_.refs_1_.refs_8_), channel_id=1, source_target_pairs={{0,1},{1,0},{2,3},{3,2},{4,5},{5,4},{6,7},{7,6},{8,9},{9,8},{10,11... | collective-permute-start | bytes 884744 | tf_op jit(solution)/shard_map/ppermute | solution.py:1095
  116.7 207.5 %reduce-scatter.5.cloned.1.call-start = ((), (), s32[]{:S(2)}) async-start(), calls=%async_computation.3 | async-start | bytes 3133440 | tf_op jit(solution)/shard_map/reduce_scatter | solution.py:1294
  132.8 24.6 %collective-permute-start.9 = (bf16[144,1024]{1,0:T(8,128)(2,1)}, bf16[144,1024]{1,0:T(8,128)(2,1)S(1)}, u32[]{:S(2)}, u32[]{:S(2)}) collective-permute-start(bf16[144,1024]{1,0:T(8,128)(2,1)} %get-tuple-element.135), channel_id=1, source_target_pairs={{0,1},{1,0},{2,3},{3,2},{4,5},{5,4},{6,7},{7,6},{8,9},{9,8},{10,11... | collective-permute-start | bytes 884744 | tf_op jit(solution)/shard_map/ppermute | solution.py:1095
  132.9 28.1 %collective-permute-start.10 = (bf16[144,1024]{1,0:T(8,128)(2,1)}, bf16[144,1024]{1,0:T(8,128)(2,1)S(1)}, u32[]{:S(2)}, u32[]{:S(2)}) collective-permute-start(bf16[144,1024]{1,0:T(8,128)(2,1)} %get-tuple-element.136), channel_id=1, source_target_pairs={{0,2},{1,3},{2,0},{3,1},{4,6},{5,7},{6,4},{7,5},{8,10},{9,11},{10,... | collective-permute-start | bytes 884744 | tf_op jit(solution)/shard_map/ppermute | solution.py:1095
  133.4 33.6 %collective-permute-start.11 = (bf16[144,1024]{1,0:T(8,128)(2,1)}, bf16[144,1024]{1,0:T(8,128)(2,1)S(1)}, u32[]{:S(2)}, u32[]{:S(2)}) collective-permute-start(bf16[144,1024]{1,0:T(8,128)(2,1)} %get-tuple-element.137), channel_id=1, source_target_pairs={{0,3},{1,2},{2,1},{3,0},{4,7},{5,6},{6,5},{7,4},{8,11},{9,10},{10,... | collective-permute-start | bytes 884744 | tf_op jit(solution)/shard_map/ppermute | solution.py:1095
  145.4 110.9 %collective-permute-start.16 = (bf16[4,128,2048]{2,1,0:T(8,128)(2,1)}, bf16[4,128,2048]{2,1,0:T(8,128)(2,1)S(1)}, u32[]{:S(2)}, u32[]{:S(2)}) collective-permute-start(bf16[4,128,2048]{2,1,0:T(8,128)(2,1)} %get-tuple-element.170), channel_id=1, source_target_pairs={{0,4},{4,0},{8,12},{12,8},{1,5},{5,1},{9,13},{13,9},{2,6},{6,2},{1... | collective-permute-start | bytes 6291464 | tf_op jit(solution)/shard_map/ppermute | solution.py:1095
  171.3 54.0 %collective-permute-start.14 = (bf16[144,1024]{1,0:T(8,128)(2,1)}, bf16[144,1024]{1,0:T(8,128)(2,1)S(1)}, u32[]{:S(2)}, u32[]{:S(2)}) collective-permute-start(bf16[144,1024]{1,0:T(8,128)(2,1)} %get-tuple-element.151.refs_1_), channel_id=1, source_target_pairs={{0,3},{1,2},{2,1},{3,0},{4,7},{5,6},{6,5},{7,4},{8,11},{9,10},{10,... | collective-permute-start | bytes 884744 | tf_op jit(solution)/shard_map/ppermute | solution.py:1095
  172.2 62.5 %collective-permute-start.13 = (bf16[144,1024]{1,0:T(8,128)(2,1)}, bf16[144,1024]{1,0:T(8,128)(2,1)S(1)}, u32[]{:S(2)}, u32[]{:S(2)}) collective-permute-start(bf16[144,1024]{1,0:T(8,128)(2,1)} %get-tuple-element.151.refs_1_), channel_id=1, source_target_pairs={{0,2},{1,3},{2,0},{3,1},{4,6},{5,7},{6,4},{7,5},{8,10},{9,11},{10,... | collective-permute-start | bytes 884744 | tf_op jit(solution)/shard_map/ppermute | solution.py:1095
  186.5 48.2 %collective-permute-start.12 = (bf16[144,1024]{1,0:T(8,128)(2,1)}, bf16[144,1024]{1,0:T(8,128)(2,1)S(1)}, u32[]{:S(2)}, u32[]{:S(2)}) collective-permute-start(bf16[144,1024]{1,0:T(8,128)(2,1)} %get-tuple-element.151.refs_1_), channel_id=1, source_target_pairs={{0,1},{1,0},{2,3},{3,2},{4,5},{5,4},{6,7},{7,6},{8,9},{9,8},{10,11... | collective-permute-start | bytes 884744 | tf_op jit(solution)/shard_map/ppermute | solution.py:1095
  225.2 39.1 %collective-permute-start.15 = (bf16[4,192,3072]{2,1,0:T(8,128)(2,1)}, bf16[4,192,3072]{2,1,0:T(8,128)(2,1)}, u32[]{:S(2)}, u32[]{:S(2)}) collective-permute-start(bf16[4,192,3072]{2,1,0:T(8,128)(2,1)} %get-tuple-element.169), channel_id=1, source_target_pairs={{0,4},{4,0},{8,12},{12,8},{1,5},{5,1},{9,13},{13,9},{2,6},{6,2},{1... | collective-permute-start | bytes 14155784 | tf_op jit(solution)/shard_map/ppermute | solution.py:1095
  251.9 28.8 %collective-permute-start.19 = (bf16[592,256]{1,0:T(8,128)(2,1)}, bf16[592,256]{1,0:T(8,128)(2,1)S(1)}, u32[]{:S(2)}, u32[]{:S(2)}) collective-permute-start(bf16[592,256]{1,0:T(8,128)(2,1)} %get-tuple-element.177), channel_id=1, source_target_pairs={{0,1},{1,0},{2,3},{3,2},{4,5},{5,4},{6,7},{7,6},{8,9},{9,8},{10,11... | collective-permute-start | bytes 909320 | tf_op jit(solution)/shard_map/ppermute | solution.py:1095
  251.9 34.0 %collective-permute-start.20 = (bf16[592,256]{1,0:T(8,128)(2,1)}, bf16[592,256]{1,0:T(8,128)(2,1)S(1)}, u32[]{:S(2)}, u32[]{:S(2)}) collective-permute-start(bf16[592,256]{1,0:T(8,128)(2,1)} %get-tuple-element.178), channel_id=1, source_target_pairs={{0,2},{1,3},{2,0},{3,1},{4,6},{5,7},{6,4},{7,5},{8,10},{9,11},{10,... | collective-permute-start | bytes 909320 | tf_op jit(solution)/shard_map/ppermute | solution.py:1095
  253.6 39.7 %collective-permute-start.21 = (bf16[592,256]{1,0:T(8,128)(2,1)}, bf16[592,256]{1,0:T(8,128)(2,1)S(1)}, u32[]{:S(2)}, u32[]{:S(2)}) collective-permute-start(bf16[592,256]{1,0:T(8,128)(2,1)} %get-tuple-element.179), channel_id=1, source_target_pairs={{0,3},{1,2},{2,1},{3,0},{4,7},{5,6},{6,5},{7,4},{8,11},{9,10},{10,... | collective-permute-start | bytes 909320 | tf_op jit(solution)/shard_map/ppermute | solution.py:1095
  262.2 31.0 %collective-permute-start.18 = (bf16[1,2,128,2048]{3,2,1,0:T(8,128)(2,1)}, bf16[1,2,128,2048]{3,2,1,0:T(8,128)(2,1)S(1)}, u32[]{:S(2)}, u32[]{:S(2)}) collective-permute-start(bf16[1,2,128,2048]{3,2,1,0:T(8,128)(2,1)} %get-tuple-element.175), channel_id=1, source_target_pairs={{0,16},{16,0},{1,17},{17,1},{2,18},{18,2},{3,19},{19,3},{4,20},{20... | collective-permute-start | bytes 3145736 | tf_op jit(solution)/shard_map/ppermute | solution.py:1095
  298.7 9.6 %collective-permute-start.32 = (bf16[288,256]{1,0:T(8,128)(2,1)}, bf16[288,256]{1,0:T(8,128)(2,1)S(1)}, u32[]{:S(2)}, u32[]{:S(2)}) collective-permute-start(bf16[288,256]{1,0:T(8,128)(2,1)} %get-tuple-element.207), channel_id=1, source_target_pairs={{0,16},{16,0},{1,17},{17,1},{2,18},{18,2},{3,19},{19,3},{4,20},{20... | collective-permute-start | bytes 442376 | tf_op jit(solution)/shard_map/ppermute | solution.py:1095
  303.8 15.1 %collective-permute-start.38 = (bf16[1,128,2048]{2,1,0:T(8,128)(2,1)}, bf16[1,128,2048]{2,1,0:T(8,128)(2,1)S(1)}, u32[]{:S(2)}, u32[]{:S(2)}) collective-permute-start(bf16[1,128,2048]{2,1,0:T(8,128)(2,1)} %get-tuple-element.213), channel_id=1, source_target_pairs={{0,8},{4,12},{8,0},{12,4},{1,9},{5,13},{9,1},{13,5},{2,10},{6,14},... | collective-permute-start | bytes 1572872 | tf_op jit(solution)/shard_map/ppermute | solution.py:1095
  305.3 15.6 %collective-permute-start.17 = (bf16[4,128,1024]{2,1,0:T(8,128)(2,1)}, bf16[4,128,1024]{2,1,0:T(8,128)(2,1)}, u32[]{:S(2)}, u32[]{:S(2)}) collective-permute-start(bf16[4,128,1024]{2,1,0:T(8,128)(2,1)} %get-tuple-element.174), channel_id=1, source_target_pairs={{0,4},{4,0},{8,12},{12,8},{1,5},{5,1},{9,13},{13,9},{2,6},{6,2},{1... | collective-permute-start | bytes 3145736 | tf_op jit(solution)/shard_map/ppermute | solution.py:1095
  305.3 54.6 %collective-permute-start.25 = (bf16[1,2,192,1536]{3,2,1,0:T(8,128)(2,1)}, bf16[1,2,192,1536]{3,2,1,0:T(8,128)(2,1)S(1)}, u32[]{:S(2)}, u32[]{:S(2)}) collective-permute-start(bf16[1,2,192,1536]{3,2,1,0:T(8,128)(2,1)} %get-tuple-element.187), channel_id=1, source_target_pairs={{0,16},{16,0},{1,17},{17,1},{2,18},{18,2},{3,19},{19,3},{4,20},{20... | collective-permute-start | bytes 3538952 | tf_op jit(solution)/shard_map/ppermute | solution.py:1095
  305.9 54.1 %collective-permute-start.26 = (bf16[2,1,192,1536]{3,2,1,0:T(8,128)(2,1)}, bf16[2,1,192,1536]{3,2,1,0:T(8,128)(2,1)S(1)}, u32[]{:S(2)}, u32[]{:S(2)}) collective-permute-start(bf16[2,1,192,1536]{3,2,1,0:T(8,128)(2,1)} %get-tuple-element.189), channel_id=1, source_target_pairs={{0,8},{4,12},{8,0},{12,4},{1,9},{5,13},{9,1},{13,5},{2,10},{6,14},... | collective-permute-start | bytes 3538952 | tf_op jit(solution)/shard_map/ppermute | solution.py:1095
  332.2 53.3 %collective-permute-start.29 = (f32[7,1024]{1,0:T(8,128)S(1)}, f32[7,1024]{1,0:T(8,128)S(1)}, u32[]{:S(2)}, u32[]{:S(2)}) collective-permute-start(f32[7,1024]{1,0:T(8,128)S(1)} %concatenate.15.refs_0_), channel_id=1, source_target_pairs={{0,3},{1,2},{2,1},{3,0},{4,7},{5,6},{6,5},{7,4},{8,11},{9,10},{10,... | collective-permute-start | bytes 86024 | tf_op jit(solution)/shard_map/ppermute | solution.py:1095
  334.7 53.0 %collective-permute-start.28 = (f32[7,1024]{1,0:T(8,128)S(1)}, f32[7,1024]{1,0:T(8,128)S(1)}, u32[]{:S(2)}, u32[]{:S(2)}) collective-permute-start(f32[7,1024]{1,0:T(8,128)S(1)} %concatenate.15.refs_0_), channel_id=1, source_target_pairs={{0,2},{1,3},{2,0},{3,1},{4,6},{5,7},{6,4},{7,5},{8,10},{9,11},{10,... | collective-permute-start | bytes 86024 | tf_op jit(solution)/shard_map/ppermute | solution.py:1095
  352.8 9.2 %collective-permute-start.30 = (bf16[1,2,128,1024]{3,2,1,0:T(8,128)(2,1)S(1)}, bf16[1,2,128,1024]{3,2,1,0:T(8,128)(2,1)S(1)}, u32[]{:S(2)}, u32[]{:S(2)}) collective-permute-start(bf16[1,2,128,1024]{3,2,1,0:T(8,128)(2,1)S(1)} %copy-done.27), channel_id=1, source_target_pairs={{0,16},{16,0},{1,17},{17,1},{2,18},{18,2},{3,19},{19,3},{4,20},{20... | collective-permute-start | bytes 1572872 | tf_op jit(solution)/shard_map/ppermute | solution.py:1095
  359.9 27.9 %collective-permute-start.27 = (f32[7,1024]{1,0:T(8,128)S(1)}, f32[7,1024]{1,0:T(8,128)S(1)}, u32[]{:S(2)}, u32[]{:S(2)}) collective-permute-start(f32[7,1024]{1,0:T(8,128)S(1)} %concatenate.15.refs_0_), channel_id=1, source_target_pairs={{0,1},{1,0},{2,3},{3,2},{4,5},{5,4},{6,7},{7,6},{8,9},{9,8},{10,11... | collective-permute-start | bytes 86024 | tf_op jit(solution)/shard_map/ppermute | solution.py:1095
  360.0 35.2 %collective-permute-start.22 = (bf16[576,256]{1,0:T(8,128)(2,1)}, bf16[576,256]{1,0:T(8,128)(2,1)}, u32[]{:S(2)}, u32[]{:S(2)}) collective-permute-start(bf16[576,256]{1,0:T(8,128)(2,1)} %get-tuple-element.184), channel_id=1, source_target_pairs={{0,1},{1,0},{2,3},{3,2},{4,5},{5,4},{6,7},{7,6},{8,9},{9,8},{10,11... | collective-permute-start | bytes 884744 | tf_op jit(solution)/shard_map/ppermute | solution.py:1095
  362.0 33.2 %collective-permute-start.23 = (bf16[576,256]{1,0:T(8,128)(2,1)}, bf16[576,256]{1,0:T(8,128)(2,1)}, u32[]{:S(2)}, u32[]{:S(2)}) collective-permute-start(bf16[576,256]{1,0:T(8,128)(2,1)} %get-tuple-element.185), channel_id=1, source_target_pairs={{0,2},{1,3},{2,0},{3,1},{4,6},{5,7},{6,4},{7,5},{8,10},{9,11},{10,... | collective-permute-start | bytes 884744 | tf_op jit(solution)/shard_map/ppermute | solution.py:1095
  385.4 9.8 %collective-permute-start.24 = (bf16[576,256]{1,0:T(8,128)(2,1)S(1)}, bf16[576,256]{1,0:T(8,128)(2,1)S(1)}, u32[]{:S(2)}, u32[]{:S(2)}) collective-permute-start(bf16[576,256]{1,0:T(8,128)(2,1)S(1)} %copy-done.33), channel_id=1, source_target_pairs={{0,3},{1,2},{2,1},{3,0},{4,7},{5,6},{6,5},{7,4},{8,11},{9,10},{10,... | collective-permute-start | bytes 884744 | tf_op jit(solution)/shard_map/ppermute | solution.py:1095
  387.7 14.8 %collective-permute-start.39 = (bf16[4,128,384]{2,1,0:T(8,128)(2,1)S(1)}, bf16[4,128,384]{2,1,0:T(8,128)(2,1)S(1)}, u32[]{:S(2)}, u32[]{:S(2)}) collective-permute-start(bf16[4,128,384]{2,1,0:T(8,128)(2,1)S(1)} %copy-done.28), channel_id=1, source_target_pairs={{0,4},{4,0},{8,12},{12,8},{1,5},{5,1},{9,13},{13,9},{2,6},{6,2},{1... | collective-permute-start | bytes 1179656 | tf_op jit(solution)/shard_map/ppermute | solution.py:1095
  390.1 21.6 %collective-permute-start.34 = (f32[40,1024]{1,0:T(8,128)}, f32[40,1024]{1,0:T(8,128)S(1)}, u32[]{:S(2)}, u32[]{:S(2)}) collective-permute-start(f32[40,1024]{1,0:T(8,128)} %pack.1.refs_5_), channel_id=1, source_target_pairs={{0,4},{4,0},{8,12},{12,8},{1,5},{5,1},{9,13},{13,9},{2,6},{6,2},{1... | collective-permute-start | bytes 491528 | tf_op jit(solution)/shard_map/ppermute | solution.py:1095
  399.1 10.4 %collective-permute-start.31 = (bf16[288,256]{1,0:T(8,128)(2,1)}, bf16[288,256]{1,0:T(8,128)(2,1)S(1)}, u32[]{:S(2)}, u32[]{:S(2)}) collective-permute-start(bf16[288,256]{1,0:T(8,128)(2,1)} %get-tuple-element.205), channel_id=1, source_target_pairs={{0,16},{16,0},{1,17},{17,1},{2,18},{18,2},{3,19},{19,3},{4,20},{20... | collective-permute-start | bytes 442376 | tf_op jit(solution)/shard_map/ppermute | solution.py:1095
  406.0 8.0 %collective-permute-start.40 = (bf16[1,2,128,384]{3,2,1,0:T(8,128)(2,1)}, bf16[1,2,128,384]{3,2,1,0:T(8,128)(2,1)S(1)}, u32[]{:S(2)}, u32[]{:S(2)}) collective-permute-start(bf16[1,2,128,384]{3,2,1,0:T(8,128)(2,1)} %get-tuple-element.217), channel_id=1, source_target_pairs={{0,16},{16,0},{1,17},{17,1},{2,18},{18,2},{3,19},{19,3},{4,20},{20... | collective-permute-start | bytes 589832 | tf_op jit(solution)/shard_map/ppermute | solution.py:1095
  407.4 9.9 %collective-permute-start.37 = (bf16[1,128,1024]{2,1,0:T(8,128)(2,1)S(1)}, bf16[1,128,1024]{2,1,0:T(8,128)(2,1)S(1)}, u32[]{:S(2)}, u32[]{:S(2)}) collective-permute-start(bf16[1,128,1024]{2,1,0:T(8,128)(2,1)S(1)} %copy-done.44), channel_id=1, source_target_pairs={{0,8},{4,12},{8,0},{12,4},{1,9},{5,13},{9,1},{13,5},{2,10},{6,14},... | collective-permute-start | bytes 786440 | tf_op jit(solution)/shard_map/ppermute | solution.py:1095
  408.7 28.1 %collective-permute-start.33 = (bf16[16,32,384]{2,1,0:T(8,128)(2,1)}, bf16[16,32,384]{2,1,0:T(8,128)(2,1)S(1)}, u32[]{:S(2)}, u32[]{:S(2)}) collective-permute-start(bf16[16,32,384]{2,1,0:T(8,128)(2,1)} %dynamic-slice_bitcast_fusion.1), channel_id=1, source_target_pairs={{0,16},{16,0},{1,17},{17,1},{2,18},{18,2},{3,19},{19,3},{4,20},{20... | collective-permute-start | bytes 1179656 | tf_op jit(solution)/shard_map/ppermute | solution.py:1095
  409.4 41.6 %collective-permute-start.42 = (bf16[1,192,1536]{2,1,0:T(8,128)(2,1)}, bf16[1,192,1536]{2,1,0:T(8,128)(2,1)S(1)}, u32[]{:S(2)}, u32[]{:S(2)}) collective-permute-start(bf16[1,192,1536]{2,1,0:T(8,128)(2,1)} %get-tuple-element.222), channel_id=1, source_target_pairs={{0,8},{4,12},{8,0},{12,4},{1,9},{5,13},{9,1},{13,5},{2,10},{6,14},... | collective-permute-start | bytes 1769480 | tf_op jit(solution)/shard_map/ppermute | solution.py:1095
  411.7 40.5 %collective-permute-start.43 = (bf16[1,192,1536]{2,1,0:T(8,128)(2,1)}, bf16[1,192,1536]{2,1,0:T(8,128)(2,1)S(1)}, u32[]{:S(2)}, u32[]{:S(2)}) collective-permute-start(bf16[1,192,1536]{2,1,0:T(8,128)(2,1)} %get-tuple-element.225), channel_id=1, source_target_pairs={{0,16},{16,0},{1,17},{17,1},{2,18},{18,2},{3,19},{19,3},{4,20},{20... | collective-permute-start | bytes 1769480 | tf_op jit(solution)/shard_map/ppermute | solution.py:1095
  414.0 21.1 %collective-permute-start.35 = (f32[40,1024]{1,0:T(8,128)S(1)}, f32[40,1024]{1,0:T(8,128)}, u32[]{:S(2)}, u32[]{:S(2)}) collective-permute-start(f32[40,1024]{1,0:T(8,128)S(1)} %add.71), channel_id=1, source_target_pairs={{0,8},{4,12},{8,0},{12,4},{1,9},{5,13},{9,1},{13,5},{2,10},{6,14},... | collective-permute-start | bytes 491528 | tf_op jit(solution)/shard_map/ppermute | solution.py:1095
  417.3 16.2 %collective-permute-start.41 = (bf16[1,128,384]{2,1,0:T(8,128)(2,1)}, bf16[1,128,384]{2,1,0:T(8,128)(2,1)}, u32[]{:S(2)}, u32[]{:S(2)}) collective-permute-start(bf16[1,128,384]{2,1,0:T(8,128)(2,1)} %get-tuple-element.219), channel_id=1, source_target_pairs={{0,8},{4,12},{8,0},{12,4},{1,9},{5,13},{9,1},{13,5},{2,10},{6,14},... | collective-permute-start | bytes 294920 | tf_op jit(solution)/shard_map/ppermute | solution.py:1095
  436.1 5.4 %collective-permute-start.36 = (f32[40,1024]{1,0:T(8,128)S(1)}, f32[40,1024]{1,0:T(8,128)S(1)}, u32[]{:S(2)}, u32[]{:S(2)}) collective-permute-start(f32[40,1024]{1,0:T(8,128)S(1)} %add.72.refs_0_), channel_id=1, source_target_pairs={{0,16},{16,0},{1,17},{17,1},{2,18},{18,2},{3,19},{19,3},{4,20},{20... | collective-permute-start | bytes 491528 | tf_op jit(solution)/shard_map/ppermute | solution.py:1095
  (50 other events, 418.5 us)
Sparse Core Ops, SparseCore 0:
  22.0 73.5 all-gather.4
  97.2 59.0 all-gather.6
  158.7 75.6 reduce-scatter.2
  236.6 73.0 reduce-scatter.4

commit v3 on v2

--- a/solution.py
+++ b/solution.py
@@ -67,28 +67,31 @@
 
 
 KERNEL_US = {
-    "front": 8,
+    "front": 0.5,
     "attention_forward": 10,
-    "conv_mlp": 21,
-    "vit_mlp": 15,
-    "norm2_backward": 4,
-    "attention_backward": 42,
-    "norm1_backward": 3,
+    "conv_mlp": 0.5,
+    "vit_mlp": 33,
+    "norm2_backward": 0.5,
+    "attention_backward": 31,
+    "norm1_backward": 0.5,
+    "adapter": 0.5,
+    "conv_backward": 0.5,
     "output_halves": 3,
     "pack": 3,
     "unpack": 3,
-    "adapter": 7,
-    "conv_backward": 21,
-    "grad_fc": 8,
-    "grad_pw": 8,
-    "grad_qkv": 6,
-    "grad_adapt": 5,
-    "fold_fc": 2,
-    "fold_pw": 2,
-    "fold_qkv": 1,
-    "fold_adapt": 3,
-    "fold_fc_last": 1,
-    "fold_pw_last": 5,
+    "grad_fc": 0.5,
+    "grad_pw1": 0.5,
+    "grad_pw2": 0.5,
+    "grad_qkv": 0.5,
+    "grad_adapt": 0.5,
+    "fold_fc": 0.5,
+    "fold_pw1": 0.5,
+    "fold_pw2": 0.5,
+    "fold_qkv": 3,
+    "fold_adapt": 0.5,
+    "fold_fc_last": 3,
+    "fold_pw1_last": 3,
+    "fold_pw2_last": 3,
     "fold_qkv_last": 3,
     "fold_adapt_last": 3,
 }
@@ -193,10 +196,11 @@
 
 def front_kernel(
     base, count, s_ref, field_ref, k_ref, bias_ref, pool_ref, dy_ref, gate_ref, wa_ref, scale_ref,
-    send_ref, field_pooled_ref, d_pooled_ref, d_adapted_ref, sums_ref, shifted,
+    send_ref, field_pooled_ref, d_pooled_ref, d_adapted_ref, sums_ref, rank_ref, shifted,
 ):
     hi_valid = s_ref[5]
     cb = field_ref.shape[2]
+    rank_ref[...] = jnp.full(rank_ref.shape, s_ref[6], jnp.int32)
 
     @pl.when(pl.program_id(0) == 0)
     def _():
@@ -234,8 +238,9 @@
     d_pooled = jnp.where(row < s_ref[0] * GRID_LO, d_pooled, 0.0)
     d_pooled_ref[...] = d_pooled.astype(BF16)
     scaled = (d_pooled * scale_ref[...]).astype(BF16)
-    send_ref[count * GRID_HI :, :] = scaled
-    sums_ref[...] = jnp.sum(scaled.astype(F32), axis=0, keepdims=True)
+    sums_ref[0:1, :] = jnp.sum(scaled.astype(F32), axis=0, keepdims=True)
+    sums_ref[1:2, :] = jnp.sum(d_pooled, axis=0, keepdims=True)
+    sums_ref[2:, :] = jnp.zeros((6, cb), F32)
 
 
 def front(hires, kernel, bias, cotangent, gate, w_adapt, layer_scale, scalars, base, count, after=()):
@@ -264,11 +269,12 @@
             column(1),
         ],
         [
-            (column(cells + pooled_rows), array((cells + pooled_rows, channels))),
+            (column(cells), array((cells, channels))),
             (column(pooled_rows), array((pooled_rows, channels), F32)),
             (column(pooled_rows), array((pooled_rows, channels))),
             (whole((pooled_rows, width)), array((pooled_rows, width))),
-            (column(1), array((1, channels), F32)),
+            (column(8), array((8, channels), F32)),
+            (whole((8, LANES)), array((8, LANES), jnp.int32)),
         ],
         (hires, kernel, bias.reshape(1, -1), pool_block(), cotangent, gate.reshape(1, -1), w_adapt)
         + (layer_scale.reshape(1, -1),),
@@ -335,7 +341,7 @@
     pieces, refs = refs[:n_mp], refs[n_mp:]
     x_ref, gain_ref, w_out_ref, q_ref, k_ref, v_ref, wq_ref, wk_ref, wv_ref = refs[:9]
     d_attn_ref, dq_ref, dk_ref, dv_ref = refs[9:13]
-    sends, total = refs[13 : 13 + n_mp], refs[13 + n_mp]
+    send_ref, total = refs[13:]
     step = pl.program_id(0)
     mp = scalars_ref[1]
     part = pieces[0].shape[0]
@@ -374,17 +380,17 @@
 
     @pl.when(step == pl.num_programs(0) - 1)
     def _():
-        features = sends[0].shape[1]
+        features = send_ref.shape[2]
         xhat, _ = standardize(x_ref[...].astype(F32), norm_epsilon)
         weighted = total[...] * gain_ref[...]
         ones = jnp.sum(weighted, axis=-1, keepdims=True)
         twos = jnp.sum(weighted * xhat, axis=-1, keepdims=True)
         pad = jnp.zeros((-TOKENS % LANES, 1), F32)
         stats = stat_rows([jnp.concatenate([ones, pad]), jnp.concatenate([twos, pad])], features)
-        for k in range(n_mp):
-            at = pl.multiple_of((mp ^ k) * features, features)
-            sends[k][:TOKENS, :] = total[:, pl.ds(at, features)].astype(BF16)
-            sends[k][TOKENS:, :] = stats
+        for g in range(n_mp):
+            mine = slice(g * features, (g + 1) * features)
+            send_ref[g, :TOKENS, :] = total[:, mine].astype(BF16)
+            send_ref[g, TOKENS:, :] = stats
 
 
 def attention_backward(
@@ -398,7 +404,7 @@
     def weight(t):
         return pl.BlockSpec((width, LANES), lambda j, s: (0, t * blocks + j))
 
-    send_shape = (TOKENS + STAT_ROWS, width // n_mp)
+    send_shape = (n_mp, TOKENS + STAT_ROWS, width // n_mp)
     return call(
         functools.partial(attention_back_kernel, n_mp),
         "attention_backward",
@@ -408,7 +414,7 @@
         + [column, column, column, weight(0), weight(1), weight(2)],
         [(whole((TOKENS, width)), array((TOKENS, width)))]
         + [(column, array((TOKENS, heads_width)))] * 3
-        + [(whole(send_shape), array(send_shape))] * n_mp,
+        + [(held(send_shape), array(send_shape))],
         (*d_attn_pieces, tokens, gain.reshape(1, -1), w_out, q, k, v, w_flat, w_flat, w_flat),
         [pltpu.VMEM((TOKENS, width), F32)],
         after,
@@ -417,24 +423,22 @@
 
 
 def conv_mlp_kernel(
-    n_mp, cells, rows_ref, gain_ref, shift_ref, w1_hbm, b_ref, w2_hbm, pool_ref,
+    n_mp, chunk, s_ref, rows_ref, gain_ref, shift_ref, w1_hbm, b_ref, w2_hbm, wa_hbm, d_adapted_ref, pool_ref,
     normed_ref, inner_ref, pooled_ref, back_ref, send_ref, mean_ref, inv_ref, bias_ref,
-    full, w1_ref, w2_ref, sems,
+    branch_ref, adapted_ref, scale_ref, full, w1_ref, w2_ref, wa_ref, sems,
 ):
-    channels = rows_ref.shape[2]
+    cells, channels = rows_ref.shape[1:]
     cut = 256
     steps = w1_ref.shape[1] // cut
     cuts = [slice(j * cut, (j + 1) * cut) for j in range(steps)]
-    loads = []
+    loads = [pltpu.make_async_copy(wa_hbm, wa_ref, sems.at[2 * steps])]
     for j, at in enumerate(cuts):
         loads.append(pltpu.make_async_copy(w1_hbm.at[:, at], w1_ref.at[:, at], sems.at[j]))
         loads.append(pltpu.make_async_copy(w2_hbm.at[at, :], w2_ref.at[at, :], sems.at[steps + j]))
     for load in loads:
         load.start()
     for g in range(n_mp):
-        mine = slice(g * channels, (g + 1) * channels)
-        full[:, mine] = rows_ref[g, :cells].astype(F32)
-        back_ref[:, mine] = rows_ref[g, cells:]
+        full[:, g * channels : (g + 1) * channels] = rows_ref[g].astype(F32)
     spatial = full[...]
     mean = jnp.mean(spatial, axis=-1, keepdims=True)
     centred = spatial - mean
@@ -444,11 +448,16 @@
     mean_ref[...] = jnp.broadcast_to(mean, mean_ref.shape)
     inv_ref[...] = jnp.broadcast_to(inv, inv_ref.shape)
     normed_ref[...] = (xhat * gain_ref[...] + shift_ref[...]).astype(BF16)
+    loads[0].wait()
+    count = back_ref.shape[0]
+    valid = lax.broadcasted_iota(jnp.int32, (count, 1), 0) + chunk * count < s_ref[0] * GRID_LO
+    back = dot_nt(d_adapted_ref[...], wa_ref[...])
+    back_ref[...] = jnp.where(valid, back, 0.0).astype(BF16)
     for j, at in enumerate(cuts):
-        loads[2 * j].wait()
+        loads[2 * j + 1].wait()
         active, slope = gelu_pair(dot(normed_ref[...], w1_ref[:, at]) + b_ref[:, at])
         active = active.astype(BF16)
-        loads[2 * j + 1].wait()
+        loads[2 * j + 2].wait()
         d_active = dot_nt(back_ref[...], w2_ref[at, :]).astype(BF16)
         backs = []
         for i in range(cells // CELL_BLOCK):
@@ -460,36 +469,38 @@
         inner_ref[:, at] = d_inner
         bias_ref[:, at] = jnp.sum(d_inner.astype(F32), axis=0, keepdims=True)
 
-    branch = dot(pooled_ref[...], w2_ref[...]).astype(BF16)
     d_normed = dot_nt(inner_ref[...], w1_ref[...])
     weighted = d_normed * gain_ref[...]
     ones = jnp.sum(weighted, axis=-1, keepdims=True)
     twos = jnp.sum(weighted * full[...], axis=-1, keepdims=True)
     stats = stat_rows([ones, twos], channels)
     for g in range(n_mp):
-        mine = slice(g * channels, (g + 1) * channels)
-        send_ref[g, :cells, :] = d_normed[:, mine].astype(BF16)
-        send_ref[g, cells : cells + STAT_ROWS, :] = stats
-        send_ref[g, cells + STAT_ROWS :, :] = branch[:, mine]
-
-
-def conv_mlp(rows, gain, shift, w1, b, w2, after=()):
-    n_mp, both, channels = rows.shape
+        send_ref[g, :cells, :] = d_normed[:, g * channels : (g + 1) * channels].astype(BF16)
+        send_ref[g, cells:, :] = stats
+    branch = dot(pooled_ref[...], w2_ref[...])
+    scale_ref[...] = jnp.sum(back_ref[...].astype(F32) * branch, axis=0, keepdims=True)
+    branch_ref[...] = jnp.where(valid, branch, 0.0).astype(BF16)
+    adapted_ref[...] = dot(branch_ref[...], wa_ref[...])
+
+
+def conv_mlp(rows, gain, shift, w1, b, w2, wa, d_adapted, chunk, scalars, after=()):
+    n_mp, cells, channels = rows.shape
     total, hidden = w1.shape
-    cells = both * 16 // 25
-    pooled = both - cells
-    send_shape = (n_mp, both + STAT_ROWS, channels)
+    width = wa.shape[1]
+    pooled = cells * 9 // 16
+    send_shape = (n_mp, cells + STAT_ROWS, channels)
     anywhere = pl.BlockSpec(memory_space=pl.ANY)
 
     def out(shape, dtype=BF16):
         return (held(shape), array(shape, dtype))
 
     return call(
-        functools.partial(conv_mlp_kernel, n_mp, cells),
+        functools.partial(conv_mlp_kernel, n_mp, chunk),
         "conv_mlp",
         (1,),
-        [held((n_mp, both, channels)), held((1, total)), held((1, total)), anywhere]
-        + [held((1, hidden)), anywhere, held((POOL_BLOCK, CELL_BLOCK))],
+        [held((n_mp, cells, channels)), held((1, total)), held((1, total)), anywhere]
+        + [held((1, hidden)), anywhere, anywhere, held((pooled, width))]
+        + [held((POOL_BLOCK, CELL_BLOCK))],
         [
             out((cells, total)),
             out((cells, hidden)),
@@ -499,15 +510,21 @@
             out((cells, LANES), F32),
             out((cells, LANES), F32),
             out((1, hidden), F32),
+            out((pooled, total)),
+            out((pooled, width), F32),
+            out((1, total), F32),
         ],
-        (rows, gain.reshape(1, -1), shift.reshape(1, -1), w1, b.reshape(1, -1), w2, pool_block()),
+        (rows, gain.reshape(1, -1), shift.reshape(1, -1), w1, b.reshape(1, -1), w2, wa, d_adapted)
+        + (pool_block(),),
         [
             pltpu.VMEM((cells, total), F32),
             pltpu.VMEM((total, hidden), BF16),
             pltpu.VMEM((hidden, total), BF16),
-            pltpu.SemaphoreType.DMA((2 * (hidden // 256),)),
+            pltpu.VMEM((total, width), BF16),
+            pltpu.SemaphoreType.DMA((2 * (hidden // 256) + 1,)),
         ],
         after,
+        prefetch=scalars,
     )
 
 
@@ -738,54 +755,51 @@
 
 
 def adapter_kernel(chunks, scalars_ref, *refs):
-    received, d_pooled, fields = (refs[i * chunks : (i + 1) * chunks] for i in range(3))
-    refs = refs[3 * chunks :]
+    parts, fields = refs[:chunks], refs[chunks : 2 * chunks]
+    refs = refs[2 * chunks :]
     pb_ref, scale_ref, wa_ref, active_ref, w2_ref, gate_ref, dy_ref = refs[:7]
-    pooled_ref, scale_sum_ref, gate_sum_ref = refs[7:10]
-    sends, total = refs[10:-1], refs[-1]
-    sums = jnp.zeros(scale_sum_ref.shape, F32)
+    pooled_ref, gate_sum_ref = refs[7:9]
+    send_ref, total = refs[9:]
     first = 0
-    for c in range(chunks):
-        count = fields[c].shape[0]
-        branch = received[c][received[c].shape[0] - count :, :].astype(F32) + pb_ref[...]
-        sums = sums + jnp.sum(d_pooled[c][...].astype(F32) * branch, axis=0, keepdims=True)
-        value = fields[c][...] + scale_ref[...] * branch
+    for field in fields:
+        rows = slice(first, first + field.shape[0])
+        value = field[...] + scale_ref[...] * pb_ref[...]
         row = lax.broadcasted_iota(jnp.int32, value.shape, 0) + first
         value = jnp.where(row < scalars_ref[0] * GRID_LO, value, 0.0)
-        pooled_ref[first : first + count, :] = value.astype(BF16)
-        first += count
-    scale_sum_ref[...] = sums
+        pooled_ref[rows, :] = value.astype(BF16)
+        first += field.shape[0]
+    total[...] = dot(pooled_ref[...], wa_ref[...])
+    first = 0
+    for part in parts:
+        total[first : first + part.shape[0], :] += part[...]
+        first += part.shape[0]
     gate = gate_ref[...]
-    adapted = dot(pooled_ref[...], wa_ref[...])
+    adapted = total[...]
     sums = jnp.sum(dy_ref[...].astype(F32) * adapted, axis=0, keepdims=True)
     gate_sum_ref[...] = (1.0 - gate * gate) * sums
     total[...] = dot(active_ref[...], w2_ref[...]) + gate * adapted
-    features = sends[0].shape[1]
-    for k, send in enumerate(sends):
-        at = pl.multiple_of((scalars_ref[1] ^ k) * features, features)
-        send[...] = total[:, pl.ds(at, features)].astype(BF16)
-
-
-def adapter(
-    n_mp, received, d_pooled, fields, pw2_bias, layer_scale, w_adapt, active, w2, gate, cotangent, scalars, after=()
-):
+    features = send_ref.shape[2]
+    for g in range(send_ref.shape[0]):
+        send_ref[g] = total[:, g * features : (g + 1) * features].astype(BF16)
+
+
+def adapter(n_mp, parts, fields, pw2_bias, layer_scale, w_adapt, active, w2, gate, cotangent, scalars, after=()):
     channels, width = w_adapt.shape
     hidden = w2.shape[0]
-    send_shape = (TOKENS, width // n_mp)
+    send_shape = (n_mp, TOKENS, width // n_mp)
     return call(
         functools.partial(adapter_kernel, len(fields)),
         "adapter",
         (1,),
-        [held(v.shape) for v in (*received, *d_pooled, *fields)]
+        [held(v.shape) for v in (*parts, *fields)]
         + [held((1, channels)), held((1, channels)), held((channels, width))]
         + [held((TOKENS, hidden)), held((hidden, width)), held((1, width)), image(width)],
         [
             (held((TOKENS, channels)), array((TOKENS, channels))),
-            (held((1, channels)), array((1, channels), F32)),
             (held((1, width)), array((1, width), F32)),
-        ]
-        + [(held(send_shape), array(send_shape))] * n_mp,
-        (*received, *d_pooled, *fields, pw2_bias.reshape(1, -1), layer_scale.reshape(1, -1), w_adapt)
+            (held(send_shape), array(send_shape)),
+        ],
+        (*parts, *fields, pw2_bias.reshape(1, -1), layer_scale.reshape(1, -1), w_adapt)
         + (active, w2, gate.reshape(1, -1), cotangent),
         [pltpu.VMEM((TOKENS, width), F32)],
         after,
@@ -967,17 +981,16 @@
 
 
 def norm1_backward(got, tokens, d_attn, gain, cotangent, scalars, after=()):
-    n_mp = len(got)
     rows, features = got[0].shape
     width = tokens.shape[2]
     mine = pl.BlockSpec((TOKENS, features), lambda j, s: (0, s[1]))
     mine_of = pl.BlockSpec((None, TOKENS, features), lambda j, s: (s[3], 0, s[1]))
     half = (held((TOKENS // 2, features)), array((TOKENS // 2, features)))
     return call(
-        functools.partial(norm1_back_kernel, n_mp),
+        functools.partial(norm1_back_kernel, len(got)),
         "norm1_backward",
         (1,),
-        [held((rows, features))] * n_mp
+        [held((rows, features))] * len(got)
         + [image(width), mine_of, mine]
         + [pl.BlockSpec((1, features), lambda j, s: (0, s[1])), mine_of],
         [half, half, (held((8, features)), array((8, features), F32))],
@@ -1020,6 +1033,9 @@
     )
 
 
+WIDE_ROWS = 7
+
+
 def slots_of(shapes, width):
     row, lane, slots = 0, 0, []
     for rows, n in shapes:
@@ -1037,33 +1053,42 @@
     return slots, -(-(row + 1) // 8) * 8
 
 
-def pack_kernel(n_mp, slots, *refs):
-    wide, arrays, packed_ref = refs[:n_mp], refs[n_mp:-1], refs[-1]
+def pack_kernel(n_mp, slots, s_ref, *refs):
+    wide, refs = refs[:n_mp], refs[n_mp:]
+    sums_ref, bias_ref, scale_ref, *arrays, packed_ref, total_ref = refs
     packed_ref[...] = jnp.zeros(packed_ref.shape, F32)
     total = wide[0][...]
     for piece in wide[1:]:
         total = total + piece[...]
-    for r, pieces in enumerate(slots[0]):
-        for row, lane, at, n in pieces:
-            packed_ref[row : row + 1, lane : lane + n] = total[r : r + 1, at : at + n]
-    for array_ref, mine in zip(arrays, slots[1:]):
+    total_ref[...] = total
+    channels = scale_ref.shape[1]
+    mine = total_ref[pl.ds(WIDE_ROWS + s_ref[1], 1), :][:, :channels]
+    g_scale = mine / scale_ref[...] + bias_ref[...] * sums_ref[1:2, :]
+    values = [total[:WIDE_ROWS], g_scale, sums_ref[0:1, :]] + [v[...] for v in arrays]
+    for value, mine in zip(values, slots):
         for r, pieces in enumerate(mine):
             for row, lane, at, n in pieces:
-                packed_ref[row : row + 1, lane : lane + n] = array_ref[r : r + 1, at : at + n]
-
-
-def pack(wide_pieces, arrays, rows, after=()):
+                packed_ref[row : row + 1, lane : lane + n] = value[r : r + 1, at : at + n]
+
+
+def pack(wide_pieces, sums, pw2_bias, layer_scale, arrays, rows, scalars, after=()):
+    n_mp = len(wide_pieces)
     width = wide_pieces[0].shape[1]
-    shapes = [wide_pieces[0].shape] + [(count, v.shape[1]) for v, count in zip(arrays, rows)]
+    channels = sums.shape[1]
+    shapes = [(WIDE_ROWS, width), (1, channels), (1, channels)]
+    shapes += [(count, v.shape[1]) for v, count in zip(arrays, rows)]
     slots, total = slots_of(shapes, width)
+    operands = (*wide_pieces, sums, pw2_bias.reshape(1, -1), layer_scale.reshape(1, -1), *arrays)
     packed = call(
-        functools.partial(pack_kernel, len(wide_pieces), slots),
+        functools.partial(pack_kernel, n_mp, slots),
         "pack",
         (1,),
-        [held(v.shape) for v in (*wide_pieces, *arrays)],
+        [held(v.shape) for v in operands],
         [(held((total, width)), array((total, width), F32))],
-        (*wide_pieces, *arrays),
+        operands,
+        [pltpu.VMEM(wide_pieces[0].shape, F32)],
         after=after,
+        prefetch=scalars,
     )[0]
     return packed, slots
 
@@ -1107,17 +1132,23 @@
     return blocks[:1] + [swap(block, axis, k) for k, block in enumerate(blocks) if k]
 
 
-def spread(value, axis):
-    value = value[:, None]
+def in_order(values, axis):
+    me = lax.axis_index(axis)
     apart = 1
-    while apart < lax.axis_size(axis):
+    while apart < len(values):
+        turned = (me & apart) > 0
+        values = [jnp.where(turned, values[i ^ apart], values[i]) for i in range(len(values))]
+        apart *= 2
+    return values
+
+
+def spread(value, steps):
+    for axis, apart, place in steps:
         other = swap(value, axis, apart)
         turned = (lax.axis_index(axis) & apart) > 0
-        value = jnp.concatenate(
-            [jnp.where(turned, other, value), jnp.where(turned, value, other)], axis=1
-        )
-        apart *= 2
-    return value.reshape((value.shape[0], -1) + value.shape[3:])
+        pair = [jnp.where(turned, other, value), jnp.where(turned, value, other)]
+        value = jnp.stack(pair, axis=place)
+    return value.reshape(value.shape[0], -1, value.shape[-1])
 
 
 def halve(value, dim, axis, apart, bit):
@@ -1130,39 +1161,21 @@
     return keep, swap(send, "dp", 1)
 
 
-def first_fold(name, keep, got, scalars, after, cut=False):
+def first_fold(name, halves, scalars, after, dp_first=False):
     n_path, n_dp = lax.axis_size("path"), lax.axis_size("dp")
-    block, lanes = keep.shape[1:]
+    block, lanes = halves[0].shape[1:]
     shape = (n_path, n_dp // 4, 2, block, lanes)
-    got = got.reshape(shape)
-    keep = keep.reshape(shape)
-    if cut:
-        half = lanes // 2
-        parts = [(keep, got, 0, 3, half, 0), (keep, got, 2, 4, half, 1)]
-    else:
-        parts = [(keep, got, 0, 3, lanes, 0)]
-    out = fold(name, parts, scalars, after)
-    result = [(out[1], swap(out[0], "path", 1), False)]
-    if cut:
-        result.append((out[3], swap(out[2], "dp", 2), True))
-    return result
-
-
-def second_fold(name, parts, scalars, after):
-    ins = []
-    for hold, got, path_next in parts:
-        dim, slot = (0, 3) if path_next else (1, 4)
-        ins.append((hold, got, dim, slot, hold.shape[-1], 0))
-    out = fold(name, ins, scalars, after)
-    result = []
-    for i, (_, _, path_next) in enumerate(parts):
-        send, hold = out[2 * i : 2 * i + 2]
-        result.append((hold, swap(send, *(("path", 1) if path_next else ("dp", 2)))))
-    return result
-
-
-def arrived(parts):
-    return tuple(part[1] for part in parts)
+    keep, got = (half.reshape(shape) for half in halves)
+    dim, slot = (2, 4) if dp_first else (0, 3)
+    send, hold = fold(name, [(keep, got, dim, slot, lanes, 0)], scalars, after)
+    return hold, swap(send, *(("dp", 2) if dp_first else ("path", 1))), dp_first
+
+
+def second_fold(name, part, scalars, after):
+    hold, got, path_next = part
+    dim, slot = (0, 3) if path_next else (1, 4)
+    send, hold = fold(name, [(hold, got, dim, slot, hold.shape[-1], 0)], scalars, after)
+    return hold, swap(send, *(("path", 1) if path_next else ("dp", 2)))
 
 
 def last_sum(hold, got):
@@ -1237,24 +1250,18 @@
 
     valid = pick(valid_rows, 0, path)
     hi_valid = (valid * GRID_HI + GRID_LO - 1) // GRID_LO
-    scalars = jnp.stack([valid, mp, dp & 1, path, (dp >> 1) & 1, hi_valid])
+    rank = path * lax.axis_size("dp") + dp
+    scalars = jnp.stack([valid, mp, dp & 1, path, (dp >> 1) & 1, hi_valid, rank])
     gate = jnp.tanh(gate_param)
 
     def my_features(v):
         return lax.dynamic_slice_in_dim(v, mp * features, features, v.ndim - 1)
 
-    share_rows = heads_width // groups
-    share = lax.dynamic_slice_in_dim(
-        w_out, (path * lax.axis_size("dp") + dp) * share_rows, share_rows, 0
-    )
-    w_out_pieces = jnp.stack(gathered(share, "mp"))
-    w_out_pieces = spread(spread(w_out_pieces, "dp"), "path")
-
     rows, rows_all, pooled_field, d_pooled, d_adapted = [], [], [], [], []
-    g_pw2_bias = 0.0
+    front_sums, ranks = 0.0, []
     last = ()
     for c in range(CHUNKS):
-        send, *chunk, sums = front(
+        send, *chunk, sums, rank_out = front(
             hires,
             dw_kernel,
             dw_bias,
@@ -1268,15 +1275,35 @@
             last,
         )
         last = (sums,)
-        g_pw2_bias = g_pw2_bias + sums
+        front_sums = front_sums + sums
+        ranks.append(rank_out)
         rows.append(send)
         rows_all.append(lax.all_gather(send, "mp", axis=0, tiled=False))
         for kept, value in zip((pooled_field, d_pooled, d_adapted), chunk):
             kept.append(value)
 
+    rank = ranks[-1][0, 0]
+    out_rows, adapt_rows = heads_width // groups, channels // groups
+    scaled = w_adapt.astype(F32) * layer_scale[:, None]
+    share = jnp.concatenate(
+        [
+            lax.dynamic_slice_in_dim(w_out, rank * out_rows, out_rows, 0),
+            lax.dynamic_slice_in_dim(scaled, rank * adapt_rows, adapt_rows, 0).astype(BF16),
+        ]
+    )
+    shares = gathered(share, "mp")
+    chips = [("dp", 1 << b, -3) for b in range(lax.axis_size("dp").bit_length() - 2, 0, -1)]
+    w_out_pieces = spread(
+        jnp.stack([v[:out_rows] for v in shares]), [("path", 1, -3)] + chips + [("dp", 1, -3)]
+    )
+    w_adapt_all = spread(
+        jnp.stack(in_order([v[out_rows:] for v in shares], "mp")),
+        chips + [("path", 1, 1), ("dp", 1, -3)],
+    ).reshape(all_channels, width)
+
     w_flat = w_qkv.reshape(width, 3 * heads_width)
     normed1, query, keys, values, attended = attention_forward(
-        tokens, attention_norm_gain, attention_norm_bias, w_flat, qv_bias, scalars, last
+        tokens, attention_norm_gain, attention_norm_bias, w_flat, qv_bias, scalars, last + tuple(rows_all[:1])
     )
     attended_pieces = gathered(attended, "mp")
     last = (attended,)
@@ -1289,6 +1316,10 @@
             w_pw1,
             pw1_bias,
             w_pw2,
+            w_adapt_all,
+            d_adapted[c],
+            c,
+            scalars,
             after,
         )
         return out, lax.psum_scatter(out[4], "mp", scatter_dimension=0, tiled=False), (out[7],)
@@ -1311,36 +1342,79 @@
         scalars,
         last,
     )
+    d_normed2_pieces = exchanged(sends, "mp")
     last = (g_fc1_bias,)
-    d_normed2_pieces = exchanged(sends, "mp")
-    dy = pick(cotangent, 0, path)
-    fc_halves = weight_grads(
-        "grad_fc", groups, [[(normed2, d_fc_inner)], [(dy, fc_active)]], scalars, last
-    )
-    fc_halves = across(fc_halves)
-    last = (fc_halves[0],)
-    d_attn_part, norm2_sums = norm2_backward(
-        d_normed2_pieces, hidden1, cotangent, mlp_norm_gain, scalars, last
-    )
-    d_attn_pieces = gathered(d_attn_part, "mp")
-    last = (norm2_sums,)
     for c in range(1, CHUNKS):
         out, got, last = conv(c, last)
         conv_out.append(out)
         received.append(got)
-    conv_normed, conv_inner, pooled_active, backs, _, means, invs, bias_sums = zip(*conv_out)
+    (
+        conv_normed,
+        conv_inner,
+        pooled_active,
+        backs,
+        _,
+        means,
+        invs,
+        bias_sums,
+        branches,
+        adapted_parts,
+        scale_sums,
+    ) = zip(*conv_out)
     g_pw1_bias = sum(bias_sums)
-    pw_halves = weight_grads(
-        "grad_pw",
-        groups,
-        [list(zip(conv_normed, conv_inner)), list(zip(backs, pooled_active))],
+
+    pooled, g_gate, send = adapter(
+        n_mp,
+        adapted_parts,
+        pooled_field,
+        pw2_bias,
+        layer_scale,
+        w_adapt,
+        fc_active,
+        down_weight,
+        gate,
+        cotangent,
         scalars,
-        last,
-    )
-    pw_halves = across(pw_halves)
-    last = (pw_halves[0],)
-
-    d_attn, d_query, d_keys, d_values, *sends = attention_backward(
+        last + tuple(received[:-1]),
+    )
+    branch_sum = lax.psum_scatter(send, "mp", scatter_dimension=0, tiled=False)
+    d_attn_part, norm2_sums = norm2_backward(
+        d_normed2_pieces, hidden1, cotangent, mlp_norm_gain, scalars, (g_gate,)
+    )
+    d_attn_pieces = gathered(d_attn_part, "mp")
+    dy = pick(cotangent, 0, path)
+    fc_halves = across(
+        weight_grads(
+            "grad_fc",
+            groups,
+            [[(normed2, d_fc_inner)], [(dy, fc_active)]],
+            scalars,
+            (norm2_sums,),
+        )
+    )
+    pooled_rows = d_adapted[0].shape[0]
+    pooled_cuts = [pooled[c * pooled_rows : (c + 1) * pooled_rows] for c in range(CHUNKS)]
+    adapt_halves = across(
+        weight_grads(
+            "grad_adapt",
+            groups,
+            [list(zip(d_adapted, branches)), list(zip(d_adapted, pooled_cuts))],
+            scalars,
+            fc_halves[:1],
+        )
+    )
+    pw2_halves = across(
+        weight_grads(
+            "grad_pw2", groups, [list(zip(backs, pooled_active))], scalars, adapt_halves[:1]
+        )
+    )
+    pw1_halves = across(
+        weight_grads(
+            "grad_pw1", groups, [list(zip(conv_normed, conv_inner))], scalars, pw2_halves[:1]
+        )
+    )
+
+    d_attn, d_query, d_keys, d_values, send = attention_backward(
         n_mp,
         tokens,
         attention_norm_gain,
@@ -1351,85 +1425,51 @@
         values,
         w_flat,
         scalars,
-        last,
-    )
-    d_normed1_pieces = exchanged(sends, "mp")
-    last = (d_query,)
-    fc_parts = first_fold("fold_fc", *fc_halves, scalars, last)
-    last = (fc_parts[0][0],)
-    pw_parts = first_fold("fold_pw", *pw_halves, scalars, last, True)
-    last = (pw_parts[0][0],)
-    qkv_halves = weight_grads(
-        "grad_qkv",
-        groups,
-        [
-            [(normed1, d_query)],
-            [(normed1, d_keys)],
-            [(normed1, d_values)],
-            [(d_attn, attended)],
-        ],
-        scalars,
-        last,
-    )
-    qkv_halves = across(qkv_halves)
-    last = (qkv_halves[0],)
+        pw1_halves[:1],
+    )
+    d_normed1 = lax.psum_scatter(send, "mp", scatter_dimension=0, tiled=False)
+    fc_part = first_fold("fold_fc", fc_halves, scalars, (d_query, *received[1:]))
+    adapt_part = first_fold("fold_adapt", adapt_halves, scalars, fc_part[:1], True)
+    pw2_part = first_fold("fold_pw2", pw2_halves, scalars, adapt_part[:1], True)
+    pw1_part = first_fold("fold_pw1", pw1_halves, scalars, pw2_part[:1])
+    qkv_halves = across(
+        weight_grads(
+            "grad_qkv",
+            groups,
+            [
+                [(normed1, d_query)],
+                [(normed1, d_keys)],
+                [(normed1, d_values)],
+                [(d_attn, attended)],
+            ],
+            scalars,
+            pw1_part[:1],
+        )
+    )
     g_qv_bias = jnp.stack(
         [jnp.sum(d_query.astype(F32), axis=0), jnp.sum(d_values.astype(F32), axis=0)]
     )
+
     tokens_keep, tokens_send, norm1_sums = norm1_backward(
-        d_normed1_pieces,
+        [d_normed1],
         tokens,
         d_attn,
         attention_norm_gain,
         cotangent,
         scalars,
-        last + arrived(fc_parts)
-    )
-    last = (norm1_sums,)
-    fc_parts = second_fold("fold_fc_last", fc_parts, scalars, last)
-    last = (fc_parts[0][0],)
-    qkv_parts = first_fold("fold_qkv", *qkv_halves, scalars, last)
-    last = (qkv_parts[0][0],)
-
-    pooled, g_scale, g_gate, *sends = adapter(
-        n_mp,
-        received,
-        d_pooled,
-        pooled_field,
-        pw2_bias,
-        layer_scale,
-        w_adapt,
-        fc_active,
-        down_weight,
-        gate,
-        cotangent,
-        scalars,
-        last,
-    )
-    branch_pieces = exchanged(sends, "mp")
-    pooled_rows = d_adapted[0].shape[0]
-    adapt_halves = weight_grads(
-        "grad_adapt",
-        groups,
-        [
-            [
-                (d_adapted[c], pooled[c * pooled_rows : (c + 1) * pooled_rows])
-                for c in range(CHUNKS)
-            ]
-        ],
-        scalars,
-        (g_scale,),
-    )
-    adapt_halves = across(adapt_halves)
-    last = (adapt_halves[0],)
+        qkv_halves[:1],
+    )
+
     def placed(v):
         return lax.dynamic_update_slice(jnp.zeros((width,), F32), v, (mp * features,))
 
+    scale_rows = jnp.pad(sum(scale_sums).reshape(n_mp, channels), ((0, 0), (0, width - channels)))
     wide = jnp.concatenate(
-        [norm2_sums[:3]] + [placed(norm1_sums[i])[None] for i in range(3)] + [g_gate]
+        [norm2_sums[:3]]
+        + [placed(norm1_sums[i])[None] for i in range(3)]
+        + [g_gate, scale_rows]
     )
     wide_pieces = gathered(wide, "mp")
-
     d_field, g_kernel, conv_sums = conv_backward(
         received,
         rows,
@@ -1441,21 +1481,30 @@
         lax.dynamic_slice_in_dim(channel_norm_gain, mp * channels, channels, 0),
         all_channels,
         scalars,
-        last + arrived(pw_parts) + arrived(qkv_parts),
-    )
-    last = (conv_sums,)
-    small = [g_qv_bias, g_fc1_bias, g_pw1_bias, g_kernel, conv_sums, g_pw2_bias, g_scale]
-    packed, slots = pack(wide_pieces, small, (2, 1, 1, 49, 3, 1, 1), last)
-    last = (packed,)
+        (norm1_sums, fc_part[1], adapt_part[1]),
+    )
+
+    packed, slots = pack(
+        wide_pieces,
+        front_sums,
+        pw2_bias,
+        layer_scale,
+        [g_qv_bias, g_fc1_bias, g_pw1_bias, g_kernel, conv_sums],
+        (2, 1, 1, 49, 3),
+        scalars,
+        (conv_sums,),
+    )
+    packed_first = packed
     packed = summed(packed, ("dp",))
-    pw_parts = second_fold("fold_pw_last", pw_parts, scalars, last)
-    last = (pw_parts[0][0],)
-    output_keep, output_send = output_halves(branch_pieces, hidden1, fc2_bias, scalars, last)
-    last = (output_keep,)
-    qkv_parts = second_fold("fold_qkv_last", qkv_parts, scalars, last)
-    last = (qkv_parts[0][0],)
-    adapt_parts = first_fold("fold_adapt", *adapt_halves, scalars, last)
-    last = (adapt_parts[0][0],)
+    output_keep, output_send = output_halves(
+        [branch_sum], hidden1, fc2_bias, scalars, (packed_first, pw2_part[1], pw1_part[1])
+    )
+    adapt_part = second_fold("fold_adapt_last", adapt_part, scalars, (output_keep,))
+    fc_part = second_fold("fold_fc_last", fc_part, scalars, adapt_part[:1])
+    pw2_part = second_fold("fold_pw2_last", pw2_part, scalars, fc_part[:1])
+    pw1_part = second_fold("fold_pw1_last", pw1_part, scalars, pw2_part[:1])
+    qkv_part = first_fold("fold_qkv", qkv_halves, scalars, pw1_part[:1], True)
+    qkv_part = second_fold("fold_qkv_last", qkv_part, scalars, qkv_part[:1])
 
     def both_images(mine, send):
         other = swap(send, "path", 1)
@@ -1469,19 +1518,28 @@
     output = both_images(output_keep, output_send)
     tokens_grad = both_images(tokens_keep, tokens_send)
     hires_grad = keep_half(d_field)
-    adapt_parts = second_fold("fold_adapt_last", adapt_parts, scalars, last)
-
-    (both,) = (last_sum(*part) for part in fc_parts)
-    g_fc1_mine, g_fc2_mine = both[:, : w_fc1.shape[1]], both[:, w_fc1.shape[1] :]
-    g_pw1_mine, g_pw2_mine = (last_sum(*part) for part in pw_parts)
-    (g_rest,) = (last_sum(*part) for part in qkv_parts)
+
+    g_adapt = last_sum(*adapt_part)
+    g_adapt_mine = sum(
+        piece.astype(F32)
+        for piece in exchanged(
+            [
+                lax.dynamic_slice_in_dim(g_adapt, (mp ^ k) * channels, channels, 1).astype(BF16)
+                for k in range(n_mp)
+            ],
+            "mp",
+        )
+    )
+    g_adapt_mine = g_adapt_mine * layer_scale + g_adapt[:, all_channels:]
+    g_fc = last_sum(*fc_part)
+    g_fc1_mine, g_fc2_mine = g_fc[:, : w_fc1.shape[1]], g_fc[:, w_fc1.shape[1] :]
+    g_pw1_mine, g_pw2_mine = last_sum(*pw1_part), last_sum(*pw2_part)
+    g_rest = last_sum(*qkv_part)
     g_qkv_mine = g_rest[:, : 3 * heads_width].reshape(-1, 3, heads_width)
     g_out_mine = g_rest[:, 3 * heads_width :]
-    (g_adapt_mine,) = (last_sum(*part) for part in adapt_parts)
-
 
     small = unpack(packed, swap(packed, "path", 1), slots)
-    wide, g_qv_bias, g_fc1_bias, g_pw1_bias, g_kernel, conv_sums, g_pw2_bias, g_scale = small
+    wide, g_scale, g_pw2_bias, g_qv_bias, g_fc1_bias, g_pw1_bias, g_kernel, conv_sums = small
     g_out_bias, g_norm2_gain, g_norm2_bias, g_norm1_gain, g_norm1_bias, g_fc2_bias, g_gate = wide
     g_dw_bias, g_cnorm_gain, g_cnorm_bias = conv_sums
     return (

time: 467 us -> 444 us (0.951)
  waiting for transfers between devices: 99.9 us -> 63.5 us
  starting transfers between devices: 80.2 us -> 59 us
  Pallas kernels: 212 us -> 232 us
  other arithmetic: 13.5 us -> 25.3 us
    ppermute x44 -> x45, starting transfers between devices: 80.1 us -> 58.7 us  [swap(): return lax.ppermute(value, axis, [(i, i ^ apart) for i in range(n)])]
    pallas_call x26 -> x29, Pallas kernels: 212 us -> 232 us  [call(): pl.pallas_call(run, grid_spec=pltpu.PrefetchScalarGridSpec(num_scalar_pre...]
    all_gather x2, waiting for transfers between devices: 18.8 us -> 0.01 us  [body(): rows_all.append(lax.all_gather(send, 'mp', axis=0, tiled=False))]
    ppermute x44 -> x45, waiting for transfers between devices: 81.1 us -> 63.3 us  [swap(): return lax.ppermute(value, axis, [(i, i ^ apart) for i in range(n)])]
    another operation x0 -> x15, other arithmetic: none -> 9.81 us  [the longest x12 8.67 us: spread(): value = jnp.stack(pair, axis=place)]
    unnamed x105 -> x93, local copies, waits for them, and re-layouts: 13.1 us -> 11.6 us
  transfers between devices with their start and end apart: 48 -> 51, of which waited for: 17 -> 15; matrix products, arithmetic and copies ran while one was open for 8% -> 10% of each run, Pallas kernels for 44% -> 50%
where the time goes in v3:
time: 444 us; the launch traced here: 436 us
  Pallas kernels  232 us (52%)
  waiting for transfers between devices  63.5 us (14%)
  starting transfers between devices  59 us (13%)
  local copies, waits for them, and re-layouts  38.5 us (9%)
  other arithmetic  25.3 us (6%)
  between operations  17.1 us (4%)
    pallas_call x29, Pallas kernels, call(): pl.pallas_call(run, grid_spec=pltpu.PrefetchScalarGridSpec(num_scalar_pre...  232 us
    ppermute x45, waiting for transfers between devices, swap(): return lax.ppermute(value, axis, [(i, i ^ apart) for i in range(n)])  63.3 us
    ppermute x45, starting transfers between devices, swap(): return lax.ppermute(value, axis, [(i, i ^ apart) for i in range(n)])  58.7 us
    unnamed x93, local copies, waits for them, and re-layouts  11.6 us
  transfers between devices with their start and end apart: 51, of which 15 were waited for; matrix products, arithmetic and copies ran while one was open for 10% of the time, Pallas kernels for 50%

profile of v3, /device:TPU:0, one launch (start us, length us, event | category | flops | bytes accessed | tf_op | source)
XLA Modules:
  0.0 435.5 jit_solution(11567917689213187272)
XLA Ops:
  14.3 7.7 %front.2 = (bf16[512,384]{1,0:T(8,128)(2,1)}, f32[288,384]{1,0:T(8,128)}, bf16[288,384]{1,0:T(8,128)(2,1)}, bf16[288,1024]{1,0:T(8,128)(2,1)}, f32[8,384]{1,0:T(8,128)}, /*index=5*/s32[8,128]{1,0:T(8,128)}) custom-call(s32[7]{0:T(128)} %stack.148.refs_0_, bf16[2,32,32,384]{3,2,1,0:T(8,128)(2,1)} %refs_11_.3, f32[49,384]{1,0:T(8,128)} %refs_12_.3, ...), custom_call_target="tpu_custom_call" | custom-call | flops 575000000 | bytes 1 | tf_op jit(solution)/shard_map/front/pallas_call | solution.py:111
  22.0 7.7 %front.3 = (bf16[512,384]{1,0:T(8,128)(2,1)}, f32[288,384]{1,0:T(8,128)}, bf16[288,384]{1,0:T(8,128)(2,1)}, bf16[288,1024]{1,0:T(8,128)(2,1)}, f32[8,384]{1,0:T(8,128)}, /*index=5*/s32[8,128]{1,0:T(8,128)}) custom-call(s32[7]{0:T(128)} %stack.148.refs_0_, bf16[2,32,32,384]{3,2,1,0:T(8,128)(2,1)} %refs_11_.3, f32[49,384]{1,0:T(8,128)} %refs_12_.3, ...), custom_call_target="tpu_custom_call" | custom-call | flops 575000000 | bytes 1 | tf_op jit(solution)/shard_map/front/pallas_call | solution.py:111
  34.9 3.1 collective-permute-start.2
  38.0 2.6 collective-permute-start.1
  41.5 3.1 collective-permute-done.2
  44.7 8.4 %collective-permute-done.1 = bf16[80,1024]{1,0:T(8,128)(2,1)S(1)} collective-permute-done((bf16[80,1024]{1,0:T(8,128)(2,1)S(1)}, bf16[80,1024]{1,0:T(8,128)(2,1)S(1)}, u32[]{:S(2)}, u32[]{:S(2)}) %collective-permute-start.1) | collective-permute-done | bytes 163872 | tf_op jit(solution)/shard_map/ppermute | solution.py:1120
  61.2 6.7 %collective-permute-done.3 = bf16[4,48,1024]{2,1,0:T(8,128)(2,1)} collective-permute-done((bf16[4,48,1024]{2,1,0:T(8,128)(2,1)S(1)}, bf16[4,48,1024]{2,1,0:T(8,128)(2,1)}, u32[]{:S(2)}, u32[]{:S(2)}) %collective-permute-start.3) | collective-permute-done | bytes 393248 | tf_op jit(solution)/shard_map/ppermute | solution.py:1120
  69.7 5.4 %collective-permute-done.10 = bf16[4,2,32,1024]{3,2,0,1:T(8,128)(2,1)S(1)} collective-permute-done((bf16[4,2,32,1024]{3,2,0,1:T(8,128)(2,1)S(1)}, bf16[4,2,32,1024]{3,2,0,1:T(8,128)(2,1)S(1)}, u32[]{:S(2)}, u32[]{:S(2)}) %collective-permute-start.10) | collective-permute-done | bytes 524320 | tf_op jit(solution)/shard_map/ppermute | solution.py:1120
  77.2 4.2 collective-permute-done.4
  92.4 10.3 %attention_forward.1 = (bf16[576,1024]{1,0:T(8,128)(2,1)}, bf16[576,256]{1,0:T(8,128)(2,1)}, bf16[576,256]{1,0:T(8,128)(2,1)}, bf16[576,256]{1,0:T(8,128)(2,1)}, bf16[576,256]{1,0:T(8,128)(2,1)}) custom-call(s32[7]{0:T(128)} %stack.148.refs_0_, bf16[2,576,1024]{2,1,0:T(8,128)(2,1)} %refs_3_.1, f32[1,1024]{1,0:T(1,128)} %bitcast.171, f32[1,1024]{1,0:T(1,128)} %bitcast.185, ...), custom_call_target="tpu_custom_call" | custom-call | flops 11500000256 | bytes 1 | tf_op jit(solution)/shard_map/attention_forward/pallas_call | solution.py:111
  102.7 3.1 collective-permute-start.8
  105.8 8.2 %collective-permute-start.7 = (bf16[576,256]{1,0:T(8,128)(2,1)}, bf16[576,256]{1,0:T(8,128)(2,1)S(1)}, u32[]{:S(2)}, u32[]{:S(2)}) collective-permute-start(bf16[576,256]{1,0:T(8,128)(2,1)} %get-tuple-element.134.refs_10_.refs_1_.refs_8_), channel_id=1, source_target_pairs={{0,2},{1,3},{2,0},{3,1},{4,6},{5,7},{6,4},{7,5},{8,10},{9,11},{10,... | collective-permute-start | bytes 884744 | tf_op jit(solution)/shard_map/ppermute | solution.py:1120
  116.4 2.2 copy.65
  118.6 24.3 %conv_mlp.2 = (bf16[512,1536]{1,0:T(8,128)(2,1)}, bf16[512,1536]{1,0:T(8,128)(2,1)}, bf16[288,1536]{1,0:T(8,128)(2,1)}, bf16[288,1536]{1,0:T(8,128)(2,1)}, bf16[...) custom-call(s32[7]{0:T(128)} %stack.148.refs_0_, ...), custom_call_target="tpu_custom_call" | custom-call | flops 575000000 | bytes 1 | tf_op jit(solution)/shard_map/conv_mlp/pallas_call | solution.py:111
  143.0 4.9 %collective-permute-done.7.refs_3_ = bf16[576,256]{1,0:T(8,128)(2,1)S(1)} collective-permute-done((bf16[576,256]{1,0:T(8,128)(2,1)}, bf16[576,256]{1,0:T(8,128)(2,1)S(1)}, u32[]{:S(2)}, u32[]{:S(2)}) %collective-permute-start.7) | collective-permute-done | bytes 294944 | tf_op jit(solution)/shard_map/ppermute | solution.py:1120
  148.7 15.5 %vit_mlp.1 = (f32[576,1024]{1,0:T(8,128)}, bf16[576,1024]{1,0:T(8,128)(2,1)}, bf16[576,1024]{1,0:T(8,128)(2,1)}, bf16[576,1024]{1,0:T(8,128)(2,1)}, f32[1,1024]{...) custom-call(s32[7]{0:T(128)} %stack.148.refs_0_, ...), custom_call_target="tpu_custom_call" | custom-call | flops 37950001152 | bytes 1 | tf_op jit(solution)/shard_map/vit_mlp/pallas_call | solution.py:111
  165.9 2.8 collective-permute-start.14
  170.3 24.6 %conv_mlp.3 = (bf16[512,1536]{1,0:T(8,128)(2,1)}, bf16[512,1536]{1,0:T(8,128)(2,1)}, bf16[288,1536]{1,0:T(8,128)(2,1)}, bf16[288,1536]{1,0:T(8,128)(2,1)}, bf16[...) custom-call(s32[7]{0:T(128)} %stack.148.refs_0_, ...), custom_call_target="tpu_custom_call" | custom-call | flops 575000000 | bytes 1 | tf_op jit(solution)/shard_map/conv_mlp/pallas_call | solution.py:111
  195.0 7.2 %adapter.1 = (bf16[576,384]{1,0:T(8,128)(2,1)}, f32[1,1024]{1,0:T(1,128)}, bf16[4,576,256]{2,1,0:T(8,128)(2,1)}) custom-call(s32[7]{0:T(128)} %stack.148.refs_0_, f32[288,1024]{1,0:T(8,128)} %get-tuple-element.135.refs_1_, f32[288,1024]{1,0:T(8,128)} %get-tuple-element.140.refs_2_, f32[288,384]{1,0:T(8,128)} %get-tuple-element.141.refs_3_, ...), custom_call_target="tpu_custom_call" | custom-call | flops 575000000 | bytes 1 | tf_op jit(solution)/shard_map/adapter/pallas_call | solution.py:111
  203.2 3.7 norm2_backward.1
  207.9 3.8 collective-permute-start.16
  212.5 8.2 %grad_fc.1 = (bf16[4,128,2048]{2,1,0:T(8,128)(2,1)}, bf16[4,128,2048]{2,1,0:T(8,128)(2,1)}) custom-call(s32[7]{0:T(128)} %stack.148.refs_0_, bf16[576,1024]{1,0:T(8,128)(2,1)} %get-tuple-element.169.refs_1_, bf16[576,1024]{1,0:T(8,128)(2,1)} %dynamic-slice_bitcast_fusion.refs_2_, bf16[576,1024]{1,0:T(8,128)(2,1)} %get-tuple-element.170.refs_3_, ...), custom_call_target="tpu_custom_call" | custom-call | flops 575000000 | bytes 1 | tf_op jit(solution)/shard_map/grad_fc/pallas_call | solution.py:111
  220.7 9.4 %grad_adapt.1 = (bf16[4,128,1920]{2,1,0:T(8,128)(2,1)}, bf16[4,128,1920]{2,1,0:T(8,128)(2,1)}) custom-call(s32[7]{0:T(128)} %stack.148.refs_0_, bf16[288,1024]{1,0:T(8,128)(2,1)} %get-tuple-element.132.refs_8_.refs_1_.refs_3_, bf16[288,1024]{1,0:T(8,128)(2,1)} %get-tuple-element.137.refs_8_.refs_2_.refs_4_, ...), custom_call_target="tpu_custom_call" | custom-call | flops 575000000 | bytes 1 | tf_op jit(solution)/shard_map/grad_adapt/pallas_call | solution.py:111
  230.1 9.0 %grad_pw2.1 = (bf16[4,192,1536]{2,1,0:T(8,128)(2,1)}, bf16[4,192,1536]{2,1,0:T(8,128)(2,1)}) custom-call(s32[7]{0:T(128)} %stack.148.refs_0_, bf16[288,1536]{1,0:T(8,128)(2,1)} %get-tuple-element.162.refs_1_, bf16[288,1536]{1,0:T(8,128)(2,1)} %get-tuple-element.163.refs_2_, bf16[288,1536]{1,0:T(8,128)(2,1)} %get-tuple-element.164.refs_3_, ...), custom_call_target="tpu_custom_call" | custom-call | flops 575000000 | bytes 1 | tf_op jit(solution)/shard_map/grad_pw2/pallas_call | solution.py:111
  239.1 9.4 %grad_pw1.1 = (bf16[4,192,1536]{2,1,0:T(8,128)(2,1)}, bf16[4,192,1536]{2,1,0:T(8,128)(2,1)}) custom-call(s32[7]{0:T(128)} %stack.148.refs_0_, bf16[512,1536]{1,0:T(8,128)(2,1)} %get-tuple-element.158.refs_1_, bf16[512,1536]{1,0:T(8,128)(2,1)} %get-tuple-element.159.refs_2_, bf16[512,1536]{1,0:T(8,128)(2,1)} %get-tuple-element.160.refs_3_, ...), custom_call_target="tpu_custom_call" | custom-call | flops 575000000 | bytes 1 | tf_op jit(solution)/shard_map/grad_pw1/pallas_call | solution.py:111
  248.5 6.4 %collective-permute-done.16.refs_3_ = bf16[144,1024]{1,0:T(8,128)(2,1)S(1)} collective-permute-done((bf16[144,1024]{1,0:T(8,128)(2,1)}, bf16[144,1024]{1,0:T(8,128)(2,1)S(1)}, u32[]{:S(2)}, u32[]{:S(2)}) %collective-permute-start.16) | collective-permute-done | bytes 294944 | tf_op jit(solution)/shard_map/ppermute | solution.py:1120
  255.7 16.4 %attention_backward.1 = (bf16[576,1024]{1,0:T(8,128)(2,1)}, bf16[576,256]{1,0:T(8,128)(2,1)}, bf16[576,256]{1,0:T(8,128)(2,1)}, bf16[576,256]{1,0:T(8,128)(2,1)}, bf16[4,592,256]{2,1,0:T(8,128)(2,1)}) custom-call(s32[7]{0:T(128)} %stack.148.refs_0_, bf16[144,1024]{1,0:T(8,128)(2,1)} %get-tuple-element.154.refs_1_, bf16[144,1024]{1,0:T(8,128)(2,1)} %copy-done.39, ...), custom_call_target="tpu_custom_call" | custom-call | flops 35649998848 | bytes 1 | tf_op jit(solution)/shard_map/attention_backward/pallas_call | solution.py:111
  275.5 7.7 %collective-permute-done.21 = bf16[4,128,2048]{2,1,0:T(8,128)(2,1)} collective-permute-done((bf16[4,128,2048]{2,1,0:T(8,128)(2,1)}, bf16[4,128,2048]{2,1,0:T(8,128)(2,1)}, u32[]{:S(2)}, u32[]{:S(2)}) %collective-permute-start.21) | collective-permute-done | bytes 2097184 | tf_op jit(solution)/shard_map/ppermute | solution.py:1120
  283.2 4.7 %fold_fc.1 = (bf16[1,2,128,2048]{3,2,1,0:T(8,128)(2,1)}, bf16[1,2,128,2048]{3,2,1,0:T(8,128)(2,1)}) custom-call(s32[7]{0:T(128)} %stack.148.refs_0_, bf16[2,1,2,128,2048]{4,3,2,1,0:T(8,128)(2,1)} %bitcast.147, bf16[2,1,2,128,2048]{4,3,2,1,0:T(8,128)(2,1)} %bitcast.56.refs_2_, bf16[576,256]{1,0:T(8,128)(2,1)} %get-tuple-element.178.refs_3_.refs_5_, ...), custom_call_target="tpu_custom_call" | custom-call | flops 575000000 | bytes 1 | tf_op jit(solution)/shard_map/fold_fc/pallas_call | solution.py:111
  289.4 4.3 fold_adapt.1
  295.8 4.8 %fold_pw2.1 = (bf16[2,1,192,1536]{3,2,1,0:T(8,128)(2,1)}, bf16[2,1,192,1536]{3,2,1,0:T(8,128)(2,1)}) custom-call(s32[7]{0:T(128)} %stack.148.refs_0_, bf16[2,1,2,192,1536]{4,3,2,1,0:T(8,128)(2,1)} %bitcast.146, bf16[2,1,2,192,1536]{4,3,2,1,0:T(8,128)(2,1)} %bitcast.52.refs_2_, bf16[2,1,128,1920]{3,2,1,0:T(8,128)(2,1)} %get-tuple-element.187.refs_3_.refs_1_), custom_call_target="tpu_custom_call" | custom-call | flops 575000000 | bytes 1 | tf_op jit(solution)/shard_map/fold_pw2/pallas_call | solution.py:111
  302.1 4.7 %fold_pw1.1 = (bf16[1,2,192,1536]{3,2,1,0:T(8,128)(2,1)}, bf16[1,2,192,1536]{3,2,1,0:T(8,128)(2,1)}) custom-call(s32[7]{0:T(128)} %stack.148.refs_0_, bf16[2,1,2,192,1536]{4,3,2,1,0:T(8,128)(2,1)} %bitcast.150, bf16[2,1,2,192,1536]{4,3,2,1,0:T(8,128)(2,1)} %bitcast.151, bf16[2,1,192,1536]{3,2,1,0:T(8,128)(2,1)} %get-tuple-element.188.refs_3_.refs_1_), custom_call_target="tpu_custom_call" | custom-call | flops 575000000 | bytes 1 | tf_op jit(solution)/shard_map/fold_pw1/pallas_call | solution.py:111
  307.9 9.1 %grad_qkv.1 = (bf16[4,128,1024]{2,1,0:T(8,128)(2,1)}, bf16[4,128,1024]{2,1,0:T(8,128)(2,1)}) custom-call(s32[7]{0:T(128)} %stack.148.refs_0_, bf16[576,1024]{1,0:T(8,128)(2,1)} %get-tuple-element.177.refs_1_.refs_2_.refs_3_, bf16[576,1024]{1,0:T(8,128)(2,1)} %get-tuple-element.177.refs_1_.refs_2_.refs_3_, ...), custom_call_target="tpu_custom_call" | custom-call | flops 575000000 | bytes 1 | tf_op jit(solution)/shard_map/grad_qkv/pallas_call | solution.py:111
  316.9 4.0 norm1_backward.1
  324.7 2.9 collective-permute-start.22
  327.7 21.0 %conv_backward.1 = (bf16[32,32,384]{2,1,0:T(8,128)(2,1)}, f32[49,384]{1,0:T(8,128)}, f32[8,384]{1,0:T(8,128)}) custom-call(s32[7]{0:T(128)} %stack.148.refs_0_, bf16[528,384]{1,0:T(8,128)(2,1)} %bitcast.155, bf16[528,384]{1,0:T(8,128)(2,1)} %bitcast.157, bf16[512,384]{1,0:T(8,128)(2,1)} %get-tuple-element.129.refs_3_, ...), custom_call_target="tpu_custom_call" | custom-call | flops 575000000 | bytes 1 | tf_op jit(solution)/shard_map/conv_backward/pallas_call | solution.py:111
  351.0 2.6 pack.1.refs_4_
  359.9 2.5 collective-permute-done.33
  363.5 2.6 output_halves.1
  367.3 3.2 fold_adapt_last.1
  371.4 3.3 fold_fc_last.1
  374.7 3.5 fold_pw2_last.1
  378.1 3.4 fold_pw1_last.1
  382.6 3.3 fold_qkv.1
  402.3 9.9 %collective-permute-done.38 = bf16[1,128,2048]{2,1,0:T(8,128)(2,1)S(1)} collective-permute-done((bf16[1,128,2048]{2,1,0:T(8,128)(2,1)}, bf16[1,128,2048]{2,1,0:T(8,128)(2,1)S(1)}, u32[]{:S(2)}, u32[]{:S(2)}) %collective-permute-start.38) | collective-permute-done | bytes 524320 | tf_op jit(solution)/shard_map/ppermute | solution.py:1120
  414.8 2.7 fold_qkv_last.1
  421.8 2.4 add_bitcast_fusion.1
  424.3 2.3 add_bitcast_fusion
  (263 shorter events, 95.3 us)
Async XLA Ops:
  7.2 85.2 %all-gather.5.cloned.1.call-start = ((), (), s32[]{:S(2)}) async-start(), calls=%async_computation.8 | async-start | bytes 1966080 | tf_op jit(solution)/shard_map/all_gather | solution.py:1281
  34.9 9.8 %collective-permute-start.2 = (bf16[80,1024]{1,0:T(8,128)(2,1)S(1)}, bf16[80,1024]{1,0:T(8,128)(2,1)S(1)}, u32[]{:S(2)}, u32[]{:S(2)}) collective-permute-start(bf16[80,1024]{1,0:T(8,128)(2,1)S(1)} %pad_maximum_fusion.11), channel_id=1, source_target_pairs={{0,1},{1,0},{2,3},{3,2},{4,5},{5,4},{6,7},{7,6},{8,9},{9,8},{10,11... | collective-permute-start | bytes 491528 | tf_op jit(solution)/shard_map/ppermute | solution.py:1120
  38.0 15.0 %collective-permute-start.1 = (bf16[80,1024]{1,0:T(8,128)(2,1)S(1)}, bf16[80,1024]{1,0:T(8,128)(2,1)S(1)}, u32[]{:S(2)}, u32[]{:S(2)}) collective-permute-start(bf16[80,1024]{1,0:T(8,128)(2,1)S(1)} %pad_maximum_fusion.11), channel_id=1, source_target_pairs={{0,2},{1,3},{2,0},{3,1},{4,6},{5,7},{6,4},{7,5},{8,10},{9,11},{10,... | collective-permute-start | bytes 491528 | tf_op jit(solution)/shard_map/ppermute | solution.py:1120
  40.6 12.5 %collective-permute-start = (bf16[80,1024]{1,0:T(8,128)(2,1)S(1)}, bf16[80,1024]{1,0:T(8,128)(2,1)S(1)}, u32[]{:S(2)}, u32[]{:S(2)}) collective-permute-start(bf16[80,1024]{1,0:T(8,128)(2,1)S(1)} %pad_maximum_fusion.11), channel_id=1, source_target_pairs={{0,3},{1,2},{2,1},{3,0},{4,7},{5,6},{6,5},{7,4},{8,11},{9,10},{10,... | collective-permute-start | bytes 491528 | tf_op jit(solution)/shard_map/ppermute | solution.py:1120
  40.6 129.8 %all-gather.7.cloned.1.call-start = ((), (), s32[]{:S(2)}) async-start(), calls=%async_computation.9 | async-start | bytes 1966080 | tf_op jit(solution)/shard_map/all_gather | solution.py:1281
  53.1 6.4 %collective-permute-start.9 = (bf16[4,32,1024]{2,1,0:T(8,128)(2,1)S(1)}, bf16[4,32,1024]{2,1,0:T(8,128)(2,1)S(1)}, u32[]{:S(2)}, u32[]{:S(2)}) collective-permute-start(bf16[4,32,1024]{2,1,0:T(8,128)(2,1)S(1)} %pad_maximum_fusion.10), channel_id=1, source_target_pairs={{0,16},{16,0},{1,17},{17,1},{2,18},{18,2},{3,19},{19,3},{4,20},{20... | collective-permute-start | bytes 786440 | tf_op jit(solution)/shard_map/ppermute | solution.py:1120
  55.8 12.2 %collective-permute-start.3 = (bf16[4,48,1024]{2,1,0:T(8,128)(2,1)S(1)}, bf16[4,48,1024]{2,1,0:T(8,128)(2,1)}, u32[]{:S(2)}, u32[]{:S(2)}) collective-permute-start(bf16[4,48,1024]{2,1,0:T(8,128)(2,1)S(1)} %pad_maximum_fusion.7), channel_id=1, source_target_pairs={{0,8},{4,12},{8,0},{12,4},{1,9},{5,13},{9,1},{13,5},{2,10},{6,14},... | collective-permute-start | bytes 1179656 | tf_op jit(solution)/shard_map/ppermute | solution.py:1120
  59.7 15.5 %collective-permute-start.10 = (bf16[4,2,32,1024]{3,2,0,1:T(8,128)(2,1)S(1)}, bf16[4,2,32,1024]{3,2,0,1:T(8,128)(2,1)S(1)}, u32[]{:S(2)}, u32[]{:S(2)}) collective-permute-start(bf16[4,2,32,1024]{3,2,0,1:T(8,128)(2,1)S(1)} %pad_maximum_fusion.6), channel_id=1, source_target_pairs={{0,8},{4,12},{8,0},{12,4},{1,9},{5,13},{9,1},{13,5},{2,10},{6,14},... | collective-permute-start | bytes 1572872 | tf_op jit(solution)/shard_map/ppermute | solution.py:1120
  69.1 12.2 %collective-permute-start.4 = (bf16[4,2,48,1024]{3,2,0,1:T(8,128)(2,1)S(1)}, bf16[4,2,48,1024]{3,2,0,1:T(8,128)(2,1)}, u32[]{:S(2)}, u32[]{:S(2)}) collective-permute-start(bf16[4,2,48,1024]{3,2,0,1:T(8,128)(2,1)S(1)} %pad_maximum_fusion.4), channel_id=1, source_target_pairs={{0,16},{16,0},{1,17},{17,1},{2,18},{18,2},{3,19},{19,3},{4,20},{20... | collective-permute-start | bytes 2359304 | tf_op jit(solution)/shard_map/ppermute | solution.py:1120
  77.1 11.9 %collective-permute-start.11 = (bf16[4,2,2,32,1024]{4,3,0,1,2:T(8,128)(2,1)}, bf16[4,2,2,32,1024]{4,3,0,1,2:T(8,128)(2,1)}, u32[]{:S(2)}, u32[]{:S(2)}) collective-permute-start(bf16[4,2,2,32,1024]{4,3,0,1,2:T(8,128)(2,1)} %pad_maximum_fusion.3), channel_id=1, source_target_pairs={{0,4},{4,0},{8,12},{12,8},{1,5},{5,1},{9,13},{13,9},{2,6},{6,2},{1... | collective-permute-start | bytes 3145736 | tf_op jit(solution)/shard_map/ppermute | solution.py:1120
  77.1 117.9 %reduce-scatter.5.cloned.1.call-start = ((), (), s32[]{:S(2)}) async-start(), calls=%async_computation.4 | async-start | bytes 2027520 | tf_op jit(solution)/shard_map/reduce_scatter | solution.py:1325
  83.9 30.6 %collective-permute-start.5 = (bf16[4,2,2,48,1024]{4,3,0,2,1:T(8,128)(2,1)}, bf16[4,2,2,48,1024]{4,3,0,2,1:T(8,128)(2,1)}, u32[]{:S(2)}, u32[]{:S(2)}) collective-permute-start(bf16[4,2,2,48,1024]{4,3,0,2,1:T(8,128)(2,1)} %pad_maximum_fusion.2), channel_id=1, source_target_pairs={{0,4},{4,0},{8,12},{12,8},{1,5},{5,1},{9,13},{13,9},{2,6},{6,2},{1... | collective-permute-start | bytes 4718600 | tf_op jit(solution)/shard_map/ppermute | solution.py:1120
  102.7 40.3 %collective-permute-start.8 = (bf16[576,256]{1,0:T(8,128)(2,1)}, bf16[576,256]{1,0:T(8,128)(2,1)S(1)}, u32[]{:S(2)}, u32[]{:S(2)}) collective-permute-start(bf16[576,256]{1,0:T(8,128)(2,1)} %get-tuple-element.134.refs_10_.refs_1_.refs_8_), channel_id=1, source_target_pairs={{0,3},{1,2},{2,1},{3,0},{4,7},{5,6},{6,5},{7,4},{8,11},{9,10},{10,... | collective-permute-start | bytes 884744 | tf_op jit(solution)/shard_map/ppermute | solution.py:1120
  105.8 42.1 %collective-permute-start.7 = (bf16[576,256]{1,0:T(8,128)(2,1)}, bf16[576,256]{1,0:T(8,128)(2,1)S(1)}, u32[]{:S(2)}, u32[]{:S(2)}) collective-permute-start(bf16[576,256]{1,0:T(8,128)(2,1)} %get-tuple-element.134.refs_10_.refs_1_.refs_8_), channel_id=1, source_target_pairs={{0,2},{1,3},{2,0},{3,1},{4,6},{5,7},{6,4},{7,5},{8,10},{9,11},{10,... | collective-permute-start | bytes 884744 | tf_op jit(solution)/shard_map/ppermute | solution.py:1120
  114.0 34.0 %collective-permute-start.6 = (bf16[576,256]{1,0:T(8,128)(2,1)}, bf16[576,256]{1,0:T(8,128)(2,1)S(1)}, u32[]{:S(2)}, u32[]{:S(2)}) collective-permute-start(bf16[576,256]{1,0:T(8,128)(2,1)} %get-tuple-element.134.refs_10_.refs_1_.refs_8_), channel_id=1, source_target_pairs={{0,1},{1,0},{2,3},{3,2},{4,5},{5,4},{6,7},{7,6},{8,9},{9,8},{10,11... | collective-permute-start | bytes 884744 | tf_op jit(solution)/shard_map/ppermute | solution.py:1120
  142.9 132.6 %reduce-scatter.11.cloned.1.call-start = ((), (), s32[]{:S(2)}) async-start(), calls=%async_computation.7 | async-start | bytes 2027520 | tf_op jit(solution)/shard_map/reduce_scatter | solution.py:1325
  164.2 38.0 %collective-permute-start.12 = (bf16[144,1024]{1,0:T(8,128)(2,1)}, bf16[144,1024]{1,0:T(8,128)(2,1)S(1)}, u32[]{:S(2)}, u32[]{:S(2)}) collective-permute-start(bf16[144,1024]{1,0:T(8,128)(2,1)} %get-tuple-element.149), channel_id=1, source_target_pairs={{0,1},{1,0},{2,3},{3,2},{4,5},{5,4},{6,7},{7,6},{8,9},{9,8},{10,11... | collective-permute-start | bytes 884744 | tf_op jit(solution)/shard_map/ppermute | solution.py:1120
  164.3 38.0 %collective-permute-start.13 = (bf16[144,1024]{1,0:T(8,128)(2,1)}, bf16[144,1024]{1,0:T(8,128)(2,1)S(1)}, u32[]{:S(2)}, u32[]{:S(2)}) collective-permute-start(bf16[144,1024]{1,0:T(8,128)(2,1)} %get-tuple-element.150), channel_id=1, source_target_pairs={{0,2},{1,3},{2,0},{3,1},{4,6},{5,7},{6,4},{7,5},{8,10},{9,11},{10,... | collective-permute-start | bytes 884744 | tf_op jit(solution)/shard_map/ppermute | solution.py:1120
  165.9 36.4 %collective-permute-start.14 = (bf16[144,1024]{1,0:T(8,128)(2,1)}, bf16[144,1024]{1,0:T(8,128)(2,1)S(1)}, u32[]{:S(2)}, u32[]{:S(2)}) collective-permute-start(bf16[144,1024]{1,0:T(8,128)(2,1)} %get-tuple-element.151), channel_id=1, source_target_pairs={{0,3},{1,2},{2,1},{3,0},{4,7},{5,6},{6,5},{7,4},{8,11},{9,10},{10,... | collective-permute-start | bytes 884744 | tf_op jit(solution)/shard_map/ppermute | solution.py:1120
  194.9 122.0 %reduce-scatter.9.cloned.1.call-start = ((), (), s32[]{:S(2)}) async-start(), calls=%async_computation.6 | async-start | bytes 1515520 | tf_op jit(solution)/shard_map/reduce_scatter | solution.py:1430
  206.8 41.7 %collective-permute-start.17 = (bf16[144,1024]{1,0:T(8,128)(2,1)}, bf16[144,1024]{1,0:T(8,128)(2,1)S(1)}, u32[]{:S(2)}, u32[]{:S(2)}) collective-permute-start(bf16[144,1024]{1,0:T(8,128)(2,1)} %get-tuple-element.154.refs_1_), channel_id=1, source_target_pairs={{0,3},{1,2},{2,1},{3,0},{4,7},{5,6},{6,5},{7,4},{8,11},{9,10},{10,... | collective-permute-start | bytes 884744 | tf_op jit(solution)/shard_map/ppermute | solution.py:1120
  207.9 47.0 %collective-permute-start.16 = (bf16[144,1024]{1,0:T(8,128)(2,1)}, bf16[144,1024]{1,0:T(8,128)(2,1)S(1)}, u32[]{:S(2)}, u32[]{:S(2)}) collective-permute-start(bf16[144,1024]{1,0:T(8,128)(2,1)} %get-tuple-element.154.refs_1_), channel_id=1, source_target_pairs={{0,2},{1,3},{2,0},{3,1},{4,6},{5,7},{6,4},{7,5},{8,10},{9,11},{10,... | collective-permute-start | bytes 884744 | tf_op jit(solution)/shard_map/ppermute | solution.py:1120
  211.7 43.2 %collective-permute-start.15 = (bf16[144,1024]{1,0:T(8,128)(2,1)}, bf16[144,1024]{1,0:T(8,128)(2,1)S(1)}, u32[]{:S(2)}, u32[]{:S(2)}) collective-permute-start(bf16[144,1024]{1,0:T(8,128)(2,1)} %get-tuple-element.154.refs_1_), channel_id=1, source_target_pairs={{0,1},{1,0},{2,3},{3,2},{4,5},{5,4},{6,7},{7,6},{8,9},{9,8},{10,11... | collective-permute-start | bytes 884744 | tf_op jit(solution)/shard_map/ppermute | solution.py:1120
  272.2 91.3 %reduce-scatter.7.cloned.1.call-start = ((), (), s32[]{:S(2)}) async-start(), calls=%async_computation.5 | async-start | bytes 1474560 | tf_op jit(solution)/shard_map/reduce_scatter | solution.py:1380
  272.3 23.5 %collective-permute-start.19 = (bf16[4,192,1536]{2,1,0:T(8,128)(2,1)}, bf16[4,192,1536]{2,1,0:T(8,128)(2,1)}, u32[]{:S(2)}, u32[]{:S(2)}) collective-permute-start(bf16[4,192,1536]{2,1,0:T(8,128)(2,1)} %get-tuple-element.182), channel_id=1, source_target_pairs={{0,4},{4,0},{8,12},{12,8},{1,5},{5,1},{9,13},{13,9},{2,6},{6,2},{1... | collective-permute-start | bytes 7077896 | tf_op jit(solution)/shard_map/ppermute | solution.py:1120
  272.4 10.9 %collective-permute-start.21 = (bf16[4,128,2048]{2,1,0:T(8,128)(2,1)}, bf16[4,128,2048]{2,1,0:T(8,128)(2,1)}, u32[]{:S(2)}, u32[]{:S(2)}) collective-permute-start(bf16[4,128,2048]{2,1,0:T(8,128)(2,1)} %get-tuple-element.184), channel_id=1, source_target_pairs={{0,4},{4,0},{8,12},{12,8},{1,5},{5,1},{9,13},{13,9},{2,6},{6,2},{1... | collective-permute-start | bytes 6291464 | tf_op jit(solution)/shard_map/ppermute | solution.py:1120
  272.9 27.7 %collective-permute-start.18 = (bf16[4,192,1536]{2,1,0:T(8,128)(2,1)}, bf16[4,192,1536]{2,1,0:T(8,128)(2,1)S(1)}, u32[]{:S(2)}, u32[]{:S(2)}) collective-permute-start(bf16[4,192,1536]{2,1,0:T(8,128)(2,1)} %get-tuple-element.181), channel_id=1, source_target_pairs={{0,4},{4,0},{8,12},{12,8},{1,5},{5,1},{9,13},{13,9},{2,6},{6,2},{1... | collective-permute-start | bytes 7077896 | tf_op jit(solution)/shard_map/ppermute | solution.py:1120
  272.9 16.5 %collective-permute-start.20 = (bf16[4,128,1920]{2,1,0:T(8,128)(2,1)}, bf16[4,128,1920]{2,1,0:T(8,128)(2,1)}, u32[]{:S(2)}, u32[]{:S(2)}) collective-permute-start(bf16[4,128,1920]{2,1,0:T(8,128)(2,1)} %get-tuple-element.183), channel_id=1, source_target_pairs={{0,4},{4,0},{8,12},{12,8},{1,5},{5,1},{9,13},{13,9},{2,6},{6,2},{1... | collective-permute-start | bytes 5898248 | tf_op jit(solution)/shard_map/ppermute | solution.py:1120
  287.9 36.8 %collective-permute-start.25 = (bf16[1,2,128,2048]{3,2,1,0:T(8,128)(2,1)}, bf16[1,2,128,2048]{3,2,1,0:T(8,128)(2,1)S(1)}, u32[]{:S(2)}, u32[]{:S(2)}) collective-permute-start(bf16[1,2,128,2048]{3,2,1,0:T(8,128)(2,1)} %get-tuple-element.200), channel_id=1, source_target_pairs={{0,16},{16,0},{1,17},{17,1},{2,18},{18,2},{3,19},{19,3},{4,20},{20... | collective-permute-start | bytes 3145736 | tf_op jit(solution)/shard_map/ppermute | solution.py:1120
  293.7 31.0 %collective-permute-start.26 = (bf16[2,1,128,1920]{3,2,1,0:T(8,128)(2,1)}, bf16[2,1,128,1920]{3,2,1,0:T(8,128)(2,1)}, u32[]{:S(2)}, u32[]{:S(2)}) collective-permute-start(bf16[2,1,128,1920]{3,2,1,0:T(8,128)(2,1)} %get-tuple-element.201), channel_id=1, source_target_pairs={{0,8},{4,12},{8,0},{12,4},{1,9},{5,13},{9,1},{13,5},{2,10},{6,14},... | collective-permute-start | bytes 2949128 | tf_op jit(solution)/shard_map/ppermute | solution.py:1120
  306.7 56.7 %collective-permute-start.28 = (bf16[1,2,192,1536]{3,2,1,0:T(8,128)(2,1)}, bf16[1,2,192,1536]{3,2,1,0:T(8,128)(2,1)}, u32[]{:S(2)}, u32[]{:S(2)}) collective-permute-start(bf16[1,2,192,1536]{3,2,1,0:T(8,128)(2,1)} %get-tuple-element.205), channel_id=1, source_target_pairs={{0,16},{16,0},{1,17},{17,1},{2,18},{18,2},{3,19},{19,3},{4,20},{20... | collective-permute-start | bytes 3538952 | tf_op jit(solution)/shard_map/ppermute | solution.py:1120
  307.3 56.2 %collective-permute-start.27 = (bf16[2,1,192,1536]{3,2,1,0:T(8,128)(2,1)}, bf16[2,1,192,1536]{3,2,1,0:T(8,128)(2,1)}, u32[]{:S(2)}, u32[]{:S(2)}) collective-permute-start(bf16[2,1,192,1536]{3,2,1,0:T(8,128)(2,1)} %get-tuple-element.204), channel_id=1, source_target_pairs={{0,8},{4,12},{8,0},{12,4},{1,9},{5,13},{9,1},{13,5},{2,10},{6,14},... | collective-permute-start | bytes 3538952 | tf_op jit(solution)/shard_map/ppermute | solution.py:1120
  323.2 25.5 %collective-permute-start.24 = (f32[11,1024]{1,0:T(8,128)S(1)}, f32[11,1024]{1,0:T(8,128)S(1)}, u32[]{:S(2)}, u32[]{:S(2)}) collective-permute-start(f32[11,1024]{1,0:T(8,128)S(1)} %concatenate.7.refs_1_), channel_id=1, source_target_pairs={{0,3},{1,2},{2,1},{3,0},{4,7},{5,6},{6,5},{7,4},{8,11},{9,10},{10,... | collective-permute-start | bytes 135176 | tf_op jit(solution)/shard_map/ppermute | solution.py:1120
  324.7 24.1 %collective-permute-start.23 = (f32[11,1024]{1,0:T(8,128)S(1)}, f32[11,1024]{1,0:T(8,128)S(1)}, u32[]{:S(2)}, u32[]{:S(2)}) collective-permute-start(f32[11,1024]{1,0:T(8,128)S(1)} %concatenate.7.refs_1_), channel_id=1, source_target_pairs={{0,2},{1,3},{2,0},{3,1},{4,6},{5,7},{6,4},{7,5},{8,10},{9,11},{10,... | collective-permute-start | bytes 135176 | tf_op jit(solution)/shard_map/ppermute | solution.py:1120
  324.7 25.6 %collective-permute-start.22 = (f32[11,1024]{1,0:T(8,128)S(1)}, f32[11,1024]{1,0:T(8,128)S(1)}, u32[]{:S(2)}, u32[]{:S(2)}) collective-permute-start(f32[11,1024]{1,0:T(8,128)S(1)} %concatenate.7.refs_1_), channel_id=1, source_target_pairs={{0,1},{1,0},{2,3},{3,2},{4,5},{5,4},{6,7},{7,6},{8,9},{9,8},{10,11... | collective-permute-start | bytes 135176 | tf_op jit(solution)/shard_map/ppermute | solution.py:1120
  348.7 32.9 %collective-permute-start.35 = (bf16[4,128,1024]{2,1,0:T(8,128)(2,1)}, bf16[4,128,1024]{2,1,0:T(8,128)(2,1)S(1)}, u32[]{:S(2)}, u32[]{:S(2)}) collective-permute-start(bf16[4,128,1024]{2,1,0:T(8,128)(2,1)} %get-tuple-element.212), channel_id=1, source_target_pairs={{0,4},{4,0},{8,12},{12,8},{1,5},{5,1},{9,13},{13,9},{2,6},{6,2},{1... | collective-permute-start | bytes 3145736 | tf_op jit(solution)/shard_map/ppermute | solution.py:1120
  358.4 28.9 %collective-permute-start.31 = (bf16[16,32,384]{2,1,0:T(8,128)(2,1)S(1)}, bf16[16,32,384]{2,1,0:T(8,128)(2,1)S(1)}, u32[]{:S(2)}, u32[]{:S(2)}) collective-permute-start(bf16[16,32,384]{2,1,0:T(8,128)(2,1)S(1)} %dynamic-slice_bitcast_fusion.1), channel_id=1, source_target_pairs={{0,16},{16,0},{1,17},{17,1},{2,18},{18,2},{3,19},{19,3},{4,20},{20... | collective-permute-start | bytes 1179656 | tf_op jit(solution)/shard_map/ppermute | solution.py:1120
  362.5 26.4 %collective-permute-start.34 = (f32[40,1024]{1,0:T(8,128)S(1)}, f32[40,1024]{1,0:T(8,128)}, u32[]{:S(2)}, u32[]{:S(2)}) collective-permute-start(f32[40,1024]{1,0:T(8,128)S(1)} %add.110.refs_0_), channel_id=1, source_target_pairs={{0,16},{16,0},{1,17},{17,1},{2,18},{18,2},{3,19},{19,3},{4,20},{20... | collective-permute-start | bytes 491528 | tf_op jit(solution)/shard_map/ppermute | solution.py:1120
  366.1 32.9 %collective-permute-start.29 = (bf16[288,256]{1,0:T(8,128)(2,1)}, bf16[288,256]{1,0:T(8,128)(2,1)S(1)}, u32[]{:S(2)}, u32[]{:S(2)}) collective-permute-start(bf16[288,256]{1,0:T(8,128)(2,1)} %get-tuple-element.207), channel_id=1, source_target_pairs={{0,16},{16,0},{1,17},{17,1},{2,18},{18,2},{3,19},{19,3},{4,20},{20... | collective-permute-start | bytes 442376 | tf_op jit(solution)/shard_map/ppermute | solution.py:1120
  370.5 30.5 %collective-permute-start.39 = (bf16[1,128,1920]{2,1,0:T(8,128)(2,1)}, bf16[1,128,1920]{2,1,0:T(8,128)(2,1)S(1)}, u32[]{:S(2)}, u32[]{:S(2)}) collective-permute-start(bf16[1,128,1920]{2,1,0:T(8,128)(2,1)} %get-tuple-element.224), channel_id=1, source_target_pairs={{0,16},{16,0},{1,17},{17,1},{2,18},{18,2},{3,19},{19,3},{4,20},{20... | collective-permute-start | bytes 1474568 | tf_op jit(solution)/shard_map/ppermute | solution.py:1120
  385.9 27.9 %collective-permute-start.36 = (bf16[2,1,128,1024]{3,2,1,0:T(8,128)(2,1)}, bf16[2,1,128,1024]{3,2,1,0:T(8,128)(2,1)}, u32[]{:S(2)}, u32[]{:S(2)}) collective-permute-start(bf16[2,1,128,1024]{3,2,1,0:T(8,128)(2,1)} %get-tuple-element.218), channel_id=1, source_target_pairs={{0,8},{4,12},{8,0},{12,4},{1,9},{5,13},{9,1},{13,5},{2,10},{6,14},... | collective-permute-start | bytes 1572872 | tf_op jit(solution)/shard_map/ppermute | solution.py:1120
  387.3 24.8 %collective-permute-start.38 = (bf16[1,128,2048]{2,1,0:T(8,128)(2,1)}, bf16[1,128,2048]{2,1,0:T(8,128)(2,1)S(1)}, u32[]{:S(2)}, u32[]{:S(2)}) collective-permute-start(bf16[1,128,2048]{2,1,0:T(8,128)(2,1)} %get-tuple-element.222), channel_id=1, source_target_pairs={{0,8},{4,12},{8,0},{12,4},{1,9},{5,13},{9,1},{13,5},{2,10},{6,14},... | collective-permute-start | bytes 1572872 | tf_op jit(solution)/shard_map/ppermute | solution.py:1120
  388.9 32.9 %collective-permute-start.43 = (bf16[1,192,1536]{2,1,0:T(8,128)(2,1)}, bf16[1,192,1536]{2,1,0:T(8,128)(2,1)}, u32[]{:S(2)}, u32[]{:S(2)}) collective-permute-start(bf16[1,192,1536]{2,1,0:T(8,128)(2,1)} %get-tuple-element.227), channel_id=1, source_target_pairs={{0,8},{4,12},{8,0},{12,4},{1,9},{5,13},{9,1},{13,5},{2,10},{6,14},... | collective-permute-start | bytes 1769480 | tf_op jit(solution)/shard_map/ppermute | solution.py:1120
  399.1 25.2 %collective-permute-start.44 = (bf16[1,192,1536]{2,1,0:T(8,128)(2,1)}, bf16[1,192,1536]{2,1,0:T(8,128)(2,1)}, u32[]{:S(2)}, u32[]{:S(2)}) collective-permute-start(bf16[1,192,1536]{2,1,0:T(8,128)(2,1)} %get-tuple-element.229), channel_id=1, source_target_pairs={{0,16},{16,0},{1,17},{17,1},{2,18},{18,2},{3,19},{19,3},{4,20},{20... | collective-permute-start | bytes 1769480 | tf_op jit(solution)/shard_map/ppermute | solution.py:1120
  401.2 18.2 %collective-permute-start.40 = (bf16[128,384]{1,0:T(8,128)(2,1)S(1)}, bf16[128,384]{1,0:T(8,128)(2,1)S(1)}, u32[]{:S(2)}, u32[]{:S(2)}) collective-permute-start(bf16[128,384]{1,0:T(8,128)(2,1)S(1)} %get-tuple-element.307), channel_id=1, source_target_pairs={{0,1},{1,0},{2,3},{3,2},{4,5},{5,4},{6,7},{7,6},{8,9},{9,8},{10,11... | collective-permute-start | bytes 294920 | tf_op jit(solution)/shard_map/ppermute | solution.py:1120
  412.2 8.4 %collective-permute-start.42 = (bf16[128,384]{1,0:T(8,128)(2,1)S(1)}, bf16[128,384]{1,0:T(8,128)(2,1)S(1)}, u32[]{:S(2)}, u32[]{:S(2)}) collective-permute-start(bf16[128,384]{1,0:T(8,128)(2,1)S(1)} %get-tuple-element.308), channel_id=1, source_target_pairs={{0,3},{1,2},{2,1},{3,0},{4,7},{5,6},{6,5},{7,4},{8,11},{9,10},{10,... | collective-permute-start | bytes 294920 | tf_op jit(solution)/shard_map/ppermute | solution.py:1120
  413.8 6.9 %collective-permute-start.41 = (bf16[128,384]{1,0:T(8,128)(2,1)S(1)}, bf16[128,384]{1,0:T(8,128)(2,1)S(1)}, u32[]{:S(2)}, u32[]{:S(2)}) collective-permute-start(bf16[128,384]{1,0:T(8,128)(2,1)S(1)} %get-tuple-element.309), channel_id=1, source_target_pairs={{0,2},{1,3},{2,0},{3,1},{4,6},{5,7},{6,4},{7,5},{8,10},{9,11},{10,... | collective-permute-start | bytes 294920 | tf_op jit(solution)/shard_map/ppermute | solution.py:1120
  419.4 7.1 %collective-permute-start.37 = (bf16[1,128,1024]{2,1,0:T(8,128)(2,1)}, bf16[1,128,1024]{2,1,0:T(8,128)(2,1)S(1)}, u32[]{:S(2)}, u32[]{:S(2)}) collective-permute-start(bf16[1,128,1024]{2,1,0:T(8,128)(2,1)} %get-tuple-element.220), channel_id=1, source_target_pairs={{0,16},{16,0},{1,17},{17,1},{2,18},{18,2},{3,19},{19,3},{4,20},{20... | collective-permute-start | bytes 786440 | tf_op jit(solution)/shard_map/ppermute | solution.py:1120
  (47 other events, 229.8 us)
Sparse Core Ops, SparseCore 0:
  40.7 40.0 all-gather.4
  82.3 58.9 all-gather.6
  143.7 46.7 reduce-scatter.4
  195.1 52.5 reduce-scatter.10
  272.4 28.6 reduce-scatter.8
  303.4 30.7 reduce-scatter.6

commit v4 on v3

--- a/solution.py
+++ b/solution.py
@@ -1499,12 +1499,12 @@
     output_keep, output_send = output_halves(
         [branch_sum], hidden1, fc2_bias, scalars, (packed_first, pw2_part[1], pw1_part[1])
     )
-    adapt_part = second_fold("fold_adapt_last", adapt_part, scalars, (output_keep,))
+    qkv_part = first_fold("fold_qkv", qkv_halves, scalars, (output_keep,), True)
+    adapt_part = second_fold("fold_adapt_last", adapt_part, scalars, qkv_part[:1])
     fc_part = second_fold("fold_fc_last", fc_part, scalars, adapt_part[:1])
     pw2_part = second_fold("fold_pw2_last", pw2_part, scalars, fc_part[:1])
     pw1_part = second_fold("fold_pw1_last", pw1_part, scalars, pw2_part[:1])
-    qkv_part = first_fold("fold_qkv", qkv_halves, scalars, pw1_part[:1], True)
-    qkv_part = second_fold("fold_qkv_last", qkv_part, scalars, qkv_part[:1])
+    qkv_part = second_fold("fold_qkv_last", qkv_part, scalars, pw1_part[:1])
 
     def both_images(mine, send):
         other = swap(send, "path", 1)

time: 444 us -> 436 us (0.982)
  waiting for transfers between devices: 63.5 us -> 56.3 us
    ppermute x45, waiting for transfers between devices: 63.3 us -> 56.1 us  [swap(): return lax.ppermute(value, axis, [(i, i ^ apart) for i in range(n)])]
    unnamed x93 -> x95, local copies, waits for them, and re-layouts: 11.6 us -> 11.6 us
  transfers between devices with their start and end apart: 51 -> 51, of which waited for: 15 -> 15; matrix products, arithmetic and copies ran while one was open for 10% -> 11% of each run, Pallas kernels for 50% -> 51%
where the time goes in v4:
time: 436 us; the launch traced here: 428 us
  Pallas kernels  232 us (53%)
  starting transfers between devices  58.8 us (13%)
  waiting for transfers between devices  56.3 us (13%)
  local copies, waits for them, and re-layouts  39 us (9%)
  other arithmetic  25.1 us (6%)
  between operations  17.1 us (4%)
    pallas_call x29, Pallas kernels, call(): pl.pallas_call(run, grid_spec=pltpu.PrefetchScalarGridSpec(num_scalar_pre...  232 us
    ppermute x45, starting transfers between devices, swap(): return lax.ppermute(value, axis, [(i, i ^ apart) for i in range(n)])  58.6 us
    ppermute x45, waiting for transfers between devices, swap(): return lax.ppermute(value, axis, [(i, i ^ apart) for i in range(n)])  56.1 us
    unnamed x95, local copies, waits for them, and re-layouts  11.6 us
  transfers between devices with their start and end apart: 51, of which 15 were waited for; matrix products, arithmetic and copies ran while one was open for 11% of the time, Pallas kernels for 51%

profile of v4, /device:TPU:0, one launch (start us, length us, event | category | flops | bytes accessed | tf_op | source)
XLA Modules:
  0.0 428.2 jit_solution(15965446855242742415)
XLA Ops:
  14.3 7.7 %front.2 = (bf16[512,384]{1,0:T(8,128)(2,1)}, f32[288,384]{1,0:T(8,128)}, bf16[288,384]{1,0:T(8,128)(2,1)}, bf16[288,1024]{1,0:T(8,128)(2,1)}, f32[8,384]{1,0:T(8,128)}, /*index=5*/s32[8,128]{1,0:T(8,128)}) custom-call(s32[7]{0:T(128)} %stack.148.refs_0_, bf16[2,32,32,384]{3,2,1,0:T(8,128)(2,1)} %refs_11_.3, f32[49,384]{1,0:T(8,128)} %refs_12_.3, ...), custom_call_target="tpu_custom_call" | custom-call | flops 575000000 | bytes 1 | tf_op jit(solution)/shard_map/front/pallas_call | solution.py:111
  22.0 7.8 %front.3 = (bf16[512,384]{1,0:T(8,128)(2,1)}, f32[288,384]{1,0:T(8,128)}, bf16[288,384]{1,0:T(8,128)(2,1)}, bf16[288,1024]{1,0:T(8,128)(2,1)}, f32[8,384]{1,0:T(8,128)}, /*index=5*/s32[8,128]{1,0:T(8,128)}) custom-call(s32[7]{0:T(128)} %stack.148.refs_0_, bf16[2,32,32,384]{3,2,1,0:T(8,128)(2,1)} %refs_11_.3, f32[49,384]{1,0:T(8,128)} %refs_12_.3, ...), custom_call_target="tpu_custom_call" | custom-call | flops 575000000 | bytes 1 | tf_op jit(solution)/shard_map/front/pallas_call | solution.py:111
  34.9 3.1 collective-permute-start.2
  37.9 2.6 collective-permute-start.1
  41.5 3.2 collective-permute-done.2
  44.6 8.4 %collective-permute-done.1 = bf16[80,1024]{1,0:T(8,128)(2,1)S(1)} collective-permute-done((bf16[80,1024]{1,0:T(8,128)(2,1)S(1)}, bf16[80,1024]{1,0:T(8,128)(2,1)S(1)}, u32[]{:S(2)}, u32[]{:S(2)}) %collective-permute-start.1) | collective-permute-done | bytes 163872 | tf_op jit(solution)/shard_map/ppermute | solution.py:1120
  57.3 2.2 collective-permute-done.9
  61.2 6.7 %collective-permute-done.3 = bf16[4,48,1024]{2,1,0:T(8,128)(2,1)} collective-permute-done((bf16[4,48,1024]{2,1,0:T(8,128)(2,1)S(1)}, bf16[4,48,1024]{2,1,0:T(8,128)(2,1)}, u32[]{:S(2)}, u32[]{:S(2)}) %collective-permute-start.3) | collective-permute-done | bytes 393248 | tf_op jit(solution)/shard_map/ppermute | solution.py:1120
  69.7 5.4 %collective-permute-done.10 = bf16[4,2,32,1024]{3,2,0,1:T(8,128)(2,1)S(1)} collective-permute-done((bf16[4,2,32,1024]{3,2,0,1:T(8,128)(2,1)S(1)}, bf16[4,2,32,1024]{3,2,0,1:T(8,128)(2,1)S(1)}, u32[]{:S(2)}, u32[]{:S(2)}) %collective-permute-start.10) | collective-permute-done | bytes 524320 | tf_op jit(solution)/shard_map/ppermute | solution.py:1120
  77.1 4.2 collective-permute-done.4
  92.4 10.3 %attention_forward.1 = (bf16[576,1024]{1,0:T(8,128)(2,1)}, bf16[576,256]{1,0:T(8,128)(2,1)}, bf16[576,256]{1,0:T(8,128)(2,1)}, bf16[576,256]{1,0:T(8,128)(2,1)}, bf16[576,256]{1,0:T(8,128)(2,1)}) custom-call(s32[7]{0:T(128)} %stack.148.refs_0_, bf16[2,576,1024]{2,1,0:T(8,128)(2,1)} %refs_3_.1, f32[1,1024]{1,0:T(1,128)} %bitcast.171, f32[1,1024]{1,0:T(1,128)} %bitcast.185, ...), custom_call_target="tpu_custom_call" | custom-call | flops 11500000256 | bytes 1 | tf_op jit(solution)/shard_map/attention_forward/pallas_call | solution.py:111
  102.7 3.1 collective-permute-start.8
  105.8 8.2 %collective-permute-start.7 = (bf16[576,256]{1,0:T(8,128)(2,1)}, bf16[576,256]{1,0:T(8,128)(2,1)S(1)}, u32[]{:S(2)}, u32[]{:S(2)}) collective-permute-start(bf16[576,256]{1,0:T(8,128)(2,1)} %get-tuple-element.134.refs_10_.refs_1_.refs_8_), channel_id=1, source_target_pairs={{0,2},{1,3},{2,0},{3,1},{4,6},{5,7},{6,4},{7,5},{8,10},{9,11},{10,... | collective-permute-start | bytes 884744 | tf_op jit(solution)/shard_map/ppermute | solution.py:1120
  116.3 2.1 copy.65
  118.5 24.3 %conv_mlp.2 = (bf16[512,1536]{1,0:T(8,128)(2,1)}, bf16[512,1536]{1,0:T(8,128)(2,1)}, bf16[288,1536]{1,0:T(8,128)(2,1)}, bf16[288,1536]{1,0:T(8,128)(2,1)}, bf16[...) custom-call(s32[7]{0:T(128)} %stack.148.refs_0_, ...), custom_call_target="tpu_custom_call" | custom-call | flops 575000000 | bytes 1 | tf_op jit(solution)/shard_map/conv_mlp/pallas_call | solution.py:111
  142.9 5.0 %collective-permute-done.7.refs_3_ = bf16[576,256]{1,0:T(8,128)(2,1)S(1)} collective-permute-done((bf16[576,256]{1,0:T(8,128)(2,1)}, bf16[576,256]{1,0:T(8,128)(2,1)S(1)}, u32[]{:S(2)}, u32[]{:S(2)}) %collective-permute-start.7) | collective-permute-done | bytes 294944 | tf_op jit(solution)/shard_map/ppermute | solution.py:1120
  148.7 15.3 %vit_mlp.1 = (f32[576,1024]{1,0:T(8,128)}, bf16[576,1024]{1,0:T(8,128)(2,1)}, bf16[576,1024]{1,0:T(8,128)(2,1)}, bf16[576,1024]{1,0:T(8,128)(2,1)}, f32[1,1024]{...) custom-call(s32[7]{0:T(128)} %stack.148.refs_0_, ...), custom_call_target="tpu_custom_call" | custom-call | flops 37950001152 | bytes 1 | tf_op jit(solution)/shard_map/vit_mlp/pallas_call | solution.py:111
  165.8 2.7 collective-permute-start.14
  170.2 24.5 %conv_mlp.3 = (bf16[512,1536]{1,0:T(8,128)(2,1)}, bf16[512,1536]{1,0:T(8,128)(2,1)}, bf16[288,1536]{1,0:T(8,128)(2,1)}, bf16[288,1536]{1,0:T(8,128)(2,1)}, bf16[...) custom-call(s32[7]{0:T(128)} %stack.148.refs_0_, ...), custom_call_target="tpu_custom_call" | custom-call | flops 575000000 | bytes 1 | tf_op jit(solution)/shard_map/conv_mlp/pallas_call | solution.py:111
  194.8 7.2 %adapter.1 = (bf16[576,384]{1,0:T(8,128)(2,1)}, f32[1,1024]{1,0:T(1,128)}, bf16[4,576,256]{2,1,0:T(8,128)(2,1)}) custom-call(s32[7]{0:T(128)} %stack.148.refs_0_, f32[288,1024]{1,0:T(8,128)} %get-tuple-element.135.refs_1_, f32[288,1024]{1,0:T(8,128)} %get-tuple-element.140.refs_2_, f32[288,384]{1,0:T(8,128)} %get-tuple-element.141.refs_3_, ...), custom_call_target="tpu_custom_call" | custom-call | flops 575000000 | bytes 1 | tf_op jit(solution)/shard_map/adapter/pallas_call | solution.py:111
  203.0 3.7 norm2_backward.1
  207.8 3.9 collective-permute-start.16
  212.5 8.2 %grad_fc.1 = (bf16[4,128,2048]{2,1,0:T(8,128)(2,1)}, bf16[4,128,2048]{2,1,0:T(8,128)(2,1)}) custom-call(s32[7]{0:T(128)} %stack.148.refs_0_, bf16[576,1024]{1,0:T(8,128)(2,1)} %get-tuple-element.169.refs_1_, bf16[576,1024]{1,0:T(8,128)(2,1)} %dynamic-slice_bitcast_fusion.refs_2_, bf16[576,1024]{1,0:T(8,128)(2,1)} %get-tuple-element.170.refs_3_, ...), custom_call_target="tpu_custom_call" | custom-call | flops 575000000 | bytes 1 | tf_op jit(solution)/shard_map/grad_fc/pallas_call | solution.py:111
  220.7 9.4 %grad_adapt.1 = (bf16[4,128,1920]{2,1,0:T(8,128)(2,1)}, bf16[4,128,1920]{2,1,0:T(8,128)(2,1)}) custom-call(s32[7]{0:T(128)} %stack.148.refs_0_, bf16[288,1024]{1,0:T(8,128)(2,1)} %get-tuple-element.132.refs_8_.refs_1_.refs_3_, bf16[288,1024]{1,0:T(8,128)(2,1)} %get-tuple-element.137.refs_8_.refs_2_.refs_4_, ...), custom_call_target="tpu_custom_call" | custom-call | flops 575000000 | bytes 1 | tf_op jit(solution)/shard_map/grad_adapt/pallas_call | solution.py:111
  230.1 8.9 %grad_pw2.1 = (bf16[4,192,1536]{2,1,0:T(8,128)(2,1)}, bf16[4,192,1536]{2,1,0:T(8,128)(2,1)}) custom-call(s32[7]{0:T(128)} %stack.148.refs_0_, bf16[288,1536]{1,0:T(8,128)(2,1)} %get-tuple-element.162.refs_1_, bf16[288,1536]{1,0:T(8,128)(2,1)} %get-tuple-element.163.refs_2_, bf16[288,1536]{1,0:T(8,128)(2,1)} %get-tuple-element.164.refs_3_, ...), custom_call_target="tpu_custom_call" | custom-call | flops 575000000 | bytes 1 | tf_op jit(solution)/shard_map/grad_pw2/pallas_call | solution.py:111
  239.0 9.4 %grad_pw1.1 = (bf16[4,192,1536]{2,1,0:T(8,128)(2,1)}, bf16[4,192,1536]{2,1,0:T(8,128)(2,1)}) custom-call(s32[7]{0:T(128)} %stack.148.refs_0_, bf16[512,1536]{1,0:T(8,128)(2,1)} %get-tuple-element.158.refs_1_, bf16[512,1536]{1,0:T(8,128)(2,1)} %get-tuple-element.159.refs_2_, bf16[512,1536]{1,0:T(8,128)(2,1)} %get-tuple-element.160.refs_3_, ...), custom_call_target="tpu_custom_call" | custom-call | flops 575000000 | bytes 1 | tf_op jit(solution)/shard_map/grad_pw1/pallas_call | solution.py:111
  248.5 6.4 %collective-permute-done.16.refs_3_ = bf16[144,1024]{1,0:T(8,128)(2,1)S(1)} collective-permute-done((bf16[144,1024]{1,0:T(8,128)(2,1)}, bf16[144,1024]{1,0:T(8,128)(2,1)S(1)}, u32[]{:S(2)}, u32[]{:S(2)}) %collective-permute-start.16) | collective-permute-done | bytes 294944 | tf_op jit(solution)/shard_map/ppermute | solution.py:1120
  255.7 16.3 %attention_backward.1 = (bf16[576,1024]{1,0:T(8,128)(2,1)}, bf16[576,256]{1,0:T(8,128)(2,1)}, bf16[576,256]{1,0:T(8,128)(2,1)}, bf16[576,256]{1,0:T(8,128)(2,1)}, bf16[4,592,256]{2,1,0:T(8,128)(2,1)}) custom-call(s32[7]{0:T(128)} %stack.148.refs_0_, bf16[144,1024]{1,0:T(8,128)(2,1)} %get-tuple-element.154.refs_1_, bf16[144,1024]{1,0:T(8,128)(2,1)} %copy-done.40, ...), custom_call_target="tpu_custom_call" | custom-call | flops 35649998848 | bytes 1 | tf_op jit(solution)/shard_map/attention_backward/pallas_call | solution.py:111
  275.5 7.7 %collective-permute-done.21 = bf16[4,128,2048]{2,1,0:T(8,128)(2,1)} collective-permute-done((bf16[4,128,2048]{2,1,0:T(8,128)(2,1)}, bf16[4,128,2048]{2,1,0:T(8,128)(2,1)}, u32[]{:S(2)}, u32[]{:S(2)}) %collective-permute-start.21) | collective-permute-done | bytes 2097184 | tf_op jit(solution)/shard_map/ppermute | solution.py:1120
  283.2 4.7 %fold_fc.1 = (bf16[1,2,128,2048]{3,2,1,0:T(8,128)(2,1)}, bf16[1,2,128,2048]{3,2,1,0:T(8,128)(2,1)}) custom-call(s32[7]{0:T(128)} %stack.148.refs_0_, bf16[2,1,2,128,2048]{4,3,2,1,0:T(8,128)(2,1)} %bitcast.147, bf16[2,1,2,128,2048]{4,3,2,1,0:T(8,128)(2,1)} %bitcast.56.refs_2_, bf16[576,256]{1,0:T(8,128)(2,1)} %get-tuple-element.178.refs_3_.refs_5_, ...), custom_call_target="tpu_custom_call" | custom-call | flops 575000000 | bytes 1 | tf_op jit(solution)/shard_map/fold_fc/pallas_call | solution.py:111
  289.3 4.4 %fold_adapt.1 = (bf16[2,1,128,1920]{3,2,1,0:T(8,128)(2,1)}, bf16[2,1,128,1920]{3,2,1,0:T(8,128)(2,1)}) custom-call(s32[7]{0:T(128)} %stack.148.refs_0_, bf16[2,1,2,128,1920]{4,3,2,1,0:T(8,128)(2,1)} %bitcast.148, bf16[2,1,2,128,1920]{4,3,2,1,0:T(8,128)(2,1)} %bitcast.54.refs_2_, bf16[1,2,128,2048]{3,2,1,0:T(8,128)(2,1)} %get-tuple-element.186.refs_3_.refs_1_), custom_call_target="tpu_custom_call" | custom-call | flops 575000000 | bytes 1 | tf_op jit(solution)/shard_map/fold_adapt/pallas_call | solution.py:111
  295.7 4.7 %fold_pw2.1 = (bf16[2,1,192,1536]{3,2,1,0:T(8,128)(2,1)}, bf16[2,1,192,1536]{3,2,1,0:T(8,128)(2,1)}) custom-call(s32[7]{0:T(128)} %stack.148.refs_0_, bf16[2,1,2,192,1536]{4,3,2,1,0:T(8,128)(2,1)} %bitcast.146, bf16[2,1,2,192,1536]{4,3,2,1,0:T(8,128)(2,1)} %bitcast.52.refs_2_, bf16[2,1,128,1920]{3,2,1,0:T(8,128)(2,1)} %get-tuple-element.187.refs_3_.refs_1_), custom_call_target="tpu_custom_call" | custom-call | flops 575000000 | bytes 1 | tf_op jit(solution)/shard_map/fold_pw2/pallas_call | solution.py:111
  301.9 4.7 %fold_pw1.1 = (bf16[1,2,192,1536]{3,2,1,0:T(8,128)(2,1)}, bf16[1,2,192,1536]{3,2,1,0:T(8,128)(2,1)}) custom-call(s32[7]{0:T(128)} %stack.148.refs_0_, bf16[2,1,2,192,1536]{4,3,2,1,0:T(8,128)(2,1)} %bitcast.150, bf16[2,1,2,192,1536]{4,3,2,1,0:T(8,128)(2,1)} %bitcast.151, bf16[2,1,192,1536]{3,2,1,0:T(8,128)(2,1)} %get-tuple-element.188.refs_3_.refs_1_), custom_call_target="tpu_custom_call" | custom-call | flops 575000000 | bytes 1 | tf_op jit(solution)/shard_map/fold_pw1/pallas_call | solution.py:111
  307.7 8.9 %grad_qkv.1 = (bf16[4,128,1024]{2,1,0:T(8,128)(2,1)}, bf16[4,128,1024]{2,1,0:T(8,128)(2,1)}) custom-call(s32[7]{0:T(128)} %stack.148.refs_0_, bf16[576,1024]{1,0:T(8,128)(2,1)} %get-tuple-element.177.refs_1_.refs_2_.refs_3_, bf16[576,1024]{1,0:T(8,128)(2,1)} %get-tuple-element.177.refs_1_.refs_2_.refs_3_, ...), custom_call_target="tpu_custom_call" | custom-call | flops 575000000 | bytes 1 | tf_op jit(solution)/shard_map/grad_qkv/pallas_call | solution.py:111
  316.6 4.0 norm1_backward.1
  324.4 3.0 collective-permute-start.22
  327.4 21.0 %conv_backward.1 = (bf16[32,32,384]{2,1,0:T(8,128)(2,1)}, f32[49,384]{1,0:T(8,128)}, f32[8,384]{1,0:T(8,128)}) custom-call(s32[7]{0:T(128)} %stack.148.refs_0_, bf16[528,384]{1,0:T(8,128)(2,1)} %bitcast.155, bf16[528,384]{1,0:T(8,128)(2,1)} %bitcast.157, bf16[512,384]{1,0:T(8,128)(2,1)} %get-tuple-element.129.refs_3_, ...), custom_call_target="tpu_custom_call" | custom-call | flops 575000000 | bytes 1 | tf_op jit(solution)/shard_map/conv_backward/pallas_call | solution.py:111
  350.7 2.6 pack.1.refs_4_
  359.7 2.5 collective-permute-done.33
  363.2 2.6 output_halves.1
  368.0 3.3 fold_qkv.1
  371.3 3.2 fold_adapt_last.1
  375.4 3.3 fold_fc_last.1
  380.2 3.4 fold_pw2_last.1
  383.6 3.5 fold_pw1_last.1
  406.0 2.7 fold_qkv_last.1
  414.7 2.2 add_bitcast_fusion.1
  416.9 2.3 add_bitcast_fusion
  (265 shorter events, 96.2 us)
Async XLA Ops:
  7.2 85.2 %all-gather.5.cloned.1.call-start = ((), (), s32[]{:S(2)}) async-start(), calls=%async_computation.8 | async-start | bytes 1966080 | tf_op jit(solution)/shard_map/all_gather | solution.py:1281
  34.9 9.8 %collective-permute-start.2 = (bf16[80,1024]{1,0:T(8,128)(2,1)S(1)}, bf16[80,1024]{1,0:T(8,128)(2,1)S(1)}, u32[]{:S(2)}, u32[]{:S(2)}) collective-permute-start(bf16[80,1024]{1,0:T(8,128)(2,1)S(1)} %pad_maximum_fusion.11), channel_id=1, source_target_pairs={{0,1},{1,0},{2,3},{3,2},{4,5},{5,4},{6,7},{7,6},{8,9},{9,8},{10,11... | collective-permute-start | bytes 491528 | tf_op jit(solution)/shard_map/ppermute | solution.py:1120
  37.9 15.0 %collective-permute-start.1 = (bf16[80,1024]{1,0:T(8,128)(2,1)S(1)}, bf16[80,1024]{1,0:T(8,128)(2,1)S(1)}, u32[]{:S(2)}, u32[]{:S(2)}) collective-permute-start(bf16[80,1024]{1,0:T(8,128)(2,1)S(1)} %pad_maximum_fusion.11), channel_id=1, source_target_pairs={{0,2},{1,3},{2,0},{3,1},{4,6},{5,7},{6,4},{7,5},{8,10},{9,11},{10,... | collective-permute-start | bytes 491528 | tf_op jit(solution)/shard_map/ppermute | solution.py:1120
  40.5 12.5 %collective-permute-start = (bf16[80,1024]{1,0:T(8,128)(2,1)S(1)}, bf16[80,1024]{1,0:T(8,128)(2,1)S(1)}, u32[]{:S(2)}, u32[]{:S(2)}) collective-permute-start(bf16[80,1024]{1,0:T(8,128)(2,1)S(1)} %pad_maximum_fusion.11), channel_id=1, source_target_pairs={{0,3},{1,2},{2,1},{3,0},{4,7},{5,6},{6,5},{7,4},{8,11},{9,10},{10,... | collective-permute-start | bytes 491528 | tf_op jit(solution)/shard_map/ppermute | solution.py:1120
  40.6 129.6 %all-gather.7.cloned.1.call-start = ((), (), s32[]{:S(2)}) async-start(), calls=%async_computation.9 | async-start | bytes 1966080 | tf_op jit(solution)/shard_map/all_gather | solution.py:1281
  53.1 6.4 %collective-permute-start.9 = (bf16[4,32,1024]{2,1,0:T(8,128)(2,1)S(1)}, bf16[4,32,1024]{2,1,0:T(8,128)(2,1)S(1)}, u32[]{:S(2)}, u32[]{:S(2)}) collective-permute-start(bf16[4,32,1024]{2,1,0:T(8,128)(2,1)S(1)} %pad_maximum_fusion.10), channel_id=1, source_target_pairs={{0,16},{16,0},{1,17},{17,1},{2,18},{18,2},{3,19},{19,3},{4,20},{20... | collective-permute-start | bytes 786440 | tf_op jit(solution)/shard_map/ppermute | solution.py:1120
  55.7 12.2 %collective-permute-start.3 = (bf16[4,48,1024]{2,1,0:T(8,128)(2,1)S(1)}, bf16[4,48,1024]{2,1,0:T(8,128)(2,1)}, u32[]{:S(2)}, u32[]{:S(2)}) collective-permute-start(bf16[4,48,1024]{2,1,0:T(8,128)(2,1)S(1)} %pad_maximum_fusion.7), channel_id=1, source_target_pairs={{0,8},{4,12},{8,0},{12,4},{1,9},{5,13},{9,1},{13,5},{2,10},{6,14},... | collective-permute-start | bytes 1179656 | tf_op jit(solution)/shard_map/ppermute | solution.py:1120
  59.6 15.5 %collective-permute-start.10 = (bf16[4,2,32,1024]{3,2,0,1:T(8,128)(2,1)S(1)}, bf16[4,2,32,1024]{3,2,0,1:T(8,128)(2,1)S(1)}, u32[]{:S(2)}, u32[]{:S(2)}) collective-permute-start(bf16[4,2,32,1024]{3,2,0,1:T(8,128)(2,1)S(1)} %pad_maximum_fusion.6), channel_id=1, source_target_pairs={{0,8},{4,12},{8,0},{12,4},{1,9},{5,13},{9,1},{13,5},{2,10},{6,14},... | collective-permute-start | bytes 1572872 | tf_op jit(solution)/shard_map/ppermute | solution.py:1120
  69.1 12.2 %collective-permute-start.4 = (bf16[4,2,48,1024]{3,2,0,1:T(8,128)(2,1)S(1)}, bf16[4,2,48,1024]{3,2,0,1:T(8,128)(2,1)}, u32[]{:S(2)}, u32[]{:S(2)}) collective-permute-start(bf16[4,2,48,1024]{3,2,0,1:T(8,128)(2,1)S(1)} %pad_maximum_fusion.4), channel_id=1, source_target_pairs={{0,16},{16,0},{1,17},{17,1},{2,18},{18,2},{3,19},{19,3},{4,20},{20... | collective-permute-start | bytes 2359304 | tf_op jit(solution)/shard_map/ppermute | solution.py:1120
  77.1 11.9 %collective-permute-start.11 = (bf16[4,2,2,32,1024]{4,3,0,1,2:T(8,128)(2,1)}, bf16[4,2,2,32,1024]{4,3,0,1,2:T(8,128)(2,1)}, u32[]{:S(2)}, u32[]{:S(2)}) collective-permute-start(bf16[4,2,2,32,1024]{4,3,0,1,2:T(8,128)(2,1)} %pad_maximum_fusion.3), channel_id=1, source_target_pairs={{0,4},{4,0},{8,12},{12,8},{1,5},{5,1},{9,13},{13,9},{2,6},{6,2},{1... | collective-permute-start | bytes 3145736 | tf_op jit(solution)/shard_map/ppermute | solution.py:1120
  77.1 117.8 %reduce-scatter.5.cloned.1.call-start = ((), (), s32[]{:S(2)}) async-start(), calls=%async_computation.4 | async-start | bytes 2027520 | tf_op jit(solution)/shard_map/reduce_scatter | solution.py:1325
  83.9 30.5 %collective-permute-start.5 = (bf16[4,2,2,48,1024]{4,3,0,2,1:T(8,128)(2,1)}, bf16[4,2,2,48,1024]{4,3,0,2,1:T(8,128)(2,1)}, u32[]{:S(2)}, u32[]{:S(2)}) collective-permute-start(bf16[4,2,2,48,1024]{4,3,0,2,1:T(8,128)(2,1)} %pad_maximum_fusion.2), channel_id=1, source_target_pairs={{0,4},{4,0},{8,12},{12,8},{1,5},{5,1},{9,13},{13,9},{2,6},{6,2},{1... | collective-permute-start | bytes 4718600 | tf_op jit(solution)/shard_map/ppermute | solution.py:1120
  102.7 40.2 %collective-permute-start.8 = (bf16[576,256]{1,0:T(8,128)(2,1)}, bf16[576,256]{1,0:T(8,128)(2,1)S(1)}, u32[]{:S(2)}, u32[]{:S(2)}) collective-permute-start(bf16[576,256]{1,0:T(8,128)(2,1)} %get-tuple-element.134.refs_10_.refs_1_.refs_8_), channel_id=1, source_target_pairs={{0,3},{1,2},{2,1},{3,0},{4,7},{5,6},{6,5},{7,4},{8,11},{9,10},{10,... | collective-permute-start | bytes 884744 | tf_op jit(solution)/shard_map/ppermute | solution.py:1120
  105.8 42.1 %collective-permute-start.7 = (bf16[576,256]{1,0:T(8,128)(2,1)}, bf16[576,256]{1,0:T(8,128)(2,1)S(1)}, u32[]{:S(2)}, u32[]{:S(2)}) collective-permute-start(bf16[576,256]{1,0:T(8,128)(2,1)} %get-tuple-element.134.refs_10_.refs_1_.refs_8_), channel_id=1, source_target_pairs={{0,2},{1,3},{2,0},{3,1},{4,6},{5,7},{6,4},{7,5},{8,10},{9,11},{10,... | collective-permute-start | bytes 884744 | tf_op jit(solution)/shard_map/ppermute | solution.py:1120
  113.9 34.0 %collective-permute-start.6 = (bf16[576,256]{1,0:T(8,128)(2,1)}, bf16[576,256]{1,0:T(8,128)(2,1)S(1)}, u32[]{:S(2)}, u32[]{:S(2)}) collective-permute-start(bf16[576,256]{1,0:T(8,128)(2,1)} %get-tuple-element.134.refs_10_.refs_1_.refs_8_), channel_id=1, source_target_pairs={{0,1},{1,0},{2,3},{3,2},{4,5},{5,4},{6,7},{7,6},{8,9},{9,8},{10,11... | collective-permute-start | bytes 884744 | tf_op jit(solution)/shard_map/ppermute | solution.py:1120
  142.8 132.6 %reduce-scatter.11.cloned.1.call-start = ((), (), s32[]{:S(2)}) async-start(), calls=%async_computation.7 | async-start | bytes 2027520 | tf_op jit(solution)/shard_map/reduce_scatter | solution.py:1325
  164.0 38.1 %collective-permute-start.12 = (bf16[144,1024]{1,0:T(8,128)(2,1)}, bf16[144,1024]{1,0:T(8,128)(2,1)S(1)}, u32[]{:S(2)}, u32[]{:S(2)}) collective-permute-start(bf16[144,1024]{1,0:T(8,128)(2,1)} %get-tuple-element.149), channel_id=1, source_target_pairs={{0,1},{1,0},{2,3},{3,2},{4,5},{5,4},{6,7},{7,6},{8,9},{9,8},{10,11... | collective-permute-start | bytes 884744 | tf_op jit(solution)/shard_map/ppermute | solution.py:1120
  164.1 38.0 %collective-permute-start.13 = (bf16[144,1024]{1,0:T(8,128)(2,1)}, bf16[144,1024]{1,0:T(8,128)(2,1)S(1)}, u32[]{:S(2)}, u32[]{:S(2)}) collective-permute-start(bf16[144,1024]{1,0:T(8,128)(2,1)} %get-tuple-element.150), channel_id=1, source_target_pairs={{0,2},{1,3},{2,0},{3,1},{4,6},{5,7},{6,4},{7,5},{8,10},{9,11},{10,... | collective-permute-start | bytes 884744 | tf_op jit(solution)/shard_map/ppermute | solution.py:1120
  165.8 36.3 %collective-permute-start.14 = (bf16[144,1024]{1,0:T(8,128)(2,1)}, bf16[144,1024]{1,0:T(8,128)(2,1)S(1)}, u32[]{:S(2)}, u32[]{:S(2)}) collective-permute-start(bf16[144,1024]{1,0:T(8,128)(2,1)} %get-tuple-element.151), channel_id=1, source_target_pairs={{0,3},{1,2},{2,1},{3,0},{4,7},{5,6},{6,5},{7,4},{8,11},{9,10},{10,... | collective-permute-start | bytes 884744 | tf_op jit(solution)/shard_map/ppermute | solution.py:1120
  194.8 121.8 %reduce-scatter.9.cloned.1.call-start = ((), (), s32[]{:S(2)}) async-start(), calls=%async_computation.6 | async-start | bytes 1515520 | tf_op jit(solution)/shard_map/reduce_scatter | solution.py:1430
  206.7 41.8 %collective-permute-start.17 = (bf16[144,1024]{1,0:T(8,128)(2,1)}, bf16[144,1024]{1,0:T(8,128)(2,1)S(1)}, u32[]{:S(2)}, u32[]{:S(2)}) collective-permute-start(bf16[144,1024]{1,0:T(8,128)(2,1)} %get-tuple-element.154.refs_1_), channel_id=1, source_target_pairs={{0,3},{1,2},{2,1},{3,0},{4,7},{5,6},{6,5},{7,4},{8,11},{9,10},{10,... | collective-permute-start | bytes 884744 | tf_op jit(solution)/shard_map/ppermute | solution.py:1120
  207.8 47.1 %collective-permute-start.16 = (bf16[144,1024]{1,0:T(8,128)(2,1)}, bf16[144,1024]{1,0:T(8,128)(2,1)S(1)}, u32[]{:S(2)}, u32[]{:S(2)}) collective-permute-start(bf16[144,1024]{1,0:T(8,128)(2,1)} %get-tuple-element.154.refs_1_), channel_id=1, source_target_pairs={{0,2},{1,3},{2,0},{3,1},{4,6},{5,7},{6,4},{7,5},{8,10},{9,11},{10,... | collective-permute-start | bytes 884744 | tf_op jit(solution)/shard_map/ppermute | solution.py:1120
  211.7 43.2 %collective-permute-start.15 = (bf16[144,1024]{1,0:T(8,128)(2,1)}, bf16[144,1024]{1,0:T(8,128)(2,1)S(1)}, u32[]{:S(2)}, u32[]{:S(2)}) collective-permute-start(bf16[144,1024]{1,0:T(8,128)(2,1)} %get-tuple-element.154.refs_1_), channel_id=1, source_target_pairs={{0,1},{1,0},{2,3},{3,2},{4,5},{5,4},{6,7},{7,6},{8,9},{9,8},{10,11... | collective-permute-start | bytes 884744 | tf_op jit(solution)/shard_map/ppermute | solution.py:1120
  272.2 91.1 %reduce-scatter.7.cloned.1.call-start = ((), (), s32[]{:S(2)}) async-start(), calls=%async_computation.5 | async-start | bytes 1474560 | tf_op jit(solution)/shard_map/reduce_scatter | solution.py:1380
  272.2 23.5 %collective-permute-start.19 = (bf16[4,192,1536]{2,1,0:T(8,128)(2,1)}, bf16[4,192,1536]{2,1,0:T(8,128)(2,1)}, u32[]{:S(2)}, u32[]{:S(2)}) collective-permute-start(bf16[4,192,1536]{2,1,0:T(8,128)(2,1)} %get-tuple-element.182), channel_id=1, source_target_pairs={{0,4},{4,0},{8,12},{12,8},{1,5},{5,1},{9,13},{13,9},{2,6},{6,2},{1... | collective-permute-start | bytes 7077896 | tf_op jit(solution)/shard_map/ppermute | solution.py:1120
  272.3 10.9 %collective-permute-start.21 = (bf16[4,128,2048]{2,1,0:T(8,128)(2,1)}, bf16[4,128,2048]{2,1,0:T(8,128)(2,1)}, u32[]{:S(2)}, u32[]{:S(2)}) collective-permute-start(bf16[4,128,2048]{2,1,0:T(8,128)(2,1)} %get-tuple-element.184), channel_id=1, source_target_pairs={{0,4},{4,0},{8,12},{12,8},{1,5},{5,1},{9,13},{13,9},{2,6},{6,2},{1... | collective-permute-start | bytes 6291464 | tf_op jit(solution)/shard_map/ppermute | solution.py:1120
  272.8 27.7 %collective-permute-start.18 = (bf16[4,192,1536]{2,1,0:T(8,128)(2,1)}, bf16[4,192,1536]{2,1,0:T(8,128)(2,1)S(1)}, u32[]{:S(2)}, u32[]{:S(2)}) collective-permute-start(bf16[4,192,1536]{2,1,0:T(8,128)(2,1)} %get-tuple-element.181), channel_id=1, source_target_pairs={{0,4},{4,0},{8,12},{12,8},{1,5},{5,1},{9,13},{13,9},{2,6},{6,2},{1... | collective-permute-start | bytes 7077896 | tf_op jit(solution)/shard_map/ppermute | solution.py:1120
  272.9 16.4 %collective-permute-start.20 = (bf16[4,128,1920]{2,1,0:T(8,128)(2,1)}, bf16[4,128,1920]{2,1,0:T(8,128)(2,1)}, u32[]{:S(2)}, u32[]{:S(2)}) collective-permute-start(bf16[4,128,1920]{2,1,0:T(8,128)(2,1)} %get-tuple-element.183), channel_id=1, source_target_pairs={{0,4},{4,0},{8,12},{12,8},{1,5},{5,1},{9,13},{13,9},{2,6},{6,2},{1... | collective-permute-start | bytes 5898248 | tf_op jit(solution)/shard_map/ppermute | solution.py:1120
  287.8 36.6 %collective-permute-start.25 = (bf16[1,2,128,2048]{3,2,1,0:T(8,128)(2,1)}, bf16[1,2,128,2048]{3,2,1,0:T(8,128)(2,1)S(1)}, u32[]{:S(2)}, u32[]{:S(2)}) collective-permute-start(bf16[1,2,128,2048]{3,2,1,0:T(8,128)(2,1)} %get-tuple-element.200), channel_id=1, source_target_pairs={{0,16},{16,0},{1,17},{17,1},{2,18},{18,2},{3,19},{19,3},{4,20},{20... | collective-permute-start | bytes 3145736 | tf_op jit(solution)/shard_map/ppermute | solution.py:1120
  293.7 30.7 %collective-permute-start.26 = (bf16[2,1,128,1920]{3,2,1,0:T(8,128)(2,1)}, bf16[2,1,128,1920]{3,2,1,0:T(8,128)(2,1)}, u32[]{:S(2)}, u32[]{:S(2)}) collective-permute-start(bf16[2,1,128,1920]{3,2,1,0:T(8,128)(2,1)} %get-tuple-element.201), channel_id=1, source_target_pairs={{0,8},{4,12},{8,0},{12,4},{1,9},{5,13},{9,1},{13,5},{2,10},{6,14},... | collective-permute-start | bytes 2949128 | tf_op jit(solution)/shard_map/ppermute | solution.py:1120
  306.6 56.7 %collective-permute-start.28 = (bf16[1,2,192,1536]{3,2,1,0:T(8,128)(2,1)}, bf16[1,2,192,1536]{3,2,1,0:T(8,128)(2,1)}, u32[]{:S(2)}, u32[]{:S(2)}) collective-permute-start(bf16[1,2,192,1536]{3,2,1,0:T(8,128)(2,1)} %get-tuple-element.205), channel_id=1, source_target_pairs={{0,16},{16,0},{1,17},{17,1},{2,18},{18,2},{3,19},{19,3},{4,20},{20... | collective-permute-start | bytes 3538952 | tf_op jit(solution)/shard_map/ppermute | solution.py:1120
  307.1 56.1 %collective-permute-start.27 = (bf16[2,1,192,1536]{3,2,1,0:T(8,128)(2,1)}, bf16[2,1,192,1536]{3,2,1,0:T(8,128)(2,1)}, u32[]{:S(2)}, u32[]{:S(2)}) collective-permute-start(bf16[2,1,192,1536]{3,2,1,0:T(8,128)(2,1)} %get-tuple-element.204), channel_id=1, source_target_pairs={{0,8},{4,12},{8,0},{12,4},{1,9},{5,13},{9,1},{13,5},{2,10},{6,14},... | collective-permute-start | bytes 3538952 | tf_op jit(solution)/shard_map/ppermute | solution.py:1120
  322.9 25.5 %collective-permute-start.24 = (f32[11,1024]{1,0:T(8,128)S(1)}, f32[11,1024]{1,0:T(8,128)S(1)}, u32[]{:S(2)}, u32[]{:S(2)}) collective-permute-start(f32[11,1024]{1,0:T(8,128)S(1)} %concatenate.7.refs_1_), channel_id=1, source_target_pairs={{0,3},{1,2},{2,1},{3,0},{4,7},{5,6},{6,5},{7,4},{8,11},{9,10},{10,... | collective-permute-start | bytes 135176 | tf_op jit(solution)/shard_map/ppermute | solution.py:1120
  324.4 24.1 %collective-permute-start.23 = (f32[11,1024]{1,0:T(8,128)S(1)}, f32[11,1024]{1,0:T(8,128)S(1)}, u32[]{:S(2)}, u32[]{:S(2)}) collective-permute-start(f32[11,1024]{1,0:T(8,128)S(1)} %concatenate.7.refs_1_), channel_id=1, source_target_pairs={{0,2},{1,3},{2,0},{3,1},{4,6},{5,7},{6,4},{7,5},{8,10},{9,11},{10,... | collective-permute-start | bytes 135176 | tf_op jit(solution)/shard_map/ppermute | solution.py:1120
  324.4 25.7 %collective-permute-start.22 = (f32[11,1024]{1,0:T(8,128)S(1)}, f32[11,1024]{1,0:T(8,128)S(1)}, u32[]{:S(2)}, u32[]{:S(2)}) collective-permute-start(f32[11,1024]{1,0:T(8,128)S(1)} %concatenate.7.refs_1_), channel_id=1, source_target_pairs={{0,1},{1,0},{2,3},{3,2},{4,5},{5,4},{6,7},{7,6},{8,9},{9,8},{10,11... | collective-permute-start | bytes 135176 | tf_op jit(solution)/shard_map/ppermute | solution.py:1120
  348.4 18.6 %collective-permute-start.35 = (bf16[4,128,1024]{2,1,0:T(8,128)(2,1)}, bf16[4,128,1024]{2,1,0:T(8,128)(2,1)S(1)}, u32[]{:S(2)}, u32[]{:S(2)}) collective-permute-start(bf16[4,128,1024]{2,1,0:T(8,128)(2,1)} %get-tuple-element.212), channel_id=1, source_target_pairs={{0,4},{4,0},{8,12},{12,8},{1,5},{5,1},{9,13},{13,9},{2,6},{6,2},{1... | collective-permute-start | bytes 3145736 | tf_op jit(solution)/shard_map/ppermute | solution.py:1120
  358.2 28.9 %collective-permute-start.31 = (bf16[16,32,384]{2,1,0:T(8,128)(2,1)S(1)}, bf16[16,32,384]{2,1,0:T(8,128)(2,1)S(1)}, u32[]{:S(2)}, u32[]{:S(2)}) collective-permute-start(bf16[16,32,384]{2,1,0:T(8,128)(2,1)S(1)} %dynamic-slice_bitcast_fusion.1), channel_id=1, source_target_pairs={{0,16},{16,0},{1,17},{17,1},{2,18},{18,2},{3,19},{19,3},{4,20},{20... | collective-permute-start | bytes 1179656 | tf_op jit(solution)/shard_map/ppermute | solution.py:1120
  362.3 26.4 %collective-permute-start.34 = (f32[40,1024]{1,0:T(8,128)S(1)}, f32[40,1024]{1,0:T(8,128)}, u32[]{:S(2)}, u32[]{:S(2)}) collective-permute-start(f32[40,1024]{1,0:T(8,128)S(1)} %add.110.refs_0_), channel_id=1, source_target_pairs={{0,16},{16,0},{1,17},{17,1},{2,18},{18,2},{3,19},{19,3},{4,20},{20... | collective-permute-start | bytes 491528 | tf_op jit(solution)/shard_map/ppermute | solution.py:1120
  365.9 32.9 %collective-permute-start.29 = (bf16[288,256]{1,0:T(8,128)(2,1)}, bf16[288,256]{1,0:T(8,128)(2,1)S(1)}, u32[]{:S(2)}, u32[]{:S(2)}) collective-permute-start(bf16[288,256]{1,0:T(8,128)(2,1)} %get-tuple-element.207), channel_id=1, source_target_pairs={{0,16},{16,0},{1,17},{17,1},{2,18},{18,2},{3,19},{19,3},{4,20},{20... | collective-permute-start | bytes 442376 | tf_op jit(solution)/shard_map/ppermute | solution.py:1120
  374.5 26.2 %collective-permute-start.39 = (bf16[1,128,1920]{2,1,0:T(8,128)(2,1)}, bf16[1,128,1920]{2,1,0:T(8,128)(2,1)S(1)}, u32[]{:S(2)}, u32[]{:S(2)}) collective-permute-start(bf16[1,128,1920]{2,1,0:T(8,128)(2,1)} %get-tuple-element.224), channel_id=1, source_target_pairs={{0,16},{16,0},{1,17},{17,1},{2,18},{18,2},{3,19},{19,3},{4,20},{20... | collective-permute-start | bytes 1474568 | tf_op jit(solution)/shard_map/ppermute | solution.py:1120
  378.7 23.9 %collective-permute-start.38 = (bf16[1,128,2048]{2,1,0:T(8,128)(2,1)}, bf16[1,128,2048]{2,1,0:T(8,128)(2,1)S(1)}, u32[]{:S(2)}, u32[]{:S(2)}) collective-permute-start(bf16[1,128,2048]{2,1,0:T(8,128)(2,1)} %get-tuple-element.222), channel_id=1, source_target_pairs={{0,8},{4,12},{8,0},{12,4},{1,9},{5,13},{9,1},{13,5},{2,10},{6,14},... | collective-permute-start | bytes 1572872 | tf_op jit(solution)/shard_map/ppermute | solution.py:1120
  387.1 18.0 %collective-permute-start.36 = (bf16[2,1,128,1024]{3,2,1,0:T(8,128)(2,1)}, bf16[2,1,128,1024]{3,2,1,0:T(8,128)(2,1)}, u32[]{:S(2)}, u32[]{:S(2)}) collective-permute-start(bf16[2,1,128,1024]{3,2,1,0:T(8,128)(2,1)} %get-tuple-element.214), channel_id=1, source_target_pairs={{0,8},{4,12},{8,0},{12,4},{1,9},{5,13},{9,1},{13,5},{2,10},{6,14},... | collective-permute-start | bytes 1572872 | tf_op jit(solution)/shard_map/ppermute | solution.py:1120
  388.7 26.0 %collective-permute-start.43 = (bf16[1,192,1536]{2,1,0:T(8,128)(2,1)}, bf16[1,192,1536]{2,1,0:T(8,128)(2,1)}, u32[]{:S(2)}, u32[]{:S(2)}) collective-permute-start(bf16[1,192,1536]{2,1,0:T(8,128)(2,1)} %get-tuple-element.227), channel_id=1, source_target_pairs={{0,8},{4,12},{8,0},{12,4},{1,9},{5,13},{9,1},{13,5},{2,10},{6,14},... | collective-permute-start | bytes 1769480 | tf_op jit(solution)/shard_map/ppermute | solution.py:1120
  398.8 18.1 %collective-permute-start.44 = (bf16[1,192,1536]{2,1,0:T(8,128)(2,1)}, bf16[1,192,1536]{2,1,0:T(8,128)(2,1)}, u32[]{:S(2)}, u32[]{:S(2)}) collective-permute-start(bf16[1,192,1536]{2,1,0:T(8,128)(2,1)} %get-tuple-element.229), channel_id=1, source_target_pairs={{0,16},{16,0},{1,17},{17,1},{2,18},{18,2},{3,19},{19,3},{4,20},{20... | collective-permute-start | bytes 1769480 | tf_op jit(solution)/shard_map/ppermute | solution.py:1120
  401.5 9.0 %collective-permute-start.40 = (bf16[128,384]{1,0:T(8,128)(2,1)}, bf16[128,384]{1,0:T(8,128)(2,1)S(1)}, u32[]{:S(2)}, u32[]{:S(2)}) collective-permute-start(bf16[128,384]{1,0:T(8,128)(2,1)} %get-tuple-element.307), channel_id=1, source_target_pairs={{0,1},{1,0},{2,3},{3,2},{4,5},{5,4},{6,7},{7,6},{8,9},{9,8},{10,11... | collective-permute-start | bytes 294920 | tf_op jit(solution)/shard_map/ppermute | solution.py:1120
  402.6 9.1 %collective-permute-start.42 = (bf16[128,384]{1,0:T(8,128)(2,1)}, bf16[128,384]{1,0:T(8,128)(2,1)S(1)}, u32[]{:S(2)}, u32[]{:S(2)}) collective-permute-start(bf16[128,384]{1,0:T(8,128)(2,1)} %get-tuple-element.308), channel_id=1, source_target_pairs={{0,3},{1,2},{2,1},{3,0},{4,7},{5,6},{6,5},{7,4},{8,11},{9,10},{10,... | collective-permute-start | bytes 294920 | tf_op jit(solution)/shard_map/ppermute | solution.py:1120
  405.1 6.7 %collective-permute-start.41 = (bf16[128,384]{1,0:T(8,128)(2,1)S(1)}, bf16[128,384]{1,0:T(8,128)(2,1)S(1)}, u32[]{:S(2)}, u32[]{:S(2)}) collective-permute-start(bf16[128,384]{1,0:T(8,128)(2,1)S(1)} %get-tuple-element.309), channel_id=1, source_target_pairs={{0,2},{1,3},{2,0},{3,1},{4,6},{5,7},{6,4},{7,5},{8,10},{9,11},{10,... | collective-permute-start | bytes 294920 | tf_op jit(solution)/shard_map/ppermute | solution.py:1120
  410.6 8.6 %collective-permute-start.37 = (bf16[1,128,1024]{2,1,0:T(8,128)(2,1)}, bf16[1,128,1024]{2,1,0:T(8,128)(2,1)S(1)}, u32[]{:S(2)}, u32[]{:S(2)}) collective-permute-start(bf16[1,128,1024]{2,1,0:T(8,128)(2,1)} %get-tuple-element.220), channel_id=1, source_target_pairs={{0,16},{16,0},{1,17},{17,1},{2,18},{18,2},{3,19},{19,3},{4,20},{20... | collective-permute-start | bytes 786440 | tf_op jit(solution)/shard_map/ppermute | solution.py:1120
  (48 other events, 227.2 us)
Sparse Core Ops, SparseCore 0:
  40.7 40.0 all-gather.4
  82.3 58.9 all-gather.6
  143.6 46.8 reduce-scatter.4
  194.9 52.8 reduce-scatter.10
  272.3 28.6 reduce-scatter.8
  303.3 30.9 reduce-scatter.6

commit v5 on v4

--- a/solution.py
+++ b/solution.py
@@ -1496,11 +1496,11 @@
     )
     packed_first = packed
     packed = summed(packed, ("dp",))
+    qkv_part = first_fold("fold_qkv", qkv_halves, scalars, (packed_first,), True)
     output_keep, output_send = output_halves(
-        [branch_sum], hidden1, fc2_bias, scalars, (packed_first, pw2_part[1], pw1_part[1])
-    )
-    qkv_part = first_fold("fold_qkv", qkv_halves, scalars, (output_keep,), True)
-    adapt_part = second_fold("fold_adapt_last", adapt_part, scalars, qkv_part[:1])
+        [branch_sum], hidden1, fc2_bias, scalars, (qkv_part[0], pw2_part[1], pw1_part[1])
+    )
+    adapt_part = second_fold("fold_adapt_last", adapt_part, scalars, (output_keep,))
     fc_part = second_fold("fold_fc_last", fc_part, scalars, adapt_part[:1])
     pw2_part = second_fold("fold_pw2_last", pw2_part, scalars, fc_part[:1])
     pw1_part = second_fold("fold_pw1_last", pw1_part, scalars, pw2_part[:1])

time: 436 us -> 443 us (1.016)
  waiting for transfers between devices: 56.3 us -> 61 us
    ppermute x45, waiting for transfers between devices: 56.1 us -> 60.9 us  [swap(): return lax.ppermute(value, axis, [(i, i ^ apart) for i in range(n)])]
    unnamed x95 -> x93, local copies, waits for them, and re-layouts: 11.6 us -> 12.4 us
  transfers between devices with their start and end apart: 51 -> 51, of which waited for: 15 -> 15; matrix products, arithmetic and copies ran while one was open for 11% -> 11% of each run, Pallas kernels for 51% -> 50%
where the time goes in v5:
time: 443 us; the launch traced here: 435 us
  Pallas kernels  232 us (52%)
  waiting for transfers between devices  61 us (14%)
  starting transfers between devices  57.5 us (13%)
  local copies, waits for them, and re-layouts  39.9 us (9%)
  other arithmetic  26.9 us (6%)
  between operations  17 us (4%)
    pallas_call x29, Pallas kernels, call(): pl.pallas_call(run, grid_spec=pltpu.PrefetchScalarGridSpec(num_scalar_pre...  232 us
    ppermute x45, waiting for transfers between devices, swap(): return lax.ppermute(value, axis, [(i, i ^ apart) for i in range(n)])  60.9 us
    ppermute x45, starting transfers between devices, swap(): return lax.ppermute(value, axis, [(i, i ^ apart) for i in range(n)])  57.3 us
    unnamed x93, local copies, waits for them, and re-layouts  12.4 us
  transfers between devices with their start and end apart: 51, of which 15 were waited for; matrix products, arithmetic and copies ran while one was open for 11% of the time, Pallas kernels for 50%

profile of v5, /device:TPU:0, one launch (start us, length us, event | category | flops | bytes accessed | tf_op | source)
XLA Modules:
  0.0 434.9 jit_solution(256353296297388001)
XLA Ops:
  14.3 7.7 %front.2 = (bf16[512,384]{1,0:T(8,128)(2,1)}, f32[288,384]{1,0:T(8,128)}, bf16[288,384]{1,0:T(8,128)(2,1)}, bf16[288,1024]{1,0:T(8,128)(2,1)}, f32[8,384]{1,0:T(8,128)}, /*index=5*/s32[8,128]{1,0:T(8,128)}) custom-call(s32[7]{0:T(128)} %stack.148.refs_0_, bf16[2,32,32,384]{3,2,1,0:T(8,128)(2,1)} %refs_11_.3, f32[49,384]{1,0:T(8,128)} %refs_12_.3, ...), custom_call_target="tpu_custom_call" | custom-call | flops 575000000 | bytes 1 | tf_op jit(solution)/shard_map/front/pallas_call | solution.py:111
  22.0 7.7 %front.3 = (bf16[512,384]{1,0:T(8,128)(2,1)}, f32[288,384]{1,0:T(8,128)}, bf16[288,384]{1,0:T(8,128)(2,1)}, bf16[288,1024]{1,0:T(8,128)(2,1)}, f32[8,384]{1,0:T(8,128)}, /*index=5*/s32[8,128]{1,0:T(8,128)}) custom-call(s32[7]{0:T(128)} %stack.148.refs_0_, bf16[2,32,32,384]{3,2,1,0:T(8,128)(2,1)} %refs_11_.3, f32[49,384]{1,0:T(8,128)} %refs_12_.3, ...), custom_call_target="tpu_custom_call" | custom-call | flops 575000000 | bytes 1 | tf_op jit(solution)/shard_map/front/pallas_call | solution.py:111
  34.9 3.1 collective-permute-start.2
  38.0 2.6 collective-permute-start.1
  41.5 3.1 collective-permute-done.2
  44.7 8.4 %collective-permute-done.1 = bf16[80,1024]{1,0:T(8,128)(2,1)S(1)} collective-permute-done((bf16[80,1024]{1,0:T(8,128)(2,1)S(1)}, bf16[80,1024]{1,0:T(8,128)(2,1)S(1)}, u32[]{:S(2)}, u32[]{:S(2)}) %collective-permute-start.1) | collective-permute-done | bytes 163872 | tf_op jit(solution)/shard_map/ppermute | solution.py:1120
  57.4 2.2 collective-permute-done.9
  61.2 6.7 %collective-permute-done.3 = bf16[4,48,1024]{2,1,0:T(8,128)(2,1)S(1)} collective-permute-done((bf16[4,48,1024]{2,1,0:T(8,128)(2,1)S(1)}, bf16[4,48,1024]{2,1,0:T(8,128)(2,1)S(1)}, u32[]{:S(2)}, u32[]{:S(2)}) %collective-permute-start.3) | collective-permute-done | bytes 393248 | tf_op jit(solution)/shard_map/ppermute | solution.py:1120
  68.6 6.6 %collective-permute-done.10 = bf16[4,2,32,1024]{3,2,0,1:T(8,128)(2,1)} collective-permute-done((bf16[4,2,32,1024]{3,2,0,1:T(8,128)(2,1)S(1)}, bf16[4,2,32,1024]{3,2,0,1:T(8,128)(2,1)}, u32[]{:S(2)}, u32[]{:S(2)}) %collective-permute-start.10) | collective-permute-done | bytes 524320 | tf_op jit(solution)/shard_map/ppermute | solution.py:1120
  91.3 10.2 %attention_forward.1 = (bf16[576,1024]{1,0:T(8,128)(2,1)}, bf16[576,256]{1,0:T(8,128)(2,1)}, bf16[576,256]{1,0:T(8,128)(2,1)}, bf16[576,256]{1,0:T(8,128)(2,1)}, bf16[576,256]{1,0:T(8,128)(2,1)}) custom-call(s32[7]{0:T(128)} %stack.148.refs_0_, bf16[2,576,1024]{2,1,0:T(8,128)(2,1)} %refs_3_.1, f32[1,1024]{1,0:T(1,128)} %bitcast.171, f32[1,1024]{1,0:T(1,128)} %bitcast.184, ...), custom_call_target="tpu_custom_call" | custom-call | flops 11500000256 | bytes 1 | tf_op jit(solution)/shard_map/attention_forward/pallas_call | solution.py:111
  101.5 3.1 collective-permute-start.8
  104.6 8.4 %collective-permute-start.7 = (bf16[576,256]{1,0:T(8,128)(2,1)}, bf16[576,256]{1,0:T(8,128)(2,1)S(1)}, u32[]{:S(2)}, u32[]{:S(2)}) collective-permute-start(bf16[576,256]{1,0:T(8,128)(2,1)} %get-tuple-element.134.refs_10_.refs_1_.refs_8_), channel_id=1, source_target_pairs={{0,2},{1,3},{2,0},{3,1},{4,6},{5,7},{6,4},{7,5},{8,10},{9,11},{10,... | collective-permute-start | bytes 884744 | tf_op jit(solution)/shard_map/ppermute | solution.py:1120
  115.4 2.2 copy.65
  117.6 24.3 %conv_mlp.2 = (bf16[512,1536]{1,0:T(8,128)(2,1)}, bf16[512,1536]{1,0:T(8,128)(2,1)}, bf16[288,1536]{1,0:T(8,128)(2,1)}, bf16[288,1536]{1,0:T(8,128)(2,1)}, bf16[...) custom-call(s32[7]{0:T(128)} %stack.148.refs_0_, ...), custom_call_target="tpu_custom_call" | custom-call | flops 575000000 | bytes 1 | tf_op jit(solution)/shard_map/conv_mlp/pallas_call | solution.py:111
  142.1 7.4 %collective-permute-done.7.refs_3_ = bf16[576,256]{1,0:T(8,128)(2,1)S(1)} collective-permute-done((bf16[576,256]{1,0:T(8,128)(2,1)}, bf16[576,256]{1,0:T(8,128)(2,1)S(1)}, u32[]{:S(2)}, u32[]{:S(2)}) %collective-permute-start.7) | collective-permute-done | bytes 294944 | tf_op jit(solution)/shard_map/ppermute | solution.py:1120
  150.3 15.4 %vit_mlp.1 = (f32[576,1024]{1,0:T(8,128)}, bf16[576,1024]{1,0:T(8,128)(2,1)}, bf16[576,1024]{1,0:T(8,128)(2,1)}, bf16[576,1024]{1,0:T(8,128)(2,1)}, f32[1,1024]{...) custom-call(s32[7]{0:T(128)} %stack.148.refs_0_, ...), custom_call_target="tpu_custom_call" | custom-call | flops 37950001152 | bytes 1 | tf_op jit(solution)/shard_map/vit_mlp/pallas_call | solution.py:111
  167.5 2.6 collective-permute-start.14
  171.8 24.5 %conv_mlp.3 = (bf16[512,1536]{1,0:T(8,128)(2,1)}, bf16[512,1536]{1,0:T(8,128)(2,1)}, bf16[288,1536]{1,0:T(8,128)(2,1)}, bf16[288,1536]{1,0:T(8,128)(2,1)}, bf16[...) custom-call(s32[7]{0:T(128)} %stack.148.refs_0_, ...), custom_call_target="tpu_custom_call" | custom-call | flops 575000000 | bytes 1 | tf_op jit(solution)/shard_map/conv_mlp/pallas_call | solution.py:111
  196.5 7.2 %adapter.1 = (bf16[576,384]{1,0:T(8,128)(2,1)}, f32[1,1024]{1,0:T(1,128)}, bf16[4,576,256]{2,1,0:T(8,128)(2,1)}) custom-call(s32[7]{0:T(128)} %stack.148.refs_0_, f32[288,1024]{1,0:T(8,128)} %get-tuple-element.135.refs_1_, f32[288,1024]{1,0:T(8,128)} %get-tuple-element.140.refs_2_, f32[288,384]{1,0:T(8,128)} %get-tuple-element.141.refs_3_, ...), custom_call_target="tpu_custom_call" | custom-call | flops 575000000 | bytes 1 | tf_op jit(solution)/shard_map/adapter/pallas_call | solution.py:111
  204.6 3.7 norm2_backward.1
  209.6 4.2 collective-permute-start.16
  214.6 8.2 %grad_fc.1 = (bf16[4,128,2048]{2,1,0:T(8,128)(2,1)}, bf16[4,128,2048]{2,1,0:T(8,128)(2,1)}) custom-call(s32[7]{0:T(128)} %stack.148.refs_0_, bf16[576,1024]{1,0:T(8,128)(2,1)} %get-tuple-element.169.refs_1_, bf16[576,1024]{1,0:T(8,128)(2,1)} %dynamic-slice_bitcast_fusion.refs_2_, bf16[576,1024]{1,0:T(8,128)(2,1)} %get-tuple-element.170.refs_3_, ...), custom_call_target="tpu_custom_call" | custom-call | flops 575000000 | bytes 1 | tf_op jit(solution)/shard_map/grad_fc/pallas_call | solution.py:111
  222.8 9.4 %grad_adapt.1 = (bf16[4,128,1920]{2,1,0:T(8,128)(2,1)}, bf16[4,128,1920]{2,1,0:T(8,128)(2,1)}) custom-call(s32[7]{0:T(128)} %stack.148.refs_0_, bf16[288,1024]{1,0:T(8,128)(2,1)} %get-tuple-element.132.refs_8_.refs_1_.refs_3_, bf16[288,1024]{1,0:T(8,128)(2,1)} %get-tuple-element.137.refs_8_.refs_2_.refs_4_, ...), custom_call_target="tpu_custom_call" | custom-call | flops 575000000 | bytes 1 | tf_op jit(solution)/shard_map/grad_adapt/pallas_call | solution.py:111
  232.2 8.9 %grad_pw2.1 = (bf16[4,192,1536]{2,1,0:T(8,128)(2,1)}, bf16[4,192,1536]{2,1,0:T(8,128)(2,1)}) custom-call(s32[7]{0:T(128)} %stack.148.refs_0_, bf16[288,1536]{1,0:T(8,128)(2,1)} %get-tuple-element.162.refs_1_, bf16[288,1536]{1,0:T(8,128)(2,1)} %get-tuple-element.163.refs_2_, bf16[288,1536]{1,0:T(8,128)(2,1)} %get-tuple-element.164.refs_3_, ...), custom_call_target="tpu_custom_call" | custom-call | flops 575000000 | bytes 1 | tf_op jit(solution)/shard_map/grad_pw2/pallas_call | solution.py:111
  241.2 9.4 %grad_pw1.1 = (bf16[4,192,1536]{2,1,0:T(8,128)(2,1)}, bf16[4,192,1536]{2,1,0:T(8,128)(2,1)}) custom-call(s32[7]{0:T(128)} %stack.148.refs_0_, bf16[512,1536]{1,0:T(8,128)(2,1)} %get-tuple-element.158.refs_1_, bf16[512,1536]{1,0:T(8,128)(2,1)} %get-tuple-element.159.refs_2_, bf16[512,1536]{1,0:T(8,128)(2,1)} %get-tuple-element.160.refs_3_, ...), custom_call_target="tpu_custom_call" | custom-call | flops 575000000 | bytes 1 | tf_op jit(solution)/shard_map/grad_pw1/pallas_call | solution.py:111
  250.6 6.1 %collective-permute-done.16.refs_3_ = bf16[144,1024]{1,0:T(8,128)(2,1)S(1)} collective-permute-done((bf16[144,1024]{1,0:T(8,128)(2,1)}, bf16[144,1024]{1,0:T(8,128)(2,1)S(1)}, u32[]{:S(2)}, u32[]{:S(2)}) %collective-permute-start.16) | collective-permute-done | bytes 294944 | tf_op jit(solution)/shard_map/ppermute | solution.py:1120
  257.6 16.5 %attention_backward.1 = (bf16[576,1024]{1,0:T(8,128)(2,1)}, bf16[576,256]{1,0:T(8,128)(2,1)}, bf16[576,256]{1,0:T(8,128)(2,1)}, bf16[576,256]{1,0:T(8,128)(2,1)}, bf16[4,592,256]{2,1,0:T(8,128)(2,1)}) custom-call(s32[7]{0:T(128)} %stack.148.refs_0_, bf16[144,1024]{1,0:T(8,128)(2,1)} %get-tuple-element.154.refs_1_, bf16[144,1024]{1,0:T(8,128)(2,1)} %copy-done.39, ...), custom_call_target="tpu_custom_call" | custom-call | flops 35649998848 | bytes 1 | tf_op jit(solution)/shard_map/attention_backward/pallas_call | solution.py:111
  277.4 8.1 %collective-permute-done.21 = bf16[4,128,2048]{2,1,0:T(8,128)(2,1)} collective-permute-done((bf16[4,128,2048]{2,1,0:T(8,128)(2,1)}, bf16[4,128,2048]{2,1,0:T(8,128)(2,1)}, u32[]{:S(2)}, u32[]{:S(2)}) %collective-permute-start.21) | collective-permute-done | bytes 2097184 | tf_op jit(solution)/shard_map/ppermute | solution.py:1120
  285.5 4.8 %fold_fc.1 = (bf16[1,2,128,2048]{3,2,1,0:T(8,128)(2,1)}, bf16[1,2,128,2048]{3,2,1,0:T(8,128)(2,1)}) custom-call(s32[7]{0:T(128)} %stack.148.refs_0_, bf16[2,1,2,128,2048]{4,3,2,1,0:T(8,128)(2,1)} %bitcast.147, bf16[2,1,2,128,2048]{4,3,2,1,0:T(8,128)(2,1)} %bitcast.55.refs_2_, bf16[576,256]{1,0:T(8,128)(2,1)} %get-tuple-element.177.refs_3_.refs_5_, ...), custom_call_target="tpu_custom_call" | custom-call | flops 575000000 | bytes 1 | tf_op jit(solution)/shard_map/fold_fc/pallas_call | solution.py:111
  290.3 4.4 %fold_adapt.1 = (bf16[2,1,128,1920]{3,2,1,0:T(8,128)(2,1)}, bf16[2,1,128,1920]{3,2,1,0:T(8,128)(2,1)}) custom-call(s32[7]{0:T(128)} %stack.148.refs_0_, bf16[2,1,2,128,1920]{4,3,2,1,0:T(8,128)(2,1)} %bitcast.148, bf16[2,1,2,128,1920]{4,3,2,1,0:T(8,128)(2,1)} %bitcast.53.refs_2_, bf16[1,2,128,2048]{3,2,1,0:T(8,128)(2,1)} %get-tuple-element.185.refs_3_.refs_1_), custom_call_target="tpu_custom_call" | custom-call | flops 575000000 | bytes 1 | tf_op jit(solution)/shard_map/fold_adapt/pallas_call | solution.py:111
  297.6 4.8 %fold_pw2.1 = (bf16[2,1,192,1536]{3,2,1,0:T(8,128)(2,1)}, bf16[2,1,192,1536]{3,2,1,0:T(8,128)(2,1)}) custom-call(s32[7]{0:T(128)} %stack.148.refs_0_, bf16[2,1,2,192,1536]{4,3,2,1,0:T(8,128)(2,1)} %bitcast.146, bf16[2,1,2,192,1536]{4,3,2,1,0:T(8,128)(2,1)} %bitcast.51.refs_2_, bf16[2,1,128,1920]{3,2,1,0:T(8,128)(2,1)} %get-tuple-element.186.refs_3_.refs_1_), custom_call_target="tpu_custom_call" | custom-call | flops 575000000 | bytes 1 | tf_op jit(solution)/shard_map/fold_pw2/pallas_call | solution.py:111
  303.9 4.7 %fold_pw1.1 = (bf16[1,2,192,1536]{3,2,1,0:T(8,128)(2,1)}, bf16[1,2,192,1536]{3,2,1,0:T(8,128)(2,1)}) custom-call(s32[7]{0:T(128)} %stack.148.refs_0_, bf16[2,1,2,192,1536]{4,3,2,1,0:T(8,128)(2,1)} %bitcast.150, bf16[2,1,2,192,1536]{4,3,2,1,0:T(8,128)(2,1)} %bitcast.151, bf16[2,1,192,1536]{3,2,1,0:T(8,128)(2,1)} %get-tuple-element.187.refs_3_.refs_1_), custom_call_target="tpu_custom_call" | custom-call | flops 575000000 | bytes 1 | tf_op jit(solution)/shard_map/fold_pw1/pallas_call | solution.py:111
  308.6 9.1 %grad_qkv.1 = (bf16[4,128,1024]{2,1,0:T(8,128)(2,1)}, bf16[4,128,1024]{2,1,0:T(8,128)(2,1)}) custom-call(s32[7]{0:T(128)} %stack.148.refs_0_, bf16[576,1024]{1,0:T(8,128)(2,1)} %get-tuple-element.148.refs_1_.refs_2_.refs_3_, bf16[576,1024]{1,0:T(8,128)(2,1)} %get-tuple-element.148.refs_1_.refs_2_.refs_3_, ...), custom_call_target="tpu_custom_call" | custom-call | flops 575000000 | bytes 1 | tf_op jit(solution)/shard_map/grad_qkv/pallas_call | solution.py:111
  317.7 4.0 norm1_backward.1
  326.4 6.0 %collective-permute-done.25.refs_4_ = f32[11,1024]{1,0:T(8,128)S(1)} collective-permute-done((f32[11,1024]{1,0:T(8,128)S(1)}, f32[11,1024]{1,0:T(8,128)S(1)}, u32[]{:S(2)}, u32[]{:S(2)}) %collective-permute-start.25) | collective-permute-done | bytes 45088 | tf_op jit(solution)/shard_map/ppermute | solution.py:1120
  335.5 2.5 collective-permute-start.24
  338.9 20.9 %conv_backward.1 = (bf16[32,32,384]{2,1,0:T(8,128)(2,1)}, f32[49,384]{1,0:T(8,128)}, f32[8,384]{1,0:T(8,128)}) custom-call(s32[7]{0:T(128)} %stack.148.refs_0_, bf16[528,384]{1,0:T(8,128)(2,1)} %bitcast.155, bf16[528,384]{1,0:T(8,128)(2,1)} %bitcast.157, bf16[512,384]{1,0:T(8,128)(2,1)} %get-tuple-element.129.refs_3_, ...), custom_call_target="tpu_custom_call" | custom-call | flops 575000000 | bytes 1 | tf_op jit(solution)/shard_map/conv_backward/pallas_call | solution.py:111
  360.4 2.6 pack.1.refs_3_
  366.6 3.3 fold_qkv.1
  373.4 2.6 output_halves.1
  376.7 3.2 fold_adapt_last.1
  381.3 3.3 fold_fc_last.1
  384.6 3.4 fold_pw2_last.1
  388.0 3.4 fold_pw1_last.1
  405.4 2.9 fold_qkv_last.1
  417.1 2.5 collective-permute-done.41
  421.3 2.2 add_bitcast_fusion.1
  423.6 2.3 add_bitcast_fusion
  (263 shorter events, 96.8 us)
Async XLA Ops:
  7.2 84.1 %all-gather.5.cloned.1.call-start = ((), (), s32[]{:S(2)}) async-start(), calls=%async_computation.8 | async-start | bytes 1966080 | tf_op jit(solution)/shard_map/all_gather | solution.py:1281
  34.9 9.8 %collective-permute-start.2 = (bf16[80,1024]{1,0:T(8,128)(2,1)S(1)}, bf16[80,1024]{1,0:T(8,128)(2,1)S(1)}, u32[]{:S(2)}, u32[]{:S(2)}) collective-permute-start(bf16[80,1024]{1,0:T(8,128)(2,1)S(1)} %pad_maximum_fusion.11), channel_id=1, source_target_pairs={{0,1},{1,0},{2,3},{3,2},{4,5},{5,4},{6,7},{7,6},{8,9},{9,8},{10,11... | collective-permute-start | bytes 491528 | tf_op jit(solution)/shard_map/ppermute | solution.py:1120
  38.0 15.0 %collective-permute-start.1 = (bf16[80,1024]{1,0:T(8,128)(2,1)S(1)}, bf16[80,1024]{1,0:T(8,128)(2,1)S(1)}, u32[]{:S(2)}, u32[]{:S(2)}) collective-permute-start(bf16[80,1024]{1,0:T(8,128)(2,1)S(1)} %pad_maximum_fusion.11), channel_id=1, source_target_pairs={{0,2},{1,3},{2,0},{3,1},{4,6},{5,7},{6,4},{7,5},{8,10},{9,11},{10,... | collective-permute-start | bytes 491528 | tf_op jit(solution)/shard_map/ppermute | solution.py:1120
  40.6 12.5 %collective-permute-start = (bf16[80,1024]{1,0:T(8,128)(2,1)S(1)}, bf16[80,1024]{1,0:T(8,128)(2,1)S(1)}, u32[]{:S(2)}, u32[]{:S(2)}) collective-permute-start(bf16[80,1024]{1,0:T(8,128)(2,1)S(1)} %pad_maximum_fusion.11), channel_id=1, source_target_pairs={{0,3},{1,2},{2,1},{3,0},{4,7},{5,6},{6,5},{7,4},{8,11},{9,10},{10,... | collective-permute-start | bytes 491528 | tf_op jit(solution)/shard_map/ppermute | solution.py:1120
  40.6 131.2 %all-gather.7.cloned.1.call-start = ((), (), s32[]{:S(2)}) async-start(), calls=%async_computation.9 | async-start | bytes 1966080 | tf_op jit(solution)/shard_map/all_gather | solution.py:1281
  53.1 6.4 %collective-permute-start.9 = (bf16[4,32,1024]{2,1,0:T(8,128)(2,1)S(1)}, bf16[4,32,1024]{2,1,0:T(8,128)(2,1)S(1)}, u32[]{:S(2)}, u32[]{:S(2)}) collective-permute-start(bf16[4,32,1024]{2,1,0:T(8,128)(2,1)S(1)} %pad_maximum_fusion.10), channel_id=1, source_target_pairs={{0,16},{16,0},{1,17},{17,1},{2,18},{18,2},{3,19},{19,3},{4,20},{20... | collective-permute-start | bytes 786440 | tf_op jit(solution)/shard_map/ppermute | solution.py:1120
  55.8 12.1 %collective-permute-start.3 = (bf16[4,48,1024]{2,1,0:T(8,128)(2,1)S(1)}, bf16[4,48,1024]{2,1,0:T(8,128)(2,1)S(1)}, u32[]{:S(2)}, u32[]{:S(2)}) collective-permute-start(bf16[4,48,1024]{2,1,0:T(8,128)(2,1)S(1)} %pad_maximum_fusion.7), channel_id=1, source_target_pairs={{0,8},{4,12},{8,0},{12,4},{1,9},{5,13},{9,1},{13,5},{2,10},{6,14},... | collective-permute-start | bytes 1179656 | tf_op jit(solution)/shard_map/ppermute | solution.py:1120
  59.6 15.6 %collective-permute-start.10 = (bf16[4,2,32,1024]{3,2,0,1:T(8,128)(2,1)S(1)}, bf16[4,2,32,1024]{3,2,0,1:T(8,128)(2,1)}, u32[]{:S(2)}, u32[]{:S(2)}) collective-permute-start(bf16[4,2,32,1024]{3,2,0,1:T(8,128)(2,1)S(1)} %pad_maximum_fusion.6), channel_id=1, source_target_pairs={{0,8},{4,12},{8,0},{12,4},{1,9},{5,13},{9,1},{13,5},{2,10},{6,14},... | collective-permute-start | bytes 1572872 | tf_op jit(solution)/shard_map/ppermute | solution.py:1120
  68.0 12.2 %collective-permute-start.4 = (bf16[4,2,48,1024]{3,2,0,1:T(8,128)(2,1)S(1)}, bf16[4,2,48,1024]{3,2,0,1:T(8,128)(2,1)}, u32[]{:S(2)}, u32[]{:S(2)}) collective-permute-start(bf16[4,2,48,1024]{3,2,0,1:T(8,128)(2,1)S(1)} %pad_maximum_fusion.4), channel_id=1, source_target_pairs={{0,16},{16,0},{1,17},{17,1},{2,18},{18,2},{3,19},{19,3},{4,20},{20... | collective-permute-start | bytes 2359304 | tf_op jit(solution)/shard_map/ppermute | solution.py:1120
  78.2 9.7 %collective-permute-start.11 = (bf16[4,2,2,32,1024]{4,3,0,1,2:T(8,128)(2,1)}, bf16[4,2,2,32,1024]{4,3,0,1,2:T(8,128)(2,1)}, u32[]{:S(2)}, u32[]{:S(2)}) collective-permute-start(bf16[4,2,2,32,1024]{4,3,0,1,2:T(8,128)(2,1)} %pad_maximum_fusion.3), channel_id=1, source_target_pairs={{0,4},{4,0},{8,12},{12,8},{1,5},{5,1},{9,13},{13,9},{2,6},{6,2},{1... | collective-permute-start | bytes 3145736 | tf_op jit(solution)/shard_map/ppermute | solution.py:1120
  78.3 118.2 %reduce-scatter.5.cloned.1.call-start = ((), (), s32[]{:S(2)}) async-start(), calls=%async_computation.4 | async-start | bytes 2027520 | tf_op jit(solution)/shard_map/reduce_scatter | solution.py:1325
  82.8 30.7 %collective-permute-start.5 = (bf16[4,2,2,48,1024]{4,3,0,2,1:T(8,128)(2,1)}, bf16[4,2,2,48,1024]{4,3,0,2,1:T(8,128)(2,1)}, u32[]{:S(2)}, u32[]{:S(2)}) collective-permute-start(bf16[4,2,2,48,1024]{4,3,0,2,1:T(8,128)(2,1)} %pad_maximum_fusion.2), channel_id=1, source_target_pairs={{0,4},{4,0},{8,12},{12,8},{1,5},{5,1},{9,13},{13,9},{2,6},{6,2},{1... | collective-permute-start | bytes 4718600 | tf_op jit(solution)/shard_map/ppermute | solution.py:1120
  101.5 40.5 %collective-permute-start.8 = (bf16[576,256]{1,0:T(8,128)(2,1)}, bf16[576,256]{1,0:T(8,128)(2,1)S(1)}, u32[]{:S(2)}, u32[]{:S(2)}) collective-permute-start(bf16[576,256]{1,0:T(8,128)(2,1)} %get-tuple-element.134.refs_10_.refs_1_.refs_8_), channel_id=1, source_target_pairs={{0,3},{1,2},{2,1},{3,0},{4,7},{5,6},{6,5},{7,4},{8,11},{9,10},{10,... | collective-permute-start | bytes 884744 | tf_op jit(solution)/shard_map/ppermute | solution.py:1120
  104.6 44.9 %collective-permute-start.7 = (bf16[576,256]{1,0:T(8,128)(2,1)}, bf16[576,256]{1,0:T(8,128)(2,1)S(1)}, u32[]{:S(2)}, u32[]{:S(2)}) collective-permute-start(bf16[576,256]{1,0:T(8,128)(2,1)} %get-tuple-element.134.refs_10_.refs_1_.refs_8_), channel_id=1, source_target_pairs={{0,2},{1,3},{2,0},{3,1},{4,6},{5,7},{6,4},{7,5},{8,10},{9,11},{10,... | collective-permute-start | bytes 884744 | tf_op jit(solution)/shard_map/ppermute | solution.py:1120
  113.0 36.5 %collective-permute-start.6 = (bf16[576,256]{1,0:T(8,128)(2,1)}, bf16[576,256]{1,0:T(8,128)(2,1)S(1)}, u32[]{:S(2)}, u32[]{:S(2)}) collective-permute-start(bf16[576,256]{1,0:T(8,128)(2,1)} %get-tuple-element.134.refs_10_.refs_1_.refs_8_), channel_id=1, source_target_pairs={{0,1},{1,0},{2,3},{3,2},{4,5},{5,4},{6,7},{7,6},{8,9},{9,8},{10,11... | collective-permute-start | bytes 884744 | tf_op jit(solution)/shard_map/ppermute | solution.py:1120
  142.0 135.4 %reduce-scatter.9.cloned.1.call-start = ((), (), s32[]{:S(2)}) async-start(), calls=%async_computation.6 | async-start | bytes 2027520 | tf_op jit(solution)/shard_map/reduce_scatter | solution.py:1325
  165.7 38.0 %collective-permute-start.12 = (bf16[144,1024]{1,0:T(8,128)(2,1)}, bf16[144,1024]{1,0:T(8,128)(2,1)S(1)}, u32[]{:S(2)}, u32[]{:S(2)}) collective-permute-start(bf16[144,1024]{1,0:T(8,128)(2,1)} %get-tuple-element.150), channel_id=1, source_target_pairs={{0,1},{1,0},{2,3},{3,2},{4,5},{5,4},{6,7},{7,6},{8,9},{9,8},{10,11... | collective-permute-start | bytes 884744 | tf_op jit(solution)/shard_map/ppermute | solution.py:1120
  165.8 37.9 %collective-permute-start.13 = (bf16[144,1024]{1,0:T(8,128)(2,1)}, bf16[144,1024]{1,0:T(8,128)(2,1)S(1)}, u32[]{:S(2)}, u32[]{:S(2)}) collective-permute-start(bf16[144,1024]{1,0:T(8,128)(2,1)} %get-tuple-element.151), channel_id=1, source_target_pairs={{0,2},{1,3},{2,0},{3,1},{4,6},{5,7},{6,4},{7,5},{8,10},{9,11},{10,... | collective-permute-start | bytes 884744 | tf_op jit(solution)/shard_map/ppermute | solution.py:1120
  167.5 36.2 %collective-permute-start.14 = (bf16[144,1024]{1,0:T(8,128)(2,1)}, bf16[144,1024]{1,0:T(8,128)(2,1)S(1)}, u32[]{:S(2)}, u32[]{:S(2)}) collective-permute-start(bf16[144,1024]{1,0:T(8,128)(2,1)} %get-tuple-element.152), channel_id=1, source_target_pairs={{0,3},{1,2},{2,1},{3,0},{4,7},{5,6},{6,5},{7,4},{8,11},{9,10},{10,... | collective-permute-start | bytes 884744 | tf_op jit(solution)/shard_map/ppermute | solution.py:1120
  196.4 121.3 %reduce-scatter.11.cloned.1.call-start = ((), (), s32[]{:S(2)}) async-start(), calls=%async_computation.7 | async-start | bytes 1515520 | tf_op jit(solution)/shard_map/reduce_scatter | solution.py:1430
  208.3 42.3 %collective-permute-start.17 = (bf16[144,1024]{1,0:T(8,128)(2,1)}, bf16[144,1024]{1,0:T(8,128)(2,1)S(1)}, u32[]{:S(2)}, u32[]{:S(2)}) collective-permute-start(bf16[144,1024]{1,0:T(8,128)(2,1)} %get-tuple-element.154.refs_1_), channel_id=1, source_target_pairs={{0,3},{1,2},{2,1},{3,0},{4,7},{5,6},{6,5},{7,4},{8,11},{9,10},{10,... | collective-permute-start | bytes 884744 | tf_op jit(solution)/shard_map/ppermute | solution.py:1120
  209.6 47.2 %collective-permute-start.16 = (bf16[144,1024]{1,0:T(8,128)(2,1)}, bf16[144,1024]{1,0:T(8,128)(2,1)S(1)}, u32[]{:S(2)}, u32[]{:S(2)}) collective-permute-start(bf16[144,1024]{1,0:T(8,128)(2,1)} %get-tuple-element.154.refs_1_), channel_id=1, source_target_pairs={{0,2},{1,3},{2,0},{3,1},{4,6},{5,7},{6,4},{7,5},{8,10},{9,11},{10,... | collective-permute-start | bytes 884744 | tf_op jit(solution)/shard_map/ppermute | solution.py:1120
  213.8 43.0 %collective-permute-start.15 = (bf16[144,1024]{1,0:T(8,128)(2,1)}, bf16[144,1024]{1,0:T(8,128)(2,1)S(1)}, u32[]{:S(2)}, u32[]{:S(2)}) collective-permute-start(bf16[144,1024]{1,0:T(8,128)(2,1)} %get-tuple-element.154.refs_1_), channel_id=1, source_target_pairs={{0,1},{1,0},{2,3},{3,2},{4,5},{5,4},{6,7},{7,6},{8,9},{9,8},{10,11... | collective-permute-start | bytes 884744 | tf_op jit(solution)/shard_map/ppermute | solution.py:1120
  274.1 99.2 %reduce-scatter.7.cloned.1.call-start = ((), (), s32[]{:S(2)}) async-start(), calls=%async_computation.5 | async-start | bytes 1474560 | tf_op jit(solution)/shard_map/reduce_scatter | solution.py:1380
  274.2 23.4 %collective-permute-start.19 = (bf16[4,192,1536]{2,1,0:T(8,128)(2,1)}, bf16[4,192,1536]{2,1,0:T(8,128)(2,1)}, u32[]{:S(2)}, u32[]{:S(2)}) collective-permute-start(bf16[4,192,1536]{2,1,0:T(8,128)(2,1)} %get-tuple-element.181), channel_id=1, source_target_pairs={{0,4},{4,0},{8,12},{12,8},{1,5},{5,1},{9,13},{13,9},{2,6},{6,2},{1... | collective-permute-start | bytes 7077896 | tf_op jit(solution)/shard_map/ppermute | solution.py:1120
  274.3 28.2 %collective-permute-start.18 = (bf16[4,192,1536]{2,1,0:T(8,128)(2,1)}, bf16[4,192,1536]{2,1,0:T(8,128)(2,1)S(1)}, u32[]{:S(2)}, u32[]{:S(2)}) collective-permute-start(bf16[4,192,1536]{2,1,0:T(8,128)(2,1)} %get-tuple-element.180), channel_id=1, source_target_pairs={{0,4},{4,0},{8,12},{12,8},{1,5},{5,1},{9,13},{13,9},{2,6},{6,2},{1... | collective-permute-start | bytes 7077896 | tf_op jit(solution)/shard_map/ppermute | solution.py:1120
  274.8 10.7 %collective-permute-start.21 = (bf16[4,128,2048]{2,1,0:T(8,128)(2,1)}, bf16[4,128,2048]{2,1,0:T(8,128)(2,1)}, u32[]{:S(2)}, u32[]{:S(2)}) collective-permute-start(bf16[4,128,2048]{2,1,0:T(8,128)(2,1)} %get-tuple-element.183), channel_id=1, source_target_pairs={{0,4},{4,0},{8,12},{12,8},{1,5},{5,1},{9,13},{13,9},{2,6},{6,2},{1... | collective-permute-start | bytes 6291464 | tf_op jit(solution)/shard_map/ppermute | solution.py:1120
  274.8 15.4 %collective-permute-start.20 = (bf16[4,128,1920]{2,1,0:T(8,128)(2,1)}, bf16[4,128,1920]{2,1,0:T(8,128)(2,1)}, u32[]{:S(2)}, u32[]{:S(2)}) collective-permute-start(bf16[4,128,1920]{2,1,0:T(8,128)(2,1)} %get-tuple-element.182), channel_id=1, source_target_pairs={{0,4},{4,0},{8,12},{12,8},{1,5},{5,1},{9,13},{13,9},{2,6},{6,2},{1... | collective-permute-start | bytes 5898248 | tf_op jit(solution)/shard_map/ppermute | solution.py:1120
  294.7 40.8 %collective-permute-start.27 = (bf16[2,1,128,1920]{3,2,1,0:T(8,128)(2,1)}, bf16[2,1,128,1920]{3,2,1,0:T(8,128)(2,1)}, u32[]{:S(2)}, u32[]{:S(2)}) collective-permute-start(bf16[2,1,128,1920]{3,2,1,0:T(8,128)(2,1)} %get-tuple-element.202), channel_id=1, source_target_pairs={{0,8},{4,12},{8,0},{12,4},{1,9},{5,13},{9,1},{13,5},{2,10},{6,14},... | collective-permute-start | bytes 2949128 | tf_op jit(solution)/shard_map/ppermute | solution.py:1120
  296.1 41.8 %collective-permute-start.26 = (bf16[1,2,128,2048]{3,2,1,0:T(8,128)(2,1)}, bf16[1,2,128,2048]{3,2,1,0:T(8,128)(2,1)S(1)}, u32[]{:S(2)}, u32[]{:S(2)}) collective-permute-start(bf16[1,2,128,2048]{3,2,1,0:T(8,128)(2,1)} %get-tuple-element.201), channel_id=1, source_target_pairs={{0,16},{16,0},{1,17},{17,1},{2,18},{18,2},{3,19},{19,3},{4,20},{20... | collective-permute-start | bytes 3145736 | tf_op jit(solution)/shard_map/ppermute | solution.py:1120
  317.6 49.0 %collective-permute-start.22 = (bf16[4,128,1024]{2,1,0:T(8,128)(2,1)}, bf16[4,128,1024]{2,1,0:T(8,128)(2,1)}, u32[]{:S(2)}, u32[]{:S(2)}) collective-permute-start(bf16[4,128,1024]{2,1,0:T(8,128)(2,1)} %get-tuple-element.190), channel_id=1, source_target_pairs={{0,4},{4,0},{8,12},{12,8},{1,5},{5,1},{9,13},{13,9},{2,6},{6,2},{1... | collective-permute-start | bytes 3145736 | tf_op jit(solution)/shard_map/ppermute | solution.py:1120
  321.7 12.4 %collective-permute-start.31 = (bf16[288,256]{1,0:T(8,128)(2,1)}, bf16[288,256]{1,0:T(8,128)(2,1)S(1)}, u32[]{:S(2)}, u32[]{:S(2)}) collective-permute-start(bf16[288,256]{1,0:T(8,128)(2,1)} %get-tuple-element.211), channel_id=1, source_target_pairs={{0,16},{16,0},{1,17},{17,1},{2,18},{18,2},{3,19},{19,3},{4,20},{20... | collective-permute-start | bytes 442376 | tf_op jit(solution)/shard_map/ppermute | solution.py:1120
  324.4 8.1 %collective-permute-start.25 = (f32[11,1024]{1,0:T(8,128)S(1)}, f32[11,1024]{1,0:T(8,128)S(1)}, u32[]{:S(2)}, u32[]{:S(2)}) collective-permute-start(f32[11,1024]{1,0:T(8,128)S(1)} %concatenate.7.refs_1_), channel_id=1, source_target_pairs={{0,3},{1,2},{2,1},{3,0},{4,7},{5,6},{6,5},{7,4},{8,11},{9,10},{10,... | collective-permute-start | bytes 135176 | tf_op jit(solution)/shard_map/ppermute | solution.py:1120
  332.4 40.9 %collective-permute-start.29 = (bf16[1,2,192,1536]{3,2,1,0:T(8,128)(2,1)}, bf16[1,2,192,1536]{3,2,1,0:T(8,128)(2,1)}, u32[]{:S(2)}, u32[]{:S(2)}) collective-permute-start(bf16[1,2,192,1536]{3,2,1,0:T(8,128)(2,1)} %get-tuple-element.207), channel_id=1, source_target_pairs={{0,16},{16,0},{1,17},{17,1},{2,18},{18,2},{3,19},{19,3},{4,20},{20... | collective-permute-start | bytes 3538952 | tf_op jit(solution)/shard_map/ppermute | solution.py:1120
  334.1 39.3 %collective-permute-start.28 = (bf16[2,1,192,1536]{3,2,1,0:T(8,128)(2,1)}, bf16[2,1,192,1536]{3,2,1,0:T(8,128)(2,1)}, u32[]{:S(2)}, u32[]{:S(2)}) collective-permute-start(bf16[2,1,192,1536]{3,2,1,0:T(8,128)(2,1)} %get-tuple-element.206), channel_id=1, source_target_pairs={{0,8},{4,12},{8,0},{12,4},{1,9},{5,13},{9,1},{13,5},{2,10},{6,14},... | collective-permute-start | bytes 3538952 | tf_op jit(solution)/shard_map/ppermute | solution.py:1120
  335.5 24.3 %collective-permute-start.24 = (f32[11,1024]{1,0:T(8,128)S(1)}, f32[11,1024]{1,0:T(8,128)S(1)}, u32[]{:S(2)}, u32[]{:S(2)}) collective-permute-start(f32[11,1024]{1,0:T(8,128)S(1)} %concatenate.7.refs_1_), channel_id=1, source_target_pairs={{0,2},{1,3},{2,0},{3,1},{4,6},{5,7},{6,4},{7,5},{8,10},{9,11},{10,... | collective-permute-start | bytes 135176 | tf_op jit(solution)/shard_map/ppermute | solution.py:1120
  337.9 21.9 %collective-permute-start.23 = (f32[11,1024]{1,0:T(8,128)S(1)}, f32[11,1024]{1,0:T(8,128)S(1)}, u32[]{:S(2)}, u32[]{:S(2)}) collective-permute-start(f32[11,1024]{1,0:T(8,128)S(1)} %concatenate.7.refs_1_), channel_id=1, source_target_pairs={{0,1},{1,0},{2,3},{3,2},{4,5},{5,4},{6,7},{7,6},{8,9},{9,8},{10,11... | collective-permute-start | bytes 135176 | tf_op jit(solution)/shard_map/ppermute | solution.py:1120
  363.8 27.6 %collective-permute-start.32 = (bf16[16,32,384]{2,1,0:T(8,128)(2,1)S(1)}, bf16[16,32,384]{2,1,0:T(8,128)(2,1)S(1)}, u32[]{:S(2)}, u32[]{:S(2)}) collective-permute-start(bf16[16,32,384]{2,1,0:T(8,128)(2,1)S(1)} %dynamic-slice_bitcast_fusion.1), channel_id=1, source_target_pairs={{0,16},{16,0},{1,17},{17,1},{2,18},{18,2},{3,19},{19,3},{4,20},{20... | collective-permute-start | bytes 1179656 | tf_op jit(solution)/shard_map/ppermute | solution.py:1120
  369.9 34.7 %collective-permute-start.36 = (bf16[2,1,128,1024]{3,2,1,0:T(8,128)(2,1)}, bf16[2,1,128,1024]{3,2,1,0:T(8,128)(2,1)S(1)}, u32[]{:S(2)}, u32[]{:S(2)}) collective-permute-start(bf16[2,1,128,1024]{3,2,1,0:T(8,128)(2,1)} %get-tuple-element.214), channel_id=1, source_target_pairs={{0,8},{4,12},{8,0},{12,4},{1,9},{5,13},{9,1},{13,5},{2,10},{6,14},... | collective-permute-start | bytes 1572872 | tf_op jit(solution)/shard_map/ppermute | solution.py:1120
  371.9 21.5 %collective-permute-start.35 = (f32[40,1024]{1,0:T(8,128)S(1)}, f32[40,1024]{1,0:T(8,128)S(1)}, u32[]{:S(2)}, u32[]{:S(2)}) collective-permute-start(f32[40,1024]{1,0:T(8,128)S(1)} %add.110.refs_0_), channel_id=1, source_target_pairs={{0,16},{16,0},{1,17},{17,1},{2,18},{18,2},{3,19},{19,3},{4,20},{20... | collective-permute-start | bytes 491528 | tf_op jit(solution)/shard_map/ppermute | solution.py:1120
  376.0 27.2 %collective-permute-start.30 = (bf16[288,256]{1,0:T(8,128)(2,1)}, bf16[288,256]{1,0:T(8,128)(2,1)S(1)}, u32[]{:S(2)}, u32[]{:S(2)}) collective-permute-start(bf16[288,256]{1,0:T(8,128)(2,1)} %get-tuple-element.209), channel_id=1, source_target_pairs={{0,16},{16,0},{1,17},{17,1},{2,18},{18,2},{3,19},{19,3},{4,20},{20... | collective-permute-start | bytes 442376 | tf_op jit(solution)/shard_map/ppermute | solution.py:1120
  379.9 28.4 %collective-permute-start.39 = (bf16[1,128,1920]{2,1,0:T(8,128)(2,1)}, bf16[1,128,1920]{2,1,0:T(8,128)(2,1)S(1)}, u32[]{:S(2)}, u32[]{:S(2)}) collective-permute-start(bf16[1,128,1920]{2,1,0:T(8,128)(2,1)} %get-tuple-element.224), channel_id=1, source_target_pairs={{0,16},{16,0},{1,17},{17,1},{2,18},{18,2},{3,19},{19,3},{4,20},{20... | collective-permute-start | bytes 1474568 | tf_op jit(solution)/shard_map/ppermute | solution.py:1120
  391.4 20.3 %collective-permute-start.38 = (bf16[1,128,2048]{2,1,0:T(8,128)(2,1)}, bf16[1,128,2048]{2,1,0:T(8,128)(2,1)S(1)}, u32[]{:S(2)}, u32[]{:S(2)}) collective-permute-start(bf16[1,128,2048]{2,1,0:T(8,128)(2,1)} %get-tuple-element.222), channel_id=1, source_target_pairs={{0,8},{4,12},{8,0},{12,4},{1,9},{5,13},{9,1},{13,5},{2,10},{6,14},... | collective-permute-start | bytes 1572872 | tf_op jit(solution)/shard_map/ppermute | solution.py:1120
  393.4 27.9 %collective-permute-start.43 = (bf16[1,192,1536]{2,1,0:T(8,128)(2,1)}, bf16[1,192,1536]{2,1,0:T(8,128)(2,1)}, u32[]{:S(2)}, u32[]{:S(2)}) collective-permute-start(bf16[1,192,1536]{2,1,0:T(8,128)(2,1)} %get-tuple-element.227), channel_id=1, source_target_pairs={{0,8},{4,12},{8,0},{12,4},{1,9},{5,13},{9,1},{13,5},{2,10},{6,14},... | collective-permute-start | bytes 1769480 | tf_op jit(solution)/shard_map/ppermute | solution.py:1120
  403.2 20.4 %collective-permute-start.44 = (bf16[1,192,1536]{2,1,0:T(8,128)(2,1)}, bf16[1,192,1536]{2,1,0:T(8,128)(2,1)}, u32[]{:S(2)}, u32[]{:S(2)}) collective-permute-start(bf16[1,192,1536]{2,1,0:T(8,128)(2,1)} %get-tuple-element.229), channel_id=1, source_target_pairs={{0,16},{16,0},{1,17},{17,1},{2,18},{18,2},{3,19},{19,3},{4,20},{20... | collective-permute-start | bytes 1769480 | tf_op jit(solution)/shard_map/ppermute | solution.py:1120
  410.2 6.8 %collective-permute-start.42 = (bf16[128,384]{1,0:T(8,128)(2,1)}, bf16[128,384]{1,0:T(8,128)(2,1)}, u32[]{:S(2)}, u32[]{:S(2)}) collective-permute-start(bf16[128,384]{1,0:T(8,128)(2,1)} %get-tuple-element.308), channel_id=1, source_target_pairs={{0,3},{1,2},{2,1},{3,0},{4,7},{5,6},{6,5},{7,4},{8,11},{9,10},{10,... | collective-permute-start | bytes 294920 | tf_op jit(solution)/shard_map/ppermute | solution.py:1120
  411.8 7.7 %collective-permute-start.41 = (bf16[128,384]{1,0:T(8,128)(2,1)S(1)}, bf16[128,384]{1,0:T(8,128)(2,1)S(1)}, u32[]{:S(2)}, u32[]{:S(2)}) collective-permute-start(bf16[128,384]{1,0:T(8,128)(2,1)S(1)} %get-tuple-element.309), channel_id=1, source_target_pairs={{0,2},{1,3},{2,0},{3,1},{4,6},{5,7},{6,4},{7,5},{8,10},{9,11},{10,... | collective-permute-start | bytes 294920 | tf_op jit(solution)/shard_map/ppermute | solution.py:1120
  414.9 11.0 %collective-permute-start.37 = (bf16[1,128,1024]{2,1,0:T(8,128)(2,1)}, bf16[1,128,1024]{2,1,0:T(8,128)(2,1)S(1)}, u32[]{:S(2)}, u32[]{:S(2)}) collective-permute-start(bf16[1,128,1024]{2,1,0:T(8,128)(2,1)} %get-tuple-element.220), channel_id=1, source_target_pairs={{0,16},{16,0},{1,17},{17,1},{2,18},{18,2},{3,19},{19,3},{4,20},{20... | collective-permute-start | bytes 786440 | tf_op jit(solution)/shard_map/ppermute | solution.py:1120
  (47 other events, 349.1 us)
Sparse Core Ops, SparseCore 0:
  40.7 40.0 all-gather.4
  82.3 61.7 all-gather.6
  146.4 46.0 reduce-scatter.4
  196.5 52.9 reduce-scatter.8
  274.3 28.6 reduce-scatter.10
  305.3 29.3 reduce-scatter.6
